TPU v7x, 512 devices: a whole 4x4x16 slice. The times are simulated.
512 devices in a mesh: section: 8 (over z_hi, core), dp: 64 (over y, x, z_lo).
Axes of the slice: x: 4, y: 4, z: 16 (z_hi: 4, z_lo: 4; z = z_hi * 4 + z_lo), core: 2. Of those that a mesh axis runs over, the one named last changes fastest.
Arguments:
- encoder_embed: bfloat16 [128, 64, 2048], P('dp'), may hold values from -6 to 6
- decoder_embed: bfloat16 [128, 64, 2048], P('dp'), may hold values from -6 to 6
- section_weights: bfloat16 [8, 2, 2048, 1024], P('section', None, 'dp'), may hold values from -2 to 2
- norm_gains: float32 [5, 2048], replicated, may hold values from 0.1 to 1.9
- input_lengths: int32 [128], P('dp'), may hold values from 16 to 64
- target_lengths: int32 [128], P('dp'), may hold values from 16 to 64
Outputs:
- section_out: bfloat16 [8, 128, 64, 2048], P('section', 'dp')
All inputs are finite; a program needn't handle non-finite values.
Results may differ from a plain program's by a relative error of at most 0.039.
Values may be sent and summed in bfloat16 or wider, within the bound.
No kernel may reach another device: no remote copies, remote signals or barrier semaphores. Data moves between devices by JAX's collectives and lax.ppermute only.
A program may use at most 64 MiB of HBM per device.

v0:
```python
import jax
import jax.numpy as jnp
from jax import lax
from jax.sharding import PartitionSpec as P

HEAD_DIM = 128


def spread(array, axis, root):
    mine = lax.axis_index(axis) == root
    return lax.psum(jnp.where(mine, array, jnp.zeros_like(array)), axis)


def passed_along(array, axis, by):
    count = lax.axis_size(axis)
    pairs = [(i, i + by) for i in range(count) if 0 <= i + by < count]
    return lax.ppermute(array, axis, pairs)


def rms_scale(values, norm_gain):
    widened = values.astype(jnp.float32)
    mean_square = jnp.mean(widened * widened, axis=-1, keepdims=True)
    return (widened * lax.rsqrt(mean_square + 1e-06) * norm_gain).astype(jnp.bfloat16)


def layer_kind(sublayer, enc_layers):
    if sublayer < enc_layers:
        return "encoder"
    if (sublayer - enc_layers) % 2 == 0:
        return "self"
    return "cross"


def soft_attention(query_rows, key_rows, key_lengths, causal):
    doc_count, row_count, inner_width = query_rows.shape
    head_count = inner_width // HEAD_DIM
    query_heads = query_rows.reshape(doc_count, row_count, head_count, HEAD_DIM)
    key_heads = key_rows.reshape(doc_count, row_count, head_count, HEAD_DIM)
    scores = jnp.einsum(
        "bqhe,bkhe->bhqk", query_heads, key_heads, preferred_element_type=jnp.float32
    ) * HEAD_DIM ** (-0.5)
    positions = jnp.arange(row_count, dtype=jnp.int32)
    key_live = (positions[None, :] < key_lengths[:, None])[:, None, None, :]
    if causal:
        key_live = key_live & (positions[None, None, None, :] <= positions[None, None, :, None])
    scores = jnp.where(key_live, scores, -1e30)
    largest = jnp.max(scores, axis=-1, keepdims=True)
    raised = jnp.exp(scores - largest)
    return (raised / jnp.sum(raised, axis=-1, keepdims=True)).astype(jnp.bfloat16)


def front_block(stream, memory, weight_pair, norm_gain, layer_type, key_lengths):
    source = rms_scale(stream, norm_gain)
    key_source = memory if layer_type == "cross" else source
    doc_count, row_count, model_width = source.shape
    query_flat = source.reshape(doc_count * row_count, model_width)
    key_flat = key_source.reshape(doc_count * row_count, model_width)
    query_rows = jnp.dot(query_flat, weight_pair[0], preferred_element_type=jnp.float32)
    key_rows = jnp.dot(key_flat, weight_pair[1], preferred_element_type=jnp.float32)
    query_rows = query_rows.astype(jnp.bfloat16).reshape(doc_count, row_count, -1)
    key_rows = key_rows.astype(jnp.bfloat16).reshape(doc_count, row_count, -1)
    return soft_attention(query_rows, key_rows, key_lengths, layer_type == "self")


def back_block(stream, soft_weights, memory, weight_pair, norm_gain, layer_type, row_lengths):
    value_source = memory if layer_type == "cross" else rms_scale(stream, norm_gain)
    doc_count, row_count, model_width = value_source.shape
    value_flat = value_source.reshape(doc_count * row_count, model_width)
    inner_width = weight_pair.shape[2]
    head_count = inner_width // HEAD_DIM
    value_rows = jnp.dot(value_flat, weight_pair[0], preferred_element_type=jnp.float32)
    value_heads = value_rows.astype(jnp.bfloat16).reshape(
        doc_count, row_count, head_count, HEAD_DIM
    )
    mixed_rows = jnp.einsum(
        "bhqk,bkhe->bqhe", soft_weights, value_heads, preferred_element_type=jnp.float32
    ).astype(jnp.bfloat16)
    mixed_rows = mixed_rows.reshape(doc_count * row_count, inner_width)
    head_term = lax.dot_general(
        mixed_rows, weight_pair[1], (((1,), (1,)), ((), ())), preferred_element_type=jnp.float32
    )
    head_term = head_term.reshape(doc_count, row_count, model_width)
    positions = jnp.arange(row_count, dtype=jnp.int32)
    row_live = (positions[None, :] < row_lengths[:, None])[:, :, None]
    head_term = jnp.where(row_live, head_term, 0.0)
    return (stream.astype(jnp.float32) + head_term).astype(jnp.bfloat16)


def section_runner(section_id, per_section, enc_layers, sublayers, norm_gains):

    def run_blocks(carried, context, all_weights):
        stream, soft_weights, memory = carried
        decoder_rows, input_lengths, target_lengths = context
        block_index = section_id * per_section
        sublayer = block_index // 2
        layer_type = layer_kind(sublayer, enc_layers)
        weight_pair = all_weights[0]
        norm_gain = norm_gains[sublayer]
        if block_index % 2 == 0:
            if sublayer == enc_layers:
                stream = decoder_rows
            key_lengths = target_lengths if layer_type == "self" else input_lengths
            soft_weights = front_block(
                stream, memory, weight_pair, norm_gain, layer_type, key_lengths
            )
        else:
            row_lengths = input_lengths if layer_type == "encoder" else target_lengths
            stream = back_block(
                stream, soft_weights, memory, weight_pair, norm_gain, layer_type, row_lengths
            )
            if sublayer == enc_layers - 1:
                memory = rms_scale(stream, norm_gains[sublayers])
        return (stream, soft_weights, memory)

    return run_blocks


def keep_carried(carried, context, all_weights):
    return carried


def on_device(
    encoder_embed, decoder_embed, section_weights, norm_gains, input_lengths, target_lengths
):
    section_total = lax.axis_size("section")
    enc_layers = max(1, section_total // 4)
    dec_layers = max(1, section_total // 8)
    sublayers = enc_layers + 2 * dec_layers
    per_section = section_weights.shape[0]
    my_section = lax.axis_index("section")
    doc_count, row_count, model_width = encoder_embed.shape
    head_count = section_weights.shape[3] // HEAD_DIM
    joined = lax.all_gather(section_weights, "dp", axis=2, tiled=True)
    all_weights = tuple((joined[local_index] for local_index in range(per_section)))
    runners = [
        section_runner(section_id, per_section, enc_layers, sublayers, norm_gains)
        for section_id in range(section_total)
    ]
    context = (decoder_embed, input_lengths, target_lengths)
    blank_soft = jnp.zeros((doc_count, head_count, row_count, row_count), jnp.bfloat16)
    carried = (encoder_embed, blank_soft, jnp.zeros_like(encoder_embed))
    kept_rows = encoder_embed
    enc_owner = (2 * enc_layers - 1) // per_section
    for section_id in range(section_total):
        carried = lax.cond(
            my_section == section_id,
            runners[section_id],
            keep_carried,
            carried,
            context,
            all_weights,
        )
        kept_rows = jnp.where(my_section == section_id, carried[0], kept_rows)
        if section_id == enc_owner:
            memory = spread(carried[2], "section", enc_owner)
            carried = (carried[0], carried[1], memory)
        if section_id + 1 < section_total:
            stream, soft_weights = passed_along((carried[0], carried[1]), "section", 1)
            carried = (stream, soft_weights, carried[2])
    return kept_rows[None]


def solution(mesh):
    in_specs = (
        P("dp", None, None),
        P("dp", None, None),
        P("section", None, "dp", None),
        P(),
        P("dp"),
        P("dp"),
    )
    out_specs = P("section", "dp", None, None)
    return jax.shard_map(
        on_device, mesh=mesh, in_specs=in_specs, out_specs=out_specs, check_vma=False
    )
```

profile of v0, /device:TPU:481, one launch (start us, length us, event | category | flops | bytes accessed | tf_op | source)
XLA Modules:
  0.0 763.8 jit_solution(7504192073810292992)
XLA Ops:
  6.5 0.7 all-gather.2.cloned.1.call-update
  7.3 1.3 collective-permute-start
  8.6 341.3 %all-gather.2.cloned.1.call-done = bf16[1,2,2048,1024]{3,2,1,0:T(8,128)(2,1)} async-done(((bf16[1,2,32,1024]{3,2,1,0:T(8,128)(2,1)}), bf16[1,2,2048,1024]{3,2,1,0:T(8,128)(2,1)}) %all-gather.2.cloned.1.call-update) | async-done | bytes 8388624 | tf_op jit(solution)/shard_map/all_gather | solution.py:133
  350.0 1.3 collective-permute-start.1
  351.3 47.0 %collective-permute-done.1 = bf16[2,8,64,64]{2,3,1,0:T(8,128)(2,1)S(1)} collective-permute-done((bf16[2,8,64,64]{2,3,1,0:T(8,128)(2,1)S(1)}, bf16[2,8,64,64]{2,3,1,0:T(8,128)(2,1)S(1)}, u32[]{:S(2)}, u32[]{:S(2)}) %collective-permute-start.1) | collective-permute-done | bytes 131104 | tf_op jit(solution)/shard_map/ppermute | solution.py:17
  398.2 1.3 collective-permute-start.2
  399.5 16.4 %collective-permute-done.2 = bf16[2,64,2048]{2,1,0:T(8,128)(2,1)S(1)} collective-permute-done((bf16[2,64,2048]{2,1,0:T(8,128)(2,1)S(1)}, bf16[2,64,2048]{2,1,0:T(8,128)(2,1)S(1)}, u32[]{:S(2)}, u32[]{:S(2)}) %collective-permute-start.2) | collective-permute-done | bytes 524320 | tf_op jit(solution)/shard_map/ppermute | solution.py:17
  415.9 1.3 collective-permute-start.3
  417.2 1.3 collective-permute-start.4
  418.5 46.3 %collective-permute-done.4 = bf16[2,8,64,64]{2,3,1,0:T(8,128)(2,1)S(1)} collective-permute-done((bf16[2,8,64,64]{2,3,1,0:T(8,128)(2,1)S(1)}, bf16[2,8,64,64]{2,3,1,0:T(8,128)(2,1)S(1)}, u32[]{:S(2)}, u32[]{:S(2)}) %collective-permute-start.4) | collective-permute-done | bytes 131104 | tf_op jit(solution)/shard_map/ppermute | solution.py:17
  464.9 1.3 collective-permute-start.5
  466.1 33.5 %collective-permute-done.5 = bf16[2,8,64,64]{2,3,1,0:T(8,128)(2,1)S(1)} collective-permute-done((bf16[2,8,64,64]{2,3,1,0:T(8,128)(2,1)S(1)}, bf16[2,8,64,64]{2,3,1,0:T(8,128)(2,1)S(1)}, u32[]{:S(2)}, u32[]{:S(2)}) %collective-permute-start.5) | collective-permute-done | bytes 131104 | tf_op jit(solution)/shard_map/ppermute | solution.py:17
  499.7 1.4 collective-permute-start.6
  501.1 1.3 collective-permute-start.7
  502.4 25.3 %collective-permute-done.7 = bf16[2,8,64,64]{2,3,1,0:T(8,128)(2,1)} collective-permute-done((bf16[2,8,64,64]{2,3,1,0:T(8,128)(2,1)S(1)}, bf16[2,8,64,64]{2,3,1,0:T(8,128)(2,1)}, u32[]{:S(2)}, u32[]{:S(2)}) %collective-permute-start.7) | collective-permute-done | bytes 131104 | tf_op jit(solution)/shard_map/ppermute | solution.py:17
  528.0 1.4 collective-permute-start.8
  529.4 1.3 collective-permute-start.9
  530.7 61.0 %collective-permute-done.9 = bf16[2,8,64,64]{2,3,1,0:T(8,128)(2,1)S(1)} collective-permute-done((bf16[2,8,64,64]{2,3,1,0:T(8,128)(2,1)}, bf16[2,8,64,64]{2,3,1,0:T(8,128)(2,1)S(1)}, u32[]{:S(2)}, u32[]{:S(2)}) %collective-permute-start.9) | collective-permute-done | bytes 131104 | tf_op jit(solution)/shard_map/ppermute | solution.py:17
  591.8 1.4 collective-permute-start.10
  593.2 0.8 broadcast_select_fusion
  594.1 14.6 %collective-permute-done.10 = bf16[2,64,2048]{2,1,0:T(8,128)(2,1)S(1)} collective-permute-done((bf16[2,64,2048]{2,1,0:T(8,128)(2,1)S(1)}, bf16[2,64,2048]{2,1,0:T(8,128)(2,1)S(1)}, u32[]{:S(2)}, u32[]{:S(2)}) %collective-permute-start.10) | collective-permute-done | bytes 524320 | tf_op jit(solution)/shard_map/ppermute | solution.py:17
  608.7 1.3 collective-permute-start.11
  610.0 1.3 collective-permute-start.12
  611.3 119.1 %all-reduce.2.cloned.1.call-done = bf16[2,64,2048]{2,1,0:T(8,128)(2,1)} async-done(((bf16[2,64,2048]{2,1,0:T(8,128)(2,1)}), bf16[2,64,2048]{2,1,0:T(8,128)(2,1)}) %all-reduce.2.cloned.1.call-update) | async-done | bytes 524304 | tf_op jit(solution)/shard_map/psum | solution.py:11
  730.4 1.9 copy.43
  732.2 1.3 collective-permute-start.13
  733.5 13.2 %collective-permute-done.13 = bf16[2,8,64,64]{3,2,1,0:T(8,128)(2,1)S(1)} collective-permute-done((bf16[2,8,64,64]{3,2,1,0:T(8,128)(2,1)}, bf16[2,8,64,64]{3,2,1,0:T(8,128)(2,1)S(1)}, u32[]{:S(2)}, u32[]{:S(2)}) %collective-permute-start.13) | collective-permute-done | bytes 131104 | tf_op jit(solution)/shard_map/ppermute | solution.py:17
  746.8 8.1 %conditional.15 = (bf16[2,64,2048]{2,1,0:T(8,128)(2,1)}) conditional(s32[]{:T(128)} %convert_element_type.162, bf16[2,64,2048]{2,1,0:T(8,128)(2,1)} %collective-permute-done.11, (bf16[2,64,2048]{2,1,0:T(8,128)(2,1)}, s32[2]{0:T(128)S(1)}, bf16[2,64,2048]{2,1,0:T(8,128)(2,1)}, bf16[2,2048,1024]{2,1,0:T(8,128)(2,1)}, ...), branch_computations={%region_31.32_spmd, %region_32.33_spmd} | conditional | flops 1091829888 | bytes 11665680 | solution.py:145
  746.9 3.1 fusion.230
  750.0 0.2 fusion.229
  750.2 4.7 fusion.223
  754.9 2.0 select_bitcast_fusion
  (32 shorter events, 0.6 us)
Async XLA Ops:
  6.5 343.4 %all-gather.2.cloned.1.call-start = ((), (), s32[]{:S(2)}) async-start(), calls=%async_computation | async-start | bytes 8519680 | tf_op jit(solution)/shard_map/all_gather | solution.py:133
  7.3 723.1 %all-reduce.2.cloned.1.call-start = ((), (), s32[]{:S(2)}) async-start(), calls=%async_computation.1 | async-start | bytes 1048576 | tf_op jit(solution)/shard_map/psum | solution.py:11
  7.3 344.0 %collective-permute-start = (bf16[2,64,2048]{2,1,0:T(8,128)(2,1)}, bf16[2,64,2048]{2,1,0:T(8,128)(2,1)S(1)}, u32[]{:S(2)}, u32[]{:S(2)}) collective-permute-start(bf16[2,64,2048]{2,1,0:T(8,128)(2,1)} %param.22), channel_id=1, source_target_pairs={{0,64},{64,128},{128,192},{192,256},{256,320},{320,384},{384,448},... | collective-permute-start | bytes 1572872 | tf_op jit(solution)/shard_map/ppermute | solution.py:17
  350.0 48.3 %collective-permute-start.1 = (bf16[2,8,64,64]{2,3,1,0:T(8,128)(2,1)S(1)}, bf16[2,8,64,64]{2,3,1,0:T(8,128)(2,1)S(1)}, u32[]{:S(2)}, u32[]{:S(2)}) collective-permute-start(bf16[2,8,64,64]{2,3,1,0:T(8,128)(2,1)S(1)} %get-tuple-element.196), channel_id=1, source_target_pairs={{0,64},{64,128},{128,192},{192,256},{256,320},{320,384},{384,448},... | collective-permute-start | bytes 393224 | tf_op jit(solution)/shard_map/ppermute | solution.py:17
  398.2 17.7 %collective-permute-start.2 = (bf16[2,64,2048]{2,1,0:T(8,128)(2,1)S(1)}, bf16[2,64,2048]{2,1,0:T(8,128)(2,1)S(1)}, u32[]{:S(2)}, u32[]{:S(2)}) collective-permute-start(bf16[2,64,2048]{2,1,0:T(8,128)(2,1)S(1)} %get-tuple-element.197), channel_id=1, source_target_pairs={{0,64},{64,128},{128,192},{192,256},{256,320},{320,384},{384,448},... | collective-permute-start | bytes 1572872 | tf_op jit(solution)/shard_map/ppermute | solution.py:17
  415.9 83.7 %collective-permute-start.3 = (bf16[2,64,2048]{2,1,0:T(8,128)(2,1)S(1)}, bf16[2,64,2048]{2,1,0:T(8,128)(2,1)S(1)}, u32[]{:S(2)}, u32[]{:S(2)}) collective-permute-start(bf16[2,64,2048]{2,1,0:T(8,128)(2,1)S(1)} %collective-permute-done.2), channel_id=1, source_target_pairs={{0,64},{64,128},{128,192},{192,256},{256,320},{320,384},{384,448},... | collective-permute-start | bytes 1572872 | tf_op jit(solution)/shard_map/ppermute | solution.py:17
  417.2 47.6 %collective-permute-start.4 = (bf16[2,8,64,64]{2,3,1,0:T(8,128)(2,1)S(1)}, bf16[2,8,64,64]{2,3,1,0:T(8,128)(2,1)S(1)}, u32[]{:S(2)}, u32[]{:S(2)}) collective-permute-start(bf16[2,8,64,64]{2,3,1,0:T(8,128)(2,1)S(1)} %collective-permute-done.1), channel_id=1, source_target_pairs={{0,64},{64,128},{128,192},{192,256},{256,320},{320,384},{384,448},... | collective-permute-start | bytes 393224 | tf_op jit(solution)/shard_map/ppermute | solution.py:17
  464.9 34.8 %collective-permute-start.5 = (bf16[2,8,64,64]{2,3,1,0:T(8,128)(2,1)S(1)}, bf16[2,8,64,64]{2,3,1,0:T(8,128)(2,1)S(1)}, u32[]{:S(2)}, u32[]{:S(2)}) collective-permute-start(bf16[2,8,64,64]{2,3,1,0:T(8,128)(2,1)S(1)} %get-tuple-element.198), channel_id=1, source_target_pairs={{0,64},{64,128},{128,192},{192,256},{256,320},{320,384},{384,448},... | collective-permute-start | bytes 393224 | tf_op jit(solution)/shard_map/ppermute | solution.py:17
  499.6 28.1 %copy-start = (bf16[2,64,2048]{2,1,0:T(8,128)(2,1)S(1)}, bf16[2,64,2048]{2,1,0:T(8,128)(2,1)}, u32[]{:S(2)}) copy-start(bf16[2,64,2048]{2,1,0:T(8,128)(2,1)} %param.23) | copy-start | bytes 1572868
  499.6 28.2 %copy-start.8 = (s32[2]{0:T(128)S(1)}, s32[2]{0:T(128)}, u32[]{:S(2)}) copy-start(s32[2]{0:T(128)} %param.27) | copy-start | bytes 28
  499.7 28.1 %copy-start.2 = (bf16[2,64,2048]{2,1,0:T(8,128)(2,1)}, bf16[2,64,2048]{2,1,0:T(8,128)(2,1)S(1)}, u32[]{:S(2)}) copy-start(bf16[2,64,2048]{2,1,0:T(8,128)(2,1)S(1)} %get-tuple-element.151) | copy-start | bytes 1572868
  499.7 28.1 %collective-permute-start.6 = (bf16[2,64,2048]{2,1,0:T(8,128)(2,1)S(1)}, bf16[2,64,2048]{2,1,0:T(8,128)(2,1)}, u32[]{:S(2)}, u32[]{:S(2)}) collective-permute-start(bf16[2,64,2048]{2,1,0:T(8,128)(2,1)S(1)} %get-tuple-element.148), channel_id=1, source_target_pairs={{0,64},{64,128},{128,192},{192,256},{256,320},{320,384},{384,448},... | collective-permute-start | bytes 1572872 | tf_op jit(solution)/shard_map/ppermute | solution.py:17
  501.1 26.6 %collective-permute-start.7 = (bf16[2,8,64,64]{2,3,1,0:T(8,128)(2,1)S(1)}, bf16[2,8,64,64]{2,3,1,0:T(8,128)(2,1)}, u32[]{:S(2)}, u32[]{:S(2)}) collective-permute-start(bf16[2,8,64,64]{2,3,1,0:T(8,128)(2,1)S(1)} %collective-permute-done.5), channel_id=1, source_target_pairs={{0,64},{64,128},{128,192},{192,256},{256,320},{320,384},{384,448},... | collective-permute-start | bytes 393224 | tf_op jit(solution)/shard_map/ppermute | solution.py:17
  528.0 65.2 %copy-start.3 = (bf16[2,64,2048]{2,1,0:T(8,128)(2,1)S(1)}, bf16[2,64,2048]{2,1,0:T(8,128)(2,1)}, u32[]{:S(2)}) copy-start(bf16[2,64,2048]{2,1,0:T(8,128)(2,1)} %copy-done.2) | copy-start | bytes 1572868
  528.0 63.8 %collective-permute-start.8 = (bf16[2,64,2048]{2,1,0:T(8,128)(2,1)}, bf16[2,64,2048]{2,1,0:T(8,128)(2,1)S(1)}, u32[]{:S(2)}, u32[]{:S(2)}) collective-permute-start(bf16[2,64,2048]{2,1,0:T(8,128)(2,1)} %get-tuple-element.149), channel_id=1, source_target_pairs={{0,64},{64,128},{128,192},{192,256},{256,320},{320,384},{384,448},... | collective-permute-start | bytes 1572872 | tf_op jit(solution)/shard_map/ppermute | solution.py:17
  529.4 62.4 %collective-permute-start.9 = (bf16[2,8,64,64]{2,3,1,0:T(8,128)(2,1)}, bf16[2,8,64,64]{2,3,1,0:T(8,128)(2,1)S(1)}, u32[]{:S(2)}, u32[]{:S(2)}) collective-permute-start(bf16[2,8,64,64]{2,3,1,0:T(8,128)(2,1)} %get-tuple-element.150), channel_id=1, source_target_pairs={{0,64},{64,128},{128,192},{192,256},{256,320},{320,384},{384,448},... | collective-permute-start | bytes 393224 | tf_op jit(solution)/shard_map/ppermute | solution.py:17
  591.8 138.6 %copy-start.7 = (s32[2]{0:T(128)S(1)}, s32[2]{0:T(128)}, u32[]{:S(2)}) copy-start(s32[2]{0:T(128)} %param.26) | copy-start | bytes 28
  591.8 16.9 %collective-permute-start.10 = (bf16[2,64,2048]{2,1,0:T(8,128)(2,1)S(1)}, bf16[2,64,2048]{2,1,0:T(8,128)(2,1)S(1)}, u32[]{:S(2)}, u32[]{:S(2)}) collective-permute-start(bf16[2,64,2048]{2,1,0:T(8,128)(2,1)S(1)} %get-tuple-element.200), channel_id=1, source_target_pairs={{0,64},{64,128},{128,192},{192,256},{256,320},{320,384},{384,448},... | collective-permute-start | bytes 1572872 | tf_op jit(solution)/shard_map/ppermute | solution.py:17
  608.7 138.1 %collective-permute-start.11 = (bf16[2,64,2048]{2,1,0:T(8,128)(2,1)S(1)}, bf16[2,64,2048]{2,1,0:T(8,128)(2,1)}, u32[]{:S(2)}, u32[]{:S(2)}) collective-permute-start(bf16[2,64,2048]{2,1,0:T(8,128)(2,1)S(1)} %collective-permute-done.10), channel_id=1, source_target_pairs={{0,64},{64,128},{128,192},{192,256},{256,320},{320,384},{384,448},... | collective-permute-start | bytes 1572872 | tf_op jit(solution)/shard_map/ppermute | solution.py:17
  610.0 120.4 %collective-permute-start.12 = (bf16[2,8,64,64]{2,3,1,0:T(8,128)(2,1)S(1)}, bf16[2,8,64,64]{2,3,1,0:T(8,128)(2,1)}, u32[]{:S(2)}, u32[]{:S(2)}) collective-permute-start(bf16[2,8,64,64]{2,3,1,0:T(8,128)(2,1)S(1)} %collective-permute-done.9), channel_id=1, source_target_pairs={{0,64},{64,128},{128,192},{192,256},{256,320},{320,384},{384,448},... | collective-permute-start | bytes 393224 | tf_op jit(solution)/shard_map/ppermute | solution.py:17
  730.4 24.5 %copy-start.1 = (bf16[2,64,2048]{2,1,0:T(8,128)(2,1)S(1)}, bf16[2,64,2048]{2,1,0:T(8,128)(2,1)}, u32[]{:S(2)}) copy-start(bf16[2,64,2048]{2,1,0:T(8,128)(2,1)} %param.22) | copy-start | bytes 1572868
  732.2 14.5 %collective-permute-start.13 = (bf16[2,8,64,64]{3,2,1,0:T(8,128)(2,1)}, bf16[2,8,64,64]{3,2,1,0:T(8,128)(2,1)S(1)}, u32[]{:S(2)}, u32[]{:S(2)}) collective-permute-start(bf16[2,8,64,64]{3,2,1,0:T(8,128)(2,1)} %copy.43), channel_id=1, source_target_pairs={{0,64},{64,128},{128,192},{192,256},{256,320},{320,384},{384,448},... | collective-permute-start | bytes 393224 | tf_op jit(solution)/shard_map/ppermute | solution.py:17
Sparse Core Ops, SparseCore 0:
  9.4 340.4 all-gather.1
  594.2 136.1 all-reduce.1
where the time goes:
time: 772 us; the launch traced here: 764 us
  waiting for transfers between devices  719 us (93%)
  starting transfers between devices  18.5 us (2%)
  between operations  13.6 us (2%)
  matrix products  7.98 us (1%)
    all_gather x1, waiting for transfers between devices, on_device(): joined = lax.all_gather(section_weights, 'dp', axis=2, tiled=True)  341 us
    ppermute x14, waiting for transfers between devices, passed_along(): return lax.ppermute(array, axis, pairs)  257 us
    psum x1, waiting for transfers between devices, spread(): return lax.psum(jnp.where(mine, array, jnp.zeros_like(array)), axis)  119 us
    ppermute x14, starting transfers between devices, passed_along(): return lax.ppermute(array, axis, pairs)  18.4 us
  transfers between devices with their start and end apart: 16, of which 10 were waited for; matrix products, arithmetic and copies ran while one was open for 0% of the time, Pallas kernels for 0%

commit v1 on v0

v1 whole, which is shorter than its diff:
```python
import jax
import jax.numpy as jnp
from jax import lax
from jax.experimental import pallas as pl
from jax.experimental.pallas import tpu as pltpu
from jax.sharding import Mesh, PartitionSpec as P

HEAD_DIM = 128
SIDE = 4
TURNS = (0, -1, 1, 2)
AXES = ("zh", "core", "y", "x", "zl")
DP = ("y", "x", "zl")
SECTION = ("zh", "core")
F32 = jnp.float32
BF16 = jnp.bfloat16


def shift(array, axis, by):
    return lax.ppermute(array, axis, [(i, (i + by) % SIDE) for i in range(SIDE)])


def dot(a, b):
    return jnp.dot(a, b, preferred_element_type=F32)


def dot_t(a, b):
    return lax.dot_general(a, b, (((1,), (1,)), ((), ())), preferred_element_type=F32)


def rms(values, gain):
    mean_square = jnp.mean(values * values, axis=-1, keepdims=True)
    return (values * lax.rsqrt(mean_square + 1e-06) * gain).astype(BF16)


def sublayer_kernel(cross, last, *refs):
    refs = list(refs)
    scal = refs.pop(0)
    gains, mine, other = refs[:3]
    refs = refs[3:]
    if cross:
        mem_mine, mem_other = refs[:2]
        refs = refs[2:]
    a_refs, b_refs = refs[:5], refs[5:10]
    refs = refs[10:]
    out_mine, out_other = refs[:2]
    h3, m3, t3 = refs[2:]
    rows = mine.shape[0]
    x, y, sub, causal, len_mine, len_other = (scal[i] for i in range(6))
    gain = gains[pl.ds(sub, 1), :]
    for part, ref in enumerate((mine, other)):
        h = rms(ref[...].astype(F32), gain)
        for i in range(16):
            h3[i, part * rows:(part + 1) * rows, :] = h[:, i * 128:(i + 1) * 128]
    kv3 = h3
    if cross:
        kv3 = m3
        for part, ref in enumerate((mem_mine, mem_other)):
            for i in range(16):
                m3[i, part * rows:(part + 1) * rows, :] = ref[:, i * 128:(i + 1) * 128]

    def blk(dy, dx):
        return lax.rem(y + dy + SIDE, SIDE) * SIDE + lax.rem(x + dx + SIDE, SIDE)

    def piece(group, turn, which):
        own, plus, minus, far0, far1 = group
        if turn == 2:
            return (far0, far1)[which][0]
        return {0: own, -1: plus, 1: minus}[turn][which]

    q = k = v = None
    for turn in TURNS:
        cols = [blk(turn, d) for d in TURNS]
        hq = jnp.concatenate([h3[c] for c in cols], axis=1)
        hk = jnp.concatenate([kv3[c] for c in cols], axis=1) if cross else hq
        dq, dk = dot(hq, piece(a_refs, turn, 0)), dot(hk, piece(a_refs, turn, 1))
        cols = [blk(d, turn) for d in TURNS]
        dv = dot(jnp.concatenate([kv3[c] for c in cols], axis=1), piece(b_refs, turn, 0))
        q, k, v = (dq, dk, dv) if q is None else (q + dq, k + dk, v + dv)
    q, k, v = q.astype(BF16), k.astype(BF16), v.astype(BF16)
    r = lax.broadcasted_iota(jnp.int32, (2 * rows, 2 * rows), 0)
    c = lax.broadcasted_iota(jnp.int32, (2 * rows, 2 * rows), 1)
    first = c < rows
    live = (r < rows) == first
    key_at = jnp.where(first, c, c - rows)
    live = live & (key_at < jnp.where(first, len_mine, len_other))
    live = live & ((c <= r) | (causal == 0))
    mixed = []
    for head in range(4):
        at = slice(head * HEAD_DIM, (head + 1) * HEAD_DIM)
        s = dot_t(q[:, at], k[:, at]) * HEAD_DIM ** (-0.5)
        s = jnp.where(live, s, -1e30)
        e = jnp.exp(s - jnp.max(s, axis=-1, keepdims=True))
        p = (e / jnp.sum(e, axis=-1, keepdims=True)).astype(BF16)
        mixed.append(dot(p, v[:, at]).astype(BF16))
    mixed = jnp.concatenate(mixed, axis=1)
    for turn in TURNS:
        t = dot_t(mixed, piece(b_refs, turn, 1))
        for j, d in enumerate(TURNS):
            t3[blk(d, turn)] = t[:, j * 128:(j + 1) * 128]
    for i in range(16):
        at = slice(i * 128, (i + 1) * 128)
        out_mine[:, at] = t3[i, :rows, :].astype(out_mine.dtype)
        out_other[:, at] = t3[i, rows:, :].astype(out_other.dtype)


def sublayer(cross, last, scal, gains, streams, mem, a_parts, b_parts):
    import functools
    rows, width = streams[0].shape
    vmem = pl.BlockSpec(memory_space=pltpu.VMEM)
    operands = [gains, *streams, *mem, *a_parts, *b_parts]
    return pl.pallas_call(
        functools.partial(sublayer_kernel, cross, last),
        out_shape=(
            jax.ShapeDtypeStruct((rows, width), F32),
            jax.ShapeDtypeStruct((rows, width), BF16),
        ),
        in_specs=[pl.BlockSpec(memory_space=pltpu.SMEM)] + [vmem] * len(operands),
        out_specs=(vmem, vmem),
        scratch_shapes=[
            pltpu.VMEM((16, 2 * rows, 128), BF16),
            pltpu.VMEM((16, 2 * rows, 128) if cross else (1, 16, 128), BF16),
            pltpu.VMEM((16, 2 * rows, 128), F32),
        ],
        compiler_params=pltpu.CompilerParams(vmem_limit_bytes=40 * 1024 * 1024),
        cost_estimate=pl.CostEstimate(
            flops=2 * 128 * 2048 * 512 * 4, bytes_accessed=9 * 2**20, transcendentals=65536
        ),
    )(scal, *operands)


def ring(array, axis):
    parts = [array] + [shift(array, axis, -turn) for turn in TURNS[1:]]
    return jnp.concatenate(parts, axis=1)


def ring_parts(array, axis):
    plus, minus = shift(array, axis, 1), shift(array, axis, -1)
    return plus, minus


def far_parts(plus, minus, axis):
    return shift(plus[:1], axis, 1), shift(minus[1:], axis, -1)


def gather(weights):
    pair, depth, width = weights.shape[1:]
    halves = weights[0].reshape(pair, depth, 2, width // 2).transpose(2, 0, 1, 3)
    sent = jnp.broadcast_to(halves[:, None], (2, SIDE) + halves.shape[1:])
    sent = sent.reshape((2 * SIDE,) + halves.shape[1:])
    got = lax.all_to_all(sent, ("core", "zl"), 0, 0, tiled=True)
    got = got.reshape(2, SIDE, pair, depth, width // 2).transpose(0, 2, 1, 3, 4)
    got = got.reshape(2, pair, SIDE * depth, width // 2)
    a, b = ring(got[0], "x"), ring(got[1], "y")
    a, b = lax.optimization_barrier((a, b))
    ap, am = ring_parts(a, "y")
    bp, bm = ring_parts(b, "x")
    af0, af1 = far_parts(ap, am, "y")
    bf0, bf1 = far_parts(bp, bm, "x")
    return (a, ap, am, af0, af1), (b, bp, bm, bf0, bf1)


def on_device(encoder_embed, decoder_embed, section_weights, norm_gains, input_lengths, target_lengths):
    zh, core = lax.axis_index("zh"), lax.axis_index("core")
    y, x = lax.axis_index("y"), lax.axis_index("x")
    rows = encoder_embed.shape[1]
    encoder = zh < 2
    causal = zh == 2
    key_lengths = jnp.where(causal, target_lengths, input_lengths)
    row_lengths = jnp.where(encoder, input_lengths, target_lengths)
    scal = jnp.stack(
        [x, y, zh, causal.astype(jnp.int32), key_lengths[core], key_lengths[1 - core]]
    ).astype(jnp.int32)
    live = (jnp.arange(rows, dtype=jnp.int32) < row_lengths[core])[:, None]
    live_other = (jnp.arange(rows, dtype=jnp.int32) < row_lengths[1 - core])[:, None]

    a_parts, b_parts = gather(section_weights)
    source = jnp.where(encoder, encoder_embed, decoder_embed)
    mine, other = source[core], source[1 - core]

    def added(stream, term, alive):
        return stream.astype(F32) + jnp.where(alive, term, 0.0)

    def swapped(array):
        return lax.ppermute(array, "core", [(0, 1), (1, 0)])

    kept, sent = sublayer(False, False, scal, norm_gains, (mine, other), (), a_parts, b_parts)
    first = added(mine, kept + swapped(sent).astype(F32), live).astype(BF16)
    mine2 = lax.ppermute(first, "zh", [(0, 1), (2, 3)])
    other2 = swapped(mine2)
    kept, sent = sublayer(False, False, scal, norm_gains, (mine2, other2), (), a_parts, b_parts)
    second = added(mine2, kept + swapped(sent).astype(F32), live).astype(BF16)
    memory = rms(second.astype(F32), norm_gains[4:5])
    mem = lax.ppermute(memory, "zh", [(1, 3)])
    mem_other = swapped(mem)
    early = jnp.where(zh == 1, second, first)
    early_other = lax.ppermute(early, "core", [(0, 1)])
    kept, sent = sublayer(
        True, True, scal, norm_gains, (mine2, other2), (mem, mem_other), a_parts, b_parts
    )
    kept_mine, kept_other = lax.ppermute((sent, kept.astype(BF16)), SECTION, [(6, 7)])
    third = added(mine2, kept + kept_mine.astype(F32), live).astype(BF16)
    third_other = added(other2, sent.astype(F32) + kept_other.astype(F32), live_other).astype(BF16)

    back = core == 1
    final = zh == 3
    even = (zh == 0) | (zh == 2)
    front_mine = jnp.where(even, mine, mine2)
    front_other = jnp.where(even, other, other2)
    back_mine = jnp.where(final, third, early)
    back_other = jnp.where(final, third_other, early_other)
    doc0 = jnp.where(back, back_other, front_mine)
    doc1 = jnp.where(back, back_mine, front_other)
    return jnp.stack([doc0, doc1])[None]


def solution(mesh):
    fine = Mesh(mesh.devices.reshape(SIDE, 2, SIDE, SIDE, SIDE), AXES)
    in_specs = (
        P(DP, None, None),
        P(DP, None, None),
        P(SECTION, None, DP, None),
        P(),
        P(DP),
        P(DP),
    )
    out_specs = P(SECTION, DP, None, None)
    return jax.shard_map(
        on_device, mesh=fine, in_specs=in_specs, out_specs=out_specs, check_vma=False
    )
```

time: 772 us -> 192 us (0.25)
  waiting for transfers between devices: 719 us -> 74.7 us
  starting transfers between devices: 18.5 us -> 69.2 us
  blocking collectives: 0 us -> 16.6 us
  Pallas kernels: 0 us -> 15.5 us
  between operations: 13.6 us -> 0.61 us
  matrix products: 7.98 us -> 0 us
    all_gather x1 -> x0, waiting for transfers between devices: 341 us -> none  [on_device(): joined = lax.all_gather(section_weights, 'dp', axis=2, tiled=True)]
    ppermute x14 -> x23, waiting for transfers between devices: 257 us -> 74.7 us  [the longest x1 28.9 us: on_device(): mine2 = lax.ppermute(first, 'zh', [(0, 1), (2, 3)])]
    psum x1 -> x0, waiting for transfers between devices: 119 us -> none  [spread(): return lax.psum(jnp.where(mine, array, jnp.zeros_like(array)), axis)]
    ppermute x14 -> x23, starting transfers between devices: 18.4 us -> 69.2 us  [the longest x14 47.4 us: shift(): lax.ppermute(array, axis, [(i, (i + by) % SIDE) for i in range(SIDE)])]
    all_to_all x0 -> x1, blocking collectives: none -> 16.6 us  [gather(): got = lax.all_to_all(sent, ('core', 'zl'), 0, 0, tiled=True)]
    pallas_call x0 -> x3, Pallas kernels: none -> 15.5 us  [sublayer(): pl.pallas_call(functools.partial(sublayer_kernel, cross, last), out_shape...]
    dot_general x3 -> x0, matrix products: 7.98 us -> none  [the longest x1 4.7 us: back_block(): lax.dot_general(mixed_rows, weight_pair[1], (((1,), (1,)), ((), ())), pre...]
  transfers between devices with their start and end apart: 16 -> 23, of which waited for: 10 -> 12; matrix products, arithmetic and copies ran while one was open for 0% -> 5% of each run, Pallas kernels for 0% -> 0%
where the time goes in v1:
time: 192 us; the launch traced here: 190 us
  waiting for transfers between devices  74.7 us (39%)
  starting transfers between devices  69.2 us (36%)
  blocking collectives  16.6 us (9%)
  Pallas kernels  15.5 us (8%)
  local copies, waits for them, and re-layouts  7.35 us (4%)
  other arithmetic  6.47 us (3%)
    ppermute x14, starting transfers between devices, shift(): lax.ppermute(array, axis, [(i, (i + by) % SIDE) for i in range(SIDE)])  47.4 us
    ppermute x1, waiting for transfers between devices, on_device(): mine2 = lax.ppermute(first, 'zh', [(0, 1), (2, 3)])  28.9 us
    ppermute x14, waiting for transfers between devices, shift(): lax.ppermute(array, axis, [(i, (i + by) % SIDE) for i in range(SIDE)])  23.6 us
    ppermute x1, waiting for transfers between devices, on_device(): mem = lax.ppermute(memory, 'zh', [(1, 3)])  16.8 us
    all_to_all x1, blocking collectives, gather(): got = lax.all_to_all(sent, ('core', 'zl'), 0, 0, tiled=True)  16.6 us
    pallas_call x3, Pallas kernels, sublayer(): pl.pallas_call(functools.partial(sublayer_kernel, cross, last), out_shape...  15.5 us
    ppermute x4, starting transfers between devices, swapped(): return lax.ppermute(array, 'core', [(0, 1), (1, 0)])  15.1 us
    ppermute x4, waiting for transfers between devices, swapped(): return lax.ppermute(array, 'core', [(0, 1), (1, 0)])  3.89 us
  transfers between devices with their start and end apart: 23, of which 12 were waited for; matrix products, arithmetic and copies ran while one was open for 5% of the time, Pallas kernels for 0%

profile of v1, /device:TPU:481, one launch (start us, length us, event | category | flops | bytes accessed | tf_op | source)
XLA Modules:
  0.0 190.4 jit_solution(5821754876084418832)
XLA Ops:
  1.1 16.6 %all_to_all.5 = bf16[8,2,32,512]{3,2,1,0:T(8,128)(2,1)S(1)} all-to-all(bf16[8,2,32,512]{3,2,1,0:T(8,128)(2,1)S(1)} %bitcast.26), channel_id=1, replica_groups=mesh['zh'=4,'core'=2,'y'=4,'x'=4,'zl'=4] {'core','zl'}, dimensions={0} | all-to-all | bytes 1048576 | tf_op jit(solution)/shard_map/all_to_all | solution.py:150
  17.7 3.2 %collective-permute-start.3 = (bf16[2,128,512]{2,1,0:T(8,128)(2,1)S(1)}, bf16[2,128,512]{2,1,0:T(8,128)(2,1)S(1)}, u32[]{:S(2)}, u32[]{:S(2)}) collective-permute-start(bf16[2,128,512]{2,1,0:T(8,128)(2,1)S(1)} %bitcast.28), channel_id=1, source_target_pairs={{0,16},{16,32},{32,48},{48,0},{1,17},{17,33},{33,49},{49,1},{2,18}... | collective-permute-start | bytes 786440 | tf_op jit(solution)/shard_map/ppermute | solution.py:19
  20.9 3.4 %collective-permute-start.4 = (bf16[2,128,512]{2,1,0:T(8,128)(2,1)S(1)}, bf16[2,128,512]{2,1,0:T(8,128)(2,1)S(1)}, u32[]{:S(2)}, u32[]{:S(2)}) collective-permute-start(bf16[2,128,512]{2,1,0:T(8,128)(2,1)S(1)} %bitcast.29), channel_id=1, source_target_pairs={{0,48},{16,0},{32,16},{48,32},{1,49},{17,1},{33,17},{49,33},{2,50}... | collective-permute-start | bytes 786440 | tf_op jit(solution)/shard_map/ppermute | solution.py:19
  24.3 3.5 %collective-permute-start.5 = (bf16[2,128,512]{2,1,0:T(8,128)(2,1)S(1)}, bf16[2,128,512]{2,1,0:T(8,128)(2,1)S(1)}, u32[]{:S(2)}, u32[]{:S(2)}) collective-permute-start(bf16[2,128,512]{2,1,0:T(8,128)(2,1)S(1)} %bitcast.30), channel_id=1, source_target_pairs={{0,32},{16,48},{32,0},{48,16},{1,33},{17,49},{33,1},{49,17},{2,34}... | collective-permute-start | bytes 786440 | tf_op jit(solution)/shard_map/ppermute | solution.py:19
  27.9 3.1 %collective-permute-start = (bf16[2,128,512]{2,1,0:T(8,128)(2,1)S(1)}, bf16[2,128,512]{2,1,0:T(8,128)(2,1)S(1)}, u32[]{:S(2)}, u32[]{:S(2)}) collective-permute-start(bf16[2,128,512]{2,1,0:T(8,128)(2,1)S(1)} %bitcast.32), channel_id=1, source_target_pairs={{0,4},{4,8},{8,12},{12,0},{1,5},{5,9},{9,13},{13,1},{2,6},{6,10},{... | collective-permute-start | bytes 786440 | tf_op jit(solution)/shard_map/ppermute | solution.py:19
  31.0 3.4 %collective-permute-start.1 = (bf16[2,128,512]{2,1,0:T(8,128)(2,1)S(1)}, bf16[2,128,512]{2,1,0:T(8,128)(2,1)S(1)}, u32[]{:S(2)}, u32[]{:S(2)}) collective-permute-start(bf16[2,128,512]{2,1,0:T(8,128)(2,1)S(1)} %bitcast.33), channel_id=1, source_target_pairs={{0,12},{4,0},{8,4},{12,8},{1,13},{5,1},{9,5},{13,9},{2,14},{6,2},{... | collective-permute-start | bytes 786440 | tf_op jit(solution)/shard_map/ppermute | solution.py:19
  34.4 3.4 %collective-permute-start.2 = (bf16[2,128,512]{2,1,0:T(8,128)(2,1)S(1)}, bf16[2,128,512]{2,1,0:T(8,128)(2,1)S(1)}, u32[]{:S(2)}, u32[]{:S(2)}) collective-permute-start(bf16[2,128,512]{2,1,0:T(8,128)(2,1)S(1)} %bitcast.34), channel_id=1, source_target_pairs={{0,8},{4,12},{8,0},{12,4},{1,9},{5,13},{9,1},{13,5},{2,10},{6,14},... | collective-permute-start | bytes 786440 | tf_op jit(solution)/shard_map/ppermute | solution.py:19
  39.1 4.6 %collective-permute-done.2 = bf16[2,128,512]{2,1,0:T(8,128)(2,1)S(1)} collective-permute-done((bf16[2,128,512]{2,1,0:T(8,128)(2,1)S(1)}, bf16[2,128,512]{2,1,0:T(8,128)(2,1)S(1)}, u32[]{:S(2)}, u32[]{:S(2)}) %collective-permute-start.2) | collective-permute-done | bytes 262176 | tf_op jit(solution)/shard_map/ppermute | solution.py:19
  43.8 4.8 %collective-permute-start.10 = (bf16[2,512,512]{2,1,0:T(8,128)(2,1)S(1)}, bf16[2,512,512]{2,1,0:T(8,128)(2,1)S(1)}, u32[]{:S(2)}, u32[]{:S(2)}) collective-permute-start(bf16[2,512,512]{2,1,0:T(8,128)(2,1)S(1)} %pad_maximum_fusion.1.refs_9_.refs_11_), channel_id=1, source_target_pairs={{0,4},{4,8},{8,12},{12,0},{1,5},{5,9},{9,13},{13,1},{2,6},{6,10},{... | collective-permute-start | bytes 3145736 | tf_op jit(solution)/shard_map/ppermute | solution.py:19
  48.5 2.9 %collective-permute-start.11 = (bf16[2,512,512]{2,1,0:T(8,128)(2,1)S(1)}, bf16[2,512,512]{2,1,0:T(8,128)(2,1)}, u32[]{:S(2)}, u32[]{:S(2)}) collective-permute-start(bf16[2,512,512]{2,1,0:T(8,128)(2,1)S(1)} %pad_maximum_fusion.1.refs_9_.refs_11_), channel_id=1, source_target_pairs={{0,12},{4,0},{8,4},{12,8},{1,13},{5,1},{9,5},{13,9},{2,14},{6,2},{... | collective-permute-start | bytes 3145736 | tf_op jit(solution)/shard_map/ppermute | solution.py:19
  51.4 2.3 %collective-permute-start.6 = (bf16[2,512,512]{2,1,0:T(8,128)(2,1)S(1)}, bf16[2,512,512]{2,1,0:T(8,128)(2,1)}, u32[]{:S(2)}, u32[]{:S(2)}) collective-permute-start(bf16[2,512,512]{2,1,0:T(8,128)(2,1)S(1)} %pad_maximum_fusion.refs_4_.refs_6_), channel_id=1, source_target_pairs={{0,16},{16,32},{32,48},{48,0},{1,17},{17,33},{33,49},{49,1},{2,18}... | collective-permute-start | bytes 3145736 | tf_op jit(solution)/shard_map/ppermute | solution.py:19
  53.7 4.2 %collective-permute-start.7 = (bf16[2,512,512]{2,1,0:T(8,128)(2,1)S(1)}, bf16[2,512,512]{2,1,0:T(8,128)(2,1)}, u32[]{:S(2)}, u32[]{:S(2)}) collective-permute-start(bf16[2,512,512]{2,1,0:T(8,128)(2,1)S(1)} %pad_maximum_fusion.refs_4_.refs_6_), channel_id=1, source_target_pairs={{0,48},{16,0},{32,16},{48,32},{1,49},{17,1},{33,17},{49,33},{2,50}... | collective-permute-start | bytes 3145736 | tf_op jit(solution)/shard_map/ppermute | solution.py:19
  58.6 1.4 stack.32.refs_0_
  60.0 10.6 %collective-permute-done.10.refs_10_.refs_12_ = bf16[2,512,512]{2,1,0:T(8,128)(2,1)S(1)} collective-permute-done((bf16[2,512,512]{2,1,0:T(8,128)(2,1)S(1)}, bf16[2,512,512]{2,1,0:T(8,128)(2,1)S(1)}, u32[]{:S(2)}, u32[]{:S(2)}) %collective-permute-start.10) | collective-permute-done | bytes 1048608 | tf_op jit(solution)/shard_map/ppermute | solution.py:19
  70.6 2.0 %collective-permute-start.12 = (bf16[1,512,512]{2,1,0:T(8,128)(2,1)S(1)}, bf16[1,512,512]{2,1,0:T(8,128)(2,1)S(1)}, u32[]{:S(2)}, u32[]{:S(2)}) collective-permute-start(bf16[1,512,512]{2,1,0:T(8,128)(2,1)S(1)} %slice.34), channel_id=1, source_target_pairs={{0,4},{4,8},{8,12},{12,0},{1,5},{5,9},{9,13},{13,1},{2,6},{6,10},{... | collective-permute-start | bytes 1572872 | tf_op jit(solution)/shard_map/ppermute | solution.py:19
  73.8 4.6 %collective-permute-start.13 = (bf16[1,512,512]{2,1,0:T(8,128)(2,1)S(1)}, bf16[1,512,512]{2,1,0:T(8,128)(2,1)S(1)}, u32[]{:S(2)}, u32[]{:S(2)}) collective-permute-start(bf16[1,512,512]{2,1,0:T(8,128)(2,1)S(1)} %slice.35), channel_id=1, source_target_pairs={{0,12},{4,0},{8,4},{12,8},{1,13},{5,1},{9,5},{13,9},{2,14},{6,2},{... | collective-permute-start | bytes 1572872 | tf_op jit(solution)/shard_map/ppermute | solution.py:19
  79.5 2.2 %collective-permute-start.8 = (bf16[1,512,512]{2,1,0:T(8,128)(2,1)S(1)}, bf16[1,512,512]{2,1,0:T(8,128)(2,1)S(1)}, u32[]{:S(2)}, u32[]{:S(2)}) collective-permute-start(bf16[1,512,512]{2,1,0:T(8,128)(2,1)S(1)} %slice.32), channel_id=1, source_target_pairs={{0,16},{16,32},{32,48},{48,0},{1,17},{17,33},{33,49},{49,1},{2,18}... | collective-permute-start | bytes 1572872 | tf_op jit(solution)/shard_map/ppermute | solution.py:19
  82.8 4.4 %collective-permute-start.9 = (bf16[1,512,512]{2,1,0:T(8,128)(2,1)S(1)}, bf16[1,512,512]{2,1,0:T(8,128)(2,1)S(1)}, u32[]{:S(2)}, u32[]{:S(2)}) collective-permute-start(bf16[1,512,512]{2,1,0:T(8,128)(2,1)S(1)} %slice.33), channel_id=1, source_target_pairs={{0,48},{16,0},{32,16},{48,32},{1,49},{17,1},{33,17},{49,33},{2,50}... | collective-permute-start | bytes 1572872 | tf_op jit(solution)/shard_map/ppermute | solution.py:19
  87.4 5.1 %collective-permute-done.8.refs_7_.refs_9_ = bf16[1,512,512]{2,1,0:T(8,128)(2,1)S(1)} collective-permute-done((bf16[1,512,512]{2,1,0:T(8,128)(2,1)S(1)}, bf16[1,512,512]{2,1,0:T(8,128)(2,1)S(1)}, u32[]{:S(2)}, u32[]{:S(2)}) %collective-permute-start.8) | collective-permute-done | bytes 524320 | tf_op jit(solution)/shard_map/ppermute | solution.py:19
  92.5 2.1 %collective-permute-done.9.refs_8_.refs_10_ = bf16[1,512,512]{2,1,0:T(8,128)(2,1)S(1)} collective-permute-done((bf16[1,512,512]{2,1,0:T(8,128)(2,1)S(1)}, bf16[1,512,512]{2,1,0:T(8,128)(2,1)S(1)}, u32[]{:S(2)}, u32[]{:S(2)}) %collective-permute-start.9) | collective-permute-done | bytes 524320 | tf_op jit(solution)/shard_map/ppermute | solution.py:19
  94.6 4.9 %shard_map.64 = (f32[64,2048]{1,0:T(8,128)S(1)}, bf16[64,2048]{1,0:T(8,128)(2,1)S(1)}) custom-call(s32[6]{0:T(128)S(1)} %stack.32.refs_0_, f32[5,2048]{1,0:T(8,128)S(1)} %copy-done.7, bf16[64,2048]{1,0:T(8,128)(2,1)S(1)} %get-tuple-element.28.refs_2_, bf16[64,2048]{1,0:T(8,128)(2,1)S(1)} %get-tuple-element.27.refs_3_, ...), custom_call_target="tpu_custom_call" | custom-call | flops 1073741824 | bytes 9437184 | tf_op jit(solution)/shard_map/pallas_call | solution.py:111
  99.5 6.6 %collective-permute-start.14 = (bf16[64,2048]{1,0:T(8,128)(2,1)S(1)}, bf16[64,2048]{1,0:T(8,128)(2,1)S(1)}, u32[]{:S(2)}, u32[]{:S(2)}) collective-permute-start(bf16[64,2048]{1,0:T(8,128)(2,1)S(1)} %get-tuple-element.16), channel_id=1, source_target_pairs={{0,64},{64,0},{1,65},{65,1},{2,66},{66,2},{3,67},{67,3},{4,68},{68... | collective-permute-start | bytes 786440 | tf_op jit(solution)/shard_map/ppermute | solution.py:184
  108.8 28.9 %collective-permute-done.15.refs_2_ = bf16[64,2048]{1,0:T(8,128)(2,1)S(1)} collective-permute-done((bf16[64,2048]{1,0:T(8,128)(2,1)S(1)}, bf16[64,2048]{1,0:T(8,128)(2,1)S(1)}, u32[]{:S(2)}, u32[]{:S(2)}) %collective-permute-start.15) | collective-permute-done | bytes 262176 | tf_op jit(solution)/shard_map/ppermute | solution.py:188
  137.6 3.1 %collective-permute-start.16 = (bf16[64,2048]{1,0:T(8,128)(2,1)S(1)}, bf16[64,2048]{1,0:T(8,128)(2,1)S(1)}, u32[]{:S(2)}, u32[]{:S(2)}) collective-permute-start(bf16[64,2048]{1,0:T(8,128)(2,1)S(1)} %collective-permute-done.15.refs_2_), channel_id=1, source_target_pairs={{0,64},{64,0},{1,65},{65,1},{2,66},{66,2},{3,67},{67,3},{4,68},{68... | collective-permute-start | bytes 786440 | tf_op jit(solution)/shard_map/ppermute | solution.py:184
  141.9 5.0 %shard_map.65 = (f32[64,2048]{1,0:T(8,128)S(1)}, bf16[64,2048]{1,0:T(8,128)(2,1)S(1)}) custom-call(s32[6]{0:T(128)S(1)} %stack.32.refs_0_, f32[5,2048]{1,0:T(8,128)S(1)} %copy-done.7, bf16[64,2048]{1,0:T(8,128)(2,1)S(1)} %collective-permute-done.15.refs_2_, bf16[64,2048]{1,0:T(8,128)(2,1)S(1)} %collective-permute-done.16.refs_3_, ...), custom_call_target="tpu_custom_call" | custom-call | flops 1073741824 | bytes 9437184 | tf_op jit(solution)/shard_map/pallas_call | solution.py:111
  146.9 2.3 %collective-permute-start.17 = (bf16[64,2048]{1,0:T(8,128)(2,1)S(1)}, bf16[64,2048]{1,0:T(8,128)(2,1)S(1)}, u32[]{:S(2)}, u32[]{:S(2)}) collective-permute-start(bf16[64,2048]{1,0:T(8,128)(2,1)S(1)} %get-tuple-element.18), channel_id=1, source_target_pairs={{0,64},{64,0},{1,65},{65,1},{2,66},{66,2},{3,67},{67,3},{4,68},{68... | collective-permute-start | bytes 786440 | tf_op jit(solution)/shard_map/ppermute | solution.py:184
  152.0 16.8 %collective-permute-done.18.refs_4_ = bf16[64,2048]{1,0:T(8,128)(2,1)S(1)} collective-permute-done((bf16[64,2048]{1,0:T(8,128)(2,1)S(1)}, bf16[64,2048]{1,0:T(8,128)(2,1)S(1)}, u32[]{:S(2)}, u32[]{:S(2)}) %collective-permute-start.18) | collective-permute-done | bytes 262176 | tf_op jit(solution)/shard_map/ppermute | solution.py:193
  168.8 3.1 %collective-permute-start.19 = (bf16[64,2048]{1,0:T(8,128)(2,1)S(1)}, bf16[64,2048]{1,0:T(8,128)(2,1)S(1)}, u32[]{:S(2)}, u32[]{:S(2)}) collective-permute-start(bf16[64,2048]{1,0:T(8,128)(2,1)S(1)} %collective-permute-done.18.refs_4_), channel_id=1, source_target_pairs={{0,64},{64,0},{1,65},{65,1},{2,66},{66,2},{3,67},{67,3},{4,68},{68... | collective-permute-start | bytes 786440 | tf_op jit(solution)/shard_map/ppermute | solution.py:184
  173.1 5.6 %shard_map.66 = (f32[64,2048]{1,0:T(8,128)S(1)}, bf16[64,2048]{1,0:T(8,128)(2,1)}) custom-call(s32[6]{0:T(128)S(1)} %stack.32.refs_0_, f32[5,2048]{1,0:T(8,128)S(1)} %copy-done.7, bf16[64,2048]{1,0:T(8,128)(2,1)S(1)} %collective-permute-done.15.refs_2_, bf16[64,2048]{1,0:T(8,128)(2,1)S(1)} %collective-permute-done.16.refs_3_, ...), custom_call_target="tpu_custom_call" | custom-call | flops 1073741824 | bytes 9437184 | tf_op jit(solution)/shard_map/pallas_call | solution.py:111
  179.5 1.4 collective-permute-start.22
  182.1 1.4 collective-permute-start.20
  186.8 1.5 collective-permute-done.21
  (74 shorter events, 21.3 us)
Async XLA Ops:
  17.7 16.7 %collective-permute-start.3 = (bf16[2,128,512]{2,1,0:T(8,128)(2,1)S(1)}, bf16[2,128,512]{2,1,0:T(8,128)(2,1)S(1)}, u32[]{:S(2)}, u32[]{:S(2)}) collective-permute-start(bf16[2,128,512]{2,1,0:T(8,128)(2,1)S(1)} %bitcast.28), channel_id=1, source_target_pairs={{0,16},{16,32},{32,48},{48,0},{1,17},{17,33},{33,49},{49,1},{2,18}... | collective-permute-start | bytes 786440 | tf_op jit(solution)/shard_map/ppermute | solution.py:19
  20.9 16.9 %collective-permute-start.4 = (bf16[2,128,512]{2,1,0:T(8,128)(2,1)S(1)}, bf16[2,128,512]{2,1,0:T(8,128)(2,1)S(1)}, u32[]{:S(2)}, u32[]{:S(2)}) collective-permute-start(bf16[2,128,512]{2,1,0:T(8,128)(2,1)S(1)} %bitcast.29), channel_id=1, source_target_pairs={{0,48},{16,0},{32,16},{48,32},{1,49},{17,1},{33,17},{49,33},{2,50}... | collective-permute-start | bytes 786440 | tf_op jit(solution)/shard_map/ppermute | solution.py:19
  24.3 13.6 %collective-permute-start.5 = (bf16[2,128,512]{2,1,0:T(8,128)(2,1)S(1)}, bf16[2,128,512]{2,1,0:T(8,128)(2,1)S(1)}, u32[]{:S(2)}, u32[]{:S(2)}) collective-permute-start(bf16[2,128,512]{2,1,0:T(8,128)(2,1)S(1)} %bitcast.30), channel_id=1, source_target_pairs={{0,32},{16,48},{32,0},{48,16},{1,33},{17,49},{33,1},{49,17},{2,34}... | collective-permute-start | bytes 786440 | tf_op jit(solution)/shard_map/ppermute | solution.py:19
  27.9 10.1 %collective-permute-start = (bf16[2,128,512]{2,1,0:T(8,128)(2,1)S(1)}, bf16[2,128,512]{2,1,0:T(8,128)(2,1)S(1)}, u32[]{:S(2)}, u32[]{:S(2)}) collective-permute-start(bf16[2,128,512]{2,1,0:T(8,128)(2,1)S(1)} %bitcast.32), channel_id=1, source_target_pairs={{0,4},{4,8},{8,12},{12,0},{1,5},{5,9},{9,13},{13,1},{2,6},{6,10},{... | collective-permute-start | bytes 786440 | tf_op jit(solution)/shard_map/ppermute | solution.py:19
  31.0 8.1 %collective-permute-start.1 = (bf16[2,128,512]{2,1,0:T(8,128)(2,1)S(1)}, bf16[2,128,512]{2,1,0:T(8,128)(2,1)S(1)}, u32[]{:S(2)}, u32[]{:S(2)}) collective-permute-start(bf16[2,128,512]{2,1,0:T(8,128)(2,1)S(1)} %bitcast.33), channel_id=1, source_target_pairs={{0,12},{4,0},{8,4},{12,8},{1,13},{5,1},{9,5},{13,9},{2,14},{6,2},{... | collective-permute-start | bytes 786440 | tf_op jit(solution)/shard_map/ppermute | solution.py:19
  34.4 9.3 %collective-permute-start.2 = (bf16[2,128,512]{2,1,0:T(8,128)(2,1)S(1)}, bf16[2,128,512]{2,1,0:T(8,128)(2,1)S(1)}, u32[]{:S(2)}, u32[]{:S(2)}) collective-permute-start(bf16[2,128,512]{2,1,0:T(8,128)(2,1)S(1)} %bitcast.34), channel_id=1, source_target_pairs={{0,8},{4,12},{8,0},{12,4},{1,9},{5,13},{9,1},{13,5},{2,10},{6,14},... | collective-permute-start | bytes 786440 | tf_op jit(solution)/shard_map/ppermute | solution.py:19
  37.9 20.0 %copy-start.12 = (s32[2]{0:T(128)S(1)}, s32[2]{0:T(128)}, u32[]{:S(2)}) copy-start(s32[2]{0:T(128)} %param.10) | copy-start | bytes 28
  37.9 20.0 %copy-start.13 = (s32[2]{0:T(128)S(1)}, s32[2]{0:T(128)}, u32[]{:S(2)}) copy-start(s32[2]{0:T(128)} %param.11) | copy-start | bytes 28
  43.8 26.9 %collective-permute-start.10 = (bf16[2,512,512]{2,1,0:T(8,128)(2,1)S(1)}, bf16[2,512,512]{2,1,0:T(8,128)(2,1)S(1)}, u32[]{:S(2)}, u32[]{:S(2)}) collective-permute-start(bf16[2,512,512]{2,1,0:T(8,128)(2,1)S(1)} %pad_maximum_fusion.1.refs_9_.refs_11_), channel_id=1, source_target_pairs={{0,4},{4,8},{8,12},{12,0},{1,5},{5,9},{9,13},{13,1},{2,6},{6,10},{... | collective-permute-start | bytes 3145736 | tf_op jit(solution)/shard_map/ppermute | solution.py:19
  48.5 24.2 %collective-permute-start.11 = (bf16[2,512,512]{2,1,0:T(8,128)(2,1)S(1)}, bf16[2,512,512]{2,1,0:T(8,128)(2,1)}, u32[]{:S(2)}, u32[]{:S(2)}) collective-permute-start(bf16[2,512,512]{2,1,0:T(8,128)(2,1)S(1)} %pad_maximum_fusion.1.refs_9_.refs_11_), channel_id=1, source_target_pairs={{0,12},{4,0},{8,4},{12,8},{1,13},{5,1},{9,5},{13,9},{2,14},{6,2},{... | collective-permute-start | bytes 3145736 | tf_op jit(solution)/shard_map/ppermute | solution.py:19
  51.4 27.0 %collective-permute-start.6 = (bf16[2,512,512]{2,1,0:T(8,128)(2,1)S(1)}, bf16[2,512,512]{2,1,0:T(8,128)(2,1)}, u32[]{:S(2)}, u32[]{:S(2)}) collective-permute-start(bf16[2,512,512]{2,1,0:T(8,128)(2,1)S(1)} %pad_maximum_fusion.refs_4_.refs_6_), channel_id=1, source_target_pairs={{0,16},{16,32},{32,48},{48,0},{1,17},{17,33},{33,49},{49,1},{2,18}... | collective-permute-start | bytes 3145736 | tf_op jit(solution)/shard_map/ppermute | solution.py:19
  53.7 28.0 %collective-permute-start.7 = (bf16[2,512,512]{2,1,0:T(8,128)(2,1)S(1)}, bf16[2,512,512]{2,1,0:T(8,128)(2,1)}, u32[]{:S(2)}, u32[]{:S(2)}) collective-permute-start(bf16[2,512,512]{2,1,0:T(8,128)(2,1)S(1)} %pad_maximum_fusion.refs_4_.refs_6_), channel_id=1, source_target_pairs={{0,48},{16,0},{32,16},{48,32},{1,49},{17,1},{33,17},{49,33},{2,50}... | collective-permute-start | bytes 3145736 | tf_op jit(solution)/shard_map/ppermute | solution.py:19
  70.6 16.8 %collective-permute-start.12 = (bf16[1,512,512]{2,1,0:T(8,128)(2,1)S(1)}, bf16[1,512,512]{2,1,0:T(8,128)(2,1)S(1)}, u32[]{:S(2)}, u32[]{:S(2)}) collective-permute-start(bf16[1,512,512]{2,1,0:T(8,128)(2,1)S(1)} %slice.34), channel_id=1, source_target_pairs={{0,4},{4,8},{8,12},{12,0},{1,5},{5,9},{9,13},{13,1},{2,6},{6,10},{... | collective-permute-start | bytes 1572872 | tf_op jit(solution)/shard_map/ppermute | solution.py:19
  73.8 13.5 %copy-start.10 = (bf16[2,64,2048]{2,1,0:T(8,128)(2,1)S(1)}, bf16[2,64,2048]{2,1,0:T(8,128)(2,1)}, u32[]{:S(2)}) copy-start(bf16[2,64,2048]{2,1,0:T(8,128)(2,1)} %param.6) | copy-start | bytes 1572868
  73.8 13.5 %copy-start.11 = (bf16[2,64,2048]{2,1,0:T(8,128)(2,1)S(1)}, bf16[2,64,2048]{2,1,0:T(8,128)(2,1)}, u32[]{:S(2)}) copy-start(bf16[2,64,2048]{2,1,0:T(8,128)(2,1)} %param.7) | copy-start | bytes 1572868
  73.8 13.6 %collective-permute-start.13 = (bf16[1,512,512]{2,1,0:T(8,128)(2,1)S(1)}, bf16[1,512,512]{2,1,0:T(8,128)(2,1)S(1)}, u32[]{:S(2)}, u32[]{:S(2)}) collective-permute-start(bf16[1,512,512]{2,1,0:T(8,128)(2,1)S(1)} %slice.35), channel_id=1, source_target_pairs={{0,12},{4,0},{8,4},{12,8},{1,13},{5,1},{9,5},{13,9},{2,14},{6,2},{... | collective-permute-start | bytes 1572872 | tf_op jit(solution)/shard_map/ppermute | solution.py:19
  79.5 13.0 %collective-permute-start.8 = (bf16[1,512,512]{2,1,0:T(8,128)(2,1)S(1)}, bf16[1,512,512]{2,1,0:T(8,128)(2,1)S(1)}, u32[]{:S(2)}, u32[]{:S(2)}) collective-permute-start(bf16[1,512,512]{2,1,0:T(8,128)(2,1)S(1)} %slice.32), channel_id=1, source_target_pairs={{0,16},{16,32},{32,48},{48,0},{1,17},{17,33},{33,49},{49,1},{2,18}... | collective-permute-start | bytes 1572872 | tf_op jit(solution)/shard_map/ppermute | solution.py:19
  82.8 11.8 %collective-permute-start.9 = (bf16[1,512,512]{2,1,0:T(8,128)(2,1)S(1)}, bf16[1,512,512]{2,1,0:T(8,128)(2,1)S(1)}, u32[]{:S(2)}, u32[]{:S(2)}) collective-permute-start(bf16[1,512,512]{2,1,0:T(8,128)(2,1)S(1)} %slice.33), channel_id=1, source_target_pairs={{0,48},{16,0},{32,16},{48,32},{1,49},{17,1},{33,17},{49,33},{2,50}... | collective-permute-start | bytes 1572872 | tf_op jit(solution)/shard_map/ppermute | solution.py:19
  87.4 12.1 %copy-start.4 = (bf16[64,2048]{1,0:T(8,128)(2,1)}, bf16[64,2048]{1,0:T(8,128)(2,1)S(1)}, u32[]{:S(2)}) copy-start(bf16[64,2048]{1,0:T(8,128)(2,1)S(1)} %get-tuple-element.27.refs_3_) | copy-start | bytes 786436
  87.4 19.9 %copy-start = (bf16[64,2048]{1,0:T(8,128)(2,1)}, bf16[64,2048]{1,0:T(8,128)(2,1)S(1)}, u32[]{:S(2)}) copy-start(bf16[64,2048]{1,0:T(8,128)(2,1)S(1)} %get-tuple-element.28.refs_2_) | copy-start | bytes 786436
  99.5 7.8 %collective-permute-start.14 = (bf16[64,2048]{1,0:T(8,128)(2,1)S(1)}, bf16[64,2048]{1,0:T(8,128)(2,1)S(1)}, u32[]{:S(2)}, u32[]{:S(2)}) collective-permute-start(bf16[64,2048]{1,0:T(8,128)(2,1)S(1)} %get-tuple-element.16), channel_id=1, source_target_pairs={{0,64},{64,0},{1,65},{65,1},{2,66},{66,2},{3,67},{67,3},{4,68},{68... | collective-permute-start | bytes 786440 | tf_op jit(solution)/shard_map/ppermute | solution.py:184
  107.4 33.3 %copy-start.9 = (bf16[64,2048]{1,0:T(8,128)(2,1)}, bf16[64,2048]{1,0:T(8,128)(2,1)S(1)}, u32[]{:S(2)}) copy-start(bf16[64,2048]{1,0:T(8,128)(2,1)S(1)} %add_convert_fusion.1) | copy-start | bytes 786436
  107.5 30.2 %collective-permute-start.15 = (bf16[64,2048]{1,0:T(8,128)(2,1)S(1)}, bf16[64,2048]{1,0:T(8,128)(2,1)S(1)}, u32[]{:S(2)}, u32[]{:S(2)}) collective-permute-start(bf16[64,2048]{1,0:T(8,128)(2,1)S(1)} %add_convert_fusion.1), channel_id=1, source_target_pairs={{0,128},{256,384},{1,129},{257,385},{2,130},{258,386},{3,131},{259... | collective-permute-start | bytes 786440 | tf_op jit(solution)/shard_map/ppermute | solution.py:188
  137.6 4.2 %collective-permute-start.16 = (bf16[64,2048]{1,0:T(8,128)(2,1)S(1)}, bf16[64,2048]{1,0:T(8,128)(2,1)S(1)}, u32[]{:S(2)}, u32[]{:S(2)}) collective-permute-start(bf16[64,2048]{1,0:T(8,128)(2,1)S(1)} %collective-permute-done.15.refs_2_), channel_id=1, source_target_pairs={{0,64},{64,0},{1,65},{65,1},{2,66},{66,2},{3,67},{67,3},{4,68},{68... | collective-permute-start | bytes 786440 | tf_op jit(solution)/shard_map/ppermute | solution.py:184
  141.9 31.2 %copy-start.2 = (bf16[64,2048]{1,0:T(8,128)(2,1)}, bf16[64,2048]{1,0:T(8,128)(2,1)S(1)}, u32[]{:S(2)}) copy-start(bf16[64,2048]{1,0:T(8,128)(2,1)S(1)} %collective-permute-done.16.refs_3_) | copy-start | bytes 786436
  146.9 3.4 %collective-permute-start.17 = (bf16[64,2048]{1,0:T(8,128)(2,1)S(1)}, bf16[64,2048]{1,0:T(8,128)(2,1)S(1)}, u32[]{:S(2)}, u32[]{:S(2)}) collective-permute-start(bf16[64,2048]{1,0:T(8,128)(2,1)S(1)} %get-tuple-element.18), channel_id=1, source_target_pairs={{0,64},{64,0},{1,65},{65,1},{2,66},{66,2},{3,67},{67,3},{4,68},{68... | collective-permute-start | bytes 786440 | tf_op jit(solution)/shard_map/ppermute | solution.py:184
  150.6 21.4 %copy-start.8 = (bf16[64,2048]{1,0:T(8,128)(2,1)}, bf16[64,2048]{1,0:T(8,128)(2,1)S(1)}, u32[]{:S(2)}) copy-start(bf16[64,2048]{1,0:T(8,128)(2,1)S(1)} %get-tuple-element.24) | copy-start | bytes 786436
  150.7 18.1 %collective-permute-start.18 = (bf16[64,2048]{1,0:T(8,128)(2,1)S(1)}, bf16[64,2048]{1,0:T(8,128)(2,1)S(1)}, u32[]{:S(2)}, u32[]{:S(2)}) collective-permute-start(bf16[64,2048]{1,0:T(8,128)(2,1)S(1)} %fusion.4), channel_id=1, source_target_pairs={{128,384},{129,385},{130,386},{131,387},{132,388},{133,389},{134,3... | collective-permute-start | bytes 786440 | tf_op jit(solution)/shard_map/ppermute | solution.py:193
  168.8 4.2 %collective-permute-start.19 = (bf16[64,2048]{1,0:T(8,128)(2,1)S(1)}, bf16[64,2048]{1,0:T(8,128)(2,1)S(1)}, u32[]{:S(2)}, u32[]{:S(2)}) collective-permute-start(bf16[64,2048]{1,0:T(8,128)(2,1)S(1)} %collective-permute-done.18.refs_4_), channel_id=1, source_target_pairs={{0,64},{64,0},{1,65},{65,1},{2,66},{66,2},{3,67},{67,3},{4,68},{68... | collective-permute-start | bytes 786440 | tf_op jit(solution)/shard_map/ppermute | solution.py:184
  179.5 4.0 %collective-permute-start.22 = (bf16[64,2048]{1,0:T(8,128)(2,1)}, bf16[64,2048]{1,0:T(8,128)(2,1)S(1)}, u32[]{:S(2)}, u32[]{:S(2)}) collective-permute-start(bf16[64,2048]{1,0:T(8,128)(2,1)} %get-tuple-element.19), channel_id=1, source_target_pairs={{384,448},{385,449},{386,450},{387,451},{388,452},{389,453},{390,4... | collective-permute-start | bytes 786440 | tf_op jit(solution)/shard_map/ppermute | solution.py:200
  182.1 4.7 %collective-permute-start.20 = (bf16[64,2048]{1,0:T(8,128)(2,1)S(1)}, bf16[64,2048]{1,0:T(8,128)(2,1)S(1)}, u32[]{:S(2)}, u32[]{:S(2)}) collective-permute-start(bf16[64,2048]{1,0:T(8,128)(2,1)S(1)} %convert_element_type.57), channel_id=1, source_target_pairs={{384,448},{385,449},{386,450},{387,451},{388,452},{389,453},{390,4... | collective-permute-start | bytes 786440 | tf_op jit(solution)/shard_map/ppermute | solution.py:200
  184.8 3.5 %collective-permute-start.21 = (bf16[64,2048]{1,0:T(8,128)(2,1)S(1)}, bf16[64,2048]{1,0:T(8,128)(2,1)S(1)}, u32[]{:S(2)}, u32[]{:S(2)}) collective-permute-start(bf16[64,2048]{1,0:T(8,128)(2,1)S(1)} %get-tuple-element.22), channel_id=1, source_target_pairs={{0,64},{1,65},{2,66},{3,67},{4,68},{5,69},{6,70},{7,71},{8,72},{9,... | collective-permute-start | bytes 786440 | tf_op jit(solution)/shard_map/ppermute | solution.py:196
  (5 other events, 29.1 us)

commit v2 on v1

v2 whole, which is shorter than its diff:
```python
import functools

import jax
import jax.numpy as jnp
from jax import lax
from jax.experimental import pallas as pl
from jax.experimental.pallas import tpu as pltpu
from jax.sharding import Mesh, PartitionSpec as P

HEAD_DIM = 128
SIDE = 4
TURNS = (0, 1, 3, 2)
AXES = ("zh", "core", "y", "x", "zl")
DP = ("y", "x", "zl")
SECTION = ("zh", "core")
F32 = jnp.float32
BF16 = jnp.bfloat16


def exchange(array, axis, by):
    return lax.ppermute(array, axis, [(i, i ^ by) for i in range(SIDE)])


def dot(a, b):
    return jnp.dot(a, b, preferred_element_type=F32)


def dot_t(a, b):
    return lax.dot_general(a, b, (((1,), (1,)), ((), ())), preferred_element_type=F32)


def rms(values, gain):
    mean_square = jnp.mean(values * values, axis=-1, keepdims=True)
    return (values * lax.rsqrt(mean_square + 1e-06) * gain).astype(BF16)


def sublayer_kernel(cross, cube, *refs):
    refs = list(refs)
    scal = refs.pop(0)
    gains, mine, other = refs[:3]
    refs = refs[3:]
    mem = ()
    if cross:
        mem = refs[:2]
        refs = refs[2:]
    a_refs, b_refs = refs[:5], refs[5:10]
    refs = refs[10:]
    if cross:
        rows = mine.shape[0]
        out_mine, out_other = refs[0].at[:rows], refs[0].at[rows:]
        refs = refs[1:]
    else:
        out_mine, out_other = refs[:2]
        refs = refs[2:]
    h3, m3, t3 = refs

    def work():
        sublayer_body(scal, gains, (mine, other), mem, a_refs, b_refs, out_mine, out_other, h3, m3, t3)

    if cube is None:
        work()
    else:
        pl.when(scal[2] == cube)(work)


def sublayer_body(scal, gains, streams, mem, a_refs, b_refs, out_mine, out_other, h3, m3, t3):
    rows = streams[0].shape[0]
    x, y, sub, causal, len_mine, len_other = (scal[i] for i in range(6))
    gain = gains[pl.ds(sub, 1), :]
    for part, ref in enumerate(streams):
        h = rms(ref[...].astype(F32), gain)
        for i in range(16):
            h3[i, part * rows:(part + 1) * rows, :] = h[:, i * 128:(i + 1) * 128]
    kv3 = m3 if mem else h3
    for part, ref in enumerate(mem):
        for i in range(16):
            m3[i, part * rows:(part + 1) * rows, :] = ref[:, i * 128:(i + 1) * 128]

    def blk(dy, dx):
        return lax.bitwise_xor(y, dy) * SIDE + lax.bitwise_xor(x, dx)

    def piece(group, turn, which):
        if turn == 2:
            return group[3 + which][0]
        return group[TURNS.index(turn)][which]

    q = k = v = None
    for turn in TURNS:
        cols = [blk(turn, d) for d in TURNS]
        hq = jnp.concatenate([h3[c] for c in cols], axis=1)
        hk = jnp.concatenate([kv3[c] for c in cols], axis=1) if mem else hq
        dq, dk = dot(hq, piece(a_refs, turn, 0)), dot(hk, piece(a_refs, turn, 1))
        cols = [blk(d, turn) for d in TURNS]
        dv = dot(jnp.concatenate([kv3[c] for c in cols], axis=1), piece(b_refs, turn, 0))
        q, k, v = (dq, dk, dv) if q is None else (q + dq, k + dk, v + dv)
    q, k, v = q.astype(BF16), k.astype(BF16), v.astype(BF16)
    r = lax.broadcasted_iota(jnp.int32, (2 * rows, 2 * rows), 0)
    c = lax.broadcasted_iota(jnp.int32, (2 * rows, 2 * rows), 1)
    first = c < rows
    live = (r < rows) == first
    key_at = jnp.where(first, c, c - rows)
    live = live & (key_at < jnp.where(first, len_mine, len_other))
    live = live & ((c <= r) | (causal == 0))
    mixed = []
    for head in range(4):
        at = slice(head * HEAD_DIM, (head + 1) * HEAD_DIM)
        s = dot_t(q[:, at], k[:, at]) * HEAD_DIM ** (-0.5)
        s = jnp.where(live, s, -1e30)
        e = jnp.exp(s - jnp.max(s, axis=-1, keepdims=True))
        p = (e / jnp.sum(e, axis=-1, keepdims=True)).astype(BF16)
        mixed.append(dot(p, v[:, at]).astype(BF16))
    mixed = jnp.concatenate(mixed, axis=1)
    for turn in TURNS:
        t = dot_t(mixed, piece(b_refs, turn, 1))
        for j, d in enumerate(TURNS):
            t3[blk(d, turn)] = t[:, j * 128:(j + 1) * 128]
    for i in range(16):
        at = slice(i * 128, (i + 1) * 128)
        out_mine[:, at] = t3[i, :rows, :].astype(out_mine.dtype)
        out_other[:, at] = t3[i, rows:, :].astype(out_other.dtype)


VMEM = pl.BlockSpec(memory_space=pltpu.VMEM)
SMEM = pl.BlockSpec(memory_space=pltpu.SMEM)


def sublayer(cross, cube, scal, gains, streams, mem, a_parts, b_parts):
    rows, width = streams[0].shape
    operands = [gains, *streams, *mem, *a_parts, *b_parts]
    halves = tuple(jax.ShapeDtypeStruct((rows, width), kind) for kind in (F32, BF16))
    return pl.pallas_call(
        functools.partial(sublayer_kernel, cross, cube),
        out_shape=jax.ShapeDtypeStruct((2 * rows, width), BF16) if cross else halves,
        in_specs=[SMEM] + [VMEM] * len(operands),
        out_specs=VMEM if cross else (VMEM, VMEM),
        scratch_shapes=[
            pltpu.VMEM((16, 2 * rows, 128), BF16),
            pltpu.VMEM((16, 2 * rows, 128) if cross else (1, 16, 128), BF16),
            pltpu.VMEM((16, 2 * rows, 128), F32),
        ],
        compiler_params=pltpu.CompilerParams(vmem_limit_bytes=20 * 1024 * 1024),
        cost_estimate=pl.CostEstimate(
            flops=2 * 128 * 2048 * 512 * 4, bytes_accessed=9 * 2**20, transcendentals=65536
        ),
    )(scal, *operands)


def finish_kernel(scal, mine, other, in1m, in1o, in3m, in3o, early_m, early_o, own, got, out):
    rows = mine.shape[0]
    cube, core = scal[2], scal[6]
    even = (cube == 0) | (cube == 2)

    def put(doc0, doc1):
        out[0] = doc0[...]
        out[1] = doc1[...]

    @pl.when((core == 0) & even)
    def _():
        put(mine, other)

    @pl.when((core == 0) & (cube == 1))
    def _():
        put(in1m, in1o)

    @pl.when((core == 0) & (cube == 3))
    def _():
        put(in3m, in3o)

    @pl.when((core == 1) & (cube != 3))
    def _():
        put(early_o, early_m)

    @pl.when((core == 1) & (cube == 3))
    def _():
        at = lax.broadcasted_iota(jnp.int32, mine.shape, 0)
        low, high = slice(0, rows), slice(rows, 2 * rows)
        for slot, base, a, b, live in ((1, in3m, low, high, scal[7]), (0, in3o, high, low, scal[8])):
            term = own[a, :].astype(F32) + got[b, :].astype(F32)
            term = jnp.where(at < live, term, 0.0)
            out[slot] = (base[...].astype(F32) + term).astype(BF16)


def finish(scal, *parts):
    return pl.pallas_call(
        finish_kernel,
        out_shape=jax.ShapeDtypeStruct((2,) + parts[0].shape, BF16),
        in_specs=[SMEM] + [VMEM] * len(parts),
        out_specs=VMEM,
        compiler_params=pltpu.CompilerParams(vmem_limit_bytes=20 * 1024 * 1024),
    )(scal, *parts)


def ring(array, axis):
    parts = [array] + [exchange(array, axis, turn) for turn in TURNS[1:]]
    return jnp.concatenate(parts, axis=1)


def ring_parts(array, axis):
    return exchange(array, axis, 1), exchange(array, axis, 3)


def far_parts(by1, by3, axis):
    return exchange(by1[:1], axis, 3), exchange(by3[1:], axis, 1)


def gather(weights):
    pair, depth, width = weights.shape[1:]
    halves = weights[0].reshape(pair, depth, 2, width // 2).transpose(2, 0, 1, 3)
    sent = jnp.broadcast_to(halves[:, None], (2, SIDE) + halves.shape[1:])
    sent = sent.reshape((2 * SIDE,) + halves.shape[1:])
    got = lax.all_to_all(sent, ("core", "zl"), 0, 0, tiled=True)
    got = got.reshape(2, SIDE, pair, depth, width // 2).transpose(0, 2, 1, 3, 4)
    got = got.reshape(2, pair, SIDE * depth, width // 2)
    a, b = ring(got[0], "x"), ring(got[1], "y")
    a, b = lax.optimization_barrier((a, b))
    ap, am = ring_parts(a, "y")
    bp, bm = ring_parts(b, "x")
    af0, af1 = far_parts(ap, am, "y")
    bf0, bf1 = far_parts(bp, bm, "x")
    return (a, ap, am, af0, af1), (b, bp, bm, bf0, bf1)


def on_device(encoder_embed, decoder_embed, section_weights, norm_gains, input_lengths, target_lengths):
    zh, core = lax.axis_index("zh"), lax.axis_index("core")
    y, x = lax.axis_index("y"), lax.axis_index("x")
    rows = encoder_embed.shape[1]
    encoder = zh < 2
    causal = zh == 2
    key_lengths = jnp.where(causal, target_lengths, input_lengths)
    row_lengths = jnp.where(encoder, input_lengths, target_lengths)
    scal = jnp.stack(
        [
            x,
            y,
            zh,
            causal.astype(jnp.int32),
            key_lengths[core],
            key_lengths[1 - core],
            core,
            row_lengths[core],
            row_lengths[1 - core],
        ]
    ).astype(jnp.int32)
    live = (jnp.arange(rows, dtype=jnp.int32) < row_lengths[core])[:, None]

    a_parts, b_parts = gather(section_weights)
    source = jnp.where(encoder, encoder_embed, decoder_embed)
    mine, other = source[core], source[1 - core]

    def added(stream, term, alive):
        return stream.astype(F32) + jnp.where(alive, term, 0.0)

    def swapped(array, cubes=range(SIDE)):
        pairs = [(2 * c + i, 2 * c + 1 - i) for c in cubes for i in range(2)]
        return lax.ppermute(array, SECTION, pairs)

    kept, sent = sublayer(False, None, scal, norm_gains, (mine, other), (), a_parts, b_parts)
    first = added(mine, kept + swapped(sent, (0, 2)).astype(F32), live).astype(BF16)
    in1 = lax.ppermute(first, "zh", [(0, 1)])
    in3 = lax.ppermute(first, "zh", [(2, 3)])
    in1_other = swapped(in1, (1,))
    kept, sent = sublayer(False, 1, scal, norm_gains, (in1, in1_other), (), a_parts, b_parts)
    second = added(in1, kept + swapped(sent, (1,)).astype(F32), live).astype(BF16)
    memory = rms(second.astype(F32), norm_gains[4:5])
    mem = lax.ppermute(memory, "zh", [(1, 3)])
    early = jnp.where(zh == 1, second, first)
    early_other = lax.ppermute(early, SECTION, [(0, 1), (2, 3), (4, 5)])
    in3_other = swapped(in3, (3,))
    mem_other = swapped(mem, (3,))
    own = sublayer(
        True, 3, scal, norm_gains, (in3, in3_other), (mem, mem_other), a_parts, b_parts
    )
    got = lax.ppermute(own, SECTION, [(6, 7)])
    out = finish(
        scal, mine, other, in1, in1_other, in3, in3_other, early, early_other, own, got
    )
    return out[None]


def solution(mesh):
    fine = Mesh(mesh.devices.reshape(SIDE, 2, SIDE, SIDE, SIDE), AXES)
    in_specs = (
        P(DP, None, None),
        P(DP, None, None),
        P(SECTION, None, DP, None),
        P(),
        P(DP),
        P(DP),
    )
    out_specs = P(SECTION, DP, None, None)
    return jax.shard_map(
        on_device, mesh=fine, in_specs=in_specs, out_specs=out_specs, check_vma=False
    )
```

time: 192 us -> 184 us (0.958)
  starting transfers between devices: 69.2 us -> 59 us
  local copies, waits for them, and re-layouts: 7.35 us -> 12.7 us
  other arithmetic: 6.47 us -> 1.41 us
  waiting for transfers between devices: 74.7 us -> 77.7 us
    ppermute x22 -> x23, starting transfers between devices: 67.9 us -> 57.7 us  [the longest x14 45.4 us: exchange(): return lax.ppermute(array, axis, [(i, i ^ by) for i in range(SIDE)])]
    unnamed x28 -> x46, local copies, waits for them, and re-layouts: 0.86 us -> 4.96 us
    ppermute x22 -> x23, waiting for transfers between devices: 57.8 us -> 60.7 us  [the longest x14 29.7 us: exchange(): return lax.ppermute(array, axis, [(i, i ^ by) for i in range(SIDE)])]
    another operation x2 -> x0, other arithmetic: 2.55 us -> none  [on_device(): return jnp.stack([doc0, doc1])[None]]
    pallas_call x3 -> x4, Pallas kernels: 15.5 us -> 14.5 us  [the longest x3 12.4 us: sublayer(): pl.pallas_call(functools.partial(sublayer_kernel, cross, cube), out_shape...]
  transfers between devices with their start and end apart: 23 -> 24, of which waited for: 12 -> 11; matrix products, arithmetic and copies ran while one was open for 5% -> 4% of each run, Pallas kernels for 0% -> 0%
where the time goes in v2:
time: 184 us; the launch traced here: 182 us
  waiting for transfers between devices  77.7 us (42%)
  starting transfers between devices  59 us (32%)
  blocking collectives  16.6 us (9%)
  Pallas kernels  14.5 us (8%)
  local copies, waits for them, and re-layouts  12.7 us (7%)
    ppermute x14, starting transfers between devices, exchange(): return lax.ppermute(array, axis, [(i, i ^ by) for i in range(SIDE)])  45.4 us
    ppermute x14, waiting for transfers between devices, exchange(): return lax.ppermute(array, axis, [(i, i ^ by) for i in range(SIDE)])  29.7 us
    ppermute x1, waiting for transfers between devices, on_device(): in3 = lax.ppermute(first, 'zh', [(2, 3)])  27.7 us
    ppermute x1, waiting for transfers between devices, on_device(): mem = lax.ppermute(memory, 'zh', [(1, 3)])  17 us
    all_to_all x1, blocking collectives, gather(): got = lax.all_to_all(sent, ('core', 'zl'), 0, 0, tiled=True)  16.6 us
    pallas_call x3, Pallas kernels, sublayer(): pl.pallas_call(functools.partial(sublayer_kernel, cross, cube), out_shape...  12.4 us
    ppermute x5, starting transfers between devices, swapped(): return lax.ppermute(array, SECTION, pairs)  8.36 us
    unnamed x46, local copies, waits for them, and re-layouts  4.96 us
  transfers between devices with their start and end apart: 24, of which 11 were waited for; matrix products, arithmetic and copies ran while one was open for 4% of the time, Pallas kernels for 0%

profile of v2, /device:TPU:481, one launch (start us, length us, event | category | flops | bytes accessed | tf_op | source)
XLA Modules:
  0.0 182.5 jit_solution(8800995839378229170)
XLA Ops:
  1.1 16.6 %all_to_all.5 = bf16[8,2,32,512]{3,2,1,0:T(8,128)(2,1)S(1)} all-to-all(bf16[8,2,32,512]{3,2,1,0:T(8,128)(2,1)S(1)} %bitcast.21), channel_id=1, replica_groups=mesh['zh'=4,'core'=2,'y'=4,'x'=4,'zl'=4] {'core','zl'}, dimensions={0} | all-to-all | bytes 1048576 | tf_op jit(solution)/shard_map/all_to_all | solution.py:211
  17.7 4.7 %collective-permute-start.2 = (bf16[2,128,512]{2,1,0:T(8,128)(2,1)S(1)}, bf16[2,128,512]{2,1,0:T(8,128)(2,1)S(1)}, u32[]{:S(2)}, u32[]{:S(2)}) collective-permute-start(bf16[2,128,512]{2,1,0:T(8,128)(2,1)S(1)} %bitcast.23), channel_id=1, source_target_pairs={{0,8},{4,12},{8,0},{12,4},{1,9},{5,13},{9,1},{13,5},{2,10},{6,14},... | collective-permute-start | bytes 786440 | tf_op jit(solution)/shard_map/ppermute | solution.py:21
  22.4 2.8 %collective-permute-start.1 = (bf16[2,128,512]{2,1,0:T(8,128)(2,1)S(1)}, bf16[2,128,512]{2,1,0:T(8,128)(2,1)S(1)}, u32[]{:S(2)}, u32[]{:S(2)}) collective-permute-start(bf16[2,128,512]{2,1,0:T(8,128)(2,1)S(1)} %bitcast.24), channel_id=1, source_target_pairs={{0,12},{4,8},{8,4},{12,0},{1,13},{5,9},{9,5},{13,1},{2,14},{6,10},... | collective-permute-start | bytes 786440 | tf_op jit(solution)/shard_map/ppermute | solution.py:21
  25.1 1.9 %collective-permute-start = (bf16[2,128,512]{2,1,0:T(8,128)(2,1)S(1)}, bf16[2,128,512]{2,1,0:T(8,128)(2,1)S(1)}, u32[]{:S(2)}, u32[]{:S(2)}) collective-permute-start(bf16[2,128,512]{2,1,0:T(8,128)(2,1)S(1)} %bitcast.25), channel_id=1, source_target_pairs={{0,4},{4,0},{8,12},{12,8},{1,5},{5,1},{9,13},{13,9},{2,6},{6,2},{1... | collective-permute-start | bytes 786440 | tf_op jit(solution)/shard_map/ppermute | solution.py:21
  27.1 4.8 %collective-permute-start.5 = (bf16[2,128,512]{2,1,0:T(8,128)(2,1)S(1)}, bf16[2,128,512]{2,1,0:T(8,128)(2,1)S(1)}, u32[]{:S(2)}, u32[]{:S(2)}) collective-permute-start(bf16[2,128,512]{2,1,0:T(8,128)(2,1)S(1)} %bitcast.27), channel_id=1, source_target_pairs={{0,32},{16,48},{32,0},{48,16},{1,33},{17,49},{33,1},{49,17},{2,34}... | collective-permute-start | bytes 786440 | tf_op jit(solution)/shard_map/ppermute | solution.py:21
  31.9 2.7 %collective-permute-start.4 = (bf16[2,128,512]{2,1,0:T(8,128)(2,1)S(1)}, bf16[2,128,512]{2,1,0:T(8,128)(2,1)S(1)}, u32[]{:S(2)}, u32[]{:S(2)}) collective-permute-start(bf16[2,128,512]{2,1,0:T(8,128)(2,1)S(1)} %bitcast.28), channel_id=1, source_target_pairs={{0,48},{16,32},{32,16},{48,0},{1,49},{17,33},{33,17},{49,1},{2,50}... | collective-permute-start | bytes 786440 | tf_op jit(solution)/shard_map/ppermute | solution.py:21
  34.6 1.9 %collective-permute-start.3 = (bf16[2,128,512]{2,1,0:T(8,128)(2,1)S(1)}, bf16[2,128,512]{2,1,0:T(8,128)(2,1)S(1)}, u32[]{:S(2)}, u32[]{:S(2)}) collective-permute-start(bf16[2,128,512]{2,1,0:T(8,128)(2,1)S(1)} %bitcast.29), channel_id=1, source_target_pairs={{0,16},{16,0},{32,48},{48,32},{1,17},{17,1},{33,49},{49,33},{2,18}... | collective-permute-start | bytes 786440 | tf_op jit(solution)/shard_map/ppermute | solution.py:21
  37.2 6.4 %collective-permute-done.4 = bf16[2,128,512]{2,1,0:T(8,128)(2,1)S(1)} collective-permute-done((bf16[2,128,512]{2,1,0:T(8,128)(2,1)S(1)}, bf16[2,128,512]{2,1,0:T(8,128)(2,1)S(1)}, u32[]{:S(2)}, u32[]{:S(2)}) %collective-permute-start.4) | collective-permute-done | bytes 262176 | tf_op jit(solution)/shard_map/ppermute | solution.py:21
  43.7 5.3 %collective-permute-start.7 = (bf16[2,512,512]{2,1,0:T(8,128)(2,1)S(1)}, bf16[2,512,512]{2,1,0:T(8,128)(2,1)S(1)}, u32[]{:S(2)}, u32[]{:S(2)}) collective-permute-start(bf16[2,512,512]{2,1,0:T(8,128)(2,1)S(1)} %pad_maximum_fusion.refs_4_.refs_6_), channel_id=1, source_target_pairs={{0,48},{16,32},{32,16},{48,0},{1,49},{17,33},{33,17},{49,1},{2,50}... | collective-permute-start | bytes 3145736 | tf_op jit(solution)/shard_map/ppermute | solution.py:21
  49.1 1.9 %collective-permute-start.6 = (bf16[2,512,512]{2,1,0:T(8,128)(2,1)S(1)}, bf16[2,512,512]{2,1,0:T(8,128)(2,1)}, u32[]{:S(2)}, u32[]{:S(2)}) collective-permute-start(bf16[2,512,512]{2,1,0:T(8,128)(2,1)S(1)} %pad_maximum_fusion.refs_4_.refs_6_), channel_id=1, source_target_pairs={{0,16},{16,0},{32,48},{48,32},{1,17},{17,1},{33,49},{49,33},{2,18}... | collective-permute-start | bytes 3145736 | tf_op jit(solution)/shard_map/ppermute | solution.py:21
  51.0 3.7 %collective-permute-start.11 = (bf16[2,512,512]{2,1,0:T(8,128)(2,1)S(1)}, bf16[2,512,512]{2,1,0:T(8,128)(2,1)}, u32[]{:S(2)}, u32[]{:S(2)}) collective-permute-start(bf16[2,512,512]{2,1,0:T(8,128)(2,1)S(1)} %pad_maximum_fusion.1.refs_9_.refs_11_), channel_id=1, source_target_pairs={{0,12},{4,8},{8,4},{12,0},{1,13},{5,9},{9,5},{13,1},{2,14},{6,10},... | collective-permute-start | bytes 3145736 | tf_op jit(solution)/shard_map/ppermute | solution.py:21
  54.7 2.8 %collective-permute-start.10 = (bf16[2,512,512]{2,1,0:T(8,128)(2,1)S(1)}, bf16[2,512,512]{2,1,0:T(8,128)(2,1)}, u32[]{:S(2)}, u32[]{:S(2)}) collective-permute-start(bf16[2,512,512]{2,1,0:T(8,128)(2,1)S(1)} %pad_maximum_fusion.1.refs_9_.refs_11_), channel_id=1, source_target_pairs={{0,4},{4,0},{8,12},{12,8},{1,5},{5,1},{9,13},{13,9},{2,6},{6,2},{1... | collective-permute-start | bytes 3145736 | tf_op jit(solution)/shard_map/ppermute | solution.py:21
  58.2 2.6 %stack.27.refs_0_.scal = s32[9]{0:T(128)S(1)} concatenate(s32[1]{0:T(128)} %bitcast, s32[1]{0:T(128)} %bitcast.1, s32[1]{0:T(128)} %bitcast.2, s32[1]{0:T(128)} %bitcast.3, s32[1]{0:T(128)} %get-tuple-element.29, s32[1]{0:T(128)} %get-tuple-element.30, s32[1]{0:T(128)} %bitcast.4, s32[1]{0:T(128)} %get-tuple-element.26, s32[1]{0:T(128)} %get-tuple-element.25), dimensions={0} | concatenate | bytes 72 | tf_op jit(solution)/shard_map/stack | solution.py:231
  60.8 10.7 %collective-permute-done.7.refs_6_.refs_8_ = bf16[2,512,512]{2,1,0:T(8,128)(2,1)S(1)} collective-permute-done((bf16[2,512,512]{2,1,0:T(8,128)(2,1)S(1)}, bf16[2,512,512]{2,1,0:T(8,128)(2,1)S(1)}, u32[]{:S(2)}, u32[]{:S(2)}) %collective-permute-start.7) | collective-permute-done | bytes 1048608 | tf_op jit(solution)/shard_map/ppermute | solution.py:21
  71.6 2.1 %collective-permute-start.9 = (bf16[1,512,512]{2,1,0:T(8,128)(2,1)S(1)}, bf16[1,512,512]{2,1,0:T(8,128)(2,1)S(1)}, u32[]{:S(2)}, u32[]{:S(2)}) collective-permute-start(bf16[1,512,512]{2,1,0:T(8,128)(2,1)S(1)} %slice.33), channel_id=1, source_target_pairs={{0,16},{16,0},{32,48},{48,32},{1,17},{17,1},{33,49},{49,33},{2,18}... | collective-permute-start | bytes 1572872 | tf_op jit(solution)/shard_map/ppermute | solution.py:21
  76.1 3.6 %collective-permute-start.8 = (bf16[1,512,512]{2,1,0:T(8,128)(2,1)S(1)}, bf16[1,512,512]{2,1,0:T(8,128)(2,1)S(1)}, u32[]{:S(2)}, u32[]{:S(2)}) collective-permute-start(bf16[1,512,512]{2,1,0:T(8,128)(2,1)S(1)} %slice.32), channel_id=1, source_target_pairs={{0,48},{16,32},{32,16},{48,0},{1,49},{17,33},{33,17},{49,1},{2,50}... | collective-permute-start | bytes 1572872 | tf_op jit(solution)/shard_map/ppermute | solution.py:21
  80.8 3.3 %collective-permute-start.13 = (bf16[1,512,512]{2,1,0:T(8,128)(2,1)S(1)}, bf16[1,512,512]{2,1,0:T(8,128)(2,1)S(1)}, u32[]{:S(2)}, u32[]{:S(2)}) collective-permute-start(bf16[1,512,512]{2,1,0:T(8,128)(2,1)S(1)} %slice.35), channel_id=1, source_target_pairs={{0,4},{4,0},{8,12},{12,8},{1,5},{5,1},{9,13},{13,9},{2,6},{6,2},{1... | collective-permute-start | bytes 1572872 | tf_op jit(solution)/shard_map/ppermute | solution.py:21
  85.2 3.9 %collective-permute-start.12 = (bf16[1,512,512]{2,1,0:T(8,128)(2,1)S(1)}, bf16[1,512,512]{2,1,0:T(8,128)(2,1)S(1)}, u32[]{:S(2)}, u32[]{:S(2)}) collective-permute-start(bf16[1,512,512]{2,1,0:T(8,128)(2,1)S(1)} %slice.34), channel_id=1, source_target_pairs={{0,12},{4,8},{8,4},{12,0},{1,13},{5,9},{9,5},{13,1},{2,14},{6,10},... | collective-permute-start | bytes 1572872 | tf_op jit(solution)/shard_map/ppermute | solution.py:21
  89.2 1.9 %collective-permute-done.8.refs_7_.refs_9_ = bf16[1,512,512]{2,1,0:T(8,128)(2,1)S(1)} collective-permute-done((bf16[1,512,512]{2,1,0:T(8,128)(2,1)S(1)}, bf16[1,512,512]{2,1,0:T(8,128)(2,1)S(1)}, u32[]{:S(2)}, u32[]{:S(2)}) %collective-permute-start.8) | collective-permute-done | bytes 524320 | tf_op jit(solution)/shard_map/ppermute | solution.py:21
  91.1 3.5 %collective-permute-done.13.refs_13_.refs_15_ = bf16[1,512,512]{2,1,0:T(8,128)(2,1)S(1)} collective-permute-done((bf16[1,512,512]{2,1,0:T(8,128)(2,1)S(1)}, bf16[1,512,512]{2,1,0:T(8,128)(2,1)S(1)}, u32[]{:S(2)}, u32[]{:S(2)}) %collective-permute-start.13) | collective-permute-done | bytes 524320 | tf_op jit(solution)/shard_map/ppermute | solution.py:21
  94.6 5.3 %collective-permute-done.12.refs_12_.refs_14_ = bf16[1,512,512]{2,1,0:T(8,128)(2,1)S(1)} collective-permute-done((bf16[1,512,512]{2,1,0:T(8,128)(2,1)S(1)}, bf16[1,512,512]{2,1,0:T(8,128)(2,1)S(1)}, u32[]{:S(2)}, u32[]{:S(2)}) %collective-permute-start.12) | collective-permute-done | bytes 524320 | tf_op jit(solution)/shard_map/ppermute | solution.py:21
  99.9 5.1 %shard_map.64 = (f32[64,2048]{1,0:T(8,128)S(1)}, bf16[64,2048]{1,0:T(8,128)(2,1)S(1)}) custom-call(s32[9]{0:T(128)S(1)} %stack.27.refs_0_.scal, f32[5,2048]{1,0:T(8,128)S(1)} %copy-done.14, bf16[64,2048]{1,0:T(8,128)(2,1)S(1)} %get-tuple-element.22.refs_2_.mine, bf16[64,2048]{1,0:T(8,128)(2,1)S(1)} %get-tuple-element.21.refs_3_.other, ...), custom_call_target="tpu_custom_call" | custom-call | flops 1073741824 | bytes 9437184 | tf_op jit(solution)/shard_map/pallas_call | solution.py:131
  108.0 2.0 %shard_map.65 = (f32[64,2048]{1,0:T(8,128)S(1)}, bf16[64,2048]{1,0:T(8,128)(2,1)S(1)}) custom-call(s32[9]{0:T(128)S(1)} %stack.27.refs_0_.scal, f32[5,2048]{1,0:T(8,128)S(1)} %copy-done.14, bf16[64,2048]{1,0:T(8,128)(2,1)S(1)} %collective-permute-done.15.refs_2_.in1m, bf16[64,2048]{1,0:T(8,128)(2,1)S(1)} %collective-permute-done.16.refs_3_.in1o, ...), custom_call_target="tpu_custom_call" | custom-call | flops 1073741824 | bytes 9437184 | tf_op jit(solution)/shard_map/pallas_call | solution.py:131
  110.7 1.3 collective-permute-start.17
  114.4 27.7 %collective-permute-done.17.refs_2_.in3m = bf16[64,2048]{1,0:T(8,128)(2,1)} collective-permute-done((bf16[64,2048]{1,0:T(8,128)(2,1)S(1)}, bf16[64,2048]{1,0:T(8,128)(2,1)}, u32[]{:S(2)}, u32[]{:S(2)}) %collective-permute-start.17) | collective-permute-done | bytes 262176 | tf_op jit(solution)/shard_map/ppermute | solution.py:260
  142.2 3.7 %collective-permute-start.18 = (bf16[64,2048]{1,0:T(8,128)(2,1)}, bf16[64,2048]{1,0:T(8,128)(2,1)}, u32[]{:S(2)}, u32[]{:S(2)}) collective-permute-start(bf16[64,2048]{1,0:T(8,128)(2,1)} %collective-permute-done.17.refs_2_.in3m), channel_id=1, source_target_pairs={{384,448},{448,384},{385,449},{449,385},{386,450},{450,386},{387,4... | collective-permute-start | bytes 786440 | tf_op jit(solution)/shard_map/ppermute | solution.py:255
  145.9 17.0 %collective-permute-done.21.refs_4_ = bf16[64,2048]{1,0:T(8,128)(2,1)} collective-permute-done((bf16[64,2048]{1,0:T(8,128)(2,1)S(1)}, bf16[64,2048]{1,0:T(8,128)(2,1)}, u32[]{:S(2)}, u32[]{:S(2)}) %collective-permute-start.21) | collective-permute-done | bytes 262176 | tf_op jit(solution)/shard_map/ppermute | solution.py:265
  162.9 2.6 %collective-permute-start.22 = (bf16[64,2048]{1,0:T(8,128)(2,1)}, bf16[64,2048]{1,0:T(8,128)(2,1)}, u32[]{:S(2)}, u32[]{:S(2)}) collective-permute-start(bf16[64,2048]{1,0:T(8,128)(2,1)} %collective-permute-done.21.refs_4_), channel_id=1, source_target_pairs={{384,448},{448,384},{385,449},{449,385},{386,450},{450,386},{387,4... | collective-permute-start | bytes 786440 | tf_op jit(solution)/shard_map/ppermute | solution.py:255
  165.5 1.5 collective-permute-done.22.refs_5_
  171.2 5.4 %shard_map.66.own = bf16[128,2048]{1,0:T(8,128)(2,1)S(1)} custom-call(s32[9]{0:T(128)S(1)} %stack.27.refs_0_.scal, f32[5,2048]{1,0:T(8,128)S(1)} %copy-done.14, bf16[64,2048]{1,0:T(8,128)(2,1)} %collective-permute-done.17.refs_2_.in3m, bf16[64,2048]{1,0:T(8,128)(2,1)} %collective-permute-done.18.refs_3_.in3o, ...), custom_call_target="tpu_custom_call" | custom-call | flops 1073741824 | bytes 9437184 | tf_op jit(solution)/shard_map/pallas_call | solution.py:131
  178.6 1.8 collective-permute-done.23.got
  180.4 2.1 %shard_map.67 = bf16[2,64,2048]{2,1,0:T(8,128)(2,1)} custom-call(s32[9]{0:T(128)S(1)} %stack.27.refs_0_.scal, bf16[64,2048]{1,0:T(8,128)(2,1)S(1)} %get-tuple-element.22.refs_2_.mine, bf16[64,2048]{1,0:T(8,128)(2,1)S(1)} %copy-done.9, bf16[64,2048]{1,0:T(8,128)(2,1)S(1)} %copy-done.11, bf16[64,2048]{1,0:T(8,128)(2,1)S(1)} %copy-done.13, ...), custom_call_target="tpu_custom_call" | custom-call | tf_op jit(solution)/shard_map/pallas_call | solution.py:184
  (91 shorter events, 19.3 us)
Async XLA Ops:
  17.7 16.9 %collective-permute-start.2 = (bf16[2,128,512]{2,1,0:T(8,128)(2,1)S(1)}, bf16[2,128,512]{2,1,0:T(8,128)(2,1)S(1)}, u32[]{:S(2)}, u32[]{:S(2)}) collective-permute-start(bf16[2,128,512]{2,1,0:T(8,128)(2,1)S(1)} %bitcast.23), channel_id=1, source_target_pairs={{0,8},{4,12},{8,0},{12,4},{1,9},{5,13},{9,1},{13,5},{2,10},{6,14},... | collective-permute-start | bytes 786440 | tf_op jit(solution)/shard_map/ppermute | solution.py:21
  22.4 14.2 %collective-permute-start.1 = (bf16[2,128,512]{2,1,0:T(8,128)(2,1)S(1)}, bf16[2,128,512]{2,1,0:T(8,128)(2,1)S(1)}, u32[]{:S(2)}, u32[]{:S(2)}) collective-permute-start(bf16[2,128,512]{2,1,0:T(8,128)(2,1)S(1)} %bitcast.24), channel_id=1, source_target_pairs={{0,12},{4,8},{8,4},{12,0},{1,13},{5,9},{9,5},{13,1},{2,14},{6,10},... | collective-permute-start | bytes 786440 | tf_op jit(solution)/shard_map/ppermute | solution.py:21
  25.1 11.4 %collective-permute-start = (bf16[2,128,512]{2,1,0:T(8,128)(2,1)S(1)}, bf16[2,128,512]{2,1,0:T(8,128)(2,1)S(1)}, u32[]{:S(2)}, u32[]{:S(2)}) collective-permute-start(bf16[2,128,512]{2,1,0:T(8,128)(2,1)S(1)} %bitcast.25), channel_id=1, source_target_pairs={{0,4},{4,0},{8,12},{12,8},{1,5},{5,1},{9,13},{13,9},{2,6},{6,2},{1... | collective-permute-start | bytes 786440 | tf_op jit(solution)/shard_map/ppermute | solution.py:21
  27.1 10.2 %collective-permute-start.5 = (bf16[2,128,512]{2,1,0:T(8,128)(2,1)S(1)}, bf16[2,128,512]{2,1,0:T(8,128)(2,1)S(1)}, u32[]{:S(2)}, u32[]{:S(2)}) collective-permute-start(bf16[2,128,512]{2,1,0:T(8,128)(2,1)S(1)} %bitcast.27), channel_id=1, source_target_pairs={{0,32},{16,48},{32,0},{48,16},{1,33},{17,49},{33,1},{49,17},{2,34}... | collective-permute-start | bytes 786440 | tf_op jit(solution)/shard_map/ppermute | solution.py:21
  31.9 11.7 %collective-permute-start.4 = (bf16[2,128,512]{2,1,0:T(8,128)(2,1)S(1)}, bf16[2,128,512]{2,1,0:T(8,128)(2,1)S(1)}, u32[]{:S(2)}, u32[]{:S(2)}) collective-permute-start(bf16[2,128,512]{2,1,0:T(8,128)(2,1)S(1)} %bitcast.28), channel_id=1, source_target_pairs={{0,48},{16,32},{32,16},{48,0},{1,49},{17,33},{33,17},{49,1},{2,50}... | collective-permute-start | bytes 786440 | tf_op jit(solution)/shard_map/ppermute | solution.py:21
  34.6 9.0 %collective-permute-start.3 = (bf16[2,128,512]{2,1,0:T(8,128)(2,1)S(1)}, bf16[2,128,512]{2,1,0:T(8,128)(2,1)S(1)}, u32[]{:S(2)}, u32[]{:S(2)}) collective-permute-start(bf16[2,128,512]{2,1,0:T(8,128)(2,1)S(1)} %bitcast.29), channel_id=1, source_target_pairs={{0,16},{16,0},{32,48},{48,32},{1,17},{17,1},{33,49},{49,33},{2,18}... | collective-permute-start | bytes 786440 | tf_op jit(solution)/shard_map/ppermute | solution.py:21
  36.7 20.9 %copy-start.21 = (s32[2]{0:T(128)S(1)}, s32[2]{0:T(128)}, u32[]{:S(2)}) copy-start(s32[2]{0:T(128)} %param.10) | copy-start | bytes 28
  36.7 20.9 %copy-start.22 = (s32[2]{0:T(128)S(1)}, s32[2]{0:T(128)}, u32[]{:S(2)}) copy-start(s32[2]{0:T(128)} %param.11) | copy-start | bytes 28
  43.7 27.8 %collective-permute-start.7 = (bf16[2,512,512]{2,1,0:T(8,128)(2,1)S(1)}, bf16[2,512,512]{2,1,0:T(8,128)(2,1)S(1)}, u32[]{:S(2)}, u32[]{:S(2)}) collective-permute-start(bf16[2,512,512]{2,1,0:T(8,128)(2,1)S(1)} %pad_maximum_fusion.refs_4_.refs_6_), channel_id=1, source_target_pairs={{0,48},{16,32},{32,16},{48,0},{1,49},{17,33},{33,17},{49,1},{2,50}... | collective-permute-start | bytes 3145736 | tf_op jit(solution)/shard_map/ppermute | solution.py:21
  49.1 25.9 %collective-permute-start.6 = (bf16[2,512,512]{2,1,0:T(8,128)(2,1)S(1)}, bf16[2,512,512]{2,1,0:T(8,128)(2,1)}, u32[]{:S(2)}, u32[]{:S(2)}) collective-permute-start(bf16[2,512,512]{2,1,0:T(8,128)(2,1)S(1)} %pad_maximum_fusion.refs_4_.refs_6_), channel_id=1, source_target_pairs={{0,16},{16,0},{32,48},{48,32},{1,17},{17,1},{33,49},{49,33},{2,18}... | collective-permute-start | bytes 3145736 | tf_op jit(solution)/shard_map/ppermute | solution.py:21
  51.0 28.7 %collective-permute-start.11 = (bf16[2,512,512]{2,1,0:T(8,128)(2,1)S(1)}, bf16[2,512,512]{2,1,0:T(8,128)(2,1)}, u32[]{:S(2)}, u32[]{:S(2)}) collective-permute-start(bf16[2,512,512]{2,1,0:T(8,128)(2,1)S(1)} %pad_maximum_fusion.1.refs_9_.refs_11_), channel_id=1, source_target_pairs={{0,12},{4,8},{8,4},{12,0},{1,13},{5,9},{9,5},{13,1},{2,14},{6,10},... | collective-permute-start | bytes 3145736 | tf_op jit(solution)/shard_map/ppermute | solution.py:21
  54.7 29.4 %collective-permute-start.10 = (bf16[2,512,512]{2,1,0:T(8,128)(2,1)S(1)}, bf16[2,512,512]{2,1,0:T(8,128)(2,1)}, u32[]{:S(2)}, u32[]{:S(2)}) collective-permute-start(bf16[2,512,512]{2,1,0:T(8,128)(2,1)S(1)} %pad_maximum_fusion.1.refs_9_.refs_11_), channel_id=1, source_target_pairs={{0,4},{4,0},{8,12},{12,8},{1,5},{5,1},{9,13},{13,9},{2,6},{6,2},{1... | collective-permute-start | bytes 3145736 | tf_op jit(solution)/shard_map/ppermute | solution.py:21
  71.6 17.6 %collective-permute-start.9 = (bf16[1,512,512]{2,1,0:T(8,128)(2,1)S(1)}, bf16[1,512,512]{2,1,0:T(8,128)(2,1)S(1)}, u32[]{:S(2)}, u32[]{:S(2)}) collective-permute-start(bf16[1,512,512]{2,1,0:T(8,128)(2,1)S(1)} %slice.33), channel_id=1, source_target_pairs={{0,16},{16,0},{32,48},{48,32},{1,17},{17,1},{33,49},{49,33},{2,18}... | collective-permute-start | bytes 1572872 | tf_op jit(solution)/shard_map/ppermute | solution.py:21
  76.1 13.0 %copy-start.19 = (bf16[2,64,2048]{2,1,0:T(8,128)(2,1)S(1)}, bf16[2,64,2048]{2,1,0:T(8,128)(2,1)}, u32[]{:S(2)}) copy-start(bf16[2,64,2048]{2,1,0:T(8,128)(2,1)} %param.6) | copy-start | bytes 1572868
  76.1 15.0 %collective-permute-start.8 = (bf16[1,512,512]{2,1,0:T(8,128)(2,1)S(1)}, bf16[1,512,512]{2,1,0:T(8,128)(2,1)S(1)}, u32[]{:S(2)}, u32[]{:S(2)}) collective-permute-start(bf16[1,512,512]{2,1,0:T(8,128)(2,1)S(1)} %slice.32), channel_id=1, source_target_pairs={{0,48},{16,32},{32,16},{48,0},{1,49},{17,33},{33,17},{49,1},{2,50}... | collective-permute-start | bytes 1572872 | tf_op jit(solution)/shard_map/ppermute | solution.py:21
  80.8 13.8 %collective-permute-start.13 = (bf16[1,512,512]{2,1,0:T(8,128)(2,1)S(1)}, bf16[1,512,512]{2,1,0:T(8,128)(2,1)S(1)}, u32[]{:S(2)}, u32[]{:S(2)}) collective-permute-start(bf16[1,512,512]{2,1,0:T(8,128)(2,1)S(1)} %slice.35), channel_id=1, source_target_pairs={{0,4},{4,0},{8,12},{12,8},{1,5},{5,1},{9,13},{13,9},{2,6},{6,2},{1... | collective-permute-start | bytes 1572872 | tf_op jit(solution)/shard_map/ppermute | solution.py:21
  85.2 14.8 %copy-start.14 = (f32[5,2048]{1,0:T(8,128)S(1)}, f32[5,2048]{1,0:T(8,128)}, u32[]{:S(2)}) copy-start(f32[5,2048]{1,0:T(8,128)} %refs_1_.5) | copy-start | bytes 122884
  85.2 14.8 %collective-permute-start.12 = (bf16[1,512,512]{2,1,0:T(8,128)(2,1)S(1)}, bf16[1,512,512]{2,1,0:T(8,128)(2,1)S(1)}, u32[]{:S(2)}, u32[]{:S(2)}) collective-permute-start(bf16[1,512,512]{2,1,0:T(8,128)(2,1)S(1)} %slice.34), channel_id=1, source_target_pairs={{0,12},{4,8},{8,4},{12,0},{1,13},{5,9},{9,5},{13,1},{2,14},{6,10},... | collective-permute-start | bytes 1572872 | tf_op jit(solution)/shard_map/ppermute | solution.py:21
  89.2 15.9 %copy-start.8 = (bf16[64,2048]{1,0:T(8,128)(2,1)}, bf16[64,2048]{1,0:T(8,128)(2,1)S(1)}, u32[]{:S(2)}) copy-start(bf16[64,2048]{1,0:T(8,128)(2,1)S(1)} %get-tuple-element.21.refs_3_.other) | copy-start | bytes 786436
  89.2 18.7 %copy-start = (bf16[1,512,512]{2,1,0:T(8,128)(2,1)}, bf16[1,512,512]{2,1,0:T(8,128)(2,1)S(1)}, u32[]{:S(2)}) copy-start(bf16[1,512,512]{2,1,0:T(8,128)(2,1)S(1)} %collective-permute-done.9.refs_8_.refs_10_) | copy-start | bytes 1572868
  91.1 16.9 %copy-start.2 = (bf16[1,512,512]{2,1,0:T(8,128)(2,1)}, bf16[1,512,512]{2,1,0:T(8,128)(2,1)S(1)}, u32[]{:S(2)}) copy-start(bf16[1,512,512]{2,1,0:T(8,128)(2,1)S(1)} %collective-permute-done.8.refs_7_.refs_9_) | copy-start | bytes 1572868
  94.6 13.3 %copy-start.4 = (bf16[1,512,512]{2,1,0:T(8,128)(2,1)}, bf16[1,512,512]{2,1,0:T(8,128)(2,1)S(1)}, u32[]{:S(2)}) copy-start(bf16[1,512,512]{2,1,0:T(8,128)(2,1)S(1)} %collective-permute-done.13.refs_13_.refs_15_) | copy-start | bytes 1572868
  105.0 1.3 collective-permute-start.14
  106.5 0.7 collective-permute-start.15
  107.2 0.7 collective-permute-start.16
  110.0 2.0 %collective-permute-start.19 = (bf16[64,2048]{1,0:T(8,128)(2,1)S(1)}, bf16[64,2048]{1,0:T(8,128)(2,1)S(1)}, u32[]{:S(2)}, u32[]{:S(2)}) collective-permute-start(bf16[64,2048]{1,0:T(8,128)(2,1)S(1)} %get-tuple-element.16), channel_id=1, source_target_pairs={{128,192},{192,128},{129,193},{193,129},{130,194},{194,130},{131,1... | collective-permute-start | bytes 786440 | tf_op jit(solution)/shard_map/ppermute | solution.py:255
  110.7 31.5 %collective-permute-start.17 = (bf16[64,2048]{1,0:T(8,128)(2,1)S(1)}, bf16[64,2048]{1,0:T(8,128)(2,1)}, u32[]{:S(2)}, u32[]{:S(2)}) collective-permute-start(bf16[64,2048]{1,0:T(8,128)(2,1)S(1)} %add_convert_fusion.1), channel_id=1, source_target_pairs={{256,384},{257,385},{258,386},{259,387},{260,388},{261,389},{262,3... | collective-permute-start | bytes 786440 | tf_op jit(solution)/shard_map/ppermute | solution.py:260
  113.1 49.8 %collective-permute-start.21 = (bf16[64,2048]{1,0:T(8,128)(2,1)S(1)}, bf16[64,2048]{1,0:T(8,128)(2,1)}, u32[]{:S(2)}, u32[]{:S(2)}) collective-permute-start(bf16[64,2048]{1,0:T(8,128)(2,1)S(1)} %fusion.2), channel_id=1, source_target_pairs={{128,384},{129,385},{130,386},{131,387},{132,388},{133,389},{134,3... | collective-permute-start | bytes 786440 | tf_op jit(solution)/shard_map/ppermute | solution.py:265
  142.2 23.4 %collective-permute-start.18 = (bf16[64,2048]{1,0:T(8,128)(2,1)}, bf16[64,2048]{1,0:T(8,128)(2,1)}, u32[]{:S(2)}, u32[]{:S(2)}) collective-permute-start(bf16[64,2048]{1,0:T(8,128)(2,1)} %collective-permute-done.17.refs_2_.in3m), channel_id=1, source_target_pairs={{384,448},{448,384},{385,449},{449,385},{386,450},{450,386},{387,4... | collective-permute-start | bytes 786440 | tf_op jit(solution)/shard_map/ppermute | solution.py:255
  162.9 4.1 %collective-permute-start.22 = (bf16[64,2048]{1,0:T(8,128)(2,1)}, bf16[64,2048]{1,0:T(8,128)(2,1)}, u32[]{:S(2)}, u32[]{:S(2)}) collective-permute-start(bf16[64,2048]{1,0:T(8,128)(2,1)} %collective-permute-done.21.refs_4_), channel_id=1, source_target_pairs={{384,448},{448,384},{385,449},{449,385},{386,450},{450,386},{387,4... | collective-permute-start | bytes 786440 | tf_op jit(solution)/shard_map/ppermute | solution.py:255
  176.6 3.8 %collective-permute-start.23 = (bf16[128,2048]{1,0:T(8,128)(2,1)S(1)}, bf16[128,2048]{1,0:T(8,128)(2,1)S(1)}, u32[]{:S(2)}, u32[]{:S(2)}) collective-permute-start(bf16[128,2048]{1,0:T(8,128)(2,1)S(1)} %shard_map.66.own), channel_id=1, source_target_pairs={{384,448},{385,449},{386,450},{387,451},{388,452},{389,453},{390,4... | collective-permute-start | bytes 1572872 | tf_op jit(solution)/shard_map/ppermute | solution.py:273
  177.9 0.7 collective-permute-start.20
  (15 other events, 77.9 us)

commit v3 on v1

v3 whole, which is shorter than its diff:
```python
import functools

import jax
import jax.numpy as jnp
from jax import lax
from jax.experimental import pallas as pl
from jax.experimental.pallas import tpu as pltpu
from jax.sharding import Mesh, PartitionSpec as P

HEAD_DIM = 128
SIDE = 4
TURNS = (0, 1, 3, 2)
AXES = ("zh", "core", "y", "x", "zl")
DP = ("y", "x", "zl")
SECTION = ("zh", "core")
F32 = jnp.float32
BF16 = jnp.bfloat16
VMEM = pl.BlockSpec(memory_space=pltpu.VMEM)
SMEM = pl.BlockSpec(memory_space=pltpu.SMEM)
BLOCKS = 16
LANES = 128


def exchange(array, axis, by):
    return lax.ppermute(array, axis, [(i, i ^ by) for i in range(SIDE)])


def dot(a, b):
    return jnp.dot(a, b, preferred_element_type=F32)


def dot_t(a, b):
    return lax.dot_general(a, b, (((1,), (1,)), ((), ())), preferred_element_type=F32)


def rms(values, gain):
    mean_square = jnp.mean(values * values, axis=-1, keepdims=True)
    return (values * lax.rsqrt(mean_square + 1e-06) * gain).astype(BF16)


def lanes(i):
    return slice(i * LANES, (i + 1) * LANES)


def block_at(scal, dy, dx):
    return lax.bitwise_xor(scal[1], dy) * SIDE + lax.bitwise_xor(scal[0], dx)


def alive(scal, shape):
    at = lax.broadcasted_iota(jnp.int32, shape, 0)
    half = shape[0] // 2
    second = at >= half
    return jnp.where(second, at - half, at) < jnp.where(second, scal[8], scal[7])


def attend(scal, h3, m3, gather_a, gather_b):
    acc_q = acc_k = acc_b = None
    for turn, a, b in zip(TURNS, gather_a, gather_b):
        at = [block_at(scal, turn, d) for d in TURNS]
        hq = jnp.concatenate([h3[i] for i in at], axis=1)
        if m3 is h3:
            both = dot(hq, a[...])
            dq, dk = both[:, :512], both[:, 512:]
        else:
            dq = dot(hq, a[:, :512])
            dk = dot(jnp.concatenate([m3[i] for i in at], axis=1), a[:, 512:])
        at = [block_at(scal, d, turn) for d in TURNS]
        db = dot(jnp.concatenate([m3[i] for i in at], axis=1), b[...])
        if acc_q is None:
            acc_q, acc_k, acc_b = dq, dk, db
        else:
            acc_q, acc_k, acc_b = acc_q + dq, acc_k + dk, acc_b + db
    q = acc_q.astype(BF16)
    k = jnp.concatenate([acc_k, acc_b[:, :256]], axis=1).astype(BF16)
    v = acc_b[:, 256:].astype(BF16)
    count = q.shape[0]
    rows = count // 2
    r = lax.broadcasted_iota(jnp.int32, (count, count), 0)
    c = lax.broadcasted_iota(jnp.int32, (count, count), 1)
    first = c < rows
    live = (r < rows) == first
    live = live & (jnp.where(first, c, c - rows) < jnp.where(first, scal[4], scal[5]))
    live = live & ((c <= r) | (scal[3] == 0))
    mixed = []
    for head in range(4):
        at = lanes(head)
        s = dot_t(q[:, at], k[:, at]) * HEAD_DIM ** (-0.5)
        s = jnp.where(live, s, -1e30)
        e = jnp.exp(s - jnp.max(s, axis=-1, keepdims=True))
        p = (e / jnp.sum(e, axis=-1, keepdims=True)).astype(BF16)
        mixed.append(dot(p, v[:, at]).astype(BF16))
    return jnp.concatenate(mixed, axis=1)


def put_blocks(h3, h):
    for i in range(BLOCKS):
        h3[i] = h[:, lanes(i)]


def project_out(scal, mixed, gather_o, t3):
    for turn, o in zip(TURNS, gather_o):
        t = dot_t(mixed, o[...])
        for j, d in enumerate(TURNS):
            t3[block_at(scal, turn, d)] = t[:, lanes(j)]


def first_kernel(scal, gains, stream, *refs):
    gather_a, gather_b, (mixed, h3) = refs[:4], refs[4:8], refs[8:]

    @pl.when(lax.rem(scal[2], 2) == 0)
    def _():
        put_blocks(h3, rms(stream[...].astype(F32), gains[pl.ds(scal[2], 1), :]))
        mixed[...] = attend(scal, h3, h3, gather_a, gather_b)


def received_kernel(scal, mixed, out_weight, part):
    @pl.when(lax.rem(scal[2], 2) == 1)
    def _():
        for i in range(SIDE):
            at = slice(i * 512, (i + 1) * 512)
            part[:, at] = dot_t(mixed[...], out_weight[at, :]).astype(BF16)


def second_kernel(scal, gains, base, own, got, mixed_in, *refs):
    gather_a, gather_b, gather_o = refs[:4], refs[4:8], refs[8:12]
    stream, mine, other, h3, mixed, t3 = refs[12:]
    cube = scal[2]

    @pl.when(lax.rem(cube, 2) == 1)
    def _():
        term = own[...].astype(F32) + got[...].astype(F32)
        term = jnp.where(alive(scal, base.shape), term, 0.0)
        stream[...] = (base[...].astype(F32) + term).astype(BF16)

    @pl.when(cube == 1)
    def _():
        put_blocks(h3, rms(stream[...].astype(F32), gains[pl.ds(cube, 1), :]))
        mixed[...] = attend(scal, h3, h3, gather_a, gather_b)

    @pl.when(lax.rem(cube, 2) == 0)
    def _():
        mixed[...] = mixed_in[...]

    @pl.when(cube != 3)
    def _():
        project_out(scal, mixed[...], gather_o, t3)
        rows = mine.shape[0]
        here = pl.ds(pl.multiple_of(scal[6] * rows, rows), rows)
        there = pl.ds(pl.multiple_of((1 - scal[6]) * rows, rows), rows)
        for i in range(BLOCKS):
            mine[:, lanes(i)] = t3[i, here, :]
            other[:, lanes(i)] = t3[i, there, :].astype(BF16)


def joined_kernel(scal, gains, base, stream, mine, got, out, memory):
    rows = mine.shape[0]
    here = pl.ds(pl.multiple_of(scal[6] * rows, rows), rows)
    cube = scal[2]

    def join(source):
        at = lax.broadcasted_iota(jnp.int32, mine.shape, 0)
        term = mine[...] + got[...].astype(F32)
        term = jnp.where(at < jnp.where(scal[6] == 0, scal[7], scal[8]), term, 0.0)
        out[...] = (source[here, :].astype(F32) + term).astype(BF16)

    @pl.when(lax.rem(cube, 2) == 0)
    def _():
        join(base)

    @pl.when(cube == 1)
    def _():
        join(stream)
        last = gains.shape[0] - 1
        memory[...] = rms(out[...].astype(F32), gains[last:, :])


def third_kernel(scal, gains, stream, mem_mine, mem_other, *refs):
    gather_a, gather_b, gather_o = refs[:4], refs[4:8], refs[8:12]
    part, h3, m3, t3 = refs[12:]
    cube = scal[2]

    @pl.when(cube == 3)
    def _():
        rows = mem_mine.shape[0]
        here = pl.ds(pl.multiple_of(scal[6] * rows, rows), rows)
        there = pl.ds(pl.multiple_of((1 - scal[6]) * rows, rows), rows)
        put_blocks(h3, rms(stream[...].astype(F32), gains[pl.ds(cube, 1), :]))
        for i in range(BLOCKS):
            m3[i, here, :] = mem_mine[:, lanes(i)]
            m3[i, there, :] = mem_other[:, lanes(i)]
        project_out(scal, attend(scal, h3, m3, gather_a, gather_b), gather_o, t3)
        for i in range(BLOCKS):
            part[:, lanes(i)] = t3[i].astype(BF16)


def finish_kernel(scal, base, stream, early, early_other, own, got, out):
    rows = early.shape[0]
    cube, core = scal[2], scal[6]
    odd = lax.rem(cube, 2) == 1

    @pl.when((core == 0) & jnp.logical_not(odd))
    def _():
        out[...] = base[...]

    @pl.when((core == 0) & odd)
    def _():
        out[...] = stream[...]

    @pl.when((core == 1) & (cube != 3))
    def _():
        out[:rows, :] = early_other[...]
        out[rows:, :] = early[...]

    @pl.when((core == 1) & (cube == 3))
    def _():
        term = own[...].astype(F32) + got[...].astype(F32)
        term = jnp.where(alive(scal, base.shape), term, 0.0)
        out[...] = (stream[...].astype(F32) + term).astype(BF16)


def call(kernel, scal, operands, outs, scratch=(), flops=0):
    size = sum(a.size * a.dtype.itemsize for a in operands)
    return pl.pallas_call(
        kernel,
        out_shape=outs,
        in_specs=[SMEM] + [VMEM] * len(operands),
        out_specs=jax.tree.map(lambda _: VMEM, outs),
        scratch_shapes=[pltpu.VMEM(shape, kind) for shape, kind in scratch],
        compiler_params=pltpu.CompilerParams(vmem_limit_bytes=12 * 1024 * 1024),
        cost_estimate=pl.CostEstimate(flops=flops, bytes_accessed=size, transcendentals=0),
    )(scal, *operands)


def rings(array, axis):
    return [array] + [exchange(array, axis, turn) for turn in TURNS[1:]]


def on_device(encoder_embed, decoder_embed, section_weights, norm_gains, input_lengths, target_lengths):
    zh, core = lax.axis_index("zh"), lax.axis_index("core")
    y, x = lax.axis_index("y"), lax.axis_index("x")
    docs, rows, width = encoder_embed.shape
    count = docs * rows
    encoder = zh < 2
    causal = zh == 2
    key_lengths = jnp.where(causal, target_lengths, input_lengths)
    row_lengths = jnp.where(encoder, input_lengths, target_lengths)
    scal = jnp.stack(
        [x, y, zh, causal.astype(jnp.int32), key_lengths[0], key_lengths[1], core]
        + [row_lengths[0], row_lengths[1]]
    ).astype(jnp.int32)
    base = jnp.where(encoder, encoder_embed, decoder_embed).reshape(count, width)

    pair, depth, inner = section_weights.shape[1:]
    half = inner // 2
    sent = section_weights[0].reshape(pair, depth, 2, half).transpose(2, 0, 1, 3)
    sent = jnp.broadcast_to(sent[:, None], (2, SIDE, pair, depth, half))
    sent = sent.reshape(2 * SIDE, pair, depth, half)
    mats = lax.all_to_all(sent, ("core", "zl"), 0, 0, tiled=True)
    mats = mats.reshape(2, SIDE, pair, depth, half).transpose(0, 2, 1, 3, 4)
    mats = mats.reshape(2 * pair, SIDE * depth, half)
    a = jnp.concatenate([mats[0], mats[1][:, : half // 2]], axis=1)
    b = jnp.concatenate([mats[1][:, half // 2:], mats[2]], axis=1)
    own_o = mats[3]
    prev_o = lax.ppermute(own_o, "zh", [(0, 1), (2, 3)])

    a = jnp.concatenate(rings(a, "x"), axis=0)
    b = jnp.concatenate(rings(b, "y"), axis=0)
    prev_o = lax.all_gather(prev_o, ("y", "x"), axis=0, tiled=True)
    a, b = lax.optimization_barrier((a, b))
    gather_a, gather_b = rings(a, "y"), rings(b, "x")
    own_o, gather_a[1] = lax.optimization_barrier((own_o, gather_a[1]))
    own_o = jnp.concatenate(rings(own_o, "x"), axis=0)

    blocks = ((BLOCKS, count, LANES), BF16)
    totals = ((BLOCKS, count, LANES), F32)
    narrow = jax.ShapeDtypeStruct((count, half), BF16)
    wide = jax.ShapeDtypeStruct((count, width), BF16)
    doc = jax.ShapeDtypeStruct((rows, width), BF16)
    doc32 = jax.ShapeDtypeStruct((rows, width), F32)
    work = 2 * count * width * half
    mixed = call(
        first_kernel, scal, [norm_gains, base, *gather_a, *gather_b], narrow, [blocks], 3 * work
    )
    mixed_in = lax.ppermute(mixed, "zh", [(0, 1), (2, 3)])
    own_o, mixed = lax.optimization_barrier((own_o, mixed))
    gather_o = rings(own_o, "y")

    def swapped(array, cubes):
        pairs = [(2 * c + i, 2 * c + 1 - i) for c in cubes for i in range(2)]
        return lax.ppermute(array, SECTION, pairs)

    part = call(received_kernel, scal, [mixed_in, prev_o], wide, (), work)
    part_got = swapped(part, (1, 3))
    stream, mine, other = call(
        second_kernel,
        scal,
        [norm_gains, base, part, part_got, mixed, *gather_a, *gather_b, *gather_o],
        (wide, doc32, doc),
        [blocks, ((count, half), BF16), totals],
        4 * work,
    )
    other = swapped(other, (0, 1, 2))
    early, memory = call(
        joined_kernel, scal, [norm_gains, base, stream, mine, other], (doc, doc)
    )
    mem = lax.ppermute(memory, "zh", [(1, 3)])
    early_other = lax.ppermute(early, SECTION, [(0, 1), (2, 3), (4, 5)])
    mem_other = swapped(mem, (3,))
    own = call(
        third_kernel,
        scal,
        [norm_gains, stream, mem, mem_other, *gather_a, *gather_b, *gather_o],
        wide,
        [blocks, blocks, totals],
        4 * work,
    )
    got = lax.ppermute(own, SECTION, [(6, 7)])
    out = call(finish_kernel, scal, [base, stream, early, early_other, own, got], wide)
    return out.reshape(1, docs, rows, width)


def solution(mesh):
    fine = Mesh(mesh.devices.reshape(SIDE, 2, SIDE, SIDE, SIDE), AXES)
    in_specs = (
        P(DP, None, None),
        P(DP, None, None),
        P(SECTION, None, DP, None),
        P(),
        P(DP),
        P(DP),
    )
    out_specs = P(SECTION, DP, None, None)
    return jax.shard_map(
        on_device, mesh=fine, in_specs=in_specs, out_specs=out_specs, check_vma=False
    )
```

time: 192 us -> 209 us (1.089)
  between operations: 0.61 us -> 14 us
  starting transfers between devices: 69.2 us -> 78.1 us
  other arithmetic: 6.47 us -> 2.31 us
    ppermute x22 -> x25, starting transfers between devices: 67.9 us -> 76.8 us  [the longest x18 61.8 us: exchange(): return lax.ppermute(array, axis, [(i, i ^ by) for i in range(SIDE)])]
    unnamed x28, local copies, waits for them, and re-layouts: 0.86 us -> 5.12 us
    slice x8 -> x1, local copies, waits for them, and re-layouts: 3.36 us -> 0.01 us  [on_device(): b = jnp.concatenate([mats[1][:, half // 2:], mats[2]], axis=1)]
    another operation x2 -> x0, other arithmetic: 2.55 us -> none  [on_device(): return jnp.stack([doc0, doc1])[None]]
    ppermute x22 -> x25, waiting for transfers between devices: 57.8 us -> 60 us  [the longest x18 39.6 us: exchange(): return lax.ppermute(array, axis, [(i, i ^ by) for i in range(SIDE)])]
    pallas_call x3 -> x6, Pallas kernels: 15.5 us -> 14.1 us  [call(): pl.pallas_call(kernel, out_shape=outs, in_specs=[SMEM] + [VMEM] * len(ope...]
  transfers between devices with their start and end apart: 23 -> 27, of which waited for: 12 -> 10; matrix products, arithmetic and copies ran while one was open for 5% -> 1% of each run, Pallas kernels for 0% -> 2%
where the time goes in v3:
time: 209 us; the launch traced here: 208 us
  starting transfers between devices  78.1 us (37%)
  waiting for transfers between devices  76.4 us (37%)
  blocking collectives  16.6 us (8%)
  Pallas kernels  14.1 us (7%)
  between operations  14 us (7%)
  local copies, waits for them, and re-layouts  6.32 us (3%)
  other arithmetic  2.31 us (1%)
    ppermute x18, starting transfers between devices, exchange(): return lax.ppermute(array, axis, [(i, i ^ by) for i in range(SIDE)])  61.8 us
    ppermute x18, waiting for transfers between devices, exchange(): return lax.ppermute(array, axis, [(i, i ^ by) for i in range(SIDE)])  39.6 us
    ppermute x1, waiting for transfers between devices, on_device(): prev_o = lax.ppermute(own_o, 'zh', [(0, 1), (2, 3)])  17.5 us
    all_to_all x1, blocking collectives, on_device(): mats = lax.all_to_all(sent, ('core', 'zl'), 0, 0, tiled=True)  16.6 us
    ppermute x1, waiting for transfers between devices, on_device(): mem = lax.ppermute(memory, 'zh', [(1, 3)])  16.3 us
    pallas_call x6, Pallas kernels, call(): pl.pallas_call(kernel, out_shape=outs, in_specs=[SMEM] + [VMEM] * len(ope...  14.1 us
    ppermute x3, starting transfers between devices, swapped(): return lax.ppermute(array, SECTION, pairs)  10.4 us
    unnamed x28, local copies, waits for them, and re-layouts  5.12 us
  transfers between devices with their start and end apart: 27, of which 10 were waited for; matrix products, arithmetic and copies ran while one was open for 1% of the time, Pallas kernels for 2%

profile of v3, /device:TPU:481, one launch (start us, length us, event | category | flops | bytes accessed | tf_op | source)
XLA Modules:
  0.0 207.8 jit_solution(16519677651366958116)
XLA Ops:
  7.6 16.6 %all_to_all.5 = bf16[8,2,32,512]{3,2,1,0:T(8,128)(2,1)S(1)} all-to-all(bf16[8,2,32,512]{3,2,1,0:T(8,128)(2,1)S(1)} %bitcast.27), channel_id=1, replica_groups=mesh['zh'=4,'core'=2,'y'=4,'x'=4,'zl'=4] {'core','zl'}, dimensions={0} | all-to-all | bytes 1048576 | tf_op jit(solution)/shard_map/all_to_all | solution.py:258
  25.6 17.5 %collective-permute-done.13 = bf16[128,512]{1,0:T(8,128)(2,1)S(1)} collective-permute-done((bf16[128,512]{1,0:T(8,128)(2,1)S(1)}, bf16[128,512]{1,0:T(8,128)(2,1)S(1)}, u32[]{:S(2)}, u32[]{:S(2)}) %collective-permute-start.13) | collective-permute-done | bytes 131104 | tf_op jit(solution)/shard_map/ppermute | solution.py:264
  43.8 4.7 %collective-permute-start.2 = (bf16[128,768]{1,0:T(8,128)(2,1)S(1)}, bf16[128,768]{1,0:T(8,128)(2,1)S(1)}, u32[]{:S(2)}, u32[]{:S(2)}) collective-permute-start(bf16[128,768]{1,0:T(8,128)(2,1)S(1)} %pad_maximum_fusion.3), channel_id=1, source_target_pairs={{0,8},{4,12},{8,0},{12,4},{1,9},{5,13},{9,1},{13,5},{2,10},{6,14},... | collective-permute-start | bytes 589832 | tf_op jit(solution)/shard_map/ppermute | solution.py:25
  48.5 2.8 %collective-permute-start.1 = (bf16[128,768]{1,0:T(8,128)(2,1)S(1)}, bf16[128,768]{1,0:T(8,128)(2,1)S(1)}, u32[]{:S(2)}, u32[]{:S(2)}) collective-permute-start(bf16[128,768]{1,0:T(8,128)(2,1)S(1)} %pad_maximum_fusion.3), channel_id=1, source_target_pairs={{0,12},{4,8},{8,4},{12,0},{1,13},{5,9},{9,5},{13,1},{2,14},{6,10},... | collective-permute-start | bytes 589832 | tf_op jit(solution)/shard_map/ppermute | solution.py:25
  51.2 1.9 collective-permute-start
  53.2 5.0 %collective-permute-start.5 = (bf16[128,768]{1,0:T(8,128)(2,1)S(1)}, bf16[128,768]{1,0:T(8,128)(2,1)S(1)}, u32[]{:S(2)}, u32[]{:S(2)}) collective-permute-start(bf16[128,768]{1,0:T(8,128)(2,1)S(1)} %pad_maximum_fusion.4), channel_id=1, source_target_pairs={{0,32},{16,48},{32,0},{48,16},{1,33},{17,49},{33,1},{49,17},{2,34}... | collective-permute-start | bytes 589832 | tf_op jit(solution)/shard_map/ppermute | solution.py:25
  58.2 2.7 %collective-permute-start.4 = (bf16[128,768]{1,0:T(8,128)(2,1)S(1)}, bf16[128,768]{1,0:T(8,128)(2,1)S(1)}, u32[]{:S(2)}, u32[]{:S(2)}) collective-permute-start(bf16[128,768]{1,0:T(8,128)(2,1)S(1)} %pad_maximum_fusion.4), channel_id=1, source_target_pairs={{0,48},{16,32},{32,16},{48,0},{1,49},{17,33},{33,17},{49,1},{2,50}... | collective-permute-start | bytes 589832 | tf_op jit(solution)/shard_map/ppermute | solution.py:25
  60.9 1.9 collective-permute-start.3
  62.9 5.5 %collective-permute-done.4 = bf16[128,768]{1,0:T(8,128)(2,1)S(1)} collective-permute-done((bf16[128,768]{1,0:T(8,128)(2,1)S(1)}, bf16[128,768]{1,0:T(8,128)(2,1)S(1)}, u32[]{:S(2)}, u32[]{:S(2)}) %collective-permute-start.4) | collective-permute-done | bytes 196640 | tf_op jit(solution)/shard_map/ppermute | solution.py:25
  68.5 4.1 %collective-permute-start.6 = (bf16[512,768]{1,0:T(8,128)(2,1)S(1)}, bf16[512,768]{1,0:T(8,128)(2,1)S(1)}, u32[]{:S(2)}, u32[]{:S(2)}) collective-permute-start(bf16[512,768]{1,0:T(8,128)(2,1)S(1)} %pad_maximum_fusion.refs_0_), channel_id=1, source_target_pairs={{0,16},{16,0},{32,48},{48,32},{1,17},{17,1},{33,49},{49,33},{2,18}... | collective-permute-start | bytes 2359304 | tf_op jit(solution)/shard_map/ppermute | solution.py:25
  72.6 4.3 %collective-permute-start.8 = (bf16[512,768]{1,0:T(8,128)(2,1)S(1)}, bf16[512,768]{1,0:T(8,128)(2,1)}, u32[]{:S(2)}, u32[]{:S(2)}) collective-permute-start(bf16[512,768]{1,0:T(8,128)(2,1)S(1)} %pad_maximum_fusion.refs_0_), channel_id=1, source_target_pairs={{0,32},{16,48},{32,0},{48,16},{1,33},{17,49},{33,1},{49,17},{2,34}... | collective-permute-start | bytes 2359304 | tf_op jit(solution)/shard_map/ppermute | solution.py:25
  76.9 2.0 collective-permute-start.7
  78.8 5.4 %collective-permute-start.11 = (bf16[512,768]{1,0:T(8,128)(2,1)S(1)}, bf16[512,768]{1,0:T(8,128)(2,1)}, u32[]{:S(2)}, u32[]{:S(2)}) collective-permute-start(bf16[512,768]{1,0:T(8,128)(2,1)S(1)} %pad_maximum_fusion.1.refs_4_), channel_id=1, source_target_pairs={{0,8},{4,12},{8,0},{12,4},{1,9},{5,13},{9,1},{13,5},{2,10},{6,14},... | collective-permute-start | bytes 2359304 | tf_op jit(solution)/shard_map/ppermute | solution.py:25
  84.2 2.5 %collective-permute-start.10 = (bf16[512,768]{1,0:T(8,128)(2,1)S(1)}, bf16[512,768]{1,0:T(8,128)(2,1)}, u32[]{:S(2)}, u32[]{:S(2)}) collective-permute-start(bf16[512,768]{1,0:T(8,128)(2,1)S(1)} %pad_maximum_fusion.1.refs_4_), channel_id=1, source_target_pairs={{0,12},{4,8},{8,4},{12,0},{1,13},{5,9},{9,5},{13,1},{2,14},{6,10},... | collective-permute-start | bytes 2359304 | tf_op jit(solution)/shard_map/ppermute | solution.py:25
  86.8 2.0 collective-permute-done.6.refs_1_
  88.8 2.8 %collective-permute-start.9 = (bf16[512,768]{1,0:T(8,128)(2,1)S(1)}, bf16[512,768]{1,0:T(8,128)(2,1)}, u32[]{:S(2)}, u32[]{:S(2)}) collective-permute-start(bf16[512,768]{1,0:T(8,128)(2,1)S(1)} %pad_maximum_fusion.1.refs_4_), channel_id=1, source_target_pairs={{0,4},{4,0},{8,12},{12,8},{1,5},{5,1},{9,13},{13,9},{2,6},{6,2},{1... | collective-permute-start | bytes 2359304 | tf_op jit(solution)/shard_map/ppermute | solution.py:25
  92.8 18.8 %collective-permute-done.8.refs_3_ = bf16[512,768]{1,0:T(8,128)(2,1)} collective-permute-done((bf16[512,768]{1,0:T(8,128)(2,1)S(1)}, bf16[512,768]{1,0:T(8,128)(2,1)}, u32[]{:S(2)}, u32[]{:S(2)}) %collective-permute-start.8) | collective-permute-done | bytes 786464 | tf_op jit(solution)/shard_map/ppermute | solution.py:25
  111.6 5.5 %collective-permute-start.17 = (bf16[128,512]{1,0:T(8,128)(2,1)}, bf16[128,512]{1,0:T(8,128)(2,1)S(1)}, u32[]{:S(2)}, u32[]{:S(2)}) collective-permute-start(bf16[128,512]{1,0:T(8,128)(2,1)} %copy-done.7), channel_id=1, source_target_pairs={{0,8},{4,12},{8,0},{12,4},{1,9},{5,13},{9,1},{13,5},{2,10},{6,14},... | collective-permute-start | bytes 393224 | tf_op jit(solution)/shard_map/ppermute | solution.py:25
  117.8 4.0 %collective-permute-start.16 = (bf16[128,512]{1,0:T(8,128)(2,1)}, bf16[128,512]{1,0:T(8,128)(2,1)S(1)}, u32[]{:S(2)}, u32[]{:S(2)}) collective-permute-start(bf16[128,512]{1,0:T(8,128)(2,1)} %copy-done.7), channel_id=1, source_target_pairs={{0,12},{4,8},{8,4},{12,0},{1,13},{5,9},{9,5},{13,1},{2,14},{6,10},... | collective-permute-start | bytes 393224 | tf_op jit(solution)/shard_map/ppermute | solution.py:25
  121.7 3.3 %collective-permute-start.15 = (bf16[128,512]{1,0:T(8,128)(2,1)}, bf16[128,512]{1,0:T(8,128)(2,1)}, u32[]{:S(2)}, u32[]{:S(2)}) collective-permute-start(bf16[128,512]{1,0:T(8,128)(2,1)} %copy-done.7), channel_id=1, source_target_pairs={{0,4},{4,0},{8,12},{12,8},{1,5},{5,1},{9,13},{13,9},{2,6},{6,2},{1... | collective-permute-start | bytes 393224 | tf_op jit(solution)/shard_map/ppermute | solution.py:25
  125.2 3.8 %collective-permute-done.10.refs_6_ = bf16[512,768]{1,0:T(8,128)(2,1)} collective-permute-done((bf16[512,768]{1,0:T(8,128)(2,1)S(1)}, bf16[512,768]{1,0:T(8,128)(2,1)}, u32[]{:S(2)}, u32[]{:S(2)}) %collective-permute-start.10) | collective-permute-done | bytes 786464 | tf_op jit(solution)/shard_map/ppermute | solution.py:25
  129.0 2.1 %shard_map.64.mixed_in = bf16[128,512]{1,0:T(8,128)(2,1)S(1)} custom-call(s32[9]{0:T(128)S(1)} %stack.27.scal, f32[5,2048]{1,0:T(8,128)S(1)} %copy-done.1, bf16[128,2048]{1,0:T(8,128)(2,1)S(1)} %bitcast.23, bf16[512,768]{1,0:T(8,128)(2,1)S(1)} %pad_maximum_fusion.refs_0_, bf16[512,768]{1,0:T(8,128)(2,1)S(1)} %collective-permute-done.6.refs_1_, ...), custom_call_target="tpu_custom_call" | custom-call | flops 805306368 | bytes 6856704 | tf_op jit(solution)/shard_map/pallas_call | solution.py:223
  134.8 3.7 %collective-permute-start.20 = (bf16[512,512]{1,0:T(8,128)(2,1)S(1)}, bf16[512,512]{1,0:T(8,128)(2,1)}, u32[]{:S(2)}, u32[]{:S(2)}) collective-permute-start(bf16[512,512]{1,0:T(8,128)(2,1)S(1)} %pad_maximum_fusion.2.refs_8_), channel_id=1, source_target_pairs={{0,32},{16,48},{32,0},{48,16},{1,33},{17,49},{33,1},{49,17},{2,34}... | collective-permute-start | bytes 1572872 | tf_op jit(solution)/shard_map/ppermute | solution.py:25
  138.5 2.8 %collective-permute-start.19 = (bf16[512,512]{1,0:T(8,128)(2,1)S(1)}, bf16[512,512]{1,0:T(8,128)(2,1)}, u32[]{:S(2)}, u32[]{:S(2)}) collective-permute-start(bf16[512,512]{1,0:T(8,128)(2,1)S(1)} %pad_maximum_fusion.2.refs_8_), channel_id=1, source_target_pairs={{0,48},{16,32},{32,16},{48,0},{1,49},{17,33},{33,17},{49,1},{2,50}... | collective-permute-start | bytes 1572872 | tf_op jit(solution)/shard_map/ppermute | solution.py:25
  141.4 2.5 %collective-permute-start.18 = (bf16[512,512]{1,0:T(8,128)(2,1)S(1)}, bf16[512,512]{1,0:T(8,128)(2,1)}, u32[]{:S(2)}, u32[]{:S(2)}) collective-permute-start(bf16[512,512]{1,0:T(8,128)(2,1)S(1)} %pad_maximum_fusion.2.refs_8_), channel_id=1, source_target_pairs={{0,16},{16,0},{32,48},{48,32},{1,17},{17,1},{33,49},{49,33},{2,18}... | collective-permute-start | bytes 1572872 | tf_op jit(solution)/shard_map/ppermute | solution.py:25
  148.4 6.2 %collective-permute-start.14 = (bf16[128,2048]{1,0:T(8,128)(2,1)S(1)}, bf16[128,2048]{1,0:T(8,128)(2,1)S(1)}, u32[]{:S(2)}, u32[]{:S(2)}) collective-permute-start(bf16[128,2048]{1,0:T(8,128)(2,1)S(1)} %shard_map.65.own), channel_id=1, source_target_pairs={{128,192},{192,128},{384,448},{448,384},{129,193},{193,129},{385,4... | collective-permute-start | bytes 1572872 | tf_op jit(solution)/shard_map/ppermute | solution.py:290
  154.6 8.8 %collective-permute-done.19.refs_10_ = bf16[512,512]{1,0:T(8,128)(2,1)} collective-permute-done((bf16[512,512]{1,0:T(8,128)(2,1)S(1)}, bf16[512,512]{1,0:T(8,128)(2,1)}, u32[]{:S(2)}, u32[]{:S(2)}) %collective-permute-start.19) | collective-permute-done | bytes 524320 | tf_op jit(solution)/shard_map/ppermute | solution.py:25
  163.4 2.8 %shard_map.66 = (bf16[128,2048]{1,0:T(8,128)(2,1)S(1)}, f32[64,2048]{1,0:T(8,128)S(1)}, bf16[64,2048]{1,0:T(8,128)(2,1)S(1)}) custom-call(s32[9]{0:T(128)S(1)} %stack.27.scal, f32[5,2048]{1,0:T(8,128)S(1)} %copy-done.1, bf16[128,2048]{1,0:T(8,128)(2,1)S(1)} %bitcast.24, bf16[128,2048]{1,0:T(8,128)(2,1)S(1)} %shard_map.65.own, ...), custom_call_target="tpu_custom_call" | custom-call | flops 1073741824 | bytes 10133504 | tf_op jit(solution)/shard_map/pallas_call | solution.py:223
  168.8 16.3 %collective-permute-done.23.mem_mine = bf16[64,2048]{1,0:T(8,128)(2,1)S(1)} collective-permute-done((bf16[64,2048]{1,0:T(8,128)(2,1)S(1)}, bf16[64,2048]{1,0:T(8,128)(2,1)S(1)}, u32[]{:S(2)}, u32[]{:S(2)}) %collective-permute-start.23) | collective-permute-done | bytes 262176 | tf_op jit(solution)/shard_map/ppermute | solution.py:306
  185.2 3.6 %collective-permute-start.24 = (bf16[64,2048]{1,0:T(8,128)(2,1)S(1)}, bf16[64,2048]{1,0:T(8,128)(2,1)S(1)}, u32[]{:S(2)}, u32[]{:S(2)}) collective-permute-start(bf16[64,2048]{1,0:T(8,128)(2,1)S(1)} %collective-permute-done.23.mem_mine), channel_id=1, source_target_pairs={{384,448},{448,384},{385,449},{449,385},{386,450},{450,386},{387,4... | collective-permute-start | bytes 786440 | tf_op jit(solution)/shard_map/ppermute | solution.py:290
  189.9 5.6 %shard_map.68.own = bf16[128,2048]{1,0:T(8,128)(2,1)S(1)} custom-call(s32[9]{0:T(128)S(1)} %stack.27.scal, f32[5,2048]{1,0:T(8,128)S(1)} %copy-done.1, bf16[128,2048]{1,0:T(8,128)(2,1)S(1)} %get-tuple-element.22.stream, bf16[64,2048]{1,0:T(8,128)(2,1)S(1)} %collective-permute-done.23.mem_mine, bf16[64,2048]{1,0:T(8,128)(2,1)S(1)} %collective-permute-done.24.mem_other, ...), custom_call_target="tpu_custom_call" | custom-call | flops 1073741824 | bytes 9478144 | tf_op jit(solution)/shard_map/pallas_call | solution.py:223
  197.5 1.8 collective-permute-done.25.got
  (72 shorter events, 20.5 us)
Async XLA Ops:
  6.5 138.0 %all-gather.2.cloned.1.call-start = ((), (), s32[]{:S(2)}) async-start(), calls=%async_computation.1 | async-start | bytes 2228224 | tf_op jit(solution)/shard_map/all_gather | solution.py:268
  24.3 19.5 %copy-start.7 = (bf16[128,512]{1,0:T(8,128)(2,1)}, bf16[128,512]{1,0:T(8,128)(2,1)S(1)}, u32[]{:S(2)}) copy-start(bf16[128,512]{1,0:T(8,128)(2,1)S(1)} %get-tuple-element.19) | copy-start | bytes 393220
  24.3 18.8 %collective-permute-start.13 = (bf16[128,512]{1,0:T(8,128)(2,1)S(1)}, bf16[128,512]{1,0:T(8,128)(2,1)S(1)}, u32[]{:S(2)}, u32[]{:S(2)}) collective-permute-start(bf16[128,512]{1,0:T(8,128)(2,1)S(1)} %get-tuple-element.19), channel_id=1, source_target_pairs={{0,128},{256,384},{1,129},{257,385},{2,130},{258,386},{3,131},{259... | collective-permute-start | bytes 393224 | tf_op jit(solution)/shard_map/ppermute | solution.py:264
  43.8 17.1 %collective-permute-start.2 = (bf16[128,768]{1,0:T(8,128)(2,1)S(1)}, bf16[128,768]{1,0:T(8,128)(2,1)S(1)}, u32[]{:S(2)}, u32[]{:S(2)}) collective-permute-start(bf16[128,768]{1,0:T(8,128)(2,1)S(1)} %pad_maximum_fusion.3), channel_id=1, source_target_pairs={{0,8},{4,12},{8,0},{12,4},{1,9},{5,13},{9,1},{13,5},{2,10},{6,14},... | collective-permute-start | bytes 589832 | tf_op jit(solution)/shard_map/ppermute | solution.py:25
  48.5 14.3 %collective-permute-start.1 = (bf16[128,768]{1,0:T(8,128)(2,1)S(1)}, bf16[128,768]{1,0:T(8,128)(2,1)S(1)}, u32[]{:S(2)}, u32[]{:S(2)}) collective-permute-start(bf16[128,768]{1,0:T(8,128)(2,1)S(1)} %pad_maximum_fusion.3), channel_id=1, source_target_pairs={{0,12},{4,8},{8,4},{12,0},{1,13},{5,9},{9,5},{13,1},{2,14},{6,10},... | collective-permute-start | bytes 589832 | tf_op jit(solution)/shard_map/ppermute | solution.py:25
  51.2 11.6 %collective-permute-start = (bf16[128,768]{1,0:T(8,128)(2,1)S(1)}, bf16[128,768]{1,0:T(8,128)(2,1)S(1)}, u32[]{:S(2)}, u32[]{:S(2)}) collective-permute-start(bf16[128,768]{1,0:T(8,128)(2,1)S(1)} %pad_maximum_fusion.3), channel_id=1, source_target_pairs={{0,4},{4,0},{8,12},{12,8},{1,5},{5,1},{9,13},{13,9},{2,6},{6,2},{1... | collective-permute-start | bytes 589832 | tf_op jit(solution)/shard_map/ppermute | solution.py:25
  53.2 38.5 %copy-start.6 = (bf16[2,64,2048]{2,1,0:T(8,128)(2,1)S(1)}, bf16[2,64,2048]{2,1,0:T(8,128)(2,1)}, u32[]{:S(2)}) copy-start(bf16[2,64,2048]{2,1,0:T(8,128)(2,1)} %param.6) | copy-start | bytes 1572868
  53.2 9.7 %collective-permute-start.5 = (bf16[128,768]{1,0:T(8,128)(2,1)S(1)}, bf16[128,768]{1,0:T(8,128)(2,1)S(1)}, u32[]{:S(2)}, u32[]{:S(2)}) collective-permute-start(bf16[128,768]{1,0:T(8,128)(2,1)S(1)} %pad_maximum_fusion.4), channel_id=1, source_target_pairs={{0,32},{16,48},{32,0},{48,16},{1,33},{17,49},{33,1},{49,17},{2,34}... | collective-permute-start | bytes 589832 | tf_op jit(solution)/shard_map/ppermute | solution.py:25
  58.2 10.2 %collective-permute-start.4 = (bf16[128,768]{1,0:T(8,128)(2,1)S(1)}, bf16[128,768]{1,0:T(8,128)(2,1)S(1)}, u32[]{:S(2)}, u32[]{:S(2)}) collective-permute-start(bf16[128,768]{1,0:T(8,128)(2,1)S(1)} %pad_maximum_fusion.4), channel_id=1, source_target_pairs={{0,48},{16,32},{32,16},{48,0},{1,49},{17,33},{33,17},{49,1},{2,50}... | collective-permute-start | bytes 589832 | tf_op jit(solution)/shard_map/ppermute | solution.py:25
  60.9 7.5 %collective-permute-start.3 = (bf16[128,768]{1,0:T(8,128)(2,1)S(1)}, bf16[128,768]{1,0:T(8,128)(2,1)S(1)}, u32[]{:S(2)}, u32[]{:S(2)}) collective-permute-start(bf16[128,768]{1,0:T(8,128)(2,1)S(1)} %pad_maximum_fusion.4), channel_id=1, source_target_pairs={{0,16},{16,0},{32,48},{48,32},{1,17},{17,1},{33,49},{49,33},{2,18}... | collective-permute-start | bytes 589832 | tf_op jit(solution)/shard_map/ppermute | solution.py:25
  62.9 62.2 %copy-start.12 = (s32[2]{0:T(128)S(1)}, s32[2]{0:T(128)}, u32[]{:S(2)}) copy-start(s32[2]{0:T(128)} %param.10) | copy-start | bytes 28
  62.9 62.2 %copy-start.13 = (s32[2]{0:T(128)S(1)}, s32[2]{0:T(128)}, u32[]{:S(2)}) copy-start(s32[2]{0:T(128)} %param.11) | copy-start | bytes 28
  62.9 66.1 %copy-start.1 = (f32[5,2048]{1,0:T(8,128)S(1)}, f32[5,2048]{1,0:T(8,128)}, u32[]{:S(2)}) copy-start(f32[5,2048]{1,0:T(8,128)} %gains.7) | copy-start | bytes 122884
  68.5 20.3 %collective-permute-start.6 = (bf16[512,768]{1,0:T(8,128)(2,1)S(1)}, bf16[512,768]{1,0:T(8,128)(2,1)S(1)}, u32[]{:S(2)}, u32[]{:S(2)}) collective-permute-start(bf16[512,768]{1,0:T(8,128)(2,1)S(1)} %pad_maximum_fusion.refs_0_), channel_id=1, source_target_pairs={{0,16},{16,0},{32,48},{48,32},{1,17},{17,1},{33,49},{49,33},{2,18}... | collective-permute-start | bytes 2359304 | tf_op jit(solution)/shard_map/ppermute | solution.py:25
  72.6 39.0 %collective-permute-start.8 = (bf16[512,768]{1,0:T(8,128)(2,1)S(1)}, bf16[512,768]{1,0:T(8,128)(2,1)}, u32[]{:S(2)}, u32[]{:S(2)}) collective-permute-start(bf16[512,768]{1,0:T(8,128)(2,1)S(1)} %pad_maximum_fusion.refs_0_), channel_id=1, source_target_pairs={{0,32},{16,48},{32,0},{48,16},{1,33},{17,49},{33,1},{49,17},{2,34}... | collective-permute-start | bytes 2359304 | tf_op jit(solution)/shard_map/ppermute | solution.py:25
  76.9 40.9 %collective-permute-start.7 = (bf16[512,768]{1,0:T(8,128)(2,1)S(1)}, bf16[512,768]{1,0:T(8,128)(2,1)}, u32[]{:S(2)}, u32[]{:S(2)}) collective-permute-start(bf16[512,768]{1,0:T(8,128)(2,1)S(1)} %pad_maximum_fusion.refs_0_), channel_id=1, source_target_pairs={{0,48},{16,32},{32,16},{48,0},{1,49},{17,33},{33,17},{49,1},{2,50}... | collective-permute-start | bytes 2359304 | tf_op jit(solution)/shard_map/ppermute | solution.py:25
  78.8 42.9 %collective-permute-start.11 = (bf16[512,768]{1,0:T(8,128)(2,1)S(1)}, bf16[512,768]{1,0:T(8,128)(2,1)}, u32[]{:S(2)}, u32[]{:S(2)}) collective-permute-start(bf16[512,768]{1,0:T(8,128)(2,1)S(1)} %pad_maximum_fusion.1.refs_4_), channel_id=1, source_target_pairs={{0,8},{4,12},{8,0},{12,4},{1,9},{5,13},{9,1},{13,5},{2,10},{6,14},... | collective-permute-start | bytes 2359304 | tf_op jit(solution)/shard_map/ppermute | solution.py:25
  84.2 44.8 %collective-permute-start.10 = (bf16[512,768]{1,0:T(8,128)(2,1)S(1)}, bf16[512,768]{1,0:T(8,128)(2,1)}, u32[]{:S(2)}, u32[]{:S(2)}) collective-permute-start(bf16[512,768]{1,0:T(8,128)(2,1)S(1)} %pad_maximum_fusion.1.refs_4_), channel_id=1, source_target_pairs={{0,12},{4,8},{8,4},{12,0},{1,13},{5,9},{9,5},{13,1},{2,14},{6,10},... | collective-permute-start | bytes 2359304 | tf_op jit(solution)/shard_map/ppermute | solution.py:25
  88.8 40.2 %collective-permute-start.9 = (bf16[512,768]{1,0:T(8,128)(2,1)S(1)}, bf16[512,768]{1,0:T(8,128)(2,1)}, u32[]{:S(2)}, u32[]{:S(2)}) collective-permute-start(bf16[512,768]{1,0:T(8,128)(2,1)S(1)} %pad_maximum_fusion.1.refs_4_), channel_id=1, source_target_pairs={{0,4},{4,0},{8,12},{12,8},{1,5},{5,1},{9,13},{13,9},{2,6},{6,2},{1... | collective-permute-start | bytes 2359304 | tf_op jit(solution)/shard_map/ppermute | solution.py:25
  111.6 20.9 %collective-permute-start.17 = (bf16[128,512]{1,0:T(8,128)(2,1)}, bf16[128,512]{1,0:T(8,128)(2,1)S(1)}, u32[]{:S(2)}, u32[]{:S(2)}) collective-permute-start(bf16[128,512]{1,0:T(8,128)(2,1)} %copy-done.7), channel_id=1, source_target_pairs={{0,8},{4,12},{8,0},{12,4},{1,9},{5,13},{9,1},{13,5},{2,10},{6,14},... | collective-permute-start | bytes 393224 | tf_op jit(solution)/shard_map/ppermute | solution.py:25
  117.8 14.7 %collective-permute-start.16 = (bf16[128,512]{1,0:T(8,128)(2,1)}, bf16[128,512]{1,0:T(8,128)(2,1)S(1)}, u32[]{:S(2)}, u32[]{:S(2)}) collective-permute-start(bf16[128,512]{1,0:T(8,128)(2,1)} %copy-done.7), channel_id=1, source_target_pairs={{0,12},{4,8},{8,4},{12,0},{1,13},{5,9},{9,5},{13,1},{2,14},{6,10},... | collective-permute-start | bytes 393224 | tf_op jit(solution)/shard_map/ppermute | solution.py:25
  121.7 12.0 %collective-permute-start.15 = (bf16[128,512]{1,0:T(8,128)(2,1)}, bf16[128,512]{1,0:T(8,128)(2,1)}, u32[]{:S(2)}, u32[]{:S(2)}) collective-permute-start(bf16[128,512]{1,0:T(8,128)(2,1)} %copy-done.7), channel_id=1, source_target_pairs={{0,4},{4,0},{8,12},{12,8},{1,5},{5,1},{9,13},{13,9},{2,6},{6,2},{1... | collective-permute-start | bytes 393224 | tf_op jit(solution)/shard_map/ppermute | solution.py:25
  131.2 12.7 %collective-permute-start.12 = (bf16[128,512]{1,0:T(8,128)(2,1)S(1)}, bf16[128,512]{1,0:T(8,128)(2,1)S(1)}, u32[]{:S(2)}, u32[]{:S(2)}) collective-permute-start(bf16[128,512]{1,0:T(8,128)(2,1)S(1)} %shard_map.64.mixed_in), channel_id=1, source_target_pairs={{0,128},{256,384},{1,129},{257,385},{2,130},{258,386},{3,131},{259... | collective-permute-start | bytes 393224 | tf_op jit(solution)/shard_map/ppermute | solution.py:284
  134.8 19.7 %collective-permute-start.20 = (bf16[512,512]{1,0:T(8,128)(2,1)S(1)}, bf16[512,512]{1,0:T(8,128)(2,1)}, u32[]{:S(2)}, u32[]{:S(2)}) collective-permute-start(bf16[512,512]{1,0:T(8,128)(2,1)S(1)} %pad_maximum_fusion.2.refs_8_), channel_id=1, source_target_pairs={{0,32},{16,48},{32,0},{48,16},{1,33},{17,49},{33,1},{49,17},{2,34}... | collective-permute-start | bytes 1572872 | tf_op jit(solution)/shard_map/ppermute | solution.py:25
  138.5 24.9 %collective-permute-start.19 = (bf16[512,512]{1,0:T(8,128)(2,1)S(1)}, bf16[512,512]{1,0:T(8,128)(2,1)}, u32[]{:S(2)}, u32[]{:S(2)}) collective-permute-start(bf16[512,512]{1,0:T(8,128)(2,1)S(1)} %pad_maximum_fusion.2.refs_8_), channel_id=1, source_target_pairs={{0,48},{16,32},{32,16},{48,0},{1,49},{17,33},{33,17},{49,1},{2,50}... | collective-permute-start | bytes 1572872 | tf_op jit(solution)/shard_map/ppermute | solution.py:25
  141.4 22.1 %collective-permute-start.18 = (bf16[512,512]{1,0:T(8,128)(2,1)S(1)}, bf16[512,512]{1,0:T(8,128)(2,1)}, u32[]{:S(2)}, u32[]{:S(2)}) collective-permute-start(bf16[512,512]{1,0:T(8,128)(2,1)S(1)} %pad_maximum_fusion.2.refs_8_), channel_id=1, source_target_pairs={{0,16},{16,0},{32,48},{48,32},{1,17},{17,1},{33,49},{49,33},{2,18}... | collective-permute-start | bytes 1572872 | tf_op jit(solution)/shard_map/ppermute | solution.py:25
  148.4 15.0 %collective-permute-start.14 = (bf16[128,2048]{1,0:T(8,128)(2,1)S(1)}, bf16[128,2048]{1,0:T(8,128)(2,1)S(1)}, u32[]{:S(2)}, u32[]{:S(2)}) collective-permute-start(bf16[128,2048]{1,0:T(8,128)(2,1)S(1)} %shard_map.65.own), channel_id=1, source_target_pairs={{128,192},{192,128},{384,448},{448,384},{129,193},{193,129},{385,4... | collective-permute-start | bytes 1572872 | tf_op jit(solution)/shard_map/ppermute | solution.py:290
  166.3 0.7 collective-permute-start.21
  167.5 17.6 %collective-permute-start.23 = (bf16[64,2048]{1,0:T(8,128)(2,1)S(1)}, bf16[64,2048]{1,0:T(8,128)(2,1)S(1)}, u32[]{:S(2)}, u32[]{:S(2)}) collective-permute-start(bf16[64,2048]{1,0:T(8,128)(2,1)S(1)} %get-tuple-element.26), channel_id=1, source_target_pairs={{128,384},{129,385},{130,386},{131,387},{132,388},{133,389},{134,3... | collective-permute-start | bytes 786440 | tf_op jit(solution)/shard_map/ppermute | solution.py:306
  185.2 4.7 %collective-permute-start.24 = (bf16[64,2048]{1,0:T(8,128)(2,1)S(1)}, bf16[64,2048]{1,0:T(8,128)(2,1)S(1)}, u32[]{:S(2)}, u32[]{:S(2)}) collective-permute-start(bf16[64,2048]{1,0:T(8,128)(2,1)S(1)} %collective-permute-done.23.mem_mine), channel_id=1, source_target_pairs={{384,448},{448,384},{385,449},{449,385},{386,450},{450,386},{387,4... | collective-permute-start | bytes 786440 | tf_op jit(solution)/shard_map/ppermute | solution.py:290
  195.5 3.8 %collective-permute-start.25 = (bf16[128,2048]{1,0:T(8,128)(2,1)S(1)}, bf16[128,2048]{1,0:T(8,128)(2,1)S(1)}, u32[]{:S(2)}, u32[]{:S(2)}) collective-permute-start(bf16[128,2048]{1,0:T(8,128)(2,1)S(1)} %shard_map.68.own), channel_id=1, source_target_pairs={{384,448},{385,449},{386,450},{387,451},{388,452},{389,453},{390,4... | collective-permute-start | bytes 1572872 | tf_op jit(solution)/shard_map/ppermute | solution.py:317
  196.8 0.7 collective-permute-start.22
  (9 other events, 33.6 us)
Sparse Core Ops, SparseCore 0:
  43.9 84.2 all-gather.1

commit v4 on v2

--- a/solution.py
+++ b/solution.py
@@ -1,4 +1,5 @@
 import functools
+import itertools
 
 import jax
 import jax.numpy as jnp
@@ -17,8 +18,17 @@
 BF16 = jnp.bfloat16
 
 
-def exchange(array, axis, by):
-    return lax.ppermute(array, axis, [(i, i ^ by) for i in range(SIDE)])
+def place(zh, core, y, x, zl):
+    return (((zh * 2 + core) * SIDE + y) * SIDE + x) * SIDE + zl
+
+
+def exchange(array, outer, by):
+    pairs = []
+    for zh, core, y, x, zl in itertools.product(*map(range, (SIDE, 2, SIDE, SIDE, SIDE))):
+        along_y = outer == (core == 0)
+        to = (y ^ by, x) if along_y else (y, x ^ by)
+        pairs.append((place(zh, core, y, x, zl), place(zh, core, *to, zl)))
+    return lax.ppermute(array, AXES, pairs)
 
 
 def dot(a, b):
@@ -43,8 +53,8 @@
     if cross:
         mem = refs[:2]
         refs = refs[2:]
-    a_refs, b_refs = refs[:5], refs[5:10]
-    refs = refs[10:]
+    pieces = refs[:SIDE]
+    refs = refs[SIDE:]
     if cross:
         rows = mine.shape[0]
         out_mine, out_other = refs[0].at[:rows], refs[0].at[rows:]
@@ -55,7 +65,7 @@
     h3, m3, t3 = refs
 
     def work():
-        sublayer_body(scal, gains, (mine, other), mem, a_refs, b_refs, out_mine, out_other, h3, m3, t3)
+        sublayer_body(scal, gains, (mine, other), mem, pieces, out_mine, out_other, h3, m3, t3)
 
     if cube is None:
         work()
@@ -63,7 +73,7 @@
         pl.when(scal[2] == cube)(work)
 
 
-def sublayer_body(scal, gains, streams, mem, a_refs, b_refs, out_mine, out_other, h3, m3, t3):
+def sublayer_body(scal, gains, streams, mem, pieces, out_mine, out_other, h3, m3, t3):
     rows = streams[0].shape[0]
     x, y, sub, causal, len_mine, len_other = (scal[i] for i in range(6))
     gain = gains[pl.ds(sub, 1), :]
@@ -76,22 +86,18 @@
         for i in range(16):
             m3[i, part * rows:(part + 1) * rows, :] = ref[:, i * 128:(i + 1) * 128]
 
-    def blk(dy, dx):
+    back = scal[6] == 1
+
+    def blk(outer, inner):
+        dy, dx = jnp.where(back, inner, outer), jnp.where(back, outer, inner)
         return lax.bitwise_xor(y, dy) * SIDE + lax.bitwise_xor(x, dx)
 
-    def piece(group, turn, which):
-        if turn == 2:
-            return group[3 + which][0]
-        return group[TURNS.index(turn)][which]
-
     q = k = v = None
-    for turn in TURNS:
+    for turn, piece in zip(TURNS, pieces):
         cols = [blk(turn, d) for d in TURNS]
         hq = jnp.concatenate([h3[c] for c in cols], axis=1)
         hk = jnp.concatenate([kv3[c] for c in cols], axis=1) if mem else hq
-        dq, dk = dot(hq, piece(a_refs, turn, 0)), dot(hk, piece(a_refs, turn, 1))
-        cols = [blk(d, turn) for d in TURNS]
-        dv = dot(jnp.concatenate([kv3[c] for c in cols], axis=1), piece(b_refs, turn, 0))
+        dq, dk, dv = dot(hq, piece[0]), dot(hk, piece[1]), dot(hk, piece[2])
         q, k, v = (dq, dk, dv) if q is None else (q + dq, k + dk, v + dv)
     q, k, v = q.astype(BF16), k.astype(BF16), v.astype(BF16)
     r = lax.broadcasted_iota(jnp.int32, (2 * rows, 2 * rows), 0)
@@ -110,10 +116,10 @@
         p = (e / jnp.sum(e, axis=-1, keepdims=True)).astype(BF16)
         mixed.append(dot(p, v[:, at]).astype(BF16))
     mixed = jnp.concatenate(mixed, axis=1)
-    for turn in TURNS:
-        t = dot_t(mixed, piece(b_refs, turn, 1))
+    for turn, piece in zip(TURNS, pieces):
+        t = dot_t(mixed, piece[3])
         for j, d in enumerate(TURNS):
-            t3[blk(d, turn)] = t[:, j * 128:(j + 1) * 128]
+            t3[blk(turn, d)] = t[:, j * 128:(j + 1) * 128]
     for i in range(16):
         at = slice(i * 128, (i + 1) * 128)
         out_mine[:, at] = t3[i, :rows, :].astype(out_mine.dtype)
@@ -124,9 +130,9 @@
 SMEM = pl.BlockSpec(memory_space=pltpu.SMEM)
 
 
-def sublayer(cross, cube, scal, gains, streams, mem, a_parts, b_parts):
+def sublayer(cross, cube, scal, gains, streams, mem, pieces):
     rows, width = streams[0].shape
-    operands = [gains, *streams, *mem, *a_parts, *b_parts]
+    operands = [gains, *streams, *mem, *pieces]
     halves = tuple(jax.ShapeDtypeStruct((rows, width), kind) for kind in (F32, BF16))
     return pl.pallas_call(
         functools.partial(sublayer_kernel, cross, cube),
@@ -138,7 +144,7 @@
             pltpu.VMEM((16, 2 * rows, 128) if cross else (1, 16, 128), BF16),
             pltpu.VMEM((16, 2 * rows, 128), F32),
         ],
-        compiler_params=pltpu.CompilerParams(vmem_limit_bytes=20 * 1024 * 1024),
+        compiler_params=pltpu.CompilerParams(vmem_limit_bytes=12 * 1024 * 1024),
         cost_estimate=pl.CostEstimate(
             flops=2 * 128 * 2048 * 512 * 4, bytes_accessed=9 * 2**20, transcendentals=65536
         ),
@@ -186,21 +192,12 @@
         out_shape=jax.ShapeDtypeStruct((2,) + parts[0].shape, BF16),
         in_specs=[SMEM] + [VMEM] * len(parts),
         out_specs=VMEM,
-        compiler_params=pltpu.CompilerParams(vmem_limit_bytes=20 * 1024 * 1024),
+        compiler_params=pltpu.CompilerParams(vmem_limit_bytes=12 * 1024 * 1024),
     )(scal, *parts)
 
 
-def ring(array, axis):
-    parts = [array] + [exchange(array, axis, turn) for turn in TURNS[1:]]
-    return jnp.concatenate(parts, axis=1)
-
-
-def ring_parts(array, axis):
-    return exchange(array, axis, 1), exchange(array, axis, 3)
-
-
-def far_parts(by1, by3, axis):
-    return exchange(by1[:1], axis, 3), exchange(by3[1:], axis, 1)
+def turns(array, outer):
+    return [array] + [exchange(array, outer, turn) for turn in TURNS[1:]]
 
 
 def gather(weights):
@@ -210,14 +207,8 @@
     sent = sent.reshape((2 * SIDE,) + halves.shape[1:])
     got = lax.all_to_all(sent, ("core", "zl"), 0, 0, tiled=True)
     got = got.reshape(2, SIDE, pair, depth, width // 2).transpose(0, 2, 1, 3, 4)
-    got = got.reshape(2, pair, SIDE * depth, width // 2)
-    a, b = ring(got[0], "x"), ring(got[1], "y")
-    a, b = lax.optimization_barrier((a, b))
-    ap, am = ring_parts(a, "y")
-    bp, bm = ring_parts(b, "x")
-    af0, af1 = far_parts(ap, am, "y")
-    bf0, bf1 = far_parts(bp, bm, "x")
-    return (a, ap, am, af0, af1), (b, bp, bm, bf0, bf1)
+    got = got.reshape(2 * pair, SIDE * depth, width // 2)
+    return turns(jnp.concatenate(turns(got, False), axis=1), True)
 
 
 def on_device(encoder_embed, decoder_embed, section_weights, norm_gains, input_lengths, target_lengths):
@@ -243,7 +234,7 @@
     ).astype(jnp.int32)
     live = (jnp.arange(rows, dtype=jnp.int32) < row_lengths[core])[:, None]
 
-    a_parts, b_parts = gather(section_weights)
+    pieces = gather(section_weights)
     source = jnp.where(encoder, encoder_embed, decoder_embed)
     mine, other = source[core], source[1 - core]
 
@@ -254,12 +245,12 @@
         pairs = [(2 * c + i, 2 * c + 1 - i) for c in cubes for i in range(2)]
         return lax.ppermute(array, SECTION, pairs)
 
-    kept, sent = sublayer(False, None, scal, norm_gains, (mine, other), (), a_parts, b_parts)
+    kept, sent = sublayer(False, None, scal, norm_gains, (mine, other), (), pieces)
     first = added(mine, kept + swapped(sent, (0, 2)).astype(F32), live).astype(BF16)
     in1 = lax.ppermute(first, "zh", [(0, 1)])
     in3 = lax.ppermute(first, "zh", [(2, 3)])
     in1_other = swapped(in1, (1,))
-    kept, sent = sublayer(False, 1, scal, norm_gains, (in1, in1_other), (), a_parts, b_parts)
+    kept, sent = sublayer(False, 1, scal, norm_gains, (in1, in1_other), (), pieces)
     second = added(in1, kept + swapped(sent, (1,)).astype(F32), live).astype(BF16)
     memory = rms(second.astype(F32), norm_gains[4:5])
     mem = lax.ppermute(memory, "zh", [(1, 3)])
@@ -268,7 +259,7 @@
     in3_other = swapped(in3, (3,))
     mem_other = swapped(mem, (3,))
     own = sublayer(
-        True, 3, scal, norm_gains, (in3, in3_other), (mem, mem_other), a_parts, b_parts
+        True, 3, scal, norm_gains, (in3, in3_other), (mem, mem_other), pieces
     )
     got = lax.ppermute(own, SECTION, [(6, 7)])
     out = finish(

time: 184 us -> 167 us (0.908)
  starting transfers between devices: 59 us -> 37.9 us
  waiting for transfers between devices: 77.7 us -> 89.2 us
  local copies, waits for them, and re-layouts: 12.7 us -> 4.45 us
  Pallas kernels: 14.5 us -> 17 us
    ppermute x14 -> x6, starting transfers between devices: 45.4 us -> 19 us  [exchange(): return lax.ppermute(array, AXES, pairs)]
    ppermute x14 -> x6, waiting for transfers between devices: 29.7 us -> 46.8 us  [exchange(): return lax.ppermute(array, AXES, pairs)]
    ppermute x1, waiting for transfers between devices: 17 us -> 10.2 us  [on_device(): mem = lax.ppermute(memory, 'zh', [(1, 3)])]
    ppermute x5, starting transfers between devices: 8.36 us -> 13.6 us  [swapped(): return lax.ppermute(array, SECTION, pairs)]
    unnamed x46 -> x18, local copies, waits for them, and re-layouts: 4.96 us -> 0.05 us
    slice x7 -> x0, local copies, waits for them, and re-layouts: 3.34 us -> none  [the longest x4 3.26 us: far_parts(): return (exchange(by1[:1], axis, 3), exchange(by3[1:], axis, 1))]
    pallas_call x3, Pallas kernels: 12.4 us -> 15 us  [sublayer(): pl.pallas_call(functools.partial(sublayer_kernel, cross, cube), out_shape...]
  transfers between devices with their start and end apart: 24 -> 16, of which waited for: 11 -> 10; matrix products, arithmetic and copies ran while one was open for 4% -> 3% of each run, Pallas kernels for 0% -> 0%
where the time goes in v4:
time: 167 us
  waiting for transfers between devices  89.2 us (53%)
  starting transfers between devices  37.9 us (23%)
  Pallas kernels  17 us (10%)
  blocking collectives  16.6 us (10%)
  local copies, waits for them, and re-layouts  4.45 us (3%)
    ppermute x6, waiting for transfers between devices, exchange(): return lax.ppermute(array, AXES, pairs)  46.8 us
    ppermute x1, waiting for transfers between devices, on_device(): in3 = lax.ppermute(first, 'zh', [(2, 3)])  29 us
    ppermute x6, starting transfers between devices, exchange(): return lax.ppermute(array, AXES, pairs)  19 us
    all_to_all x1, blocking collectives, gather(): got = lax.all_to_all(sent, ('core', 'zl'), 0, 0, tiled=True)  16.6 us
    pallas_call x3, Pallas kernels, sublayer(): pl.pallas_call(functools.partial(sublayer_kernel, cross, cube), out_shape...  15 us
    ppermute x5, starting transfers between devices, swapped(): return lax.ppermute(array, SECTION, pairs)  13.6 us
    ppermute x1, waiting for transfers between devices, on_device(): mem = lax.ppermute(memory, 'zh', [(1, 3)])  10.2 us
  transfers between devices with their start and end apart: 16, of which 10 were waited for; matrix products, arithmetic and copies ran while one was open for 3% of the time, Pallas kernels for 0%

profile of v4, /device:TPU:481, one launch (start us, length us, event | category | flops | bytes accessed | tf_op | source)
XLA Modules:
  0.0 166.9 jit_solution(1785481200472216318)
XLA Ops:
  0.0 1.0 reshape_squeeze.3
  1.1 16.6 %all_to_all.5 = bf16[8,2,32,512]{3,2,1,0:T(8,128)(2,1)S(1)} all-to-all(bf16[8,2,32,512]{3,2,1,0:T(8,128)(2,1)S(1)} %bitcast.20), channel_id=1, replica_groups=mesh['zh'=4,'core'=2,'y'=4,'x'=4,'zl'=4] {'core','zl'}, dimensions={0} | all-to-all | bytes 1048576 | tf_op jit(solution)/shard_map/all_to_all | solution.py:208
  17.7 5.0 %collective-permute-start.2 = (bf16[4,128,512]{2,1,0:T(8,128)(2,1)S(1)}, bf16[4,128,512]{2,1,0:T(8,128)(2,1)S(1)}, u32[]{:S(2)}, u32[]{:S(2)}) collective-permute-start(bf16[4,128,512]{2,1,0:T(8,128)(2,1)S(1)} %bitcast.22), channel_id=1, source_target_pairs={{0,8},{1,9},{2,10},{3,11},{4,12},{5,13},{6,14},{7,15},{8,0},{9,1},... | collective-permute-start | bytes 1572872 | tf_op jit(solution)/shard_map/ppermute | solution.py:31
  22.7 2.7 %collective-permute-start.1 = (bf16[4,128,512]{2,1,0:T(8,128)(2,1)S(1)}, bf16[4,128,512]{2,1,0:T(8,128)(2,1)S(1)}, u32[]{:S(2)}, u32[]{:S(2)}) collective-permute-start(bf16[4,128,512]{2,1,0:T(8,128)(2,1)S(1)} %bitcast.23), channel_id=1, source_target_pairs={{0,12},{1,13},{2,14},{3,15},{4,8},{5,9},{6,10},{7,11},{8,4},{9,5},... | collective-permute-start | bytes 1572872 | tf_op jit(solution)/shard_map/ppermute | solution.py:31
  25.4 1.9 %collective-permute-start = (bf16[4,128,512]{2,1,0:T(8,128)(2,1)S(1)}, bf16[4,128,512]{2,1,0:T(8,128)(2,1)S(1)}, u32[]{:S(2)}, u32[]{:S(2)}) collective-permute-start(bf16[4,128,512]{2,1,0:T(8,128)(2,1)S(1)} %bitcast.24), channel_id=1, source_target_pairs={{0,4},{1,5},{2,6},{3,7},{4,0},{5,1},{6,2},{7,3},{8,12},{9,13},{10,... | collective-permute-start | bytes 1572872 | tf_op jit(solution)/shard_map/ppermute | solution.py:31
  27.3 2.3 %collective-permute-done.2 = bf16[4,128,512]{2,1,0:T(8,128)(2,1)S(1)} collective-permute-done((bf16[4,128,512]{2,1,0:T(8,128)(2,1)S(1)}, bf16[4,128,512]{2,1,0:T(8,128)(2,1)S(1)}, u32[]{:S(2)}, u32[]{:S(2)}) %collective-permute-start.2) | collective-permute-done | bytes 524320 | tf_op jit(solution)/shard_map/ppermute | solution.py:31
  29.6 5.6 %collective-permute-done.1 = bf16[4,128,512]{2,1,0:T(8,128)(2,1)S(1)} collective-permute-done((bf16[4,128,512]{2,1,0:T(8,128)(2,1)S(1)}, bf16[4,128,512]{2,1,0:T(8,128)(2,1)S(1)}, u32[]{:S(2)}, u32[]{:S(2)}) %collective-permute-start.1) | collective-permute-done | bytes 524320 | tf_op jit(solution)/shard_map/ppermute | solution.py:31
  35.7 4.8 %collective-permute-start.5 = (bf16[4,512,512]{2,1,0:T(8,128)(2,1)S(1)}, bf16[4,512,512]{2,1,0:T(8,128)(2,1)}, u32[]{:S(2)}, u32[]{:S(2)}) collective-permute-start(bf16[4,512,512]{2,1,0:T(8,128)(2,1)S(1)} %pad_maximum_fusion.refs_4_.refs_6_), channel_id=1, source_target_pairs={{0,32},{1,33},{2,34},{3,35},{4,36},{5,37},{6,38},{7,39},{8,40},{9,... | collective-permute-start | bytes 6291464 | tf_op jit(solution)/shard_map/ppermute | solution.py:31
  40.5 2.8 %collective-permute-start.4 = (bf16[4,512,512]{2,1,0:T(8,128)(2,1)S(1)}, bf16[4,512,512]{2,1,0:T(8,128)(2,1)}, u32[]{:S(2)}, u32[]{:S(2)}) collective-permute-start(bf16[4,512,512]{2,1,0:T(8,128)(2,1)S(1)} %pad_maximum_fusion.refs_4_.refs_6_), channel_id=1, source_target_pairs={{0,48},{1,49},{2,50},{3,51},{4,52},{5,53},{6,54},{7,55},{8,56},{9,... | collective-permute-start | bytes 6291464 | tf_op jit(solution)/shard_map/ppermute | solution.py:31
  43.3 1.9 %collective-permute-start.3 = (bf16[4,512,512]{2,1,0:T(8,128)(2,1)S(1)}, bf16[4,512,512]{2,1,0:T(8,128)(2,1)}, u32[]{:S(2)}, u32[]{:S(2)}) collective-permute-start(bf16[4,512,512]{2,1,0:T(8,128)(2,1)S(1)} %pad_maximum_fusion.refs_4_.refs_6_), channel_id=1, source_target_pairs={{0,16},{1,17},{2,18},{3,19},{4,20},{5,21},{6,22},{7,23},{8,24},{9,... | collective-permute-start | bytes 6291464 | tf_op jit(solution)/shard_map/ppermute | solution.py:31
  45.3 0.7 fusion.3
  46.0 2.6 %stack.27.refs_0_.scal = s32[9]{0:T(128)S(1)} concatenate(s32[1]{0:T(128)} %bitcast, s32[1]{0:T(128)} %bitcast.1, s32[1]{0:T(128)} %bitcast.2, s32[1]{0:T(128)} %bitcast.3, s32[1]{0:T(128)} %get-tuple-element.23, s32[1]{0:T(128)} %get-tuple-element.24, s32[1]{0:T(128)} %bitcast.4, s32[1]{0:T(128)} %get-tuple-element.20, s32[1]{0:T(128)} %get-tuple-element.19), dimensions={0} | concatenate | bytes 72 | tf_op jit(solution)/shard_map/stack | solution.py:222
  48.7 15.9 %collective-permute-done.5.refs_7_.refs_9_ = bf16[4,512,512]{2,1,0:T(8,128)(2,1)} collective-permute-done((bf16[4,512,512]{2,1,0:T(8,128)(2,1)S(1)}, bf16[4,512,512]{2,1,0:T(8,128)(2,1)}, u32[]{:S(2)}, u32[]{:S(2)}) %collective-permute-start.5) | collective-permute-done | bytes 2097184 | tf_op jit(solution)/shard_map/ppermute | solution.py:31
  64.6 22.4 %collective-permute-done.4.refs_6_.refs_8_ = bf16[4,512,512]{2,1,0:T(8,128)(2,1)} collective-permute-done((bf16[4,512,512]{2,1,0:T(8,128)(2,1)S(1)}, bf16[4,512,512]{2,1,0:T(8,128)(2,1)}, u32[]{:S(2)}, u32[]{:S(2)}) %collective-permute-start.4) | collective-permute-done | bytes 2097184 | tf_op jit(solution)/shard_map/ppermute | solution.py:31
  87.2 5.9 %shard_map.64 = (f32[64,2048]{1,0:T(8,128)S(1)}, bf16[64,2048]{1,0:T(8,128)(2,1)S(1)}) custom-call(s32[9]{0:T(128)S(1)} %stack.27.refs_0_.scal, f32[5,2048]{1,0:T(8,128)S(1)} %copy-done, bf16[64,2048]{1,0:T(8,128)(2,1)S(1)} %get-tuple-element.16.refs_2_.mine, bf16[64,2048]{1,0:T(8,128)(2,1)S(1)} %get-tuple-element.15.refs_3_.other, ...), custom_call_target="tpu_custom_call" | custom-call | flops 1073741824 | bytes 9437184 | tf_op jit(solution)/shard_map/pallas_call | solution.py:137
  93.1 0.7 collective-permute-start.6
  94.5 0.7 collective-permute-start.7
  95.2 0.7 collective-permute-start.8
  95.9 2.9 %shard_map.65 = (f32[64,2048]{1,0:T(8,128)S(1)}, bf16[64,2048]{1,0:T(8,128)(2,1)S(1)}) custom-call(s32[9]{0:T(128)S(1)} %stack.27.refs_0_.scal, f32[5,2048]{1,0:T(8,128)S(1)} %copy-done, bf16[64,2048]{1,0:T(8,128)(2,1)S(1)} %collective-permute-done.7.refs_2_.in1m, bf16[64,2048]{1,0:T(8,128)(2,1)S(1)} %collective-permute-done.8.refs_3_.in1o, ...), custom_call_target="tpu_custom_call" | custom-call | flops 1073741824 | bytes 9437184 | tf_op jit(solution)/shard_map/pallas_call | solution.py:137
  98.8 0.7 collective-permute-start.11
  99.5 1.3 collective-permute-start.9
  101.2 1.3 collective-permute-start.13
  102.5 29.0 %collective-permute-done.9.refs_2_.in3m = bf16[64,2048]{1,0:T(8,128)(2,1)S(1)} collective-permute-done((bf16[64,2048]{1,0:T(8,128)(2,1)S(1)}, bf16[64,2048]{1,0:T(8,128)(2,1)S(1)}, u32[]{:S(2)}, u32[]{:S(2)}) %collective-permute-start.9) | collective-permute-done | bytes 262176 | tf_op jit(solution)/shard_map/ppermute | solution.py:251
  131.5 8.8 %collective-permute-start.10 = (bf16[64,2048]{1,0:T(8,128)(2,1)S(1)}, bf16[64,2048]{1,0:T(8,128)(2,1)}, u32[]{:S(2)}, u32[]{:S(2)}) collective-permute-start(bf16[64,2048]{1,0:T(8,128)(2,1)S(1)} %collective-permute-done.9.refs_2_.in3m), channel_id=1, source_target_pairs={{384,448},{448,384},{385,449},{449,385},{386,450},{450,386},{387,4... | collective-permute-start | bytes 786440 | tf_op jit(solution)/shard_map/ppermute | solution.py:246
  140.4 10.2 %collective-permute-done.13.refs_4_ = bf16[64,2048]{1,0:T(8,128)(2,1)} collective-permute-done((bf16[64,2048]{1,0:T(8,128)(2,1)S(1)}, bf16[64,2048]{1,0:T(8,128)(2,1)}, u32[]{:S(2)}, u32[]{:S(2)}) %collective-permute-start.13) | collective-permute-done | bytes 262176 | tf_op jit(solution)/shard_map/ppermute | solution.py:256
  150.6 2.8 %collective-permute-start.14 = (bf16[64,2048]{1,0:T(8,128)(2,1)}, bf16[64,2048]{1,0:T(8,128)(2,1)}, u32[]{:S(2)}, u32[]{:S(2)}) collective-permute-start(bf16[64,2048]{1,0:T(8,128)(2,1)} %collective-permute-done.13.refs_4_), channel_id=1, source_target_pairs={{384,448},{448,384},{385,449},{449,385},{386,450},{450,386},{387,4... | collective-permute-start | bytes 786440 | tf_op jit(solution)/shard_map/ppermute | solution.py:246
  153.4 1.4 collective-permute-done.14.refs_5_
  154.8 6.2 %shard_map.66.own = bf16[128,2048]{1,0:T(8,128)(2,1)S(1)} custom-call(s32[9]{0:T(128)S(1)} %stack.27.refs_0_.scal, f32[5,2048]{1,0:T(8,128)S(1)} %copy-done, bf16[64,2048]{1,0:T(8,128)(2,1)S(1)} %collective-permute-done.9.refs_2_.in3m, bf16[64,2048]{1,0:T(8,128)(2,1)} %collective-permute-done.10.refs_3_.in3o, ...), custom_call_target="tpu_custom_call" | custom-call | flops 1073741824 | bytes 9437184 | tf_op jit(solution)/shard_map/pallas_call | solution.py:137
  161.1 1.3 collective-permute-start.15
  162.4 0.7 collective-permute-start.12
  163.1 1.8 %collective-permute-done.15.got = bf16[128,2048]{1,0:T(8,128)(2,1)S(1)} collective-permute-done((bf16[128,2048]{1,0:T(8,128)(2,1)S(1)}, bf16[128,2048]{1,0:T(8,128)(2,1)S(1)}, u32[]{:S(2)}, u32[]{:S(2)}) %collective-permute-start.15) | collective-permute-done | bytes 524320 | tf_op jit(solution)/shard_map/ppermute | solution.py:264
  164.9 2.0 %shard_map.67 = bf16[2,64,2048]{2,1,0:T(8,128)(2,1)} custom-call(s32[9]{0:T(128)S(1)} %stack.27.refs_0_.scal, bf16[64,2048]{1,0:T(8,128)(2,1)S(1)} %get-tuple-element.16.refs_2_.mine, bf16[64,2048]{1,0:T(8,128)(2,1)S(1)} %get-tuple-element.15.refs_3_.other, bf16[64,2048]{1,0:T(8,128)(2,1)S(1)} %collective-permute-done.7.refs_2_.in1m, ...), custom_call_target="tpu_custom_call" | custom-call | tf_op jit(solution)/shard_map/pallas_call | solution.py:190
  (40 shorter events, 2.1 us)
Async XLA Ops:
  17.7 27.6 %copy-start.7 = (s32[2]{0:T(128)S(1)}, s32[2]{0:T(128)}, u32[]{:S(2)}) copy-start(s32[2]{0:T(128)} %param.10) | copy-start | bytes 28
  17.7 27.6 %copy-start.8 = (s32[2]{0:T(128)S(1)}, s32[2]{0:T(128)}, u32[]{:S(2)}) copy-start(s32[2]{0:T(128)} %param.11) | copy-start | bytes 28
  17.7 30.9 %copy-start.5 = (bf16[2,64,2048]{2,1,0:T(8,128)(2,1)S(1)}, bf16[2,64,2048]{2,1,0:T(8,128)(2,1)}, u32[]{:S(2)}) copy-start(bf16[2,64,2048]{2,1,0:T(8,128)(2,1)} %param.6) | copy-start | bytes 1572868
  17.7 30.9 %copy-start.6 = (bf16[2,64,2048]{2,1,0:T(8,128)(2,1)S(1)}, bf16[2,64,2048]{2,1,0:T(8,128)(2,1)}, u32[]{:S(2)}) copy-start(bf16[2,64,2048]{2,1,0:T(8,128)(2,1)} %param.7) | copy-start | bytes 1572868
  17.7 11.9 %collective-permute-start.2 = (bf16[4,128,512]{2,1,0:T(8,128)(2,1)S(1)}, bf16[4,128,512]{2,1,0:T(8,128)(2,1)S(1)}, u32[]{:S(2)}, u32[]{:S(2)}) collective-permute-start(bf16[4,128,512]{2,1,0:T(8,128)(2,1)S(1)} %bitcast.22), channel_id=1, source_target_pairs={{0,8},{1,9},{2,10},{3,11},{4,12},{5,13},{6,14},{7,15},{8,0},{9,1},... | collective-permute-start | bytes 1572872 | tf_op jit(solution)/shard_map/ppermute | solution.py:31
  22.7 12.5 %collective-permute-start.1 = (bf16[4,128,512]{2,1,0:T(8,128)(2,1)S(1)}, bf16[4,128,512]{2,1,0:T(8,128)(2,1)S(1)}, u32[]{:S(2)}, u32[]{:S(2)}) collective-permute-start(bf16[4,128,512]{2,1,0:T(8,128)(2,1)S(1)} %bitcast.23), channel_id=1, source_target_pairs={{0,12},{1,13},{2,14},{3,15},{4,8},{5,9},{6,10},{7,11},{8,4},{9,5},... | collective-permute-start | bytes 1572872 | tf_op jit(solution)/shard_map/ppermute | solution.py:31
  25.4 10.2 %collective-permute-start = (bf16[4,128,512]{2,1,0:T(8,128)(2,1)S(1)}, bf16[4,128,512]{2,1,0:T(8,128)(2,1)S(1)}, u32[]{:S(2)}, u32[]{:S(2)}) collective-permute-start(bf16[4,128,512]{2,1,0:T(8,128)(2,1)S(1)} %bitcast.24), channel_id=1, source_target_pairs={{0,4},{1,5},{2,6},{3,7},{4,0},{5,1},{6,2},{7,3},{8,12},{9,13},{10,... | collective-permute-start | bytes 1572872 | tf_op jit(solution)/shard_map/ppermute | solution.py:31
  35.7 51.4 %copy-start = (f32[5,2048]{1,0:T(8,128)S(1)}, f32[5,2048]{1,0:T(8,128)}, u32[]{:S(2)}) copy-start(f32[5,2048]{1,0:T(8,128)} %refs_1_.5) | copy-start | bytes 122884
  35.7 28.9 %collective-permute-start.5 = (bf16[4,512,512]{2,1,0:T(8,128)(2,1)S(1)}, bf16[4,512,512]{2,1,0:T(8,128)(2,1)}, u32[]{:S(2)}, u32[]{:S(2)}) collective-permute-start(bf16[4,512,512]{2,1,0:T(8,128)(2,1)S(1)} %pad_maximum_fusion.refs_4_.refs_6_), channel_id=1, source_target_pairs={{0,32},{1,33},{2,34},{3,35},{4,36},{5,37},{6,38},{7,39},{8,40},{9,... | collective-permute-start | bytes 6291464 | tf_op jit(solution)/shard_map/ppermute | solution.py:31
  40.5 46.5 %collective-permute-start.4 = (bf16[4,512,512]{2,1,0:T(8,128)(2,1)S(1)}, bf16[4,512,512]{2,1,0:T(8,128)(2,1)}, u32[]{:S(2)}, u32[]{:S(2)}) collective-permute-start(bf16[4,512,512]{2,1,0:T(8,128)(2,1)S(1)} %pad_maximum_fusion.refs_4_.refs_6_), channel_id=1, source_target_pairs={{0,48},{1,49},{2,50},{3,51},{4,52},{5,53},{6,54},{7,55},{8,56},{9,... | collective-permute-start | bytes 6291464 | tf_op jit(solution)/shard_map/ppermute | solution.py:31
  43.3 43.8 %collective-permute-start.3 = (bf16[4,512,512]{2,1,0:T(8,128)(2,1)S(1)}, bf16[4,512,512]{2,1,0:T(8,128)(2,1)}, u32[]{:S(2)}, u32[]{:S(2)}) collective-permute-start(bf16[4,512,512]{2,1,0:T(8,128)(2,1)S(1)} %pad_maximum_fusion.refs_4_.refs_6_), channel_id=1, source_target_pairs={{0,16},{1,17},{2,18},{3,19},{4,20},{5,21},{6,22},{7,23},{8,24},{9,... | collective-permute-start | bytes 6291464 | tf_op jit(solution)/shard_map/ppermute | solution.py:31
  93.1 1.3 collective-permute-start.6
  94.5 5.0 %copy-start.3 = (bf16[64,2048]{1,0:T(8,128)(2,1)}, bf16[64,2048]{1,0:T(8,128)(2,1)S(1)}, u32[]{:S(2)}) copy-start(bf16[64,2048]{1,0:T(8,128)(2,1)S(1)} %add_convert_fusion.1) | copy-start | bytes 786436
  94.5 0.7 collective-permute-start.7
  95.2 0.7 collective-permute-start.8
  98.8 2.0 %collective-permute-start.11 = (bf16[64,2048]{1,0:T(8,128)(2,1)S(1)}, bf16[64,2048]{1,0:T(8,128)(2,1)S(1)}, u32[]{:S(2)}, u32[]{:S(2)}) collective-permute-start(bf16[64,2048]{1,0:T(8,128)(2,1)S(1)} %get-tuple-element.12), channel_id=1, source_target_pairs={{128,192},{192,128},{129,193},{193,129},{130,194},{194,130},{131,1... | collective-permute-start | bytes 786440 | tf_op jit(solution)/shard_map/ppermute | solution.py:246
  99.5 32.1 %collective-permute-start.9 = (bf16[64,2048]{1,0:T(8,128)(2,1)S(1)}, bf16[64,2048]{1,0:T(8,128)(2,1)S(1)}, u32[]{:S(2)}, u32[]{:S(2)}) collective-permute-start(bf16[64,2048]{1,0:T(8,128)(2,1)S(1)} %add_convert_fusion.1), channel_id=1, source_target_pairs={{256,384},{257,385},{258,386},{259,387},{260,388},{261,389},{262,3... | collective-permute-start | bytes 786440 | tf_op jit(solution)/shard_map/ppermute | solution.py:251
  101.1 30.5 %copy-start.1 = (bf16[64,2048]{1,0:T(8,128)(2,1)}, bf16[64,2048]{1,0:T(8,128)(2,1)S(1)}, u32[]{:S(2)}) copy-start(bf16[64,2048]{1,0:T(8,128)(2,1)S(1)} %get-tuple-element.14) | copy-start | bytes 786436
  101.2 49.4 %collective-permute-start.13 = (bf16[64,2048]{1,0:T(8,128)(2,1)S(1)}, bf16[64,2048]{1,0:T(8,128)(2,1)}, u32[]{:S(2)}, u32[]{:S(2)}) collective-permute-start(bf16[64,2048]{1,0:T(8,128)(2,1)S(1)} %fusion.2), channel_id=1, source_target_pairs={{128,384},{129,385},{130,386},{131,387},{132,388},{133,389},{134,3... | collective-permute-start | bytes 786440 | tf_op jit(solution)/shard_map/ppermute | solution.py:256
  131.5 21.9 %collective-permute-start.10 = (bf16[64,2048]{1,0:T(8,128)(2,1)S(1)}, bf16[64,2048]{1,0:T(8,128)(2,1)}, u32[]{:S(2)}, u32[]{:S(2)}) collective-permute-start(bf16[64,2048]{1,0:T(8,128)(2,1)S(1)} %collective-permute-done.9.refs_2_.in3m), channel_id=1, source_target_pairs={{384,448},{448,384},{385,449},{449,385},{386,450},{450,386},{387,4... | collective-permute-start | bytes 786440 | tf_op jit(solution)/shard_map/ppermute | solution.py:246
  150.6 4.3 %collective-permute-start.14 = (bf16[64,2048]{1,0:T(8,128)(2,1)}, bf16[64,2048]{1,0:T(8,128)(2,1)}, u32[]{:S(2)}, u32[]{:S(2)}) collective-permute-start(bf16[64,2048]{1,0:T(8,128)(2,1)} %collective-permute-done.13.refs_4_), channel_id=1, source_target_pairs={{384,448},{448,384},{385,449},{449,385},{386,450},{450,386},{387,4... | collective-permute-start | bytes 786440 | tf_op jit(solution)/shard_map/ppermute | solution.py:246
  153.4 9.0 %copy-start.2 = (bf16[64,2048]{1,0:T(8,128)(2,1)S(1)}, bf16[64,2048]{1,0:T(8,128)(2,1)}, u32[]{:S(2)}) copy-start(bf16[64,2048]{1,0:T(8,128)(2,1)} %copy-done.1) | copy-start | bytes 786436
  153.4 9.0 %copy-start.4 = (bf16[64,2048]{1,0:T(8,128)(2,1)S(1)}, bf16[64,2048]{1,0:T(8,128)(2,1)}, u32[]{:S(2)}) copy-start(bf16[64,2048]{1,0:T(8,128)(2,1)} %copy-done.3) | copy-start | bytes 786436
  161.1 3.8 %collective-permute-start.15 = (bf16[128,2048]{1,0:T(8,128)(2,1)S(1)}, bf16[128,2048]{1,0:T(8,128)(2,1)S(1)}, u32[]{:S(2)}, u32[]{:S(2)}) collective-permute-start(bf16[128,2048]{1,0:T(8,128)(2,1)S(1)} %shard_map.66.own), channel_id=1, source_target_pairs={{384,448},{385,449},{386,450},{387,451},{388,452},{389,453},{390,4... | collective-permute-start | bytes 1572872 | tf_op jit(solution)/shard_map/ppermute | solution.py:264
  162.4 0.7 collective-permute-start.12

commit v5 on v4

v5 whole, which is shorter than its diff:
```python
import functools
import itertools

import jax
import jax.numpy as jnp
from jax import lax
from jax.experimental import pallas as pl
from jax.experimental.pallas import tpu as pltpu
from jax.sharding import Mesh, PartitionSpec as P

HEAD_DIM = 128
SIDE = 4
TURNS = (0, 1, 3, 2)
FAR = 2
AXES = ("zh", "core", "y", "x", "zl")
DP = ("y", "x", "zl")
SECTION = ("zh", "core")
F32 = jnp.float32
BF16 = jnp.bfloat16


def place(zh, core, y, x, zl):
    return (((zh * 2 + core) * SIDE + y) * SIDE + x) * SIDE + zl


def exchange(array, outer, by):
    pairs = []
    for zh, core, y, x, zl in itertools.product(*map(range, (SIDE, 2, SIDE, SIDE, SIDE))):
        along_y = outer == (core == 0)
        to = (y ^ by, x) if along_y else (y, x ^ by)
        pairs.append((place(zh, core, y, x, zl), place(zh, core, *to, zl)))
    return lax.ppermute(array, AXES, pairs)


def dot(a, b):
    return jnp.dot(a, b, preferred_element_type=F32)


def dot_t(a, b):
    return lax.dot_general(a, b, (((1,), (1,)), ((), ())), preferred_element_type=F32)


def rms(values, gain):
    mean_square = jnp.mean(values * values, axis=-1, keepdims=True)
    return (values * lax.rsqrt(mean_square + 1e-06) * gain).astype(BF16)


def block_at(scal, outer, inner):
    back = scal[6] == 1
    dy, dx = jnp.where(back, inner, outer), jnp.where(back, outer, inner)
    return lax.bitwise_xor(scal[1], dy) * SIDE + lax.bitwise_xor(scal[0], dx)


def weight(pieces, turn, which):
    chunk, place_in = divmod(which, 2)
    if turn == FAR:
        return pieces[6 + which][0]
    return pieces[2 * TURNS.index(turn) + chunk][place_in]


def put_norm(scal, gains, streams, h3):
    rows = streams[0].shape[0]
    gain = gains[pl.ds(scal[2], 1), :]
    for part, ref in enumerate(streams):
        h = rms(ref[...].astype(F32), gain)
        for i in range(16):
            h3[i, part * rows:(part + 1) * rows, :] = h[:, i * 128:(i + 1) * 128]


def put_memory(mem, m3):
    rows = mem[0].shape[0]
    for part, ref in enumerate(mem):
        for i in range(16):
            m3[i, part * rows:(part + 1) * rows, :] = ref[:, i * 128:(i + 1) * 128]


def project(scal, h3, pieces, turns, which, totals=None):
    totals = [None] * len(which) if totals is None else list(totals)
    for turn in turns:
        h = jnp.concatenate([h3[block_at(scal, turn, d)] for d in TURNS], axis=1)
        for i, m in enumerate(which):
            term = dot(h, weight(pieces, turn, m))
            totals[i] = term if totals[i] is None else totals[i] + term
    return totals


def attend(scal, q, k, v):
    q, k, v = q.astype(BF16), k.astype(BF16), v.astype(BF16)
    count = q.shape[0]
    rows = count // 2
    r = lax.broadcasted_iota(jnp.int32, (count, count), 0)
    c = lax.broadcasted_iota(jnp.int32, (count, count), 1)
    first = c < rows
    live = (r < rows) == first
    key_at = jnp.where(first, c, c - rows)
    live = live & (key_at < jnp.where(first, scal[4], scal[5]))
    live = live & ((c <= r) | (scal[3] == 0))
    mixed = []
    for head in range(4):
        at = slice(head * HEAD_DIM, (head + 1) * HEAD_DIM)
        s = dot_t(q[:, at], k[:, at]) * HEAD_DIM ** (-0.5)
        s = jnp.where(live, s, -1e30)
        e = jnp.exp(s - jnp.max(s, axis=-1, keepdims=True))
        p = (e / jnp.sum(e, axis=-1, keepdims=True)).astype(BF16)
        mixed.append(dot(p, v[:, at]).astype(BF16))
    return jnp.concatenate(mixed, axis=1)


def project_out(scal, mixed, pieces, t3, out_mine, out_other):
    rows = out_mine.shape[0]
    for turn in TURNS:
        t = dot_t(mixed, weight(pieces, turn, 3))
        for j, d in enumerate(TURNS):
            t3[block_at(scal, turn, d)] = t[:, j * 128:(j + 1) * 128]
    for i in range(16):
        at = slice(i * 128, (i + 1) * 128)
        out_mine[:, at] = t3[i, :rows, :].astype(out_mine.dtype)
        out_other[:, at] = t3[i, rows:, :].astype(out_other.dtype)


def early_kernel(scal, gains, mine, other, *refs):
    pieces, (h3, q, k, v) = refs[:6], refs[6:]

    @pl.when(lax.rem(scal[2], 2) == 0)
    def _():
        put_norm(scal, gains, (mine, other), h3)
        q[...], k[...], v[...] = project(scal, h3, pieces, TURNS[:3], (0, 1, 2))


def first_kernel(scal, h3, q, k, v, *refs):
    pieces, (out_mine, out_other, t3) = refs[:10], refs[10:]

    @pl.when(lax.rem(scal[2], 2) == 0)
    def _():
        done = (q[...], k[...], v[...])
        done = project(scal, h3, pieces, TURNS[3:], (0, 1, 2), done)
        project_out(scal, attend(scal, *done), pieces, t3, out_mine, out_other)


def second_kernel(scal, gains, mine, other, *refs):
    pieces, (out_mine, out_other, h3, t3) = refs[:10], refs[10:]

    @pl.when(scal[2] == 1)
    def _():
        put_norm(scal, gains, (mine, other), h3)
        done = project(scal, h3, pieces, TURNS, (0, 1, 2))
        project_out(scal, attend(scal, *done), pieces, t3, out_mine, out_other)


def query_kernel(scal, gains, mine, other, *refs):
    pieces, (q, h3) = refs[:10], refs[10:]

    @pl.when(scal[2] == 3)
    def _():
        put_norm(scal, gains, (mine, other), h3)
        q[...] = project(scal, h3, pieces, TURNS, (0,))[0].astype(BF16)


def third_kernel(scal, q, mem_mine, mem_other, *refs):
    pieces, (out, m3, t3) = refs[:10], refs[10:]

    @pl.when(scal[2] == 3)
    def _():
        rows = mem_mine.shape[0]
        put_memory((mem_mine, mem_other), m3)
        k, v = project(scal, m3, pieces, TURNS, (1, 2))
        mixed = attend(scal, q[...], k, v)
        project_out(scal, mixed, pieces, t3, out.at[:rows], out.at[rows:])


VMEM = pl.BlockSpec(memory_space=pltpu.VMEM)
SMEM = pl.BlockSpec(memory_space=pltpu.SMEM)


def call(kernel, scal, operands, outs, scratch=(), flops=0):
    size = sum(a.size * a.dtype.itemsize for a in operands)
    return pl.pallas_call(
        kernel,
        out_shape=outs,
        in_specs=[SMEM] + [VMEM] * len(operands),
        out_specs=jax.tree.map(lambda _: VMEM, outs),
        scratch_shapes=[pltpu.VMEM(shape, kind) for shape, kind in scratch],
        compiler_params=pltpu.CompilerParams(vmem_limit_bytes=12 * 1024 * 1024),
        cost_estimate=pl.CostEstimate(flops=flops, bytes_accessed=size, transcendentals=0),
    )(scal, *operands)


def finish_kernel(scal, mine, other, in1m, in1o, in3m, in3o, early_m, early_o, own, got, out):
    rows = mine.shape[0]
    cube, core = scal[2], scal[6]
    even = (cube == 0) | (cube == 2)

    def put(doc0, doc1):
        out[0] = doc0[...]
        out[1] = doc1[...]

    @pl.when((core == 0) & even)
    def _():
        put(mine, other)

    @pl.when((core == 0) & (cube == 1))
    def _():
        put(in1m, in1o)

    @pl.when((core == 0) & (cube == 3))
    def _():
        put(in3m, in3o)

    @pl.when((core == 1) & (cube != 3))
    def _():
        put(early_o, early_m)

    @pl.when((core == 1) & (cube == 3))
    def _():
        at = lax.broadcasted_iota(jnp.int32, mine.shape, 0)
        low, high = slice(0, rows), slice(rows, 2 * rows)
        for slot, base, a, b, live in ((1, in3m, low, high, scal[7]), (0, in3o, high, low, scal[8])):
            term = own[a, :].astype(F32) + got[b, :].astype(F32)
            term = jnp.where(at < live, term, 0.0)
            out[slot] = (base[...].astype(F32) + term).astype(BF16)


def turns(array, outer):
    return [array] + [exchange(array, outer, turn) for turn in TURNS[1:]]


def gather(weights):
    pair, depth, width = weights.shape[1:]
    halves = weights[0].reshape(pair, depth, 2, width // 2).transpose(2, 0, 1, 3)
    sent = jnp.broadcast_to(halves[:, None], (2, SIDE) + halves.shape[1:])
    sent = sent.reshape((2 * SIDE,) + halves.shape[1:])
    got = lax.all_to_all(sent, ("core", "zl"), 0, 0, tiled=True)
    got = got.reshape(2, SIDE, pair, depth, width // 2).transpose(0, 2, 1, 3, 4)
    got = got.reshape(2 * pair, SIDE * depth, width // 2)
    near = turns(got, False)
    chunks = [jnp.concatenate([a[i:i + pair] for a in near], axis=1) for i in (0, pair)]
    by1 = [exchange(a, True, 1) for a in chunks]
    by3 = [exchange(a, True, 3) for a in chunks]
    far = []
    for a, b in zip(by1, by3):
        far += [exchange(b[:1], True, 1), exchange(a[1:], True, 3)]
    return [*chunks, *by1, *by3], far


def on_device(encoder_embed, decoder_embed, section_weights, norm_gains, input_lengths, target_lengths):
    zh, core = lax.axis_index("zh"), lax.axis_index("core")
    y, x = lax.axis_index("y"), lax.axis_index("x")
    rows = encoder_embed.shape[1]
    encoder = zh < 2
    causal = zh == 2
    key_lengths = jnp.where(causal, target_lengths, input_lengths)
    row_lengths = jnp.where(encoder, input_lengths, target_lengths)
    scal = jnp.stack(
        [
            x,
            y,
            zh,
            causal.astype(jnp.int32),
            key_lengths[core],
            key_lengths[1 - core],
            core,
            row_lengths[core],
            row_lengths[1 - core],
        ]
    ).astype(jnp.int32)
    live = (jnp.arange(rows, dtype=jnp.int32) < row_lengths[core])[:, None]

    near, far = gather(section_weights)
    pieces = near + far
    source = jnp.where(encoder, encoder_embed, decoder_embed)
    mine, other = source[core], source[1 - core]

    def added(stream, term, alive):
        return stream.astype(F32) + jnp.where(alive, term, 0.0)

    def swapped(array, cubes=range(SIDE)):
        pairs = [(2 * c + i, 2 * c + 1 - i) for c in cubes for i in range(2)]
        return lax.ppermute(array, SECTION, pairs)

    count, width = 2 * rows, mine.shape[1]
    half = near[0].shape[-1]
    blocks = (16, count, 128)
    work = 2 * count * width * half
    wide = jax.ShapeDtypeStruct((count, width), BF16)
    halves = tuple(jax.ShapeDtypeStruct((rows, width), kind) for kind in (F32, BF16))
    total = jax.ShapeDtypeStruct((count, half), F32)
    narrow = jax.ShapeDtypeStruct((count, half), BF16)

    started = call(
        early_kernel,
        scal,
        [norm_gains, mine, other, *near],
        (jax.ShapeDtypeStruct(blocks, BF16), total, total, total),
        (),
        3 * work,
    )
    kept, sent = call(
        first_kernel, scal, [*started, *pieces], halves, [(blocks, F32)], 2 * work
    )
    first = added(mine, kept + swapped(sent, (0, 2)).astype(F32), live).astype(BF16)
    in1 = lax.ppermute(first, "zh", [(0, 1)])
    in3 = lax.ppermute(first, "zh", [(2, 3)])
    in1_other = swapped(in1, (1,))
    kept, sent = call(
        second_kernel,
        scal,
        [norm_gains, in1, in1_other, *pieces],
        halves,
        [(blocks, BF16), (blocks, F32)],
        4 * work,
    )
    second = added(in1, kept + swapped(sent, (1,)).astype(F32), live).astype(BF16)
    memory = rms(second.astype(F32), norm_gains[4:5])
    mem = lax.ppermute(memory, "zh", [(1, 3)])
    early = jnp.where(zh == 1, second, first)
    early_other = lax.ppermute(early, SECTION, [(0, 1), (2, 3), (4, 5)])
    in3_other = swapped(in3, (3,))
    query = call(
        query_kernel, scal, [norm_gains, in3, in3_other, *pieces], narrow, [(blocks, BF16)], work
    )
    mem_other = swapped(mem, (3,))
    own = call(
        third_kernel,
        scal,
        [query, mem, mem_other, *pieces],
        wide,
        [(blocks, BF16), (blocks, F32)],
        3 * work,
    )
    got = lax.ppermute(own, SECTION, [(6, 7)])
    parts = [mine, other, in1, in1_other, in3, in3_other, early, early_other, own, got]
    out = call(finish_kernel, scal, parts, jax.ShapeDtypeStruct((2, rows, width), BF16))
    return out[None]


def solution(mesh):
    fine = Mesh(mesh.devices.reshape(SIDE, 2, SIDE, SIDE, SIDE), AXES)
    in_specs = (
        P(DP, None, None),
        P(DP, None, None),
        P(SECTION, None, DP, None),
        P(),
        P(DP),
        P(DP),
    )
    out_specs = P(SECTION, DP, None, None)
    return jax.shard_map(
        on_device, mesh=fine, in_specs=in_specs, out_specs=out_specs, check_vma=False
    )
```

time: 167 us -> 162 us (0.970)
  waiting for transfers between devices: 89.2 us -> 63.7 us
  local copies, waits for them, and re-layouts: 4.45 us -> 12.8 us
  starting transfers between devices: 37.9 us -> 46.1 us
  other arithmetic: 1.35 us -> 3.29 us
    ppermute x6 -> x11, waiting for transfers between devices: 46.8 us -> 15.1 us  [exchange(): return lax.ppermute(array, AXES, pairs)]
    ppermute x6 -> x11, starting transfers between devices: 19 us -> 33.4 us  [exchange(): return lax.ppermute(array, AXES, pairs)]
    ppermute x1, waiting for transfers between devices: 29 us -> 37.5 us  [on_device(): in3 = lax.ppermute(first, 'zh', [(2, 3)])]
    slice x0 -> x10, local copies, waits for them, and re-layouts: none -> 6.66 us  [the longest x4 6.47 us: gather(): far += [exchange(b[:1], True, 1), exchange(a[1:], True, 3)]]
    ppermute x5, starting transfers between devices: 13.6 us -> 7.43 us  [swapped(): return lax.ppermute(array, SECTION, pairs)]
    select_n x1, other arithmetic: 0.07 us -> 1.9 us  [on_device(): source = jnp.where(encoder, encoder_embed, decoder_embed)]
    pallas_call x4 -> x6, Pallas kernels: 17 us -> 17.8 us  [call(): pl.pallas_call(kernel, out_shape=outs, in_specs=[SMEM] + [VMEM] * len(ope...]
  transfers between devices with their start and end apart: 16 -> 21, of which waited for: 10 -> 10; matrix products, arithmetic and copies ran while one was open for 3% -> 9% of each run, Pallas kernels for 0% -> 3%
where the time goes in v5:
time: 162 us; the launch traced here: 161 us
  waiting for transfers between devices  63.7 us (39%)
  starting transfers between devices  46.1 us (28%)
  Pallas kernels  17.8 us (11%)
  blocking collectives  16.6 us (10%)
  local copies, waits for them, and re-layouts  12.8 us (8%)
  other arithmetic  3.29 us (2%)
    ppermute x1, waiting for transfers between devices, on_device(): in3 = lax.ppermute(first, 'zh', [(2, 3)])  37.5 us
    ppermute x11, starting transfers between devices, exchange(): return lax.ppermute(array, AXES, pairs)  33.4 us
    pallas_call x6, Pallas kernels, call(): pl.pallas_call(kernel, out_shape=outs, in_specs=[SMEM] + [VMEM] * len(ope...  17.8 us
    all_to_all x1, blocking collectives, gather(): got = lax.all_to_all(sent, ('core', 'zl'), 0, 0, tiled=True)  16.6 us
    ppermute x11, waiting for transfers between devices, exchange(): return lax.ppermute(array, AXES, pairs)  15.1 us
    ppermute x1, waiting for transfers between devices, on_device(): mem = lax.ppermute(memory, 'zh', [(1, 3)])  9.29 us
    ppermute x5, starting transfers between devices, swapped(): return lax.ppermute(array, SECTION, pairs)  7.43 us
    slice x4, local copies, waits for them, and re-layouts, gather(): far += [exchange(b[:1], True, 1), exchange(a[1:], True, 3)]  6.47 us
  transfers between devices with their start and end apart: 21, of which 10 were waited for; matrix products, arithmetic and copies ran while one was open for 9% of the time, Pallas kernels for 3%

profile of v5, /device:TPU:481, one launch (start us, length us, event | category | flops | bytes accessed | tf_op | source)
XLA Modules:
  0.0 160.8 jit_solution(6799534540505467935)
XLA Ops:
  1.1 16.6 %all_to_all.5 = bf16[8,2,32,512]{3,2,1,0:T(8,128)(2,1)S(1)} all-to-all(bf16[8,2,32,512]{3,2,1,0:T(8,128)(2,1)S(1)} %bitcast.24), channel_id=1, replica_groups=mesh['zh'=4,'core'=2,'y'=4,'x'=4,'zl'=4] {'core','zl'}, dimensions={0} | all-to-all | bytes 1048576 | tf_op jit(solution)/shard_map/all_to_all | solution.py:232
  17.7 4.8 %collective-permute-start.2 = (bf16[4,128,512]{2,1,0:T(8,128)(2,1)S(1)}, bf16[4,128,512]{2,1,0:T(8,128)(2,1)S(1)}, u32[]{:S(2)}, u32[]{:S(2)}) collective-permute-start(bf16[4,128,512]{2,1,0:T(8,128)(2,1)S(1)} %bitcast.27), channel_id=1, source_target_pairs={{0,8},{1,9},{2,10},{3,11},{4,12},{5,13},{6,14},{7,15},{8,0},{9,1},... | collective-permute-start | bytes 1572872 | tf_op jit(solution)/shard_map/ppermute | solution.py:32
  22.5 2.7 %collective-permute-start.1 = (bf16[4,128,512]{2,1,0:T(8,128)(2,1)S(1)}, bf16[4,128,512]{2,1,0:T(8,128)(2,1)S(1)}, u32[]{:S(2)}, u32[]{:S(2)}) collective-permute-start(bf16[4,128,512]{2,1,0:T(8,128)(2,1)S(1)} %bitcast.28), channel_id=1, source_target_pairs={{0,12},{1,13},{2,14},{3,15},{4,8},{5,9},{6,10},{7,11},{8,4},{9,5},... | collective-permute-start | bytes 1572872 | tf_op jit(solution)/shard_map/ppermute | solution.py:32
  25.2 1.9 %collective-permute-start = (bf16[4,128,512]{2,1,0:T(8,128)(2,1)S(1)}, bf16[4,128,512]{2,1,0:T(8,128)(2,1)S(1)}, u32[]{:S(2)}, u32[]{:S(2)}) collective-permute-start(bf16[4,128,512]{2,1,0:T(8,128)(2,1)S(1)} %bitcast.29), channel_id=1, source_target_pairs={{0,4},{1,5},{2,6},{3,7},{4,0},{5,1},{6,2},{7,3},{8,12},{9,13},{10,... | collective-permute-start | bytes 1572872 | tf_op jit(solution)/shard_map/ppermute | solution.py:32
  27.2 2.2 %collective-permute-done.2 = bf16[4,128,512]{2,1,0:T(8,128)(2,1)S(1)} collective-permute-done((bf16[4,128,512]{2,1,0:T(8,128)(2,1)S(1)}, bf16[4,128,512]{2,1,0:T(8,128)(2,1)S(1)}, u32[]{:S(2)}, u32[]{:S(2)}) %collective-permute-start.2) | collective-permute-done | bytes 524320 | tf_op jit(solution)/shard_map/ppermute | solution.py:32
  29.4 5.6 %collective-permute-done.1 = bf16[4,128,512]{2,1,0:T(8,128)(2,1)S(1)} collective-permute-done((bf16[4,128,512]{2,1,0:T(8,128)(2,1)S(1)}, bf16[4,128,512]{2,1,0:T(8,128)(2,1)S(1)}, u32[]{:S(2)}, u32[]{:S(2)}) %collective-permute-start.1) | collective-permute-done | bytes 524320 | tf_op jit(solution)/shard_map/ppermute | solution.py:32
  35.5 4.4 %collective-permute-start.5 = (bf16[2,512,512]{2,1,0:T(8,128)(2,1)S(1)}, bf16[2,512,512]{2,1,0:T(8,128)(2,1)S(1)}, u32[]{:S(2)}, u32[]{:S(2)}) collective-permute-start(bf16[2,512,512]{2,1,0:T(8,128)(2,1)S(1)} %pad_maximum_fusion.refs_0_), channel_id=1, source_target_pairs={{0,48},{1,49},{2,50},{3,51},{4,52},{5,53},{6,54},{7,55},{8,56},{9,... | collective-permute-start | bytes 3145736 | tf_op jit(solution)/shard_map/ppermute | solution.py:32
  39.9 1.9 %collective-permute-start.3 = (bf16[2,512,512]{2,1,0:T(8,128)(2,1)S(1)}, bf16[2,512,512]{2,1,0:T(8,128)(2,1)}, u32[]{:S(2)}, u32[]{:S(2)}) collective-permute-start(bf16[2,512,512]{2,1,0:T(8,128)(2,1)S(1)} %pad_maximum_fusion.refs_0_), channel_id=1, source_target_pairs={{0,16},{1,17},{2,18},{3,19},{4,20},{5,21},{6,22},{7,23},{8,24},{9,... | collective-permute-start | bytes 3145736 | tf_op jit(solution)/shard_map/ppermute | solution.py:32
  41.9 2.7 %collective-permute-start.6 = (bf16[2,512,512]{2,1,0:T(8,128)(2,1)S(1)}, bf16[2,512,512]{2,1,0:T(8,128)(2,1)}, u32[]{:S(2)}, u32[]{:S(2)}) collective-permute-start(bf16[2,512,512]{2,1,0:T(8,128)(2,1)S(1)} %pad_maximum_fusion.1.refs_1_), channel_id=1, source_target_pairs={{0,48},{1,49},{2,50},{3,51},{4,52},{5,53},{6,54},{7,55},{8,56},{9,... | collective-permute-start | bytes 3145736 | tf_op jit(solution)/shard_map/ppermute | solution.py:32
  44.6 2.6 %collective-permute-start.4 = (bf16[2,512,512]{2,1,0:T(8,128)(2,1)S(1)}, bf16[2,512,512]{2,1,0:T(8,128)(2,1)}, u32[]{:S(2)}, u32[]{:S(2)}) collective-permute-start(bf16[2,512,512]{2,1,0:T(8,128)(2,1)S(1)} %pad_maximum_fusion.1.refs_1_), channel_id=1, source_target_pairs={{0,16},{1,17},{2,18},{3,19},{4,20},{5,21},{6,22},{7,23},{8,24},{9,... | collective-permute-start | bytes 3145736 | tf_op jit(solution)/shard_map/ppermute | solution.py:32
  47.3 1.9 %broadcast_select_fusion = bf16[2,64,2048]{2,1,0:T(8,128)(2,1)} fusion(bf16[2,64,2048]{2,1,0:T(8,128)(2,1)} %param.6, bf16[2,64,2048]{2,1,0:T(8,128)(2,1)} %param.7, pred[]{:T(512)S(6)} %lt.26), kind=kLoop, calls=%fused_computation.9 | loop fusion | flops 262144 | bytes 1572865 | tf_op jit(solution)/shard_map/jit(_where)/select_n | solution.py:270
  49.2 3.4 %collective-permute-done.5.refs_4_ = bf16[2,512,512]{2,1,0:T(8,128)(2,1)S(1)} collective-permute-done((bf16[2,512,512]{2,1,0:T(8,128)(2,1)S(1)}, bf16[2,512,512]{2,1,0:T(8,128)(2,1)S(1)}, u32[]{:S(2)}, u32[]{:S(2)}) %collective-permute-start.5) | collective-permute-done | bytes 1048608 | tf_op jit(solution)/shard_map/ppermute | solution.py:32
  53.4 2.0 %collective-permute-start.7 = (bf16[1,512,512]{2,1,0:T(8,128)(2,1)}, bf16[1,512,512]{2,1,0:T(8,128)(2,1)}, u32[]{:S(2)}, u32[]{:S(2)}) collective-permute-start(bf16[1,512,512]{2,1,0:T(8,128)(2,1)} %slice.68), channel_id=1, source_target_pairs={{0,16},{1,17},{2,18},{3,19},{4,20},{5,21},{6,22},{7,23},{8,24},{9,... | collective-permute-start | bytes 1572872 | tf_op jit(solution)/shard_map/ppermute | solution.py:32
  55.9 1.9 %slice.69 = bf16[1,512,512]{2,1,0:T(8,128)(2,1)} slice(bf16[2,512,512]{2,1,0:T(8,128)(2,1)} %collective-permute-done.3.refs_2_), slice={[1:2], [0:512], [0:512]} | slice | bytes 1048576 | tf_op jit(solution)/shard_map/slice | solution.py:241
  57.8 4.0 %collective-permute-start.8 = (bf16[1,512,512]{2,1,0:T(8,128)(2,1)}, bf16[1,512,512]{2,1,0:T(8,128)(2,1)}, u32[]{:S(2)}, u32[]{:S(2)}) collective-permute-start(bf16[1,512,512]{2,1,0:T(8,128)(2,1)} %slice.69), channel_id=1, source_target_pairs={{0,48},{1,49},{2,50},{3,51},{4,52},{5,53},{6,54},{7,55},{8,56},{9,... | collective-permute-start | bytes 1572872 | tf_op jit(solution)/shard_map/ppermute | solution.py:32
  61.8 2.2 %collective-permute-done.6.refs_5_ = bf16[2,512,512]{2,1,0:T(8,128)(2,1)} collective-permute-done((bf16[2,512,512]{2,1,0:T(8,128)(2,1)S(1)}, bf16[2,512,512]{2,1,0:T(8,128)(2,1)}, u32[]{:S(2)}, u32[]{:S(2)}) %collective-permute-start.6) | collective-permute-done | bytes 1048608 | tf_op jit(solution)/shard_map/ppermute | solution.py:32
  63.9 1.9 %slice.70 = bf16[1,512,512]{2,1,0:T(8,128)(2,1)} slice(bf16[2,512,512]{2,1,0:T(8,128)(2,1)} %collective-permute-done.6.refs_5_), slice={[0:1], [0:512], [0:512]} | slice | bytes 1048576 | tf_op jit(solution)/shard_map/slice | solution.py:241
  65.8 2.0 %collective-permute-start.9 = (bf16[1,512,512]{2,1,0:T(8,128)(2,1)}, bf16[1,512,512]{2,1,0:T(8,128)(2,1)}, u32[]{:S(2)}, u32[]{:S(2)}) collective-permute-start(bf16[1,512,512]{2,1,0:T(8,128)(2,1)} %slice.70), channel_id=1, source_target_pairs={{0,16},{1,17},{2,18},{3,19},{4,20},{5,21},{6,22},{7,23},{8,24},{9,... | collective-permute-start | bytes 1572872 | tf_op jit(solution)/shard_map/ppermute | solution.py:32
  67.9 1.9 %slice.71 = bf16[1,512,512]{2,1,0:T(8,128)(2,1)} slice(bf16[2,512,512]{2,1,0:T(8,128)(2,1)} %collective-permute-done.4.refs_3_), slice={[1:2], [0:512], [0:512]} | slice | bytes 1048576 | tf_op jit(solution)/shard_map/slice | solution.py:241
  69.7 4.4 %collective-permute-start.10 = (bf16[1,512,512]{2,1,0:T(8,128)(2,1)}, bf16[1,512,512]{2,1,0:T(8,128)(2,1)}, u32[]{:S(2)}, u32[]{:S(2)}) collective-permute-start(bf16[1,512,512]{2,1,0:T(8,128)(2,1)} %slice.71), channel_id=1, source_target_pairs={{0,48},{1,49},{2,50},{3,51},{4,52},{5,53},{6,54},{7,55},{8,56},{9,... | collective-permute-start | bytes 1572872 | tf_op jit(solution)/shard_map/ppermute | solution.py:32
  74.8 2.6 %stack.27.scal = s32[9]{0:T(128)S(1)} concatenate(s32[1]{0:T(128)} %bitcast, s32[1]{0:T(128)} %bitcast.1, s32[1]{0:T(128)} %bitcast.2, s32[1]{0:T(128)} %bitcast.3, s32[1]{0:T(128)} %get-tuple-element.39, s32[1]{0:T(128)} %get-tuple-element.40, s32[1]{0:T(128)} %bitcast.4, s32[1]{0:T(128)} %get-tuple-element.36, s32[1]{0:T(128)} %get-tuple-element.35), dimensions={0} | concatenate | bytes 72 | tf_op jit(solution)/shard_map/stack | solution.py:253
  78.5 2.0 %shard_map.64 = (bf16[16,128,128]{2,1,0:T(8,128)(2,1)S(1)}, f32[128,512]{1,0:T(8,128)S(1)}, f32[128,512]{1,0:T(8,128)S(1)}, f32[128,512]{1,0:T(8,128)S(1)}) custom-call(s32[9]{0:T(128)S(1)} %stack.27.scal, f32[5,2048]{1,0:T(8,128)S(1)} %copy-done.6, bf16[64,2048]{1,0:T(8,128)(2,1)S(1)} %get-tuple-element.32.mine, ...), custom_call_target="tpu_custom_call" | custom-call | flops 805306368 | bytes 6856704 | tf_op jit(solution)/shard_map/pallas_call | solution.py:177
  81.5 2.5 %shard_map.65 = (f32[64,2048]{1,0:T(8,128)S(1)}, bf16[64,2048]{1,0:T(8,128)(2,1)S(1)}) custom-call(s32[9]{0:T(128)S(1)} %stack.27.scal, bf16[16,128,128]{2,1,0:T(8,128)(2,1)S(1)} %get-tuple-element.13.h3, f32[128,512]{1,0:T(8,128)S(1)} %get-tuple-element.14.q, f32[128,512]{1,0:T(8,128)S(1)} %get-tuple-element.15.k, f32[128,512]{1,0:T(8,128)S(1)} %get-tuple-element.16.v, ...), custom_call_target="tpu_custom_call" | custom-call | flops 536870912 | bytes 9699328 | tf_op jit(solution)/shard_map/pallas_call | solution.py:177
  86.9 2.6 %shard_map.66 = (f32[64,2048]{1,0:T(8,128)S(1)}, bf16[64,2048]{1,0:T(8,128)(2,1)S(1)}) custom-call(s32[9]{0:T(128)S(1)} %stack.27.scal, f32[5,2048]{1,0:T(8,128)S(1)} %copy-done.6, bf16[64,2048]{1,0:T(8,128)(2,1)S(1)} %collective-permute-done.12.mine.in1m, bf16[64,2048]{1,0:T(8,128)(2,1)S(1)} %collective-permute-done.13.other.in1o, ...), custom_call_target="tpu_custom_call" | custom-call | flops 1073741824 | bytes 8953856 | tf_op jit(solution)/shard_map/pallas_call | solution.py:177
  93.9 37.5 %collective-permute-done.14.mine.in3m = bf16[64,2048]{1,0:T(8,128)(2,1)} collective-permute-done((bf16[64,2048]{1,0:T(8,128)(2,1)S(1)}, bf16[64,2048]{1,0:T(8,128)(2,1)}, u32[]{:S(2)}, u32[]{:S(2)}) %collective-permute-start.14) | collective-permute-done | bytes 262176 | tf_op jit(solution)/shard_map/ppermute | solution.py:302
  131.4 2.8 %collective-permute-start.15 = (bf16[64,2048]{1,0:T(8,128)(2,1)}, bf16[64,2048]{1,0:T(8,128)(2,1)}, u32[]{:S(2)}, u32[]{:S(2)}) collective-permute-start(bf16[64,2048]{1,0:T(8,128)(2,1)} %collective-permute-done.14.mine.in3m), channel_id=1, source_target_pairs={{384,448},{448,384},{385,449},{449,385},{386,450},{450,386},{387,4... | collective-permute-start | bytes 786440 | tf_op jit(solution)/shard_map/ppermute | solution.py:278
  134.2 9.3 %collective-permute-done.18.mem_mine = bf16[64,2048]{1,0:T(8,128)(2,1)} collective-permute-done((bf16[64,2048]{1,0:T(8,128)(2,1)S(1)}, bf16[64,2048]{1,0:T(8,128)(2,1)}, u32[]{:S(2)}, u32[]{:S(2)}) %collective-permute-start.18) | collective-permute-done | bytes 262176 | tf_op jit(solution)/shard_map/ppermute | solution.py:314
  143.5 2.6 %collective-permute-start.19 = (bf16[64,2048]{1,0:T(8,128)(2,1)}, bf16[64,2048]{1,0:T(8,128)(2,1)}, u32[]{:S(2)}, u32[]{:S(2)}) collective-permute-start(bf16[64,2048]{1,0:T(8,128)(2,1)} %collective-permute-done.18.mem_mine), channel_id=1, source_target_pairs={{384,448},{448,384},{385,449},{449,385},{386,450},{450,386},{387,4... | collective-permute-start | bytes 786440 | tf_op jit(solution)/shard_map/ppermute | solution.py:278
  146.2 3.3 %shard_map.67.q = bf16[128,512]{1,0:T(8,128)(2,1)S(1)} custom-call(s32[9]{0:T(128)S(1)} %stack.27.scal, f32[5,2048]{1,0:T(8,128)S(1)} %copy-done.6, bf16[64,2048]{1,0:T(8,128)(2,1)} %collective-permute-done.14.mine.in3m, bf16[64,2048]{1,0:T(8,128)(2,1)} %collective-permute-done.15.other.in3o, bf16[2,512,512]{2,1,0:T(8,128)(2,1)S(1)} %pad_maximum_fusion.refs_0_, ...), custom_call_target="tpu_custom_call" | custom-call | flops 268435456 | bytes 8953856 | tf_op jit(solution)/shard_map/pallas_call | solution.py:177
  149.5 5.4 %shard_map.68.own = bf16[128,2048]{1,0:T(8,128)(2,1)S(1)} custom-call(s32[9]{0:T(128)S(1)} %stack.27.scal, bf16[128,512]{1,0:T(8,128)(2,1)S(1)} %shard_map.67.q, bf16[64,2048]{1,0:T(8,128)(2,1)} %collective-permute-done.18.mem_mine, bf16[64,2048]{1,0:T(8,128)(2,1)} %collective-permute-done.19.mem_other, bf16[2,512,512]{2,1,0:T(8,128)(2,1)S(1)} %pad_maximum_fusion.refs_0_, ...), custom_call_target="tpu_custom_call" | custom-call | flops 805306368 | bytes 9043968 | tf_op jit(solution)/shard_map/pallas_call | solution.py:177
  156.9 1.8 %collective-permute-done.20.got = bf16[128,2048]{1,0:T(8,128)(2,1)S(1)} collective-permute-done((bf16[128,2048]{1,0:T(8,128)(2,1)S(1)}, bf16[128,2048]{1,0:T(8,128)(2,1)S(1)}, u32[]{:S(2)}, u32[]{:S(2)}) %collective-permute-start.20) | collective-permute-done | bytes 524320 | tf_op jit(solution)/shard_map/ppermute | solution.py:330
  158.7 2.1 %shard_map.69 = bf16[2,64,2048]{2,1,0:T(8,128)(2,1)} custom-call(s32[9]{0:T(128)S(1)} %stack.27.scal, bf16[64,2048]{1,0:T(8,128)(2,1)S(1)} %get-tuple-element.32.mine, bf16[64,2048]{1,0:T(8,128)(2,1)S(1)} %copy-done.1, bf16[64,2048]{1,0:T(8,128)(2,1)S(1)} %copy-done.3, bf16[64,2048]{1,0:T(8,128)(2,1)S(1)} %copy-done.5, ...), custom_call_target="tpu_custom_call" | custom-call | bytes 3145728 | tf_op jit(solution)/shard_map/pallas_call | solution.py:177
  (71 shorter events, 15.1 us)
Async XLA Ops:
  17.7 11.7 %collective-permute-start.2 = (bf16[4,128,512]{2,1,0:T(8,128)(2,1)S(1)}, bf16[4,128,512]{2,1,0:T(8,128)(2,1)S(1)}, u32[]{:S(2)}, u32[]{:S(2)}) collective-permute-start(bf16[4,128,512]{2,1,0:T(8,128)(2,1)S(1)} %bitcast.27), channel_id=1, source_target_pairs={{0,8},{1,9},{2,10},{3,11},{4,12},{5,13},{6,14},{7,15},{8,0},{9,1},... | collective-permute-start | bytes 1572872 | tf_op jit(solution)/shard_map/ppermute | solution.py:32
  22.5 12.5 %collective-permute-start.1 = (bf16[4,128,512]{2,1,0:T(8,128)(2,1)S(1)}, bf16[4,128,512]{2,1,0:T(8,128)(2,1)S(1)}, u32[]{:S(2)}, u32[]{:S(2)}) collective-permute-start(bf16[4,128,512]{2,1,0:T(8,128)(2,1)S(1)} %bitcast.28), channel_id=1, source_target_pairs={{0,12},{1,13},{2,14},{3,15},{4,8},{5,9},{6,10},{7,11},{8,4},{9,5},... | collective-permute-start | bytes 1572872 | tf_op jit(solution)/shard_map/ppermute | solution.py:32
  25.2 10.2 %collective-permute-start = (bf16[4,128,512]{2,1,0:T(8,128)(2,1)S(1)}, bf16[4,128,512]{2,1,0:T(8,128)(2,1)S(1)}, u32[]{:S(2)}, u32[]{:S(2)}) collective-permute-start(bf16[4,128,512]{2,1,0:T(8,128)(2,1)S(1)} %bitcast.29), channel_id=1, source_target_pairs={{0,4},{1,5},{2,6},{3,7},{4,0},{5,1},{6,2},{7,3},{8,12},{9,13},{10,... | collective-permute-start | bytes 1572872 | tf_op jit(solution)/shard_map/ppermute | solution.py:32
  35.5 17.0 %collective-permute-start.5 = (bf16[2,512,512]{2,1,0:T(8,128)(2,1)S(1)}, bf16[2,512,512]{2,1,0:T(8,128)(2,1)S(1)}, u32[]{:S(2)}, u32[]{:S(2)}) collective-permute-start(bf16[2,512,512]{2,1,0:T(8,128)(2,1)S(1)} %pad_maximum_fusion.refs_0_), channel_id=1, source_target_pairs={{0,48},{1,49},{2,50},{3,51},{4,52},{5,53},{6,54},{7,55},{8,56},{9,... | collective-permute-start | bytes 3145736 | tf_op jit(solution)/shard_map/ppermute | solution.py:32
  39.9 15.9 %collective-permute-start.3 = (bf16[2,512,512]{2,1,0:T(8,128)(2,1)S(1)}, bf16[2,512,512]{2,1,0:T(8,128)(2,1)}, u32[]{:S(2)}, u32[]{:S(2)}) collective-permute-start(bf16[2,512,512]{2,1,0:T(8,128)(2,1)S(1)} %pad_maximum_fusion.refs_0_), channel_id=1, source_target_pairs={{0,16},{1,17},{2,18},{3,19},{4,20},{5,21},{6,22},{7,23},{8,24},{9,... | collective-permute-start | bytes 3145736 | tf_op jit(solution)/shard_map/ppermute | solution.py:32
  41.9 22.0 %collective-permute-start.6 = (bf16[2,512,512]{2,1,0:T(8,128)(2,1)S(1)}, bf16[2,512,512]{2,1,0:T(8,128)(2,1)}, u32[]{:S(2)}, u32[]{:S(2)}) collective-permute-start(bf16[2,512,512]{2,1,0:T(8,128)(2,1)S(1)} %pad_maximum_fusion.1.refs_1_), channel_id=1, source_target_pairs={{0,48},{1,49},{2,50},{3,51},{4,52},{5,53},{6,54},{7,55},{8,56},{9,... | collective-permute-start | bytes 3145736 | tf_op jit(solution)/shard_map/ppermute | solution.py:32
  44.6 23.2 %collective-permute-start.4 = (bf16[2,512,512]{2,1,0:T(8,128)(2,1)S(1)}, bf16[2,512,512]{2,1,0:T(8,128)(2,1)}, u32[]{:S(2)}, u32[]{:S(2)}) collective-permute-start(bf16[2,512,512]{2,1,0:T(8,128)(2,1)S(1)} %pad_maximum_fusion.1.refs_1_), channel_id=1, source_target_pairs={{0,16},{1,17},{2,18},{3,19},{4,20},{5,21},{6,22},{7,23},{8,24},{9,... | collective-permute-start | bytes 3145736 | tf_op jit(solution)/shard_map/ppermute | solution.py:32
  53.4 27.0 %collective-permute-start.7 = (bf16[1,512,512]{2,1,0:T(8,128)(2,1)}, bf16[1,512,512]{2,1,0:T(8,128)(2,1)}, u32[]{:S(2)}, u32[]{:S(2)}) collective-permute-start(bf16[1,512,512]{2,1,0:T(8,128)(2,1)} %slice.68), channel_id=1, source_target_pairs={{0,16},{1,17},{2,18},{3,19},{4,20},{5,21},{6,22},{7,23},{8,24},{9,... | collective-permute-start | bytes 1572872 | tf_op jit(solution)/shard_map/ppermute | solution.py:32
  57.8 16.4 %copy-start.11 = (s32[2]{0:T(128)S(1)}, s32[2]{0:T(128)}, u32[]{:S(2)}) copy-start(s32[2]{0:T(128)} %param.10) | copy-start | bytes 28
  57.8 16.4 %copy-start.12 = (s32[2]{0:T(128)S(1)}, s32[2]{0:T(128)}, u32[]{:S(2)}) copy-start(s32[2]{0:T(128)} %param.11) | copy-start | bytes 28
  57.8 22.7 %collective-permute-start.8 = (bf16[1,512,512]{2,1,0:T(8,128)(2,1)}, bf16[1,512,512]{2,1,0:T(8,128)(2,1)}, u32[]{:S(2)}, u32[]{:S(2)}) collective-permute-start(bf16[1,512,512]{2,1,0:T(8,128)(2,1)} %slice.69), channel_id=1, source_target_pairs={{0,48},{1,49},{2,50},{3,51},{4,52},{5,53},{6,54},{7,55},{8,56},{9,... | collective-permute-start | bytes 1572872 | tf_op jit(solution)/shard_map/ppermute | solution.py:32
  65.8 12.7 %copy-start.6 = (f32[5,2048]{1,0:T(8,128)S(1)}, f32[5,2048]{1,0:T(8,128)}, u32[]{:S(2)}) copy-start(f32[5,2048]{1,0:T(8,128)} %gains.5) | copy-start | bytes 122884
  65.8 14.7 %collective-permute-start.9 = (bf16[1,512,512]{2,1,0:T(8,128)(2,1)}, bf16[1,512,512]{2,1,0:T(8,128)(2,1)}, u32[]{:S(2)}, u32[]{:S(2)}) collective-permute-start(bf16[1,512,512]{2,1,0:T(8,128)(2,1)} %slice.70), channel_id=1, source_target_pairs={{0,16},{1,17},{2,18},{3,19},{4,20},{5,21},{6,22},{7,23},{8,24},{9,... | collective-permute-start | bytes 1572872 | tf_op jit(solution)/shard_map/ppermute | solution.py:32
  69.7 11.7 %collective-permute-start.10 = (bf16[1,512,512]{2,1,0:T(8,128)(2,1)}, bf16[1,512,512]{2,1,0:T(8,128)(2,1)}, u32[]{:S(2)}, u32[]{:S(2)}) collective-permute-start(bf16[1,512,512]{2,1,0:T(8,128)(2,1)} %slice.71), channel_id=1, source_target_pairs={{0,48},{1,49},{2,50},{3,51},{4,52},{5,53},{6,54},{7,55},{8,56},{9,... | collective-permute-start | bytes 1572872 | tf_op jit(solution)/shard_map/ppermute | solution.py:32
  84.0 1.4 collective-permute-start.11
  85.5 4.7 %copy-start.9 = (bf16[64,2048]{1,0:T(8,128)(2,1)}, bf16[64,2048]{1,0:T(8,128)(2,1)S(1)}, u32[]{:S(2)}) copy-start(bf16[64,2048]{1,0:T(8,128)(2,1)S(1)} %add_convert_fusion.1) | copy-start | bytes 786436
  85.5 0.7 collective-permute-start.12
  86.2 5.3 %copy-start.2 = (bf16[64,2048]{1,0:T(8,128)(2,1)}, bf16[64,2048]{1,0:T(8,128)(2,1)S(1)}, u32[]{:S(2)}) copy-start(bf16[64,2048]{1,0:T(8,128)(2,1)S(1)} %collective-permute-done.12.mine.in1m) | copy-start | bytes 786436
  86.2 0.7 collective-permute-start.13
  86.9 2.6 %copy-start.4 = (bf16[64,2048]{1,0:T(8,128)(2,1)}, bf16[64,2048]{1,0:T(8,128)(2,1)S(1)}, u32[]{:S(2)}) copy-start(bf16[64,2048]{1,0:T(8,128)(2,1)S(1)} %collective-permute-done.13.other.in1o) | copy-start | bytes 786436
  89.5 2.0 %collective-permute-start.16 = (bf16[64,2048]{1,0:T(8,128)(2,1)S(1)}, bf16[64,2048]{1,0:T(8,128)(2,1)S(1)}, u32[]{:S(2)}, u32[]{:S(2)}) collective-permute-start(bf16[64,2048]{1,0:T(8,128)(2,1)S(1)} %get-tuple-element.20), channel_id=1, source_target_pairs={{128,192},{192,128},{129,193},{193,129},{130,194},{194,130},{131,1... | collective-permute-start | bytes 786440 | tf_op jit(solution)/shard_map/ppermute | solution.py:278
  90.2 41.2 %collective-permute-start.14 = (bf16[64,2048]{1,0:T(8,128)(2,1)S(1)}, bf16[64,2048]{1,0:T(8,128)(2,1)}, u32[]{:S(2)}, u32[]{:S(2)}) collective-permute-start(bf16[64,2048]{1,0:T(8,128)(2,1)S(1)} %add_convert_fusion.1), channel_id=1, source_target_pairs={{256,384},{257,385},{258,386},{259,387},{260,388},{261,389},{262,3... | collective-permute-start | bytes 786440 | tf_op jit(solution)/shard_map/ppermute | solution.py:302
  92.6 50.9 %collective-permute-start.18 = (bf16[64,2048]{1,0:T(8,128)(2,1)S(1)}, bf16[64,2048]{1,0:T(8,128)(2,1)}, u32[]{:S(2)}, u32[]{:S(2)}) collective-permute-start(bf16[64,2048]{1,0:T(8,128)(2,1)S(1)} %fusion.2), channel_id=1, source_target_pairs={{128,384},{129,385},{130,386},{131,387},{132,388},{133,389},{134,3... | collective-permute-start | bytes 786440 | tf_op jit(solution)/shard_map/ppermute | solution.py:314
  131.4 14.7 %collective-permute-start.15 = (bf16[64,2048]{1,0:T(8,128)(2,1)}, bf16[64,2048]{1,0:T(8,128)(2,1)}, u32[]{:S(2)}, u32[]{:S(2)}) collective-permute-start(bf16[64,2048]{1,0:T(8,128)(2,1)} %collective-permute-done.14.mine.in3m), channel_id=1, source_target_pairs={{384,448},{448,384},{385,449},{449,385},{386,450},{450,386},{387,4... | collective-permute-start | bytes 786440 | tf_op jit(solution)/shard_map/ppermute | solution.py:278
  143.5 6.0 %collective-permute-start.19 = (bf16[64,2048]{1,0:T(8,128)(2,1)}, bf16[64,2048]{1,0:T(8,128)(2,1)}, u32[]{:S(2)}, u32[]{:S(2)}) collective-permute-start(bf16[64,2048]{1,0:T(8,128)(2,1)} %collective-permute-done.18.mem_mine), channel_id=1, source_target_pairs={{384,448},{448,384},{385,449},{449,385},{386,450},{450,386},{387,4... | collective-permute-start | bytes 786440 | tf_op jit(solution)/shard_map/ppermute | solution.py:278
  149.5 6.7 %copy-start.8 = (bf16[64,2048]{1,0:T(8,128)(2,1)S(1)}, bf16[64,2048]{1,0:T(8,128)(2,1)}, u32[]{:S(2)}) copy-start(bf16[64,2048]{1,0:T(8,128)(2,1)} %copy-done.7) | copy-start | bytes 786436
  149.5 6.7 %copy-start.10 = (bf16[64,2048]{1,0:T(8,128)(2,1)S(1)}, bf16[64,2048]{1,0:T(8,128)(2,1)}, u32[]{:S(2)}) copy-start(bf16[64,2048]{1,0:T(8,128)(2,1)} %copy-done.9) | copy-start | bytes 786436
  149.5 9.2 %copy-start.1 = (bf16[64,2048]{1,0:T(8,128)(2,1)S(1)}, bf16[64,2048]{1,0:T(8,128)(2,1)}, u32[]{:S(2)}) copy-start(bf16[64,2048]{1,0:T(8,128)(2,1)} %copy-done) | copy-start | bytes 786436
  149.5 9.2 %copy-start.3 = (bf16[64,2048]{1,0:T(8,128)(2,1)S(1)}, bf16[64,2048]{1,0:T(8,128)(2,1)}, u32[]{:S(2)}) copy-start(bf16[64,2048]{1,0:T(8,128)(2,1)} %copy-done.2) | copy-start | bytes 786436
  149.5 9.2 %copy-start.5 = (bf16[64,2048]{1,0:T(8,128)(2,1)S(1)}, bf16[64,2048]{1,0:T(8,128)(2,1)}, u32[]{:S(2)}) copy-start(bf16[64,2048]{1,0:T(8,128)(2,1)} %copy-done.4) | copy-start | bytes 786436
  154.9 3.8 %collective-permute-start.20 = (bf16[128,2048]{1,0:T(8,128)(2,1)S(1)}, bf16[128,2048]{1,0:T(8,128)(2,1)S(1)}, u32[]{:S(2)}, u32[]{:S(2)}) collective-permute-start(bf16[128,2048]{1,0:T(8,128)(2,1)S(1)} %shard_map.68.own), channel_id=1, source_target_pairs={{384,448},{385,449},{386,450},{387,451},{388,452},{389,453},{390,4... | collective-permute-start | bytes 1572872 | tf_op jit(solution)/shard_map/ppermute | solution.py:330
  156.2 0.7 collective-permute-start.17
  (2 other events, 2.7 us)

commit v6 on v5

v6 whole, which is shorter than its diff:
```python
import itertools

import jax
import jax.numpy as jnp
from jax import lax
from jax.experimental import pallas as pl
from jax.experimental.pallas import tpu as pltpu
from jax.sharding import Mesh, PartitionSpec as P

HEAD_DIM = 128
SIDE = 4
TURNS = (0, 1, 3, 2)
FAR = 2
AXES = ("zh", "core", "y", "x", "zl")
DP = ("y", "x", "zl")
SECTION = ("zh", "core")
F32 = jnp.float32
BF16 = jnp.bfloat16
VMEM = pl.BlockSpec(memory_space=pltpu.VMEM)
SMEM = pl.BlockSpec(memory_space=pltpu.SMEM)
BLOCKS = 16
LANES = 128
TILE = 256
ROWS = 32
X, Y, CUBE, CAUSAL, KEYS, CORE, LIVE = 0, 1, 2, 3, 4, 6, 7


def place(zh, core, y, x, zl):
    return (((zh * 2 + core) * SIDE + y) * SIDE + x) * SIDE + zl


def exchange(array, outer, by):
    pairs = []
    for zh, core, y, x, zl in itertools.product(*map(range, (SIDE, 2, SIDE, SIDE, SIDE))):
        along_y = outer == (core == 0)
        to = (y ^ by, x) if along_y else (y, x ^ by)
        pairs.append((place(zh, core, y, x, zl), place(zh, core, *to, zl)))
    return lax.ppermute(array, AXES, pairs)


def turns(array, outer):
    return [array] + [exchange(array, outer, turn) for turn in TURNS[1:]]


def dot(a, b):
    return jnp.dot(a, b, preferred_element_type=F32)


def dot_t(a, b):
    return lax.dot_general(a, b, (((1,), (1,)), ((), ())), preferred_element_type=F32)


def rms(values, gain):
    mean_square = jnp.mean(values * values, axis=-1, keepdims=True)
    return (values * lax.rsqrt(mean_square + 1e-06) * gain).astype(BF16)


def lanes(i):
    return slice(i * LANES, (i + 1) * LANES)


def span(i, size):
    return pl.ds(pl.multiple_of(i * size, size), size)


def loop(count, body):
    lax.fori_loop(0, count, lambda i, carry: (body(i), carry)[1], 0)


def block_at(scal, outer, inner):
    back = scal[CORE] == 1
    dy, dx = jnp.where(back, inner, outer), jnp.where(back, outer, inner)
    return lax.bitwise_xor(scal[Y], dy) * SIDE + lax.bitwise_xor(scal[X], dx)


def inner_turns(half):
    return 3 * half, 1 + half


def weight(pieces, turn, which):
    chunk, at = divmod(which, 2)
    if turn == FAR:
        return pieces[6 + which], 0
    return pieces[2 * TURNS.index(turn) + chunk], at


def put_blocks(h3, rows, h):
    for i in range(BLOCKS):
        h3[i, rows, :] = h[:, lanes(i)]


def project(scal, h3, pieces, spots, which, total):
    def tile(n):
        cols = span(n, TILE)
        sums = [None] * len(which)
        for turn in spots:
            for half in range(2):
                h = jnp.concatenate([h3[block_at(scal, turn, d)] for d in inner_turns(half)], axis=1)
                for i, m in enumerate(which):
                    ref, at = weight(pieces, turn, m)
                    term = dot(h, ref[at, half * TILE:(half + 1) * TILE, cols])
                    sums[i] = term if sums[i] is None else sums[i] + term
        for i, m in enumerate(which):
            total[m, :, cols] = sums[i]

    loop(2, tile)


def attend(scal, q_at, k_at, v_at, mixed):
    count = mixed.shape[0]
    rows = count // 2
    r = lax.broadcasted_iota(jnp.int32, (count, count), 0)
    c = lax.broadcasted_iota(jnp.int32, (count, count), 1)
    first = c < rows
    live = (r < rows) == first
    live = live & (jnp.where(first, c, c - rows) < jnp.where(first, scal[KEYS], scal[KEYS + 1]))
    live = live & ((c <= r) | (scal[CAUSAL] == 0))

    def pair(step):
        for side in range(2):
            at = span(step * 2 + side, LANES)
            s = dot_t(q_at(at), k_at(at)) * HEAD_DIM ** (-0.5)
            s = jnp.where(live, s, -1e30)
            e = jnp.exp(s - jnp.max(s, axis=-1, keepdims=True))
            p = (e / jnp.sum(e, axis=-1, keepdims=True)).astype(BF16)
            mixed[:, at] = dot(p, v_at(at)).astype(BF16)

    loop(2, pair)


def project_out(scal, mixed, spots, t3):
    def tile(half):
        rows = span(half, TILE)
        for turn, (ref, at) in zip(TURNS, spots):
            t = dot_t(mixed[...], ref[at, rows, :])
            for j, d in enumerate(inner_turns(half)):
                t3[block_at(scal, turn, d)] = t[:, lanes(j)]

    loop(2, tile)


def put_out(t3, rows, out):
    def block(i):
        out[:, span(i, LANES)] = t3[i, rows, :].astype(out.dtype)

    loop(BLOCKS, block)


def doc_rows(scal, rows):
    return span(scal[CORE], rows), span(1 - scal[CORE], rows)


def outs_at(pieces):
    return [weight(pieces, turn, 3) for turn in TURNS]


def put_norm(scal, gains, parts, h3):
    gain = gains[pl.ds(scal[CUBE], 1), :]
    for ref, first in parts:

        def chunk(i, ref=ref, first=first):
            h = rms(ref[span(i, ROWS), :].astype(F32), gain)
            to = pl.ds(pl.multiple_of(first + i * ROWS, ROWS), ROWS)
            put_blocks(h3, to, h)

        loop(ref.shape[0] // ROWS, chunk)


def doc_parts(scal, mine, other):
    rows = mine.shape[0]
    return (mine, scal[CORE] * rows), (other, (1 - scal[CORE]) * rows)


def put_halves(scal, t3, mine, other):
    here, there = doc_rows(scal, mine.shape[0])
    put_out(t3, here, mine)
    put_out(t3, there, other)


def early_kernel(scal, gains, base, *refs):
    pieces, (h3, total) = refs[:6], refs[6:]

    @pl.when(lax.rem(scal[CUBE], 2) == 0)
    def _():
        put_norm(scal, gains, [(base, 0)], h3)
        project(scal, h3, pieces, TURNS[:3], (0, 1, 2), total)


def first_kernel(scal, h3, early, *refs):
    pieces, (mine, other, total, mixed, t3) = refs[:10], refs[10:]

    @pl.when(lax.rem(scal[CUBE], 2) == 0)
    def _():
        project(scal, h3, pieces, (FAR,), (0, 1, 2), total)

        def read(m):
            return lambda at: (total[m, :, at] + early[m, :, at]).astype(BF16)

        attend(scal, read(0), read(1), read(2), mixed)
        project_out(scal, mixed, outs_at(pieces), t3)
        put_halves(scal, t3, mine, other)


def second_kernel(scal, gains, in_mine, in_other, *refs):
    pieces, (mine, other, h3, total, mixed, t3) = refs[:10], refs[10:]

    @pl.when(scal[CUBE] == 1)
    def _():
        put_norm(scal, gains, doc_parts(scal, in_mine, in_other), h3)
        project(scal, h3, pieces, TURNS, (0, 1, 2), total)

        def read(m):
            return lambda at: total[m, :, at].astype(BF16)

        attend(scal, read(0), read(1), read(2), mixed)
        project_out(scal, mixed, outs_at(pieces), t3)
        put_halves(scal, t3, mine, other)


def query_kernel(scal, gains, in_mine, in_other, *refs):
    pieces, (query, h3, total) = refs[:10], refs[10:]

    @pl.when(scal[CUBE] == 3)
    def _():
        put_norm(scal, gains, doc_parts(scal, in_mine, in_other), h3)
        project(scal, h3, pieces, TURNS, (0,), total)
        query[...] = total[0].astype(BF16)


def third_kernel(scal, query, mem_mine, mem_other, *refs):
    pieces, (part, m3, total, mixed, t3) = refs[:10], refs[10:]

    @pl.when(scal[CUBE] == 3)
    def _():
        here, there = doc_rows(scal, mem_mine.shape[0])

        def block(i):
            m3[i, here, :] = mem_mine[:, span(i, LANES)]
            m3[i, there, :] = mem_other[:, span(i, LANES)]

        loop(BLOCKS, block)
        project(scal, m3, pieces, TURNS, (1, 2), total)

        def read(m):
            return lambda at: total[m, :, at].astype(BF16)

        attend(scal, lambda at: query[:, at], read(1), read(2), mixed)
        project_out(scal, mixed, outs_at(pieces), t3)
        put_out(t3, slice(None), part)


def finish_kernel(scal, base, in1m, in1o, in3m, in3o, early, early_other, own, got, out):
    rows = early.shape[0]
    cube, core = scal[CUBE], scal[CORE]
    odd = lax.rem(cube, 2) == 1
    low, high = slice(0, rows), slice(rows, 2 * rows)

    @pl.when((core == 0) & jnp.logical_not(odd))
    def _():
        out[...] = base[...]

    for at, one, two in ((1, in1m, in1o), (3, in3m, in3o)):

        @pl.when((core == 0) & (cube == at))
        def _(one=one, two=two):
            out[low, :] = one[...]
            out[high, :] = two[...]

    @pl.when((core == 1) & (cube != 3))
    def _():
        out[low, :] = early_other[...]
        out[high, :] = early[...]

    @pl.when((core == 1) & (cube == 3))
    def _():
        at = lax.broadcasted_iota(jnp.int32, early.shape, 0)
        for doc, here, stream in ((0, low, in3o), (1, high, in3m)):
            term = own[here, :].astype(F32) + got[here, :].astype(F32)
            term = jnp.where(at < scal[LIVE + doc], term, 0.0)
            out[here, :] = (stream[...].astype(F32) + term).astype(BF16)


def call(kernel, scal, operands, outs, scratch=(), flops=0):
    size = sum(a.size * a.dtype.itemsize for a in operands)
    return pl.pallas_call(
        kernel,
        out_shape=outs,
        in_specs=[SMEM] + [VMEM] * len(operands),
        out_specs=jax.tree.map(lambda _: VMEM, outs),
        scratch_shapes=[pltpu.VMEM(shape, kind) for shape, kind in scratch],
        compiler_params=pltpu.CompilerParams(vmem_limit_bytes=12 * 1024 * 1024),
        cost_estimate=pl.CostEstimate(flops=flops, bytes_accessed=size, transcendentals=0),
    )(scal, *operands)


def gather(weights):
    pair, depth, width = weights.shape[1:]
    halves = weights[0].reshape(pair, depth, 2, width // 2).transpose(2, 0, 1, 3)
    sent = jnp.broadcast_to(halves[:, None], (2, SIDE) + halves.shape[1:])
    sent = sent.reshape((2 * SIDE,) + halves.shape[1:])
    got = lax.all_to_all(sent, ("core", "zl"), 0, 0, tiled=True)
    got = got.reshape(2, SIDE, pair, depth, width // 2).transpose(0, 2, 1, 3, 4)
    got = got.reshape(2 * pair, SIDE * depth, width // 2)
    near = turns(got, False)
    chunks = [jnp.concatenate([a[i:i + pair] for a in near], axis=1) for i in (0, pair)]
    by1 = [exchange(a, True, 1) for a in chunks]
    by3 = [exchange(a, True, 3) for a in chunks]
    far = []
    for a, b in zip(by1, by3):
        far += [exchange(b[:1], True, 1), exchange(a[1:], True, 3)]
    return [*chunks, *by1, *by3], far


def on_device(encoder_embed, decoder_embed, section_weights, norm_gains, input_lengths, target_lengths):
    zh, core = lax.axis_index("zh"), lax.axis_index("core")
    y, x = lax.axis_index("y"), lax.axis_index("x")
    docs, rows, width = encoder_embed.shape
    count = docs * rows
    encoder = zh < 2
    causal = zh == 2
    key_lengths = jnp.where(causal, target_lengths, input_lengths)
    row_lengths = jnp.where(encoder, input_lengths, target_lengths)
    scal = jnp.stack(
        [x, y, zh, causal.astype(jnp.int32), key_lengths[0], key_lengths[1], core]
        + [row_lengths[0], row_lengths[1]]
    ).astype(jnp.int32)
    base = jnp.where(encoder, encoder_embed, decoder_embed).reshape(count, width)
    near, far = gather(section_weights)
    pieces = near + far

    def swapped(array, cubes):
        pairs = [(2 * c + i, 2 * c + 1 - i) for c in cubes for i in range(2)]
        return lax.ppermute(array, SECTION, pairs)

    half = near[0].shape[-1]
    blocks = (BLOCKS, count, LANES)
    totals = (3, count, half)
    work = 2 * count * width * half
    wide = jax.ShapeDtypeStruct((count, width), BF16)
    narrow = jax.ShapeDtypeStruct((count, half), BF16)
    halves = tuple(jax.ShapeDtypeStruct((rows, width), kind) for kind in (F32, BF16))
    rest = [(totals, F32), ((count, half), BF16), (blocks, F32)]
    own_doc = lax.dynamic_slice(base, (core * rows, 0), (rows, width))
    live = (jnp.arange(rows, dtype=jnp.int32) < row_lengths[core])[:, None]

    def added(stream, kept, sent, cubes):
        term = kept + swapped(sent, cubes).astype(F32)
        return (stream.astype(F32) + jnp.where(live, term, 0.0)).astype(BF16)

    h3, early = call(
        early_kernel,
        scal,
        [norm_gains, base, *near],
        (jax.ShapeDtypeStruct(blocks, BF16), jax.ShapeDtypeStruct(totals, F32)),
        (),
        3 * work,
    )
    kept, sent = call(first_kernel, scal, [h3, early, *pieces], halves, rest, 2 * work)
    first = added(own_doc, kept, sent, (0, 2))
    in1 = lax.ppermute(first, "zh", [(0, 1)])
    in3 = lax.ppermute(first, "zh", [(2, 3)])
    in1_other = swapped(in1, (1,))
    kept, sent = call(
        second_kernel,
        scal,
        [norm_gains, in1, in1_other, *pieces],
        halves,
        [(blocks, BF16), *rest],
        4 * work,
    )
    second = added(in1, kept, sent, (1,))
    memory = rms(second.astype(F32), norm_gains[4:5])
    mem = lax.ppermute(memory, "zh", [(1, 3)])
    early_doc = jnp.where(zh == 1, second, first)
    early_other = lax.ppermute(early_doc, SECTION, [(0, 1), (2, 3), (4, 5)])
    in3_other = swapped(in3, (3,))
    query = call(
        query_kernel,
        scal,
        [norm_gains, in3, in3_other, *pieces],
        narrow,
        [(blocks, BF16), (totals, F32)],
        work,
    )
    mem_other = swapped(mem, (3,))
    own = call(
        third_kernel, scal, [query, mem, mem_other, *pieces], wide, [(blocks, BF16), *rest], 3 * work
    )
    got = lax.ppermute(own, SECTION, [(6, 7)])
    parts = [base, in1, in1_other, in3, in3_other, early_doc, early_other, own, got]
    out = call(finish_kernel, scal, parts, wide)
    return out.reshape(1, docs, rows, width)


def solution(mesh):
    fine = Mesh(mesh.devices.reshape(SIDE, 2, SIDE, SIDE, SIDE), AXES)
    in_specs = (
        P(DP, None, None),
        P(DP, None, None),
        P(SECTION, None, DP, None),
        P(),
        P(DP),
        P(DP),
    )
    out_specs = P(SECTION, DP, None, None)
    return jax.shard_map(
        on_device, mesh=fine, in_specs=in_specs, out_specs=out_specs, check_vma=False
    )
```

time: 162 us -> 171 us (1.056)
  waiting for transfers between devices: 63.7 us -> 73.4 us
    ppermute x11, waiting for transfers between devices: 15.1 us -> 23.4 us  [exchange(): return lax.ppermute(array, AXES, pairs)]
    unnamed x26 -> x56, local copies, waits for them, and re-layouts: 0.75 us -> 7.84 us
    ppermute x1, waiting for transfers between devices: 9.29 us -> 16 us  [on_device(): mem = lax.ppermute(memory, 'zh', [(1, 3)])]
    ppermute x1, waiting for transfers between devices: 37.5 us -> 32.2 us  [on_device(): in3 = lax.ppermute(first, 'zh', [(2, 3)])]
    slice x4, local copies, waits for them, and re-layouts: 6.47 us -> 3.26 us  [gather(): far += [exchange(b[:1], True, 1), exchange(a[1:], True, 3)]]
    another operation x1, local copies, waits for them, and re-layouts: 2.55 us -> 0.08 us  [on_device(): jnp.stack([x, y, zh, causal.astype(jnp.int32), key_lengths[0], key_length...]
    select_n x2, other arithmetic: 1.93 us -> 0.09 us  [the longest x1 0.06 us: on_device(): jnp.where(encoder, encoder_embed, decoder_embed).reshape(count, width)]
  transfers between devices with their start and end apart: 21 -> 21, of which waited for: 10 -> 12; matrix products, arithmetic and copies ran while one was open for 9% -> 3% of each run, Pallas kernels for 3% -> 3%
where the time goes in v6:
time: 171 us; the launch traced here: 170 us
  waiting for transfers between devices  73.4 us (43%)
  starting transfers between devices  45.9 us (27%)
  Pallas kernels  17.3 us (10%)
  blocking collectives  16.6 us (10%)
  local copies, waits for them, and re-layouts  13.1 us (8%)
  other arithmetic  2.68 us (2%)
    ppermute x11, starting transfers between devices, exchange(): return lax.ppermute(array, AXES, pairs)  32.5 us
    ppermute x1, waiting for transfers between devices, on_device(): in3 = lax.ppermute(first, 'zh', [(2, 3)])  32.2 us
    ppermute x11, waiting for transfers between devices, exchange(): return lax.ppermute(array, AXES, pairs)  23.4 us
    pallas_call x6, Pallas kernels, call(): pl.pallas_call(kernel, out_shape=outs, in_specs=[SMEM] + [VMEM] * len(ope...  17.3 us
    all_to_all x1, blocking collectives, gather(): got = lax.all_to_all(sent, ('core', 'zl'), 0, 0, tiled=True)  16.6 us
    ppermute x1, waiting for transfers between devices, on_device(): mem = lax.ppermute(memory, 'zh', [(1, 3)])  16 us
    ppermute x5, starting transfers between devices, swapped(): return lax.ppermute(array, SECTION, pairs)  8.02 us
    unnamed x56, local copies, waits for them, and re-layouts  7.84 us
  transfers between devices with their start and end apart: 21, of which 12 were waited for; matrix products, arithmetic and copies ran while one was open for 3% of the time, Pallas kernels for 3%

profile of v6, /device:TPU:481, one launch (start us, length us, event | category | flops | bytes accessed | tf_op | source)
XLA Modules:
  0.0 169.6 jit_solution(4975203103889635193)
XLA Ops:
  1.1 16.6 %all_to_all.5 = bf16[8,2,32,512]{3,2,1,0:T(8,128)(2,1)S(1)} all-to-all(bf16[8,2,32,512]{3,2,1,0:T(8,128)(2,1)S(1)} %bitcast.24), channel_id=1, replica_groups=mesh['zh'=4,'core'=2,'y'=4,'x'=4,'zl'=4] {'core','zl'}, dimensions={0} | all-to-all | bytes 1048576 | tf_op jit(solution)/shard_map/all_to_all | solution.py:301
  17.7 4.8 %collective-permute-start.2 = (bf16[4,128,512]{2,1,0:T(8,128)(2,1)S(1)}, bf16[4,128,512]{2,1,0:T(8,128)(2,1)S(1)}, u32[]{:S(2)}, u32[]{:S(2)}) collective-permute-start(bf16[4,128,512]{2,1,0:T(8,128)(2,1)S(1)} %bitcast.27), channel_id=1, source_target_pairs={{0,8},{1,9},{2,10},{3,11},{4,12},{5,13},{6,14},{7,15},{8,0},{9,1},... | collective-permute-start | bytes 1572872 | tf_op jit(solution)/shard_map/ppermute | solution.py:38
  22.5 2.7 %collective-permute-start.1 = (bf16[4,128,512]{2,1,0:T(8,128)(2,1)S(1)}, bf16[4,128,512]{2,1,0:T(8,128)(2,1)S(1)}, u32[]{:S(2)}, u32[]{:S(2)}) collective-permute-start(bf16[4,128,512]{2,1,0:T(8,128)(2,1)S(1)} %bitcast.28), channel_id=1, source_target_pairs={{0,12},{1,13},{2,14},{3,15},{4,8},{5,9},{6,10},{7,11},{8,4},{9,5},... | collective-permute-start | bytes 1572872 | tf_op jit(solution)/shard_map/ppermute | solution.py:38
  25.2 1.9 %collective-permute-start = (bf16[4,128,512]{2,1,0:T(8,128)(2,1)S(1)}, bf16[4,128,512]{2,1,0:T(8,128)(2,1)S(1)}, u32[]{:S(2)}, u32[]{:S(2)}) collective-permute-start(bf16[4,128,512]{2,1,0:T(8,128)(2,1)S(1)} %bitcast.29), channel_id=1, source_target_pairs={{0,4},{1,5},{2,6},{3,7},{4,0},{5,1},{6,2},{7,3},{8,12},{9,13},{10,... | collective-permute-start | bytes 1572872 | tf_op jit(solution)/shard_map/ppermute | solution.py:38
  27.2 2.2 %collective-permute-done.2 = bf16[4,128,512]{2,1,0:T(8,128)(2,1)S(1)} collective-permute-done((bf16[4,128,512]{2,1,0:T(8,128)(2,1)S(1)}, bf16[4,128,512]{2,1,0:T(8,128)(2,1)S(1)}, u32[]{:S(2)}, u32[]{:S(2)}) %collective-permute-start.2) | collective-permute-done | bytes 524320 | tf_op jit(solution)/shard_map/ppermute | solution.py:38
  29.4 5.6 %collective-permute-done.1 = bf16[4,128,512]{2,1,0:T(8,128)(2,1)S(1)} collective-permute-done((bf16[4,128,512]{2,1,0:T(8,128)(2,1)S(1)}, bf16[4,128,512]{2,1,0:T(8,128)(2,1)S(1)}, u32[]{:S(2)}, u32[]{:S(2)}) %collective-permute-start.1) | collective-permute-done | bytes 524320 | tf_op jit(solution)/shard_map/ppermute | solution.py:38
  35.5 4.4 %collective-permute-start.5 = (bf16[2,512,512]{2,1,0:T(8,128)(2,1)S(1)}, bf16[2,512,512]{2,1,0:T(8,128)(2,1)S(1)}, u32[]{:S(2)}, u32[]{:S(2)}) collective-permute-start(bf16[2,512,512]{2,1,0:T(8,128)(2,1)S(1)} %pad_maximum_fusion.refs_0_), channel_id=1, source_target_pairs={{0,48},{1,49},{2,50},{3,51},{4,52},{5,53},{6,54},{7,55},{8,56},{9,... | collective-permute-start | bytes 3145736 | tf_op jit(solution)/shard_map/ppermute | solution.py:38
  39.9 1.9 %collective-permute-start.3 = (bf16[2,512,512]{2,1,0:T(8,128)(2,1)S(1)}, bf16[2,512,512]{2,1,0:T(8,128)(2,1)}, u32[]{:S(2)}, u32[]{:S(2)}) collective-permute-start(bf16[2,512,512]{2,1,0:T(8,128)(2,1)S(1)} %pad_maximum_fusion.refs_0_), channel_id=1, source_target_pairs={{0,16},{1,17},{2,18},{3,19},{4,20},{5,21},{6,22},{7,23},{8,24},{9,... | collective-permute-start | bytes 3145736 | tf_op jit(solution)/shard_map/ppermute | solution.py:38
  42.0 2.7 %collective-permute-start.6 = (bf16[2,512,512]{2,1,0:T(8,128)(2,1)S(1)}, bf16[2,512,512]{2,1,0:T(8,128)(2,1)}, u32[]{:S(2)}, u32[]{:S(2)}) collective-permute-start(bf16[2,512,512]{2,1,0:T(8,128)(2,1)S(1)} %pad_maximum_fusion.1.refs_1_), channel_id=1, source_target_pairs={{0,48},{1,49},{2,50},{3,51},{4,52},{5,53},{6,54},{7,55},{8,56},{9,... | collective-permute-start | bytes 3145736 | tf_op jit(solution)/shard_map/ppermute | solution.py:38
  44.7 2.6 %collective-permute-start.4 = (bf16[2,512,512]{2,1,0:T(8,128)(2,1)S(1)}, bf16[2,512,512]{2,1,0:T(8,128)(2,1)}, u32[]{:S(2)}, u32[]{:S(2)}) collective-permute-start(bf16[2,512,512]{2,1,0:T(8,128)(2,1)S(1)} %pad_maximum_fusion.1.refs_1_), channel_id=1, source_target_pairs={{0,16},{1,17},{2,18},{3,19},{4,20},{5,21},{6,22},{7,23},{8,24},{9,... | collective-permute-start | bytes 3145736 | tf_op jit(solution)/shard_map/ppermute | solution.py:38
  47.4 5.2 %collective-permute-done.5.refs_4_ = bf16[2,512,512]{2,1,0:T(8,128)(2,1)S(1)} collective-permute-done((bf16[2,512,512]{2,1,0:T(8,128)(2,1)S(1)}, bf16[2,512,512]{2,1,0:T(8,128)(2,1)S(1)}, u32[]{:S(2)}, u32[]{:S(2)}) %collective-permute-start.5) | collective-permute-done | bytes 1048608 | tf_op jit(solution)/shard_map/ppermute | solution.py:38
  52.6 2.0 %collective-permute-start.7 = (bf16[1,512,512]{2,1,0:T(8,128)(2,1)S(1)}, bf16[1,512,512]{2,1,0:T(8,128)(2,1)S(1)}, u32[]{:S(2)}, u32[]{:S(2)}) collective-permute-start(bf16[1,512,512]{2,1,0:T(8,128)(2,1)S(1)} %slice.74), channel_id=1, source_target_pairs={{0,16},{1,17},{2,18},{3,19},{4,20},{5,21},{6,22},{7,23},{8,24},{9,... | collective-permute-start | bytes 1572872 | tf_op jit(solution)/shard_map/ppermute | solution.py:38
  57.0 3.2 %collective-permute-start.8 = (bf16[1,512,512]{2,1,0:T(8,128)(2,1)S(1)}, bf16[1,512,512]{2,1,0:T(8,128)(2,1)S(1)}, u32[]{:S(2)}, u32[]{:S(2)}) collective-permute-start(bf16[1,512,512]{2,1,0:T(8,128)(2,1)S(1)} %slice.75), channel_id=1, source_target_pairs={{0,48},{1,49},{2,50},{3,51},{4,52},{5,53},{6,54},{7,55},{8,56},{9,... | collective-permute-start | bytes 1572872 | tf_op jit(solution)/shard_map/ppermute | solution.py:38
  60.2 3.7 %collective-permute-done.6.refs_5_ = bf16[2,512,512]{2,1,0:T(8,128)(2,1)} collective-permute-done((bf16[2,512,512]{2,1,0:T(8,128)(2,1)S(1)}, bf16[2,512,512]{2,1,0:T(8,128)(2,1)}, u32[]{:S(2)}, u32[]{:S(2)}) %collective-permute-start.6) | collective-permute-done | bytes 1048608 | tf_op jit(solution)/shard_map/ppermute | solution.py:38
  65.0 1.9 %collective-permute-start.9 = (bf16[1,512,512]{2,1,0:T(8,128)(2,1)S(1)}, bf16[1,512,512]{2,1,0:T(8,128)(2,1)S(1)}, u32[]{:S(2)}, u32[]{:S(2)}) collective-permute-start(bf16[1,512,512]{2,1,0:T(8,128)(2,1)S(1)} %slice.76), channel_id=1, source_target_pairs={{0,16},{1,17},{2,18},{3,19},{4,20},{5,21},{6,22},{7,23},{8,24},{9,... | collective-permute-start | bytes 1572872 | tf_op jit(solution)/shard_map/ppermute | solution.py:38
  68.2 4.4 %collective-permute-start.10 = (bf16[1,512,512]{2,1,0:T(8,128)(2,1)S(1)}, bf16[1,512,512]{2,1,0:T(8,128)(2,1)S(1)}, u32[]{:S(2)}, u32[]{:S(2)}) collective-permute-start(bf16[1,512,512]{2,1,0:T(8,128)(2,1)S(1)} %slice.77), channel_id=1, source_target_pairs={{0,48},{1,49},{2,50},{3,51},{4,52},{5,53},{6,54},{7,55},{8,56},{9,... | collective-permute-start | bytes 1572872 | tf_op jit(solution)/shard_map/ppermute | solution.py:38
  72.7 2.1 %shard_map.64 = (bf16[16,128,128]{2,1,0:T(8,128)(2,1)S(1)}, f32[3,128,512]{2,1,0:T(8,128)S(1)}) custom-call(s32[9]{0:T(128)S(1)} %stack.27.scal, f32[5,2048]{1,0:T(8,128)S(1)} %copy-done.18, bf16[128,2048]{1,0:T(8,128)(2,1)S(1)} %bitcast.19, bf16[2,512,512]{2,1,0:T(8,128)(2,1)S(1)} %pad_maximum_fusion.refs_0_, ...), custom_call_target="tpu_custom_call" | custom-call | flops 805306368 | bytes 6856704 | tf_op jit(solution)/shard_map/pallas_call | solution.py:285
  74.8 3.4 %collective-permute-done.9.refs_8_ = bf16[1,512,512]{2,1,0:T(8,128)(2,1)S(1)} collective-permute-done((bf16[1,512,512]{2,1,0:T(8,128)(2,1)S(1)}, bf16[1,512,512]{2,1,0:T(8,128)(2,1)S(1)}, u32[]{:S(2)}, u32[]{:S(2)}) %collective-permute-start.9) | collective-permute-done | bytes 524320 | tf_op jit(solution)/shard_map/ppermute | solution.py:38
  78.2 1.5 collective-permute-done.10.refs_9_
  79.8 2.1 %shard_map.65 = (f32[64,2048]{1,0:T(8,128)S(1)}, bf16[64,2048]{1,0:T(8,128)(2,1)S(1)}) custom-call(s32[9]{0:T(128)S(1)} %stack.27.scal, bf16[16,128,128]{2,1,0:T(8,128)(2,1)S(1)} %get-tuple-element.11.h3, f32[3,128,512]{2,1,0:T(8,128)S(1)} %get-tuple-element.12.early, bf16[2,512,512]{2,1,0:T(8,128)(2,1)S(1)} %pad_maximum_fusion.refs_0_, ...), custom_call_target="tpu_custom_call" | custom-call | flops 536870912 | bytes 9699328 | tf_op jit(solution)/shard_map/pallas_call | solution.py:285
  82.7 1.4 collective-permute-start.11
  85.4 1.3 add_convert_fusion.1
  90.2 2.0 %shard_map.66 = (f32[64,2048]{1,0:T(8,128)S(1)}, bf16[64,2048]{1,0:T(8,128)(2,1)S(1)}) custom-call(s32[9]{0:T(128)S(1)} %stack.27.scal, f32[5,2048]{1,0:T(8,128)S(1)} %copy-done.18, bf16[64,2048]{1,0:T(8,128)(2,1)S(1)} %collective-permute-done.12.in_mine.in1m, bf16[64,2048]{1,0:T(8,128)(2,1)S(1)} %collective-permute-done.13.in_other.in1o, ...), custom_call_target="tpu_custom_call" | custom-call | flops 1073741824 | bytes 8953856 | tf_op jit(solution)/shard_map/pallas_call | solution.py:285
  96.7 32.2 %collective-permute-done.14.in_mine.in3m = bf16[64,2048]{1,0:T(8,128)(2,1)} collective-permute-done((bf16[64,2048]{1,0:T(8,128)(2,1)S(1)}, bf16[64,2048]{1,0:T(8,128)(2,1)}, u32[]{:S(2)}, u32[]{:S(2)}) %collective-permute-start.14) | collective-permute-done | bytes 262176 | tf_op jit(solution)/shard_map/ppermute | solution.py:361
  128.8 2.7 %collective-permute-start.15 = (bf16[64,2048]{1,0:T(8,128)(2,1)}, bf16[64,2048]{1,0:T(8,128)(2,1)}, u32[]{:S(2)}, u32[]{:S(2)}) collective-permute-start(bf16[64,2048]{1,0:T(8,128)(2,1)} %collective-permute-done.14.in_mine.in3m), channel_id=1, source_target_pairs={{384,448},{448,384},{385,449},{449,385},{386,450},{450,386},{387,4... | collective-permute-start | bytes 786440 | tf_op jit(solution)/shard_map/ppermute | solution.py:333
  131.5 16.0 %collective-permute-done.18.mem_mine = bf16[64,2048]{1,0:T(8,128)(2,1)} collective-permute-done((bf16[64,2048]{1,0:T(8,128)(2,1)S(1)}, bf16[64,2048]{1,0:T(8,128)(2,1)}, u32[]{:S(2)}, u32[]{:S(2)}) %collective-permute-start.18) | collective-permute-done | bytes 262176 | tf_op jit(solution)/shard_map/ppermute | solution.py:373
  147.6 2.6 %collective-permute-start.19 = (bf16[64,2048]{1,0:T(8,128)(2,1)}, bf16[64,2048]{1,0:T(8,128)(2,1)}, u32[]{:S(2)}, u32[]{:S(2)}) collective-permute-start(bf16[64,2048]{1,0:T(8,128)(2,1)} %collective-permute-done.18.mem_mine), channel_id=1, source_target_pairs={{384,448},{448,384},{385,449},{449,385},{386,450},{450,386},{387,4... | collective-permute-start | bytes 786440 | tf_op jit(solution)/shard_map/ppermute | solution.py:333
  154.4 3.3 %shard_map.67.query = bf16[128,512]{1,0:T(8,128)(2,1)S(1)} custom-call(s32[9]{0:T(128)S(1)} %stack.27.scal, f32[5,2048]{1,0:T(8,128)S(1)} %copy-done.18, bf16[64,2048]{1,0:T(8,128)(2,1)} %collective-permute-done.14.in_mine.in3m, bf16[64,2048]{1,0:T(8,128)(2,1)} %collective-permute-done.15.in_other.in3o, bf16[2,512,512]{2,1,0:T(8,128)(2,1)S(1)} %pad_maximum_fusion.refs_0_, ...), custom_call_target="tpu_custom_call" | custom-call | flops 268435456 | bytes 8953856 | tf_op jit(solution)/shard_map/pallas_call | solution.py:285
  157.7 5.9 %shard_map.68.own = bf16[128,2048]{1,0:T(8,128)(2,1)S(1)} custom-call(s32[9]{0:T(128)S(1)} %stack.27.scal, bf16[128,512]{1,0:T(8,128)(2,1)S(1)} %shard_map.67.query, bf16[64,2048]{1,0:T(8,128)(2,1)} %collective-permute-done.18.mem_mine, bf16[64,2048]{1,0:T(8,128)(2,1)} %collective-permute-done.19.mem_other, ...), custom_call_target="tpu_custom_call" | custom-call | flops 805306368 | bytes 9043968 | tf_op jit(solution)/shard_map/pallas_call | solution.py:285
  163.6 1.4 collective-permute-start.20
  165.8 1.8 %collective-permute-done.20.got = bf16[128,2048]{1,0:T(8,128)(2,1)S(1)} collective-permute-done((bf16[128,2048]{1,0:T(8,128)(2,1)S(1)}, bf16[128,2048]{1,0:T(8,128)(2,1)S(1)}, u32[]{:S(2)}, u32[]{:S(2)}) %collective-permute-start.20) | collective-permute-done | bytes 524320 | tf_op jit(solution)/shard_map/ppermute | solution.py:389
  167.6 2.1 %shard_map.69 = bf16[128,2048]{1,0:T(8,128)(2,1)} custom-call(s32[9]{0:T(128)S(1)} %stack.27.scal, bf16[128,2048]{1,0:T(8,128)(2,1)S(1)} %bitcast.21, bf16[64,2048]{1,0:T(8,128)(2,1)S(1)} %collective-permute-done.12.in_mine.in1m, bf16[64,2048]{1,0:T(8,128)(2,1)S(1)} %copy-done.17, bf16[64,2048]{1,0:T(8,128)(2,1)} %collective-permute-done.14.in_mine.in3m, ...), custom_call_target="tpu_custom_call" | custom-call | bytes 3145728 | tf_op jit(solution)/shard_map/pallas_call | solution.py:285
  (100 shorter events, 21.5 us)
Async XLA Ops:
  17.7 11.7 %collective-permute-start.2 = (bf16[4,128,512]{2,1,0:T(8,128)(2,1)S(1)}, bf16[4,128,512]{2,1,0:T(8,128)(2,1)S(1)}, u32[]{:S(2)}, u32[]{:S(2)}) collective-permute-start(bf16[4,128,512]{2,1,0:T(8,128)(2,1)S(1)} %bitcast.27), channel_id=1, source_target_pairs={{0,8},{1,9},{2,10},{3,11},{4,12},{5,13},{6,14},{7,15},{8,0},{9,1},... | collective-permute-start | bytes 1572872 | tf_op jit(solution)/shard_map/ppermute | solution.py:38
  22.5 12.5 %collective-permute-start.1 = (bf16[4,128,512]{2,1,0:T(8,128)(2,1)S(1)}, bf16[4,128,512]{2,1,0:T(8,128)(2,1)S(1)}, u32[]{:S(2)}, u32[]{:S(2)}) collective-permute-start(bf16[4,128,512]{2,1,0:T(8,128)(2,1)S(1)} %bitcast.28), channel_id=1, source_target_pairs={{0,12},{1,13},{2,14},{3,15},{4,8},{5,9},{6,10},{7,11},{8,4},{9,5},... | collective-permute-start | bytes 1572872 | tf_op jit(solution)/shard_map/ppermute | solution.py:38
  25.2 10.2 %collective-permute-start = (bf16[4,128,512]{2,1,0:T(8,128)(2,1)S(1)}, bf16[4,128,512]{2,1,0:T(8,128)(2,1)S(1)}, u32[]{:S(2)}, u32[]{:S(2)}) collective-permute-start(bf16[4,128,512]{2,1,0:T(8,128)(2,1)S(1)} %bitcast.29), channel_id=1, source_target_pairs={{0,4},{1,5},{2,6},{3,7},{4,0},{5,1},{6,2},{7,3},{8,12},{9,13},{10,... | collective-permute-start | bytes 1572872 | tf_op jit(solution)/shard_map/ppermute | solution.py:38
  35.5 17.0 %collective-permute-start.5 = (bf16[2,512,512]{2,1,0:T(8,128)(2,1)S(1)}, bf16[2,512,512]{2,1,0:T(8,128)(2,1)S(1)}, u32[]{:S(2)}, u32[]{:S(2)}) collective-permute-start(bf16[2,512,512]{2,1,0:T(8,128)(2,1)S(1)} %pad_maximum_fusion.refs_0_), channel_id=1, source_target_pairs={{0,48},{1,49},{2,50},{3,51},{4,52},{5,53},{6,54},{7,55},{8,56},{9,... | collective-permute-start | bytes 3145736 | tf_op jit(solution)/shard_map/ppermute | solution.py:38
  39.9 15.9 %collective-permute-start.3 = (bf16[2,512,512]{2,1,0:T(8,128)(2,1)S(1)}, bf16[2,512,512]{2,1,0:T(8,128)(2,1)}, u32[]{:S(2)}, u32[]{:S(2)}) collective-permute-start(bf16[2,512,512]{2,1,0:T(8,128)(2,1)S(1)} %pad_maximum_fusion.refs_0_), channel_id=1, source_target_pairs={{0,16},{1,17},{2,18},{3,19},{4,20},{5,21},{6,22},{7,23},{8,24},{9,... | collective-permute-start | bytes 3145736 | tf_op jit(solution)/shard_map/ppermute | solution.py:38
  41.9 5.4 %copy-start.26 = (s32[2]{0:T(128)S(1)}, s32[2]{0:T(128)}, u32[]{:S(2)}) copy-start(s32[2]{0:T(128)} %param.10) | copy-start | bytes 28
  41.9 5.4 %copy-start.27 = (s32[2]{0:T(128)S(1)}, s32[2]{0:T(128)}, u32[]{:S(2)}) copy-start(s32[2]{0:T(128)} %param.11) | copy-start | bytes 28
  42.0 22.0 %collective-permute-start.6 = (bf16[2,512,512]{2,1,0:T(8,128)(2,1)S(1)}, bf16[2,512,512]{2,1,0:T(8,128)(2,1)}, u32[]{:S(2)}, u32[]{:S(2)}) collective-permute-start(bf16[2,512,512]{2,1,0:T(8,128)(2,1)S(1)} %pad_maximum_fusion.1.refs_1_), channel_id=1, source_target_pairs={{0,48},{1,49},{2,50},{3,51},{4,52},{5,53},{6,54},{7,55},{8,56},{9,... | collective-permute-start | bytes 3145736 | tf_op jit(solution)/shard_map/ppermute | solution.py:38
  44.7 22.4 %collective-permute-start.4 = (bf16[2,512,512]{2,1,0:T(8,128)(2,1)S(1)}, bf16[2,512,512]{2,1,0:T(8,128)(2,1)}, u32[]{:S(2)}, u32[]{:S(2)}) collective-permute-start(bf16[2,512,512]{2,1,0:T(8,128)(2,1)S(1)} %pad_maximum_fusion.1.refs_1_), channel_id=1, source_target_pairs={{0,16},{1,17},{2,18},{3,19},{4,20},{5,21},{6,22},{7,23},{8,24},{9,... | collective-permute-start | bytes 3145736 | tf_op jit(solution)/shard_map/ppermute | solution.py:38
  52.6 22.1 %collective-permute-start.7 = (bf16[1,512,512]{2,1,0:T(8,128)(2,1)S(1)}, bf16[1,512,512]{2,1,0:T(8,128)(2,1)S(1)}, u32[]{:S(2)}, u32[]{:S(2)}) collective-permute-start(bf16[1,512,512]{2,1,0:T(8,128)(2,1)S(1)} %slice.74), channel_id=1, source_target_pairs={{0,16},{1,17},{2,18},{3,19},{4,20},{5,21},{6,22},{7,23},{8,24},{9,... | collective-permute-start | bytes 1572872 | tf_op jit(solution)/shard_map/ppermute | solution.py:38
  57.0 15.6 %copy-start.24 = (bf16[2,64,2048]{2,1,0:T(8,128)(2,1)S(1)}, bf16[2,64,2048]{2,1,0:T(8,128)(2,1)}, u32[]{:S(2)}) copy-start(bf16[2,64,2048]{2,1,0:T(8,128)(2,1)} %param.6) | copy-start | bytes 1572868
  57.0 15.6 %copy-start.25 = (bf16[2,64,2048]{2,1,0:T(8,128)(2,1)S(1)}, bf16[2,64,2048]{2,1,0:T(8,128)(2,1)}, u32[]{:S(2)}) copy-start(bf16[2,64,2048]{2,1,0:T(8,128)(2,1)} %param.7) | copy-start | bytes 1572868
  57.0 17.8 %collective-permute-start.8 = (bf16[1,512,512]{2,1,0:T(8,128)(2,1)S(1)}, bf16[1,512,512]{2,1,0:T(8,128)(2,1)S(1)}, u32[]{:S(2)}, u32[]{:S(2)}) collective-permute-start(bf16[1,512,512]{2,1,0:T(8,128)(2,1)S(1)} %slice.75), channel_id=1, source_target_pairs={{0,48},{1,49},{2,50},{3,51},{4,52},{5,53},{6,54},{7,55},{8,56},{9,... | collective-permute-start | bytes 1572872 | tf_op jit(solution)/shard_map/ppermute | solution.py:38
  65.0 13.2 %collective-permute-start.9 = (bf16[1,512,512]{2,1,0:T(8,128)(2,1)S(1)}, bf16[1,512,512]{2,1,0:T(8,128)(2,1)S(1)}, u32[]{:S(2)}, u32[]{:S(2)}) collective-permute-start(bf16[1,512,512]{2,1,0:T(8,128)(2,1)S(1)} %slice.76), channel_id=1, source_target_pairs={{0,16},{1,17},{2,18},{3,19},{4,20},{5,21},{6,22},{7,23},{8,24},{9,... | collective-permute-start | bytes 1572872 | tf_op jit(solution)/shard_map/ppermute | solution.py:38
  68.2 4.5 %copy-start.18 = (f32[5,2048]{1,0:T(8,128)S(1)}, f32[5,2048]{1,0:T(8,128)}, u32[]{:S(2)}) copy-start(f32[5,2048]{1,0:T(8,128)} %gains.5) | copy-start | bytes 122884
  68.2 11.6 %collective-permute-start.10 = (bf16[1,512,512]{2,1,0:T(8,128)(2,1)S(1)}, bf16[1,512,512]{2,1,0:T(8,128)(2,1)S(1)}, u32[]{:S(2)}, u32[]{:S(2)}) collective-permute-start(bf16[1,512,512]{2,1,0:T(8,128)(2,1)S(1)} %slice.77), channel_id=1, source_target_pairs={{0,48},{1,49},{2,50},{3,51},{4,52},{5,53},{6,54},{7,55},{8,56},{9,... | collective-permute-start | bytes 1572872 | tf_op jit(solution)/shard_map/ppermute | solution.py:38
  74.8 7.1 %copy-start = (bf16[1,512,512]{2,1,0:T(8,128)(2,1)}, bf16[1,512,512]{2,1,0:T(8,128)(2,1)S(1)}, u32[]{:S(2)}) copy-start(bf16[1,512,512]{2,1,0:T(8,128)(2,1)S(1)} %collective-permute-done.7.refs_6_) | copy-start | bytes 1572868
  74.8 7.1 %copy-start.4 = (bf16[1,512,512]{2,1,0:T(8,128)(2,1)}, bf16[1,512,512]{2,1,0:T(8,128)(2,1)S(1)}, u32[]{:S(2)}) copy-start(bf16[1,512,512]{2,1,0:T(8,128)(2,1)S(1)} %collective-permute-done.8.refs_7_) | copy-start | bytes 1572868
  82.7 2.7 %collective-permute-start.11 = (bf16[64,2048]{1,0:T(8,128)(2,1)S(1)}, bf16[64,2048]{1,0:T(8,128)(2,1)}, u32[]{:S(2)}, u32[]{:S(2)}) collective-permute-start(bf16[64,2048]{1,0:T(8,128)(2,1)S(1)} %get-tuple-element.14), channel_id=1, source_target_pairs={{0,64},{64,0},{256,320},{320,256},{1,65},{65,1},{257,321},{321,257... | collective-permute-start | bytes 786440 | tf_op jit(solution)/shard_map/ppermute | solution.py:333
  86.7 6.2 %copy-start.22 = (bf16[64,2048]{1,0:T(8,128)(2,1)}, bf16[64,2048]{1,0:T(8,128)(2,1)S(1)}, u32[]{:S(2)}) copy-start(bf16[64,2048]{1,0:T(8,128)(2,1)S(1)} %add_convert_fusion.1) | copy-start | bytes 786436
  86.7 0.7 collective-permute-start.12
  87.4 0.7 collective-permute-start.13
  92.2 2.0 %collective-permute-start.16 = (bf16[64,2048]{1,0:T(8,128)(2,1)S(1)}, bf16[64,2048]{1,0:T(8,128)(2,1)S(1)}, u32[]{:S(2)}, u32[]{:S(2)}) collective-permute-start(bf16[64,2048]{1,0:T(8,128)(2,1)S(1)} %get-tuple-element.16), channel_id=1, source_target_pairs={{128,192},{192,128},{129,193},{193,129},{130,194},{194,130},{131,1... | collective-permute-start | bytes 786440 | tf_op jit(solution)/shard_map/ppermute | solution.py:333
  92.9 35.9 %collective-permute-start.14 = (bf16[64,2048]{1,0:T(8,128)(2,1)S(1)}, bf16[64,2048]{1,0:T(8,128)(2,1)}, u32[]{:S(2)}, u32[]{:S(2)}) collective-permute-start(bf16[64,2048]{1,0:T(8,128)(2,1)S(1)} %add_convert_fusion.1), channel_id=1, source_target_pairs={{256,384},{257,385},{258,386},{259,387},{260,388},{261,389},{262,3... | collective-permute-start | bytes 786440 | tf_op jit(solution)/shard_map/ppermute | solution.py:361
  95.4 52.2 %collective-permute-start.18 = (bf16[64,2048]{1,0:T(8,128)(2,1)S(1)}, bf16[64,2048]{1,0:T(8,128)(2,1)}, u32[]{:S(2)}, u32[]{:S(2)}) collective-permute-start(bf16[64,2048]{1,0:T(8,128)(2,1)S(1)} %fusion.2), channel_id=1, source_target_pairs={{128,384},{129,385},{130,386},{131,387},{132,388},{133,389},{134,3... | collective-permute-start | bytes 786440 | tf_op jit(solution)/shard_map/ppermute | solution.py:373
  128.8 21.4 %collective-permute-start.15 = (bf16[64,2048]{1,0:T(8,128)(2,1)}, bf16[64,2048]{1,0:T(8,128)(2,1)}, u32[]{:S(2)}, u32[]{:S(2)}) collective-permute-start(bf16[64,2048]{1,0:T(8,128)(2,1)} %collective-permute-done.14.in_mine.in3m), channel_id=1, source_target_pairs={{384,448},{448,384},{385,449},{449,385},{386,450},{450,386},{387,4... | collective-permute-start | bytes 786440 | tf_op jit(solution)/shard_map/ppermute | solution.py:333
  147.6 10.2 %collective-permute-start.19 = (bf16[64,2048]{1,0:T(8,128)(2,1)}, bf16[64,2048]{1,0:T(8,128)(2,1)}, u32[]{:S(2)}, u32[]{:S(2)}) collective-permute-start(bf16[64,2048]{1,0:T(8,128)(2,1)} %collective-permute-done.18.mem_mine), channel_id=1, source_target_pairs={{384,448},{448,384},{385,449},{449,385},{386,450},{450,386},{387,4... | collective-permute-start | bytes 786440 | tf_op jit(solution)/shard_map/ppermute | solution.py:333
  157.7 7.4 %copy-start.21 = (bf16[64,2048]{1,0:T(8,128)(2,1)S(1)}, bf16[64,2048]{1,0:T(8,128)(2,1)}, u32[]{:S(2)}) copy-start(bf16[64,2048]{1,0:T(8,128)(2,1)} %copy-done.20) | copy-start | bytes 786436
  157.7 7.4 %copy-start.23 = (bf16[64,2048]{1,0:T(8,128)(2,1)S(1)}, bf16[64,2048]{1,0:T(8,128)(2,1)}, u32[]{:S(2)}) copy-start(bf16[64,2048]{1,0:T(8,128)(2,1)} %copy-done.22) | copy-start | bytes 786436
  157.7 9.9 %copy-start.17 = (bf16[64,2048]{1,0:T(8,128)(2,1)S(1)}, bf16[64,2048]{1,0:T(8,128)(2,1)}, u32[]{:S(2)}) copy-start(bf16[64,2048]{1,0:T(8,128)(2,1)} %copy-done.16) | copy-start | bytes 786436
  163.6 3.9 %collective-permute-start.20 = (bf16[128,2048]{1,0:T(8,128)(2,1)S(1)}, bf16[128,2048]{1,0:T(8,128)(2,1)S(1)}, u32[]{:S(2)}, u32[]{:S(2)}) collective-permute-start(bf16[128,2048]{1,0:T(8,128)(2,1)S(1)} %shard_map.68.own), channel_id=1, source_target_pairs={{384,448},{385,449},{386,450},{387,451},{388,452},{389,453},{390,4... | collective-permute-start | bytes 1572872 | tf_op jit(solution)/shard_map/ppermute | solution.py:389
  165.1 0.7 collective-permute-start.17
  (17 other events, 35.2 us)

commit v7 on v5

--- a/solution.py
+++ b/solution.py
@@ -52,10 +52,30 @@
 
 
 def weight(pieces, turn, which):
-    chunk, place_in = divmod(which, 2)
+    chunk, at = divmod(which, 2)
     if turn == FAR:
-        return pieces[6 + which][0]
-    return pieces[2 * TURNS.index(turn) + chunk][place_in]
+        return pieces[8].at[at] if chunk else pieces[6 + which].at[0]
+    return pieces[2 * TURNS.index(turn) + chunk].at[at]
+
+
+class Fetched:
+    def __init__(self, pieces, wanted, space, sems):
+        self.space = space
+        self.copies = {}
+        self.slots = {}
+        for slot, key in enumerate(wanted):
+            copy = pltpu.make_async_copy(weight(pieces, *key), space.at[slot], sems.at[slot])
+            copy.start()
+            self.copies[key], self.slots[key] = copy, slot
+
+    def take(self, turn, which):
+        self.copies[turn, which].wait()
+        return self.space[self.slots[turn, which]]
+
+
+def wanted(spots, which, out=True):
+    keys = [(turn, m) for turn in spots for m in which]
+    return keys + [(turn, 3) for turn in TURNS] * out
 
 
 def put_norm(scal, gains, streams, h3):
@@ -74,12 +94,12 @@
             m3[i, part * rows:(part + 1) * rows, :] = ref[:, i * 128:(i + 1) * 128]
 
 
-def project(scal, h3, pieces, turns, which, totals=None):
+def project(scal, h3, fetched, turns, which, totals=None):
     totals = [None] * len(which) if totals is None else list(totals)
     for turn in turns:
         h = jnp.concatenate([h3[block_at(scal, turn, d)] for d in TURNS], axis=1)
         for i, m in enumerate(which):
-            term = dot(h, weight(pieces, turn, m))
+            term = dot(h, fetched.take(turn, m))
             totals[i] = term if totals[i] is None else totals[i] + term
     return totals
 
@@ -106,10 +126,10 @@
     return jnp.concatenate(mixed, axis=1)
 
 
-def project_out(scal, mixed, pieces, t3, out_mine, out_other):
+def project_out(scal, mixed, fetched, t3, out_mine, out_other):
     rows = out_mine.shape[0]
     for turn in TURNS:
-        t = dot_t(mixed, weight(pieces, turn, 3))
+        t = dot_t(mixed, fetched.take(turn, 3))
         for j, d in enumerate(TURNS):
             t3[block_at(scal, turn, d)] = t[:, j * 128:(j + 1) * 128]
     for i in range(16):
@@ -118,71 +138,88 @@
         out_other[:, at] = t3[i, rows:, :].astype(out_other.dtype)
 
 
+EARLY = wanted(TURNS[:3], (0, 1, 2), False)
+FIRST = wanted(TURNS[3:], (0, 1, 2))
+SECOND = wanted(TURNS, (0, 1, 2))
+QUERY = wanted(TURNS, (0,), False)
+THIRD = wanted(TURNS, (1, 2))
+
+
 def early_kernel(scal, gains, mine, other, *refs):
-    pieces, (h3, q, k, v) = refs[:6], refs[6:]
+    pieces, (h3, q, k, v, space, sems) = refs[:6], refs[6:]
 
     @pl.when(lax.rem(scal[2], 2) == 0)
     def _():
+        fetched = Fetched(pieces, EARLY, space, sems)
         put_norm(scal, gains, (mine, other), h3)
-        q[...], k[...], v[...] = project(scal, h3, pieces, TURNS[:3], (0, 1, 2))
+        q[...], k[...], v[...] = project(scal, h3, fetched, TURNS[:3], (0, 1, 2))
 
 
 def first_kernel(scal, h3, q, k, v, *refs):
-    pieces, (out_mine, out_other, t3) = refs[:10], refs[10:]
+    pieces, (out_mine, out_other, t3, space, sems) = refs[:9], refs[9:]
 
     @pl.when(lax.rem(scal[2], 2) == 0)
     def _():
+        fetched = Fetched(pieces, FIRST, space, sems)
         done = (q[...], k[...], v[...])
-        done = project(scal, h3, pieces, TURNS[3:], (0, 1, 2), done)
-        project_out(scal, attend(scal, *done), pieces, t3, out_mine, out_other)
+        done = project(scal, h3, fetched, TURNS[3:], (0, 1, 2), done)
+        project_out(scal, attend(scal, *done), fetched, t3, out_mine, out_other)
 
 
 def second_kernel(scal, gains, mine, other, *refs):
-    pieces, (out_mine, out_other, h3, t3) = refs[:10], refs[10:]
+    pieces, (out_mine, out_other, h3, t3, space, sems) = refs[:9], refs[9:]
 
     @pl.when(scal[2] == 1)
     def _():
+        fetched = Fetched(pieces, SECOND, space, sems)
         put_norm(scal, gains, (mine, other), h3)
-        done = project(scal, h3, pieces, TURNS, (0, 1, 2))
-        project_out(scal, attend(scal, *done), pieces, t3, out_mine, out_other)
+        done = project(scal, h3, fetched, TURNS, (0, 1, 2))
+        project_out(scal, attend(scal, *done), fetched, t3, out_mine, out_other)
 
 
 def query_kernel(scal, gains, mine, other, *refs):
-    pieces, (q, h3) = refs[:10], refs[10:]
+    pieces, (q, h3, space, sems) = refs[:9], refs[9:]
 
     @pl.when(scal[2] == 3)
     def _():
+        fetched = Fetched(pieces, QUERY, space, sems)
         put_norm(scal, gains, (mine, other), h3)
-        q[...] = project(scal, h3, pieces, TURNS, (0,))[0].astype(BF16)
+        q[...] = project(scal, h3, fetched, TURNS, (0,))[0].astype(BF16)
 
 
 def third_kernel(scal, q, mem_mine, mem_other, *refs):
-    pieces, (out, m3, t3) = refs[:10], refs[10:]
+    pieces, (out, m3, t3, space, sems) = refs[:9], refs[9:]
 
     @pl.when(scal[2] == 3)
     def _():
         rows = mem_mine.shape[0]
+        fetched = Fetched(pieces, THIRD, space, sems)
         put_memory((mem_mine, mem_other), m3)
-        k, v = project(scal, m3, pieces, TURNS, (1, 2))
+        k, v = project(scal, m3, fetched, TURNS, (1, 2))
         mixed = attend(scal, q[...], k, v)
-        project_out(scal, mixed, pieces, t3, out.at[:rows], out.at[rows:])
+        project_out(scal, mixed, fetched, t3, out.at[:rows], out.at[rows:])
 
 
 VMEM = pl.BlockSpec(memory_space=pltpu.VMEM)
 SMEM = pl.BlockSpec(memory_space=pltpu.SMEM)
-
-
-def call(kernel, scal, operands, outs, scratch=(), flops=0):
-    size = sum(a.size * a.dtype.itemsize for a in operands)
+ANY = pl.BlockSpec(memory_space=pl.ANY)
+
+
+def call(kernel, scal, operands, outs, scratch=(), pieces=(), fetches=0, flops=0):
+    size = sum(a.size * a.dtype.itemsize for a in [*operands, *pieces])
+    shapes = [pltpu.VMEM(shape, kind) for shape, kind in scratch]
+    if fetches:
+        shapes.append(pltpu.VMEM((fetches,) + pieces[0].shape[1:], BF16))
+        shapes.append(pltpu.SemaphoreType.DMA((fetches,)))
     return pl.pallas_call(
         kernel,
         out_shape=outs,
-        in_specs=[SMEM] + [VMEM] * len(operands),
+        in_specs=[SMEM] + [VMEM] * len(operands) + [ANY] * len(pieces),
         out_specs=jax.tree.map(lambda _: VMEM, outs),
-        scratch_shapes=[pltpu.VMEM(shape, kind) for shape, kind in scratch],
-        compiler_params=pltpu.CompilerParams(vmem_limit_bytes=12 * 1024 * 1024),
+        scratch_shapes=shapes,
+        compiler_params=pltpu.CompilerParams(vmem_limit_bytes=16 * 1024 * 1024),
         cost_estimate=pl.CostEstimate(flops=flops, bytes_accessed=size, transcendentals=0),
-    )(scal, *operands)
+    )(scal, *operands, *pieces)
 
 
 def finish_kernel(scal, mine, other, in1m, in1o, in3m, in3o, early_m, early_o, own, got, out):
@@ -236,9 +273,8 @@
     chunks = [jnp.concatenate([a[i:i + pair] for a in near], axis=1) for i in (0, pair)]
     by1 = [exchange(a, True, 1) for a in chunks]
     by3 = [exchange(a, True, 3) for a in chunks]
-    far = []
-    for a, b in zip(by1, by3):
-        far += [exchange(b[:1], True, 1), exchange(a[1:], True, 3)]
+    across = exchange(chunks[1], True, FAR)
+    far = [exchange(by3[0][:1], True, 1), exchange(by1[0][1:], True, 3), across]
     return [*chunks, *by1, *by3], far
 
 
@@ -289,13 +325,22 @@
     started = call(
         early_kernel,
         scal,
-        [norm_gains, mine, other, *near],
+        [norm_gains, mine, other],
         (jax.ShapeDtypeStruct(blocks, BF16), total, total, total),
         (),
+        near,
+        len(EARLY),
         3 * work,
     )
     kept, sent = call(
-        first_kernel, scal, [*started, *pieces], halves, [(blocks, F32)], 2 * work
+        first_kernel,
+        scal,
+        [*started],
+        halves,
+        [(blocks, F32)],
+        pieces,
+        len(FIRST),
+        2 * work,
     )
     first = added(mine, kept + swapped(sent, (0, 2)).astype(F32), live).astype(BF16)
     in1 = lax.ppermute(first, "zh", [(0, 1)])
@@ -304,9 +349,11 @@
     kept, sent = call(
         second_kernel,
         scal,
-        [norm_gains, in1, in1_other, *pieces],
+        [norm_gains, in1, in1_other],
         halves,
         [(blocks, BF16), (blocks, F32)],
+        pieces,
+        len(SECOND),
         4 * work,
     )
     second = added(in1, kept + swapped(sent, (1,)).astype(F32), live).astype(BF16)
@@ -316,15 +363,24 @@
     early_other = lax.ppermute(early, SECTION, [(0, 1), (2, 3), (4, 5)])
     in3_other = swapped(in3, (3,))
     query = call(
-        query_kernel, scal, [norm_gains, in3, in3_other, *pieces], narrow, [(blocks, BF16)], work
+        query_kernel,
+        scal,
+        [norm_gains, in3, in3_other],
+        narrow,
+        [(blocks, BF16)],
+        pieces,
+        len(QUERY),
+        work,
     )
     mem_other = swapped(mem, (3,))
     own = call(
         third_kernel,
         scal,
-        [query, mem, mem_other, *pieces],
+        [query, mem, mem_other],
         wide,
         [(blocks, BF16), (blocks, F32)],
+        pieces,
+        len(THIRD),
         3 * work,
     )
     got = lax.ppermute(own, SECTION, [(6, 7)])

time: 162 us -> 163 us (level)
  waiting for transfers between devices: 63.7 us -> 70.8 us
  Pallas kernels: 17.8 us -> 12.6 us
  local copies, waits for them, and re-layouts: 12.8 us -> 9.14 us
  starting transfers between devices: 46.1 us -> 49.1 us
    ppermute x11 -> x10, waiting for transfers between devices: 15.1 us -> 25.3 us  [exchange(): return lax.ppermute(array, AXES, pairs)]
    ppermute x5, starting transfers between devices: 7.43 us -> 13 us  [swapped(): return lax.ppermute(array, SECTION, pairs)]
    pallas_call x6, Pallas kernels: 17.8 us -> 12.6 us  [call(): pl.pallas_call(kernel, out_shape=outs, in_specs=[SMEM] + [VMEM] * len(ope...]
    ppermute x1, waiting for transfers between devices: 37.5 us -> 33.2 us  [on_device(): in3 = lax.ppermute(first, 'zh', [(2, 3)])]
    slice x4 -> x2, local copies, waits for them, and re-layouts: 6.47 us -> 2.71 us  [gather(): far = [exchange(by3[0][:1], True, 1), exchange(by1[0][1:], True, 3), across]]
    ppermute x11 -> x10, starting transfers between devices: 33.4 us -> 30.8 us  [exchange(): return lax.ppermute(array, AXES, pairs)]
  transfers between devices with their start and end apart: 21 -> 20, of which waited for: 10 -> 9; matrix products, arithmetic and copies ran while one was open for 9% -> 6% of each run, Pallas kernels for 3% -> 2%
where the time goes in v7:
time: 163 us; the launch traced here: 162 us
  waiting for transfers between devices  70.8 us (43%)
  starting transfers between devices  49.1 us (30%)
  blocking collectives  16.6 us (10%)
  Pallas kernels  12.6 us (8%)
  local copies, waits for them, and re-layouts  9.14 us (6%)
  other arithmetic  3.25 us (2%)
    ppermute x1, waiting for transfers between devices, on_device(): in3 = lax.ppermute(first, 'zh', [(2, 3)])  33.2 us
    ppermute x10, starting transfers between devices, exchange(): return lax.ppermute(array, AXES, pairs)  30.8 us
    ppermute x10, waiting for transfers between devices, exchange(): return lax.ppermute(array, AXES, pairs)  25.3 us
    all_to_all x1, blocking collectives, gather(): got = lax.all_to_all(sent, ('core', 'zl'), 0, 0, tiled=True)  16.6 us
    ppermute x5, starting transfers between devices, swapped(): return lax.ppermute(array, SECTION, pairs)  13 us
    pallas_call x6, Pallas kernels, call(): pl.pallas_call(kernel, out_shape=outs, in_specs=[SMEM] + [VMEM] * len(ope...  12.6 us
    ppermute x1, waiting for transfers between devices, on_device(): mem = lax.ppermute(memory, 'zh', [(1, 3)])  10.5 us
  transfers between devices with their start and end apart: 20, of which 9 were waited for; matrix products, arithmetic and copies ran while one was open for 6% of the time, Pallas kernels for 2%

profile of v7, /device:TPU:481, one launch (start us, length us, event | category | flops | bytes accessed | tf_op | source)
XLA Modules:
  0.0 162.0 jit_solution(12610019261169055896)
XLA Ops:
  0.0 1.0 reshape_squeeze.3
  1.1 16.6 %all_to_all.5 = bf16[8,2,32,512]{3,2,1,0:T(8,128)(2,1)S(1)} all-to-all(bf16[8,2,32,512]{3,2,1,0:T(8,128)(2,1)S(1)} %bitcast.24), channel_id=1, replica_groups=mesh['zh'=4,'core'=2,'y'=4,'x'=4,'zl'=4] {'core','zl'}, dimensions={0} | all-to-all | bytes 1048576 | tf_op jit(solution)/shard_map/all_to_all | solution.py:269
  17.7 4.8 %collective-permute-start.2 = (bf16[4,128,512]{2,1,0:T(8,128)(2,1)S(1)}, bf16[4,128,512]{2,1,0:T(8,128)(2,1)S(1)}, u32[]{:S(2)}, u32[]{:S(2)}) collective-permute-start(bf16[4,128,512]{2,1,0:T(8,128)(2,1)S(1)} %bitcast.27), channel_id=1, source_target_pairs={{0,8},{1,9},{2,10},{3,11},{4,12},{5,13},{6,14},{7,15},{8,0},{9,1},... | collective-permute-start | bytes 1572872 | tf_op jit(solution)/shard_map/ppermute | solution.py:32
  22.5 2.7 %collective-permute-start.1 = (bf16[4,128,512]{2,1,0:T(8,128)(2,1)S(1)}, bf16[4,128,512]{2,1,0:T(8,128)(2,1)S(1)}, u32[]{:S(2)}, u32[]{:S(2)}) collective-permute-start(bf16[4,128,512]{2,1,0:T(8,128)(2,1)S(1)} %bitcast.28), channel_id=1, source_target_pairs={{0,12},{1,13},{2,14},{3,15},{4,8},{5,9},{6,10},{7,11},{8,4},{9,5},... | collective-permute-start | bytes 1572872 | tf_op jit(solution)/shard_map/ppermute | solution.py:32
  25.2 1.9 %collective-permute-start = (bf16[4,128,512]{2,1,0:T(8,128)(2,1)S(1)}, bf16[4,128,512]{2,1,0:T(8,128)(2,1)S(1)}, u32[]{:S(2)}, u32[]{:S(2)}) collective-permute-start(bf16[4,128,512]{2,1,0:T(8,128)(2,1)S(1)} %bitcast.29), channel_id=1, source_target_pairs={{0,4},{1,5},{2,6},{3,7},{4,0},{5,1},{6,2},{7,3},{8,12},{9,13},{10,... | collective-permute-start | bytes 1572872 | tf_op jit(solution)/shard_map/ppermute | solution.py:32
  27.2 2.2 %collective-permute-done.2 = bf16[4,128,512]{2,1,0:T(8,128)(2,1)S(1)} collective-permute-done((bf16[4,128,512]{2,1,0:T(8,128)(2,1)S(1)}, bf16[4,128,512]{2,1,0:T(8,128)(2,1)S(1)}, u32[]{:S(2)}, u32[]{:S(2)}) %collective-permute-start.2) | collective-permute-done | bytes 524320 | tf_op jit(solution)/shard_map/ppermute | solution.py:32
  29.4 5.6 %collective-permute-done.1 = bf16[4,128,512]{2,1,0:T(8,128)(2,1)S(1)} collective-permute-done((bf16[4,128,512]{2,1,0:T(8,128)(2,1)S(1)}, bf16[4,128,512]{2,1,0:T(8,128)(2,1)S(1)}, u32[]{:S(2)}, u32[]{:S(2)}) %collective-permute-start.1) | collective-permute-done | bytes 524320 | tf_op jit(solution)/shard_map/ppermute | solution.py:32
  35.5 4.4 %collective-permute-start.5 = (bf16[2,512,512]{2,1,0:T(8,128)(2,1)S(1)}, bf16[2,512,512]{2,1,0:T(8,128)(2,1)S(1)}, u32[]{:S(2)}, u32[]{:S(2)}) collective-permute-start(bf16[2,512,512]{2,1,0:T(8,128)(2,1)S(1)} %pad_maximum_fusion.refs_0_), channel_id=1, source_target_pairs={{0,48},{1,49},{2,50},{3,51},{4,52},{5,53},{6,54},{7,55},{8,56},{9,... | collective-permute-start | bytes 3145736 | tf_op jit(solution)/shard_map/ppermute | solution.py:32
  39.9 1.9 %collective-permute-start.3 = (bf16[2,512,512]{2,1,0:T(8,128)(2,1)S(1)}, bf16[2,512,512]{2,1,0:T(8,128)(2,1)}, u32[]{:S(2)}, u32[]{:S(2)}) collective-permute-start(bf16[2,512,512]{2,1,0:T(8,128)(2,1)S(1)} %pad_maximum_fusion.refs_0_), channel_id=1, source_target_pairs={{0,16},{1,17},{2,18},{3,19},{4,20},{5,21},{6,22},{7,23},{8,24},{9,... | collective-permute-start | bytes 3145736 | tf_op jit(solution)/shard_map/ppermute | solution.py:32
  42.0 2.7 %collective-permute-start.6 = (bf16[2,512,512]{2,1,0:T(8,128)(2,1)S(1)}, bf16[2,512,512]{2,1,0:T(8,128)(2,1)}, u32[]{:S(2)}, u32[]{:S(2)}) collective-permute-start(bf16[2,512,512]{2,1,0:T(8,128)(2,1)S(1)} %pad_maximum_fusion.1.refs_1_), channel_id=1, source_target_pairs={{0,48},{1,49},{2,50},{3,51},{4,52},{5,53},{6,54},{7,55},{8,56},{9,... | collective-permute-start | bytes 3145736 | tf_op jit(solution)/shard_map/ppermute | solution.py:32
  44.7 2.6 %collective-permute-start.4 = (bf16[2,512,512]{2,1,0:T(8,128)(2,1)S(1)}, bf16[2,512,512]{2,1,0:T(8,128)(2,1)}, u32[]{:S(2)}, u32[]{:S(2)}) collective-permute-start(bf16[2,512,512]{2,1,0:T(8,128)(2,1)S(1)} %pad_maximum_fusion.1.refs_1_), channel_id=1, source_target_pairs={{0,16},{1,17},{2,18},{3,19},{4,20},{5,21},{6,22},{7,23},{8,24},{9,... | collective-permute-start | bytes 3145736 | tf_op jit(solution)/shard_map/ppermute | solution.py:32
  47.3 4.3 %collective-permute-start.9 = (bf16[2,512,512]{2,1,0:T(8,128)(2,1)S(1)}, bf16[2,512,512]{2,1,0:T(8,128)(2,1)}, u32[]{:S(2)}, u32[]{:S(2)}) collective-permute-start(bf16[2,512,512]{2,1,0:T(8,128)(2,1)S(1)} %pad_maximum_fusion.1.refs_1_), channel_id=1, source_target_pairs={{0,32},{1,33},{2,34},{3,35},{4,36},{5,37},{6,38},{7,39},{8,40},{9,... | collective-permute-start | bytes 3145736 | tf_op jit(solution)/shard_map/ppermute | solution.py:32
  51.6 1.9 %broadcast_select_fusion = bf16[2,64,2048]{2,1,0:T(8,128)(2,1)} fusion(bf16[2,64,2048]{2,1,0:T(8,128)(2,1)} %param.6, bf16[2,64,2048]{2,1,0:T(8,128)(2,1)} %param.7, pred[]{:T(512)S(6)} %lt.26), kind=kLoop, calls=%fused_computation.9 | loop fusion | flops 262144 | bytes 1572865 | tf_op jit(solution)/shard_map/jit(_where)/select_n | solution.py:306
  54.3 2.3 %collective-permute-start.7 = (bf16[1,512,512]{2,1,0:T(8,128)(2,1)}, bf16[1,512,512]{2,1,0:T(8,128)(2,1)}, u32[]{:S(2)}, u32[]{:S(2)}) collective-permute-start(bf16[1,512,512]{2,1,0:T(8,128)(2,1)} %slice.60), channel_id=1, source_target_pairs={{0,16},{1,17},{2,18},{3,19},{4,20},{5,21},{6,22},{7,23},{8,24},{9,... | collective-permute-start | bytes 1572872 | tf_op jit(solution)/shard_map/ppermute | solution.py:32
  56.6 1.9 %slice.61 = bf16[1,512,512]{2,1,0:T(8,128)(2,1)} slice(bf16[2,512,512]{2,1,0:T(8,128)(2,1)} %collective-permute-done.3.refs_2_), slice={[1:2], [0:512], [0:512]} | slice | bytes 1048576 | tf_op jit(solution)/shard_map/slice | solution.py:277
  58.5 3.2 %collective-permute-start.8 = (bf16[1,512,512]{2,1,0:T(8,128)(2,1)}, bf16[1,512,512]{2,1,0:T(8,128)(2,1)}, u32[]{:S(2)}, u32[]{:S(2)}) collective-permute-start(bf16[1,512,512]{2,1,0:T(8,128)(2,1)} %slice.61), channel_id=1, source_target_pairs={{0,48},{1,49},{2,50},{3,51},{4,52},{5,53},{6,54},{7,55},{8,56},{9,... | collective-permute-start | bytes 1572872 | tf_op jit(solution)/shard_map/ppermute | solution.py:32
  62.5 2.6 %stack.27.scal = s32[9]{0:T(128)S(1)} concatenate(s32[1]{0:T(128)} %bitcast, s32[1]{0:T(128)} %bitcast.1, s32[1]{0:T(128)} %bitcast.2, s32[1]{0:T(128)} %bitcast.3, s32[1]{0:T(128)} %get-tuple-element.39, s32[1]{0:T(128)} %get-tuple-element.40, s32[1]{0:T(128)} %bitcast.4, s32[1]{0:T(128)} %get-tuple-element.36, s32[1]{0:T(128)} %get-tuple-element.35), dimensions={0} | concatenate | bytes 72 | tf_op jit(solution)/shard_map/stack | solution.py:289
  65.1 1.1 dynamic-slice_bitcast_fusion
  66.2 0.9 collective-permute-done.4.refs_3_
  67.8 10.5 %collective-permute-done.9.refs_8_ = bf16[2,512,512]{2,1,0:T(8,128)(2,1)} collective-permute-done((bf16[2,512,512]{2,1,0:T(8,128)(2,1)S(1)}, bf16[2,512,512]{2,1,0:T(8,128)(2,1)}, u32[]{:S(2)}, u32[]{:S(2)}) %collective-permute-start.9) | collective-permute-done | bytes 1048608 | tf_op jit(solution)/shard_map/ppermute | solution.py:32
  78.3 5.7 %collective-permute-done.7.refs_6_ = bf16[1,512,512]{2,1,0:T(8,128)(2,1)} collective-permute-done((bf16[1,512,512]{2,1,0:T(8,128)(2,1)}, bf16[1,512,512]{2,1,0:T(8,128)(2,1)}, u32[]{:S(2)}, u32[]{:S(2)}) %collective-permute-start.7) | collective-permute-done | bytes 524320 | tf_op jit(solution)/shard_map/ppermute | solution.py:32
  88.9 1.3 collective-permute-start.13
  91.4 1.3 collective-permute-start.17
  92.7 33.2 %collective-permute-done.13.mine.in3m = bf16[64,2048]{1,0:T(8,128)(2,1)} collective-permute-done((bf16[64,2048]{1,0:T(8,128)(2,1)S(1)}, bf16[64,2048]{1,0:T(8,128)(2,1)}, u32[]{:S(2)}, u32[]{:S(2)}) %collective-permute-start.13) | collective-permute-done | bytes 262176 | tf_op jit(solution)/shard_map/ppermute | solution.py:347
  125.9 8.4 %collective-permute-start.14 = (bf16[64,2048]{1,0:T(8,128)(2,1)}, bf16[64,2048]{1,0:T(8,128)(2,1)}, u32[]{:S(2)}, u32[]{:S(2)}) collective-permute-start(bf16[64,2048]{1,0:T(8,128)(2,1)} %collective-permute-done.13.mine.in3m), channel_id=1, source_target_pairs={{384,448},{448,384},{385,449},{449,385},{386,450},{450,386},{387,4... | collective-permute-start | bytes 786440 | tf_op jit(solution)/shard_map/ppermute | solution.py:314
  134.3 10.5 %collective-permute-done.17.mem_mine = bf16[64,2048]{1,0:T(8,128)(2,1)} collective-permute-done((bf16[64,2048]{1,0:T(8,128)(2,1)S(1)}, bf16[64,2048]{1,0:T(8,128)(2,1)}, u32[]{:S(2)}, u32[]{:S(2)}) %collective-permute-start.17) | collective-permute-done | bytes 262176 | tf_op jit(solution)/shard_map/ppermute | solution.py:361
  144.8 2.6 %collective-permute-start.18 = (bf16[64,2048]{1,0:T(8,128)(2,1)}, bf16[64,2048]{1,0:T(8,128)(2,1)}, u32[]{:S(2)}, u32[]{:S(2)}) collective-permute-start(bf16[64,2048]{1,0:T(8,128)(2,1)} %collective-permute-done.17.mem_mine), channel_id=1, source_target_pairs={{384,448},{448,384},{385,449},{449,385},{386,450},{450,386},{387,4... | collective-permute-start | bytes 786440 | tf_op jit(solution)/shard_map/ppermute | solution.py:314
  147.4 2.7 %shard_map.67.q = bf16[128,512]{1,0:T(8,128)(2,1)S(1)} custom-call(s32[9]{0:T(128)S(1)} %stack.27.scal, f32[5,2048]{1,0:T(8,128)S(1)} %copy-done.6, bf16[64,2048]{1,0:T(8,128)(2,1)} %collective-permute-done.13.mine.in3m, bf16[64,2048]{1,0:T(8,128)(2,1)} %collective-permute-done.14.other.in3o, bf16[2,512,512]{2,1,0:T(8,128)(2,1)S(1)} %pad_maximum_fusion.refs_0_, ...), custom_call_target="tpu_custom_call" | custom-call | flops 268435456 | bytes 8953856 | tf_op jit(solution)/shard_map/pallas_call | solution.py:214
  150.2 5.8 %shard_map.68.own = bf16[128,2048]{1,0:T(8,128)(2,1)S(1)} custom-call(s32[9]{0:T(128)S(1)} %stack.27.scal, bf16[128,512]{1,0:T(8,128)(2,1)S(1)} %shard_map.67.q, bf16[64,2048]{1,0:T(8,128)(2,1)} %collective-permute-done.17.mem_mine, bf16[64,2048]{1,0:T(8,128)(2,1)} %collective-permute-done.18.mem_other, bf16[2,512,512]{2,1,0:T(8,128)(2,1)S(1)} %pad_maximum_fusion.refs_0_, ...), custom_call_target="tpu_custom_call" | custom-call | flops 805306368 | bytes 9043968 | tf_op jit(solution)/shard_map/pallas_call | solution.py:214
  156.1 1.3 collective-permute-start.19
  158.1 1.8 %collective-permute-done.19.got = bf16[128,2048]{1,0:T(8,128)(2,1)S(1)} collective-permute-done((bf16[128,2048]{1,0:T(8,128)(2,1)S(1)}, bf16[128,2048]{1,0:T(8,128)(2,1)S(1)}, u32[]{:S(2)}, u32[]{:S(2)}) %collective-permute-start.19) | collective-permute-done | bytes 524320 | tf_op jit(solution)/shard_map/ppermute | solution.py:386
  159.9 2.1 %shard_map.69 = bf16[2,64,2048]{2,1,0:T(8,128)(2,1)} custom-call(s32[9]{0:T(128)S(1)} %stack.27.scal, bf16[64,2048]{1,0:T(8,128)(2,1)S(1)} %get-tuple-element.32.mine, bf16[64,2048]{1,0:T(8,128)(2,1)S(1)} %copy-done.1, bf16[64,2048]{1,0:T(8,128)(2,1)S(1)} %copy-done.3, bf16[64,2048]{1,0:T(8,128)(2,1)S(1)} %copy-done.5, ...), custom_call_target="tpu_custom_call" | custom-call | bytes 3145728 | tf_op jit(solution)/shard_map/pallas_call | solution.py:214
  (67 shorter events, 9.6 us)
Async XLA Ops:
  17.7 11.7 %collective-permute-start.2 = (bf16[4,128,512]{2,1,0:T(8,128)(2,1)S(1)}, bf16[4,128,512]{2,1,0:T(8,128)(2,1)S(1)}, u32[]{:S(2)}, u32[]{:S(2)}) collective-permute-start(bf16[4,128,512]{2,1,0:T(8,128)(2,1)S(1)} %bitcast.27), channel_id=1, source_target_pairs={{0,8},{1,9},{2,10},{3,11},{4,12},{5,13},{6,14},{7,15},{8,0},{9,1},... | collective-permute-start | bytes 1572872 | tf_op jit(solution)/shard_map/ppermute | solution.py:32
  22.5 12.5 %collective-permute-start.1 = (bf16[4,128,512]{2,1,0:T(8,128)(2,1)S(1)}, bf16[4,128,512]{2,1,0:T(8,128)(2,1)S(1)}, u32[]{:S(2)}, u32[]{:S(2)}) collective-permute-start(bf16[4,128,512]{2,1,0:T(8,128)(2,1)S(1)} %bitcast.28), channel_id=1, source_target_pairs={{0,12},{1,13},{2,14},{3,15},{4,8},{5,9},{6,10},{7,11},{8,4},{9,5},... | collective-permute-start | bytes 1572872 | tf_op jit(solution)/shard_map/ppermute | solution.py:32
  25.2 10.2 %collective-permute-start = (bf16[4,128,512]{2,1,0:T(8,128)(2,1)S(1)}, bf16[4,128,512]{2,1,0:T(8,128)(2,1)S(1)}, u32[]{:S(2)}, u32[]{:S(2)}) collective-permute-start(bf16[4,128,512]{2,1,0:T(8,128)(2,1)S(1)} %bitcast.29), channel_id=1, source_target_pairs={{0,4},{1,5},{2,6},{3,7},{4,0},{5,1},{6,2},{7,3},{8,12},{9,13},{10,... | collective-permute-start | bytes 1572872 | tf_op jit(solution)/shard_map/ppermute | solution.py:32
  35.5 18.0 %collective-permute-start.5 = (bf16[2,512,512]{2,1,0:T(8,128)(2,1)S(1)}, bf16[2,512,512]{2,1,0:T(8,128)(2,1)S(1)}, u32[]{:S(2)}, u32[]{:S(2)}) collective-permute-start(bf16[2,512,512]{2,1,0:T(8,128)(2,1)S(1)} %pad_maximum_fusion.refs_0_), channel_id=1, source_target_pairs={{0,48},{1,49},{2,50},{3,51},{4,52},{5,53},{6,54},{7,55},{8,56},{9,... | collective-permute-start | bytes 3145736 | tf_op jit(solution)/shard_map/ppermute | solution.py:32
  39.9 16.7 %collective-permute-start.3 = (bf16[2,512,512]{2,1,0:T(8,128)(2,1)S(1)}, bf16[2,512,512]{2,1,0:T(8,128)(2,1)}, u32[]{:S(2)}, u32[]{:S(2)}) collective-permute-start(bf16[2,512,512]{2,1,0:T(8,128)(2,1)S(1)} %pad_maximum_fusion.refs_0_), channel_id=1, source_target_pairs={{0,16},{1,17},{2,18},{3,19},{4,20},{5,21},{6,22},{7,23},{8,24},{9,... | collective-permute-start | bytes 3145736 | tf_op jit(solution)/shard_map/ppermute | solution.py:32
  42.0 24.2 %collective-permute-start.6 = (bf16[2,512,512]{2,1,0:T(8,128)(2,1)S(1)}, bf16[2,512,512]{2,1,0:T(8,128)(2,1)}, u32[]{:S(2)}, u32[]{:S(2)}) collective-permute-start(bf16[2,512,512]{2,1,0:T(8,128)(2,1)S(1)} %pad_maximum_fusion.1.refs_1_), channel_id=1, source_target_pairs={{0,48},{1,49},{2,50},{3,51},{4,52},{5,53},{6,54},{7,55},{8,56},{9,... | collective-permute-start | bytes 3145736 | tf_op jit(solution)/shard_map/ppermute | solution.py:32
  44.7 22.4 %collective-permute-start.4 = (bf16[2,512,512]{2,1,0:T(8,128)(2,1)S(1)}, bf16[2,512,512]{2,1,0:T(8,128)(2,1)}, u32[]{:S(2)}, u32[]{:S(2)}) collective-permute-start(bf16[2,512,512]{2,1,0:T(8,128)(2,1)S(1)} %pad_maximum_fusion.1.refs_1_), channel_id=1, source_target_pairs={{0,16},{1,17},{2,18},{3,19},{4,20},{5,21},{6,22},{7,23},{8,24},{9,... | collective-permute-start | bytes 3145736 | tf_op jit(solution)/shard_map/ppermute | solution.py:32
  47.3 31.0 %collective-permute-start.9 = (bf16[2,512,512]{2,1,0:T(8,128)(2,1)S(1)}, bf16[2,512,512]{2,1,0:T(8,128)(2,1)}, u32[]{:S(2)}, u32[]{:S(2)}) collective-permute-start(bf16[2,512,512]{2,1,0:T(8,128)(2,1)S(1)} %pad_maximum_fusion.1.refs_1_), channel_id=1, source_target_pairs={{0,32},{1,33},{2,34},{3,35},{4,36},{5,37},{6,38},{7,39},{8,40},{9,... | collective-permute-start | bytes 3145736 | tf_op jit(solution)/shard_map/ppermute | solution.py:32
  53.5 8.3 %copy-start.11 = (s32[2]{0:T(128)S(1)}, s32[2]{0:T(128)}, u32[]{:S(2)}) copy-start(s32[2]{0:T(128)} %param.10) | copy-start | bytes 28
  53.5 8.3 %copy-start.12 = (s32[2]{0:T(128)S(1)}, s32[2]{0:T(128)}, u32[]{:S(2)}) copy-start(s32[2]{0:T(128)} %param.11) | copy-start | bytes 28
  54.3 12.8 %copy-start.6 = (f32[5,2048]{1,0:T(8,128)S(1)}, f32[5,2048]{1,0:T(8,128)}, u32[]{:S(2)}) copy-start(f32[5,2048]{1,0:T(8,128)} %gains.5) | copy-start | bytes 122884
  54.3 29.7 %collective-permute-start.7 = (bf16[1,512,512]{2,1,0:T(8,128)(2,1)}, bf16[1,512,512]{2,1,0:T(8,128)(2,1)}, u32[]{:S(2)}, u32[]{:S(2)}) collective-permute-start(bf16[1,512,512]{2,1,0:T(8,128)(2,1)} %slice.60), channel_id=1, source_target_pairs={{0,16},{1,17},{2,18},{3,19},{4,20},{5,21},{6,22},{7,23},{8,24},{9,... | collective-permute-start | bytes 1572872 | tf_op jit(solution)/shard_map/ppermute | solution.py:32
  58.5 25.5 %collective-permute-start.8 = (bf16[1,512,512]{2,1,0:T(8,128)(2,1)}, bf16[1,512,512]{2,1,0:T(8,128)(2,1)}, u32[]{:S(2)}, u32[]{:S(2)}) collective-permute-start(bf16[1,512,512]{2,1,0:T(8,128)(2,1)} %slice.61), channel_id=1, source_target_pairs={{0,48},{1,49},{2,50},{3,51},{4,52},{5,53},{6,54},{7,55},{8,56},{9,... | collective-permute-start | bytes 1572872 | tf_op jit(solution)/shard_map/ppermute | solution.py:32
  66.2 1.6 copy-start
  84.6 1.3 collective-permute-start.10
  86.1 2.8 %copy-start.9 = (bf16[64,2048]{1,0:T(8,128)(2,1)}, bf16[64,2048]{1,0:T(8,128)(2,1)S(1)}, u32[]{:S(2)}) copy-start(bf16[64,2048]{1,0:T(8,128)(2,1)S(1)} %add_convert_fusion.1) | copy-start | bytes 786436
  86.1 0.7 collective-permute-start.11
  86.8 3.5 %copy-start.2 = (bf16[64,2048]{1,0:T(8,128)(2,1)}, bf16[64,2048]{1,0:T(8,128)(2,1)S(1)}, u32[]{:S(2)}) copy-start(bf16[64,2048]{1,0:T(8,128)(2,1)S(1)} %collective-permute-done.11.mine.in1m) | copy-start | bytes 786436
  86.8 0.7 collective-permute-start.12
  88.2 2.0 %collective-permute-start.15 = (bf16[64,2048]{1,0:T(8,128)(2,1)S(1)}, bf16[64,2048]{1,0:T(8,128)(2,1)S(1)}, u32[]{:S(2)}, u32[]{:S(2)}) collective-permute-start(bf16[64,2048]{1,0:T(8,128)(2,1)S(1)} %get-tuple-element.20), channel_id=1, source_target_pairs={{128,192},{192,128},{129,193},{193,129},{130,194},{194,130},{131,1... | collective-permute-start | bytes 786440 | tf_op jit(solution)/shard_map/ppermute | solution.py:314
  88.9 36.9 %collective-permute-start.13 = (bf16[64,2048]{1,0:T(8,128)(2,1)S(1)}, bf16[64,2048]{1,0:T(8,128)(2,1)}, u32[]{:S(2)}, u32[]{:S(2)}) collective-permute-start(bf16[64,2048]{1,0:T(8,128)(2,1)S(1)} %add_convert_fusion.1), channel_id=1, source_target_pairs={{256,384},{257,385},{258,386},{259,387},{260,388},{261,389},{262,3... | collective-permute-start | bytes 786440 | tf_op jit(solution)/shard_map/ppermute | solution.py:347
  90.5 0.7 copy-start.7
  91.4 53.4 %collective-permute-start.17 = (bf16[64,2048]{1,0:T(8,128)(2,1)S(1)}, bf16[64,2048]{1,0:T(8,128)(2,1)}, u32[]{:S(2)}, u32[]{:S(2)}) collective-permute-start(bf16[64,2048]{1,0:T(8,128)(2,1)S(1)} %fusion.2), channel_id=1, source_target_pairs={{128,384},{129,385},{130,386},{131,387},{132,388},{133,389},{134,3... | collective-permute-start | bytes 786440 | tf_op jit(solution)/shard_map/ppermute | solution.py:361
  125.9 21.6 %collective-permute-start.14 = (bf16[64,2048]{1,0:T(8,128)(2,1)}, bf16[64,2048]{1,0:T(8,128)(2,1)}, u32[]{:S(2)}, u32[]{:S(2)}) collective-permute-start(bf16[64,2048]{1,0:T(8,128)(2,1)} %collective-permute-done.13.mine.in3m), channel_id=1, source_target_pairs={{384,448},{448,384},{385,449},{449,385},{386,450},{450,386},{387,4... | collective-permute-start | bytes 786440 | tf_op jit(solution)/shard_map/ppermute | solution.py:314
  144.8 5.4 %collective-permute-start.18 = (bf16[64,2048]{1,0:T(8,128)(2,1)}, bf16[64,2048]{1,0:T(8,128)(2,1)}, u32[]{:S(2)}, u32[]{:S(2)}) collective-permute-start(bf16[64,2048]{1,0:T(8,128)(2,1)} %collective-permute-done.17.mem_mine), channel_id=1, source_target_pairs={{384,448},{448,384},{385,449},{449,385},{386,450},{450,386},{387,4... | collective-permute-start | bytes 786440 | tf_op jit(solution)/shard_map/ppermute | solution.py:314
  150.2 7.2 %copy-start.8 = (bf16[64,2048]{1,0:T(8,128)(2,1)S(1)}, bf16[64,2048]{1,0:T(8,128)(2,1)}, u32[]{:S(2)}) copy-start(bf16[64,2048]{1,0:T(8,128)(2,1)} %copy-done.7) | copy-start | bytes 786436
  150.2 7.2 %copy-start.10 = (bf16[64,2048]{1,0:T(8,128)(2,1)S(1)}, bf16[64,2048]{1,0:T(8,128)(2,1)}, u32[]{:S(2)}) copy-start(bf16[64,2048]{1,0:T(8,128)(2,1)} %copy-done.9) | copy-start | bytes 786436
  150.2 9.7 %copy-start.1 = (bf16[64,2048]{1,0:T(8,128)(2,1)S(1)}, bf16[64,2048]{1,0:T(8,128)(2,1)}, u32[]{:S(2)}) copy-start(bf16[64,2048]{1,0:T(8,128)(2,1)} %copy-done) | copy-start | bytes 786436
  150.2 9.7 %copy-start.3 = (bf16[64,2048]{1,0:T(8,128)(2,1)S(1)}, bf16[64,2048]{1,0:T(8,128)(2,1)}, u32[]{:S(2)}) copy-start(bf16[64,2048]{1,0:T(8,128)(2,1)} %copy-done.2) | copy-start | bytes 786436
  150.2 9.7 %copy-start.5 = (bf16[64,2048]{1,0:T(8,128)(2,1)S(1)}, bf16[64,2048]{1,0:T(8,128)(2,1)}, u32[]{:S(2)}) copy-start(bf16[64,2048]{1,0:T(8,128)(2,1)} %copy-done.4) | copy-start | bytes 786436
  156.1 3.8 %collective-permute-start.19 = (bf16[128,2048]{1,0:T(8,128)(2,1)S(1)}, bf16[128,2048]{1,0:T(8,128)(2,1)S(1)}, u32[]{:S(2)}, u32[]{:S(2)}) collective-permute-start(bf16[128,2048]{1,0:T(8,128)(2,1)S(1)} %shard_map.68.own), channel_id=1, source_target_pairs={{384,448},{385,449},{386,450},{387,451},{388,452},{389,453},{390,4... | collective-permute-start | bytes 1572872 | tf_op jit(solution)/shard_map/ppermute | solution.py:386
  157.4 0.7 collective-permute-start.16
  (1 other events, 0.7 us)

commit v8 on v5

v8 whole, which is shorter than its diff:
```python
import functools
import itertools

import jax
import jax.numpy as jnp
from jax import lax
from jax.experimental import pallas as pl
from jax.experimental.pallas import tpu as pltpu
from jax.sharding import Mesh, PartitionSpec as P

HEAD_DIM = 128
SIDE = 4
TURNS = (0, 1, 3, 2)
FAR = 2
EVEN = (0, 2)
ODD = (1, 3)
AXES = ("zh", "core", "y", "x", "zl")
DP = ("y", "x", "zl")
SECTION = ("zh", "core")
F32 = jnp.float32
BF16 = jnp.bfloat16


def place(zh, core, y, x, zl):
    return (((zh * 2 + core) * SIDE + y) * SIDE + x) * SIDE + zl


def moved(array, cubes, move):
    pairs = []
    for zh, core, y, x, zl in itertools.product(cubes, *map(range, (2, SIDE, SIDE, SIDE))):
        pairs.append((place(zh, core, y, x, zl), place(zh, core, *move(core, y, x), zl)))
    return lax.ppermute(array, AXES, pairs)


def exchange(array, outer, by, cubes=range(SIDE)):
    return moved(
        array, cubes, lambda core, y, x: (y ^ by, x) if outer == (core == 0) else (y, x ^ by)
    )


def beside(array):
    return moved(array, EVEN, lambda core, y, x: (y, x ^ 1))


def dot(a, b):
    return jnp.dot(a, b, preferred_element_type=F32)


def dot_t(a, b):
    return lax.dot_general(a, b, (((1,), (1,)), ((), ())), preferred_element_type=F32)


def rms(values, gain):
    mean_square = jnp.mean(values * values, axis=-1, keepdims=True)
    return (values * lax.rsqrt(mean_square + 1e-06) * gain).astype(BF16)


def block_at(scal, outer, inner):
    back = scal[6] == 1
    dy, dx = jnp.where(back, inner, outer), jnp.where(back, outer, inner)
    return lax.bitwise_xor(scal[1], dy) * SIDE + lax.bitwise_xor(scal[0], dx)


class Fetched:
    def __init__(self, sources, space, sems):
        self.space = space
        self.copies = []
        for slot, source in enumerate(sources):
            self.copies.append(pltpu.make_async_copy(source, space.at[slot], sems.at[slot]))
            self.copies[-1].start()

    def take(self, slot):
        self.copies[slot].wait()
        return self.space[slot]


def put_norm(scal, gains, streams, h3):
    rows = streams[0].shape[0]
    gain = gains[pl.ds(scal[2], 1), :]
    for part, ref in enumerate(streams):
        h = rms(ref[...].astype(F32), gain)
        for i in range(16):
            h3[i, part * rows:(part + 1) * rows, :] = h[:, i * 128:(i + 1) * 128]


def put_memory(mem, m3):
    rows = mem[0].shape[0]
    for part, ref in enumerate(mem):
        for i in range(16):
            m3[i, part * rows:(part + 1) * rows, :] = ref[:, i * 128:(i + 1) * 128]


def project(scal, h3, pieces, which, space, sems):
    keys = [(i, m, n) for i in range(SIDE) for m in which for n in range(len(pieces))]
    fetched = Fetched([pieces[n][i].at[m] for i, m, n in keys], space, sems)

    def run():
        totals = {}
        for slot, (i, m, n) in enumerate(keys):
            if (m, n) == (which[0], 0):
                h = jnp.concatenate([h3[block_at(scal, TURNS[i], d)] for d in TURNS], axis=1)
            term = dot(h, fetched.take(slot))
            totals[m, n] = totals[m, n] + term if i else term
        sides = range(len(pieces))
        return [jnp.concatenate([totals[m, n] for n in sides], axis=1).astype(BF16) for m in which]

    return run


def mask(scal, first_limit, second_limit, count):
    rows = count // 2
    r = lax.broadcasted_iota(jnp.int32, (count, count), 0)
    c = lax.broadcasted_iota(jnp.int32, (count, count), 1)
    first = c < rows
    live = (r < rows) == first
    key_at = jnp.where(first, c, c - rows).astype(F32)
    live = live & (key_at < jnp.where(first, first_limit, second_limit))
    return live & ((c <= r) | (scal[3] == 0))


def attend(live, q, k, v):
    mixed = []
    for head in range(q.shape[1] // HEAD_DIM):
        at = slice(head * HEAD_DIM, (head + 1) * HEAD_DIM)
        s = dot_t(q[:, at], k[:, at]) * HEAD_DIM ** (-0.5)
        s = jnp.where(live, s, -1e30)
        e = jnp.exp(s - jnp.max(s, axis=-1, keepdims=True))
        p = (e / jnp.sum(e, axis=-1, keepdims=True)).astype(BF16)
        mixed.append(dot(p, v[:, at]).astype(BF16))
    return jnp.concatenate(mixed, axis=1)


def local_mask(scal, count):
    return mask(scal, scal[4].astype(F32), scal[5].astype(F32), count)


def project_out(scal, mixed, fetched, t3):
    for i, turn in enumerate(TURNS):
        t = dot_t(mixed, fetched.take(i))
        for j, d in enumerate(TURNS):
            t3[block_at(scal, turn, d)] = t[:, j * 128:(j + 1) * 128]


def put_out(t3, first, second, out_mine, out_other):
    for i in range(16):
        at = slice(i * 128, (i + 1) * 128)
        out_mine[:, at] = t3[i, first, :].astype(out_mine.dtype)
        out_other[:, at] = t3[i, second, :].astype(out_other.dtype)


def norm_kernel(scal, gains, own, got, h3, limits):
    @pl.when(lax.rem(scal[2], 2) == 0)
    def _():
        gain = gains[pl.ds(scal[2], 1), :]
        count = h3.shape[1] // 2
        for part, ref in enumerate((own, got)):
            for at in range(0, count, 64):
                h = rms(ref[at:at + 64, :].astype(F32), gain)
                to = part * count + at
                for i in range(16):
                    h3[i, to:to + 64, :] = h[:, i * 128:(i + 1) * 128]
            limits[part] = ref[count:, :128].astype(F32)


def first_kernel(scal, h3, limits, *refs):
    pieces, (own, sent, space, sems) = refs[:SIDE], refs[SIDE:]

    @pl.when(lax.rem(scal[2], 2) == 0)
    def _():
        q, k, v = project(scal, h3, [pieces], (0, 1, 2), space, sems)()
        count = own.shape[0]
        for part, out in enumerate((own, sent)):
            at = slice(part * count, (part + 1) * count)
            live = mask(scal, limits[part, 0:1, :], limits[part, 1:2, :], count)
            out[...] = attend(live, q[at], k[at], v[at])


def first_out_kernel(scal, own, got, *refs):
    pieces, (out_mine, out_other, mixed, t3, space, sems) = refs[:SIDE], refs[SIDE:]

    @pl.when(lax.rem(scal[2], 2) == 0)
    def _():
        fetched = Fetched([ref.at[0] for ref in pieces], space, sems)
        half = own.shape[1]
        side = lax.rem(scal[0], 2)
        mixed[:, pl.ds(pl.multiple_of(side * half, half), half)] = own[...]
        mixed[:, pl.ds(pl.multiple_of((1 - side) * half, half), half)] = got[...]
        project_out(scal, mixed[...], fetched, t3)
        rows = out_mine.shape[0]
        here = pl.ds(pl.multiple_of(scal[6] * rows, rows), rows)
        there = pl.ds(pl.multiple_of((1 - scal[6]) * rows, rows), rows)
        put_out(t3, here, there, out_mine, out_other)


def split(refs):
    return [refs[:SIDE], refs[SIDE:2 * SIDE]], refs[2 * SIDE:3 * SIDE], refs[3 * SIDE:]


def second_kernel(scal, gains, mine, other, *refs):
    pieces, outs, rest = split(refs)
    out_mine, out_other, h3, t3, space, sems, out_space, out_sems = rest

    @pl.when(scal[2] == 1)
    def _():
        run = project(scal, h3, pieces, (0, 1, 2), space, sems)
        fetched = Fetched([ref.at[0] for ref in outs], out_space, out_sems)
        put_norm(scal, gains, (mine, other), h3)
        rows = mine.shape[0]
        mixed = attend(local_mask(scal, 2 * rows), *run())
        project_out(scal, mixed, fetched, t3)
        put_out(t3, slice(0, rows), slice(rows, 2 * rows), out_mine, out_other)


def query_kernel(scal, gains, mine, other, *refs):
    pieces, _, (q, h3, space, sems) = split(refs)

    @pl.when(scal[2] == 3)
    def _():
        run = project(scal, h3, pieces, (0,), space, sems)
        put_norm(scal, gains, (mine, other), h3)
        q[...] = run()[0]


def third_kernel(scal, q, mem_mine, mem_other, *refs):
    pieces, outs, (out, m3, t3, space, sems, out_space, out_sems) = split(refs)

    @pl.when(scal[2] == 3)
    def _():
        rows = mem_mine.shape[0]
        run = project(scal, m3, pieces, (1, 2), space, sems)
        fetched = Fetched([ref.at[0] for ref in outs], out_space, out_sems)
        put_memory((mem_mine, mem_other), m3)
        k, v = run()
        mixed = attend(local_mask(scal, 2 * rows), q[...], k, v)
        project_out(scal, mixed, fetched, t3)
        put_out(t3, slice(0, rows), slice(rows, 2 * rows), out.at[:rows], out.at[rows:])


VMEM = pl.BlockSpec(memory_space=pltpu.VMEM)
SMEM = pl.BlockSpec(memory_space=pltpu.SMEM)
ANY = pl.BlockSpec(memory_space=pl.ANY)


def call(kernel, scal, operands, outs, scratch=(), pieces=(), fetches=(), flops=0):
    size = sum(a.size * a.dtype.itemsize for a in [*operands, *pieces])
    shapes = [pltpu.VMEM(shape, kind) for shape, kind in scratch]
    for shape in fetches:
        shapes += [pltpu.VMEM(shape, BF16), pltpu.SemaphoreType.DMA(shape[:1])]
    return pl.pallas_call(
        kernel,
        out_shape=outs,
        in_specs=[SMEM] + [VMEM] * len(operands) + [ANY] * len(pieces),
        out_specs=jax.tree.map(lambda _: VMEM, outs),
        scratch_shapes=shapes,
        compiler_params=pltpu.CompilerParams(vmem_limit_bytes=16 * 1024 * 1024),
        cost_estimate=pl.CostEstimate(flops=flops, bytes_accessed=size, transcendentals=0),
    )(scal, *operands, *pieces)


def finish_kernel(scal, mine, other, in1m, in1o, in3m, in3o, early_m, early_o, own, got, out):
    rows = mine.shape[0]
    cube, core = scal[2], scal[6]
    even = (cube == 0) | (cube == 2)

    def put(doc0, doc1):
        out[0] = doc0[...]
        out[1] = doc1[...]

    @pl.when((core == 0) & even)
    def _():
        put(mine, other)

    @pl.when((core == 0) & (cube == 1))
    def _():
        put(in1m, in1o)

    @pl.when((core == 0) & (cube == 3))
    def _():
        put(in3m, in3o)

    @pl.when((core == 1) & (cube != 3))
    def _():
        put(early_o, early_m)

    @pl.when((core == 1) & (cube == 3))
    def _():
        at = lax.broadcasted_iota(jnp.int32, mine.shape, 0)
        low, high = slice(0, rows), slice(rows, 2 * rows)
        for slot, base, a, b, live in ((1, in3m, low, high, scal[7]), (0, in3o, high, low, scal[8])):
            term = own[a, :].astype(F32) + got[b, :].astype(F32)
            term = jnp.where(at < live, term, 0.0)
            out[slot] = (base[...].astype(F32) + term).astype(BF16)


def turns(array, outer, cubes=range(SIDE)):
    return [array] + [exchange(array, outer, turn, cubes) for turn in TURNS[1:]]


def gather(weights):
    pair, depth, width = weights.shape[1:]
    halves = weights[0].reshape(pair, depth, 2, width // 2).transpose(2, 0, 1, 3)
    sent = jnp.broadcast_to(halves[:, None], (2, SIDE) + halves.shape[1:])
    sent = sent.reshape((2 * SIDE,) + halves.shape[1:])
    got = lax.all_to_all(sent, ("core", "zl"), 0, 0, tiled=True)
    got = got.reshape(2, SIDE, pair, depth, width // 2).transpose(0, 2, 1, 3, 4)
    got = got.reshape(2 * pair, SIDE * depth, width // 2)
    block = jnp.concatenate(turns(got, False), axis=1)
    zh, core, x = (lax.axis_index(name) for name in ("zh", "core", "x"))
    side = jnp.where(zh % 2 == 0, x % 2, 0)
    across = jnp.where((zh % 2 == 0) & (core == 1), 1 - side, side)
    half = width // 4

    def columns(at):
        return lax.dynamic_slice(block, (0, 0, at * half), (3,) + block.shape[1:2] + (half,))

    kept, sent = columns(side), columns(across)
    first = [kept, exchange(sent, True, 1), exchange(sent, True, 3), exchange(kept, True, FAR)]
    outs = turns(block[3:], True)
    second = turns(block[:3, :, half:], True, ODD)
    return first, second, outs


def on_device(encoder_embed, decoder_embed, section_weights, norm_gains, input_lengths, target_lengths):
    zh, core = lax.axis_index("zh"), lax.axis_index("core")
    y, x = lax.axis_index("y"), lax.axis_index("x")
    rows = encoder_embed.shape[1]
    encoder = zh < 2
    causal = zh == 2
    key_lengths = jnp.where(causal, target_lengths, input_lengths)
    row_lengths = jnp.where(encoder, input_lengths, target_lengths)
    scal = jnp.stack(
        [
            x,
            y,
            zh,
            causal.astype(jnp.int32),
            key_lengths[core],
            key_lengths[1 - core],
            core,
            row_lengths[core],
            row_lengths[1 - core],
        ]
    ).astype(jnp.int32)
    live = (jnp.arange(rows, dtype=jnp.int32) < row_lengths[core])[:, None]

    parts_a, parts_b, parts_o = gather(section_weights)
    pieces = [*parts_a, *parts_b, *parts_o]
    source = jnp.where(encoder, encoder_embed, decoder_embed)
    mine, other = source[core], source[1 - core]

    def added(stream, term, alive):
        return stream.astype(F32) + jnp.where(alive, term, 0.0)

    def swapped(array, cubes=range(SIDE)):
        pairs = [(2 * c + i, 2 * c + 1 - i) for c in cubes for i in range(2)]
        return lax.ppermute(array, SECTION, pairs)

    count, width = 2 * rows, mine.shape[1]
    tile = parts_a[0].shape[1:]
    square = parts_o[0].shape[1:]
    half = square[1]
    blocks = (16, count, 128)
    work = 2 * count * width * half
    wide = jax.ShapeDtypeStruct((count, width), BF16)
    halves = tuple(jax.ShapeDtypeStruct((rows, width), kind) for kind in (F32, BF16))
    narrow = jax.ShapeDtypeStruct((count, half), BF16)
    quarter = jax.ShapeDtypeStruct((count, half // 2), BF16)
    out_fetch = (SIDE,) + square

    limits = jnp.broadcast_to(key_lengths.astype(BF16)[:, None], (2, width))
    limits = jnp.concatenate([limits, jnp.zeros((14, width), BF16)], axis=0)
    shared = jnp.concatenate([source.reshape(count, width), limits], axis=0)
    h3, limits = call(
        norm_kernel,
        scal,
        [norm_gains, shared, beside(shared)],
        (
            jax.ShapeDtypeStruct((16, 2 * count, 128), BF16),
            jax.ShapeDtypeStruct((2, 16, 128), F32),
        ),
    )
    mixed, mixed_sent = call(
        first_kernel, scal, [h3, limits], (quarter, quarter), (), parts_a, [(12,) + tile], 3 * work
    )
    kept, sent = call(
        first_out_kernel,
        scal,
        [mixed, beside(mixed_sent)],
        halves,
        [((count, half), BF16), (blocks, F32)],
        parts_o,
        [out_fetch],
        work,
    )
    first = added(mine, kept + swapped(sent, (0, 2)).astype(F32), live).astype(BF16)
    in1 = lax.ppermute(first, "zh", [(0, 1)])
    in3 = lax.ppermute(first, "zh", [(2, 3)])
    in1_other = swapped(in1, (1,))
    kept, sent = call(
        second_kernel,
        scal,
        [norm_gains, in1, in1_other],
        halves,
        [(blocks, BF16), (blocks, F32)],
        pieces,
        [(24,) + tile, out_fetch],
        4 * work,
    )
    second = added(in1, kept + swapped(sent, (1,)).astype(F32), live).astype(BF16)
    memory = rms(second.astype(F32), norm_gains[4:5])
    mem = lax.ppermute(memory, "zh", [(1, 3)])
    early = jnp.where(zh == 1, second, first)
    early_other = lax.ppermute(early, SECTION, [(0, 1), (2, 3), (4, 5)])
    in3_other = swapped(in3, (3,))
    query = call(
        query_kernel,
        scal,
        [norm_gains, in3, in3_other],
        narrow,
        [(blocks, BF16)],
        pieces,
        [(8,) + tile],
        work,
    )
    mem_other = swapped(mem, (3,))
    own = call(
        third_kernel,
        scal,
        [query, mem, mem_other],
        wide,
        [(blocks, BF16), (blocks, F32)],
        pieces,
        [(16,) + tile, out_fetch],
        3 * work,
    )
    got = lax.ppermute(own, SECTION, [(6, 7)])
    parts = [mine, other, in1, in1_other, in3, in3_other, early, early_other, own, got]
    out = call(finish_kernel, scal, parts, jax.ShapeDtypeStruct((2, rows, width), BF16))
    return out[None]


def solution(mesh):
    fine = Mesh(mesh.devices.reshape(SIDE, 2, SIDE, SIDE, SIDE), AXES)
    in_specs = (
        P(DP, None, None),
        P(DP, None, None),
        P(SECTION, None, DP, None),
        P(),
        P(DP),
        P(DP),
    )
    out_specs = P(SECTION, DP, None, None)
    return jax.shard_map(
        on_device, mesh=fine, in_specs=in_specs, out_specs=out_specs, check_vma=False
    )
```

time: 162 us -> 171 us (1.056)
  starting transfers between devices: 46.1 us -> 63.5 us
  blocking collectives: 16.6 us -> 0 us
  waiting for transfers between devices: 63.7 us -> 73.7 us
  Pallas kernels: 17.8 us -> 14.7 us
    all_to_all x1 -> x0, blocking collectives: 16.6 us -> none  [gather(): got = lax.all_to_all(sent, ('core', 'zl'), 0, 0, tiled=True)]
    ppermute x11 -> x14, waiting for transfers between devices: 15.1 us -> 30.8 us  [moved(): return lax.ppermute(array, AXES, pairs)]
    all_to_all x0 -> x1, waiting for transfers between devices: none -> 9.95 us  [gather(): got = lax.all_to_all(sent, ('core', 'zl'), 0, 0, tiled=True)]
    ppermute x1, waiting for transfers between devices: 9.29 us -> 0.32 us  [on_device(): mem = lax.ppermute(memory, 'zh', [(1, 3)])]
    ppermute x5, starting transfers between devices: 7.43 us -> 14.6 us  [swapped(): return lax.ppermute(array, SECTION, pairs)]
    unnamed x26 -> x60, local copies, waits for them, and re-layouts: 0.75 us -> 7.46 us
    ppermute x1, waiting for transfers between devices: 37.5 us -> 30.9 us  [on_device(): in3 = lax.ppermute(first, 'zh', [(2, 3)])]
    all_to_all x0 -> x1, starting transfers between devices: none -> 5.63 us  [gather(): got = lax.all_to_all(sent, ('core', 'zl'), 0, 0, tiled=True)]
  transfers between devices with their start and end apart: 21 -> 25, of which waited for: 10 -> 13; matrix products, arithmetic and copies ran while one was open for 9% -> 3% of each run, Pallas kernels for 3% -> 3%
where the time goes in v8:
time: 171 us; the launch traced here: 170 us
  waiting for transfers between devices  73.7 us (43%)
  starting transfers between devices  63.5 us (37%)
  Pallas kernels  14.7 us (9%)
  local copies, waits for them, and re-layouts  14.1 us (8%)
  other arithmetic  3.5 us (2%)
    ppermute x14, starting transfers between devices, moved(): return lax.ppermute(array, AXES, pairs)  38.1 us
    ppermute x1, waiting for transfers between devices, on_device(): in3 = lax.ppermute(first, 'zh', [(2, 3)])  30.9 us
    ppermute x14, waiting for transfers between devices, moved(): return lax.ppermute(array, AXES, pairs)  30.8 us
    pallas_call x7, Pallas kernels, call(): pl.pallas_call(kernel, out_shape=outs, in_specs=[SMEM] + [VMEM] * len(ope...  14.7 us
    ppermute x5, starting transfers between devices, swapped(): return lax.ppermute(array, SECTION, pairs)  14.6 us
    all_to_all x1, waiting for transfers between devices, gather(): got = lax.all_to_all(sent, ('core', 'zl'), 0, 0, tiled=True)  9.95 us
    unnamed x60, local copies, waits for them, and re-layouts  7.46 us
    all_to_all x1, starting transfers between devices, gather(): got = lax.all_to_all(sent, ('core', 'zl'), 0, 0, tiled=True)  5.63 us
  transfers between devices with their start and end apart: 25, of which 13 were waited for; matrix products, arithmetic and copies ran while one was open for 3% of the time, Pallas kernels for 3%

profile of v8, /device:TPU:481, one launch (start us, length us, event | category | flops | bytes accessed | tf_op | source)
XLA Modules:
  0.0 170.3 jit_solution(13595194393545060615)
XLA Ops:
  2.0 5.6 %all-to-all-start = ((bf16[8,2,32,512]{3,2,1,0:T(8,128)(2,1)}), bf16[8,2,32,512]{3,2,1,0:T(8,128)(2,1)S(1)}, u32[]{:S(2)}, u32[]{:S(2)}) async-start(bf16[8,2,32,512]{3,2,1,0:T(8,128)(2,1)} %bitcast.10), calls=%async_computation | async-start | bytes 1048576 | tf_op jit(solution)/shard_map/all_to_all | solution.py:304
  7.6 9.9 %all-to-all-done = bf16[8,2,32,512]{3,2,1,0:T(8,128)(2,1)S(1)} async-done(((bf16[8,2,32,512]{3,2,1,0:T(8,128)(2,1)}), bf16[8,2,32,512]{3,2,1,0:T(8,128)(2,1)S(1)}, u32[]{:S(2)}, u32[]{:S(2)}) %all-to-all-start) | async-done | bytes 524320 | tf_op jit(solution)/shard_map/all_to_all | solution.py:304
  17.6 4.8 %collective-permute-start.3 = (bf16[4,128,512]{2,1,0:T(8,128)(2,1)S(1)}, bf16[4,128,512]{2,1,0:T(8,128)(2,1)S(1)}, u32[]{:S(2)}, u32[]{:S(2)}) collective-permute-start(bf16[4,128,512]{2,1,0:T(8,128)(2,1)S(1)} %bitcast.24), channel_id=1, source_target_pairs={{0,8},{1,9},{2,10},{3,11},{4,12},{5,13},{6,14},{7,15},{8,0},{9,1},... | collective-permute-start | bytes 1572872 | tf_op jit(solution)/shard_map/ppermute | solution.py:32
  22.4 2.7 %collective-permute-start.2 = (bf16[4,128,512]{2,1,0:T(8,128)(2,1)S(1)}, bf16[4,128,512]{2,1,0:T(8,128)(2,1)S(1)}, u32[]{:S(2)}, u32[]{:S(2)}) collective-permute-start(bf16[4,128,512]{2,1,0:T(8,128)(2,1)S(1)} %bitcast.25), channel_id=1, source_target_pairs={{0,12},{1,13},{2,14},{3,15},{4,8},{5,9},{6,10},{7,11},{8,4},{9,5},... | collective-permute-start | bytes 1572872 | tf_op jit(solution)/shard_map/ppermute | solution.py:32
  25.1 1.9 %collective-permute-start.1 = (bf16[4,128,512]{2,1,0:T(8,128)(2,1)S(1)}, bf16[4,128,512]{2,1,0:T(8,128)(2,1)}, u32[]{:S(2)}, u32[]{:S(2)}) collective-permute-start(bf16[4,128,512]{2,1,0:T(8,128)(2,1)S(1)} %bitcast.26), channel_id=1, source_target_pairs={{0,4},{1,5},{2,6},{3,7},{4,0},{5,1},{6,2},{7,3},{8,12},{9,13},{10,... | collective-permute-start | bytes 1572872 | tf_op jit(solution)/shard_map/ppermute | solution.py:32
  27.3 2.0 %collective-permute-done.3 = bf16[4,128,512]{2,1,0:T(8,128)(2,1)S(1)} collective-permute-done((bf16[4,128,512]{2,1,0:T(8,128)(2,1)S(1)}, bf16[4,128,512]{2,1,0:T(8,128)(2,1)S(1)}, u32[]{:S(2)}, u32[]{:S(2)}) %collective-permute-start.3) | collective-permute-done | bytes 524320 | tf_op jit(solution)/shard_map/ppermute | solution.py:32
  29.3 5.6 %collective-permute-done.2 = bf16[4,128,512]{2,1,0:T(8,128)(2,1)S(1)} collective-permute-done((bf16[4,128,512]{2,1,0:T(8,128)(2,1)S(1)}, bf16[4,128,512]{2,1,0:T(8,128)(2,1)S(1)}, u32[]{:S(2)}, u32[]{:S(2)}) %collective-permute-start.2) | collective-permute-done | bytes 524320 | tf_op jit(solution)/shard_map/ppermute | solution.py:32
  35.4 1.2 pad_maximum_fusion
  37.7 4.5 %collective-permute-start.5 = (bf16[3,512,256]{2,1,0:T(8,128)(2,1)}, bf16[3,512,256]{2,1,0:T(8,128)(2,1)S(1)}, u32[]{:S(2)}, u32[]{:S(2)}) collective-permute-start(bf16[3,512,256]{2,1,0:T(8,128)(2,1)} %get-tuple-element.28), channel_id=1, source_target_pairs={{0,48},{1,49},{2,50},{3,51},{4,52},{5,53},{6,54},{7,55},{8,56},{9,... | collective-permute-start | bytes 2359304 | tf_op jit(solution)/shard_map/ppermute | solution.py:32
  43.3 1.9 %collective-permute-start.4 = (bf16[3,512,256]{2,1,0:T(8,128)(2,1)}, bf16[3,512,256]{2,1,0:T(8,128)(2,1)}, u32[]{:S(2)}, u32[]{:S(2)}) collective-permute-start(bf16[3,512,256]{2,1,0:T(8,128)(2,1)} %get-tuple-element.28), channel_id=1, source_target_pairs={{0,16},{1,17},{2,18},{3,19},{4,20},{5,21},{6,22},{7,23},{8,24},{9,... | collective-permute-start | bytes 2359304 | tf_op jit(solution)/shard_map/ppermute | solution.py:32
  45.2 3.3 %collective-permute-start.6 = (bf16[3,512,256]{2,1,0:T(8,128)(2,1)S(1)}, bf16[3,512,256]{2,1,0:T(8,128)(2,1)}, u32[]{:S(2)}, u32[]{:S(2)}) collective-permute-start(bf16[3,512,256]{2,1,0:T(8,128)(2,1)S(1)} %get-tuple-element.29.refs_0_), channel_id=1, source_target_pairs={{0,32},{1,33},{2,34},{3,35},{4,36},{5,37},{6,38},{7,39},{8,40},{9,... | collective-permute-start | bytes 2359304 | tf_op jit(solution)/shard_map/ppermute | solution.py:32
  48.6 3.5 %collective-permute-start.10 = (bf16[1,512,512]{2,1,0:T(8,128)(2,1)S(1)}, bf16[1,512,512]{2,1,0:T(8,128)(2,1)S(1)}, u32[]{:S(2)}, u32[]{:S(2)}) collective-permute-start(bf16[1,512,512]{2,1,0:T(8,128)(2,1)S(1)} %slice.12.refs_0_.refs_8_), channel_id=1, source_target_pairs={{0,32},{1,33},{2,34},{3,35},{4,36},{5,37},{6,38},{7,39},{8,40},{9,... | collective-permute-start | bytes 1572872 | tf_op jit(solution)/shard_map/ppermute | solution.py:32
  52.9 2.8 %collective-permute-start.9 = (bf16[1,512,512]{2,1,0:T(8,128)(2,1)S(1)}, bf16[1,512,512]{2,1,0:T(8,128)(2,1)}, u32[]{:S(2)}, u32[]{:S(2)}) collective-permute-start(bf16[1,512,512]{2,1,0:T(8,128)(2,1)S(1)} %slice.12.refs_0_.refs_8_), channel_id=1, source_target_pairs={{0,48},{1,49},{2,50},{3,51},{4,52},{5,53},{6,54},{7,55},{8,56},{9,... | collective-permute-start | bytes 1572872 | tf_op jit(solution)/shard_map/ppermute | solution.py:32
  55.7 2.5 %collective-permute-start.8 = (bf16[1,512,512]{2,1,0:T(8,128)(2,1)S(1)}, bf16[1,512,512]{2,1,0:T(8,128)(2,1)}, u32[]{:S(2)}, u32[]{:S(2)}) collective-permute-start(bf16[1,512,512]{2,1,0:T(8,128)(2,1)S(1)} %slice.12.refs_0_.refs_8_), channel_id=1, source_target_pairs={{0,16},{1,17},{2,18},{3,19},{4,20},{5,21},{6,22},{7,23},{8,24},{9,... | collective-permute-start | bytes 1572872 | tf_op jit(solution)/shard_map/ppermute | solution.py:32
  58.9 2.7 %stack.27.scal = s32[9]{0:T(128)S(1)} concatenate(s32[1]{0:T(128)} %bitcast, s32[1]{0:T(128)} %bitcast.1, s32[1]{0:T(128)} %bitcast.2, s32[1]{0:T(128)} %bitcast.3, s32[1]{0:T(128)} %get-tuple-element.35, s32[1]{0:T(128)} %get-tuple-element.36, s32[1]{0:T(128)} %bitcast.4, s32[1]{0:T(128)} %get-tuple-element.32, s32[1]{0:T(128)} %get-tuple-element.31), dimensions={0} | concatenate | bytes 72 | tf_op jit(solution)/shard_map/stack | solution.py:331
  66.5 4.0 %collective-permute-done.10.refs_3_.refs_11_ = bf16[1,512,512]{2,1,0:T(8,128)(2,1)S(1)} collective-permute-done((bf16[1,512,512]{2,1,0:T(8,128)(2,1)S(1)}, bf16[1,512,512]{2,1,0:T(8,128)(2,1)S(1)}, u32[]{:S(2)}, u32[]{:S(2)}) %collective-permute-start.10) | collective-permute-done | bytes 524320 | tf_op jit(solution)/shard_map/ppermute | solution.py:32
  70.6 5.7 %collective-permute-done.9.refs_2_.refs_10_ = bf16[1,512,512]{2,1,0:T(8,128)(2,1)} collective-permute-done((bf16[1,512,512]{2,1,0:T(8,128)(2,1)S(1)}, bf16[1,512,512]{2,1,0:T(8,128)(2,1)}, u32[]{:S(2)}, u32[]{:S(2)}) %collective-permute-start.9) | collective-permute-done | bytes 524320 | tf_op jit(solution)/shard_map/ppermute | solution.py:32
  78.3 3.4 %collective-permute-start.18 = (bf16[3,512,256]{2,1,0:T(8,128)(2,1)S(1)}, bf16[3,512,256]{2,1,0:T(8,128)(2,1)S(1)}, u32[]{:S(2)}, u32[]{:S(2)}) collective-permute-start(bf16[3,512,256]{2,1,0:T(8,128)(2,1)S(1)} %get-tuple-element.27.refs_4_), channel_id=1, source_target_pairs={{128,160},{129,161},{130,162},{131,163},{132,164},{133,165},{134,1... | collective-permute-start | bytes 2359304 | tf_op jit(solution)/shard_map/ppermute | solution.py:32
  81.7 2.8 %collective-permute-start.17 = (bf16[3,512,256]{2,1,0:T(8,128)(2,1)S(1)}, bf16[3,512,256]{2,1,0:T(8,128)(2,1)S(1)}, u32[]{:S(2)}, u32[]{:S(2)}) collective-permute-start(bf16[3,512,256]{2,1,0:T(8,128)(2,1)S(1)} %get-tuple-element.27.refs_4_), channel_id=1, source_target_pairs={{128,176},{129,177},{130,178},{131,179},{132,180},{133,181},{134,1... | collective-permute-start | bytes 2359304 | tf_op jit(solution)/shard_map/ppermute | solution.py:32
  84.6 2.4 %collective-permute-start.16 = (bf16[3,512,256]{2,1,0:T(8,128)(2,1)S(1)}, bf16[3,512,256]{2,1,0:T(8,128)(2,1)S(1)}, u32[]{:S(2)}, u32[]{:S(2)}) collective-permute-start(bf16[3,512,256]{2,1,0:T(8,128)(2,1)S(1)} %get-tuple-element.27.refs_4_), channel_id=1, source_target_pairs={{128,144},{129,145},{130,146},{131,147},{132,148},{133,149},{134,1... | collective-permute-start | bytes 2359304 | tf_op jit(solution)/shard_map/ppermute | solution.py:32
  89.2 3.7 %collective-permute-done.18.refs_7_ = bf16[3,512,256]{2,1,0:T(8,128)(2,1)S(1)} collective-permute-done((bf16[3,512,256]{2,1,0:T(8,128)(2,1)S(1)}, bf16[3,512,256]{2,1,0:T(8,128)(2,1)S(1)}, u32[]{:S(2)}, u32[]{:S(2)}) %collective-permute-start.18) | collective-permute-done | bytes 786464 | tf_op jit(solution)/shard_map/ppermute | solution.py:32
  92.9 8.4 %collective-permute-done.17.refs_6_ = bf16[3,512,256]{2,1,0:T(8,128)(2,1)S(1)} collective-permute-done((bf16[3,512,256]{2,1,0:T(8,128)(2,1)S(1)}, bf16[3,512,256]{2,1,0:T(8,128)(2,1)S(1)}, u32[]{:S(2)}, u32[]{:S(2)}) %collective-permute-start.17) | collective-permute-done | bytes 786464 | tf_op jit(solution)/shard_map/ppermute | solution.py:32
  103.2 1.3 collective-permute-start.14
  105.6 1.3 collective-permute-start.21
  106.9 30.9 %collective-permute-done.14.mine.in3m = bf16[64,2048]{1,0:T(8,128)(2,1)} collective-permute-done((bf16[64,2048]{1,0:T(8,128)(2,1)S(1)}, bf16[64,2048]{1,0:T(8,128)(2,1)}, u32[]{:S(2)}, u32[]{:S(2)}) %collective-permute-start.14) | collective-permute-done | bytes 262176 | tf_op jit(solution)/shard_map/ppermute | solution.py:397
  137.8 10.0 %collective-permute-start.15 = (bf16[64,2048]{1,0:T(8,128)(2,1)}, bf16[64,2048]{1,0:T(8,128)(2,1)}, u32[]{:S(2)}, u32[]{:S(2)}) collective-permute-start(bf16[64,2048]{1,0:T(8,128)(2,1)} %collective-permute-done.14.mine.in3m), channel_id=1, source_target_pairs={{384,448},{448,384},{385,449},{449,385},{386,450},{450,386},{387,4... | collective-permute-start | bytes 786440 | tf_op jit(solution)/shard_map/ppermute | solution.py:356
  148.1 2.6 %collective-permute-start.22 = (bf16[64,2048]{1,0:T(8,128)(2,1)}, bf16[64,2048]{1,0:T(8,128)(2,1)}, u32[]{:S(2)}, u32[]{:S(2)}) collective-permute-start(bf16[64,2048]{1,0:T(8,128)(2,1)} %collective-permute-done.21.mem_mine), channel_id=1, source_target_pairs={{384,448},{448,384},{385,449},{449,385},{386,450},{450,386},{387,4... | collective-permute-start | bytes 786440 | tf_op jit(solution)/shard_map/ppermute | solution.py:356
  154.2 3.2 %shard_map.68.q = bf16[128,512]{1,0:T(8,128)(2,1)S(1)} custom-call(s32[9]{0:T(128)S(1)} %stack.27.scal, f32[5,2048]{1,0:T(8,128)S(1)} %copy-done.16, bf16[64,2048]{1,0:T(8,128)(2,1)} %collective-permute-done.14.mine.in3m, bf16[64,2048]{1,0:T(8,128)(2,1)} %collective-permute-done.15.other.in3o, bf16[3,512,256]{2,1,0:T(8,128)(2,1)S(1)} %get-tuple-element.29.refs_0_, ...), custom_call_target="tpu_custom_call" | custom-call | flops 268435456 | bytes 8953856 | tf_op jit(solution)/shard_map/pallas_call | solution.py:249
  157.5 6.8 %shard_map.69.own = bf16[128,2048]{1,0:T(8,128)(2,1)S(1)} custom-call(s32[9]{0:T(128)S(1)} %stack.27.scal, bf16[128,512]{1,0:T(8,128)(2,1)S(1)} %shard_map.68.q, bf16[64,2048]{1,0:T(8,128)(2,1)} %collective-permute-done.21.mem_mine, bf16[64,2048]{1,0:T(8,128)(2,1)} %collective-permute-done.22.mem_other, bf16[3,512,256]{2,1,0:T(8,128)(2,1)S(1)} %get-tuple-element.29.refs_0_, ...), custom_call_target="tpu_custom_call" | custom-call | flops 805306368 | bytes 9043968 | tf_op jit(solution)/shard_map/pallas_call | solution.py:249
  164.4 1.3 collective-permute-start.23
  166.5 1.7 %collective-permute-done.23.got = bf16[128,2048]{1,0:T(8,128)(2,1)S(1)} collective-permute-done((bf16[128,2048]{1,0:T(8,128)(2,1)S(1)}, bf16[128,2048]{1,0:T(8,128)(2,1)S(1)}, u32[]{:S(2)}, u32[]{:S(2)}) %collective-permute-start.23) | collective-permute-done | bytes 524320 | tf_op jit(solution)/shard_map/ppermute | solution.py:436
  168.2 2.1 %shard_map.70 = bf16[2,64,2048]{2,1,0:T(8,128)(2,1)} custom-call(s32[9]{0:T(128)S(1)} %stack.27.scal, bf16[64,2048]{1,0:T(8,128)(2,1)S(1)} %copy-done.15, bf16[64,2048]{1,0:T(8,128)(2,1)S(1)} %dynamic-slice_bitcast_fusion.other, bf16[64,2048]{1,0:T(8,128)(2,1)S(1)} %copy-done.12, bf16[64,2048]{1,0:T(8,128)(2,1)S(1)} %copy-done.14, ...), custom_call_target="tpu_custom_call" | custom-call | bytes 3145728 | tf_op jit(solution)/shard_map/pallas_call | solution.py:249
  (108 shorter events, 22.9 us)
Async XLA Ops:
  0.0 27.0 %copy-start.28 = (s32[2]{0:T(128)S(1)}, s32[2]{0:T(128)}, u32[]{:S(2)}) copy-start(s32[2]{0:T(128)} %param.11) | copy-start | bytes 28
  0.0 27.1 %copy-start.29 = (s32[2]{0:T(128)S(1)}, s32[2]{0:T(128)}, u32[]{:S(2)}) copy-start(s32[2]{0:T(128)} %param.10) | copy-start | bytes 28
  0.0 27.2 %copy-start.27 = (bf16[2,64,2048]{2,1,0:T(8,128)(2,1)S(1)}, bf16[2,64,2048]{2,1,0:T(8,128)(2,1)}, u32[]{:S(2)}) copy-start(bf16[2,64,2048]{2,1,0:T(8,128)(2,1)} %param.7) | copy-start | bytes 1572868
  0.0 27.2 %copy-start.26 = (bf16[2,64,2048]{2,1,0:T(8,128)(2,1)S(1)}, bf16[2,64,2048]{2,1,0:T(8,128)(2,1)}, u32[]{:S(2)}) copy-start(bf16[2,64,2048]{2,1,0:T(8,128)(2,1)} %param.6) | copy-start | bytes 1572868
  2.0 15.6 %all-to-all-start = ((bf16[8,2,32,512]{3,2,1,0:T(8,128)(2,1)}), bf16[8,2,32,512]{3,2,1,0:T(8,128)(2,1)S(1)}, u32[]{:S(2)}, u32[]{:S(2)}) async-start(bf16[8,2,32,512]{3,2,1,0:T(8,128)(2,1)} %bitcast.10), calls=%async_computation | async-start | bytes 1048576 | tf_op jit(solution)/shard_map/all_to_all | solution.py:304
  17.6 11.7 %collective-permute-start.3 = (bf16[4,128,512]{2,1,0:T(8,128)(2,1)S(1)}, bf16[4,128,512]{2,1,0:T(8,128)(2,1)S(1)}, u32[]{:S(2)}, u32[]{:S(2)}) collective-permute-start(bf16[4,128,512]{2,1,0:T(8,128)(2,1)S(1)} %bitcast.24), channel_id=1, source_target_pairs={{0,8},{1,9},{2,10},{3,11},{4,12},{5,13},{6,14},{7,15},{8,0},{9,1},... | collective-permute-start | bytes 1572872 | tf_op jit(solution)/shard_map/ppermute | solution.py:32
  22.4 12.5 %collective-permute-start.2 = (bf16[4,128,512]{2,1,0:T(8,128)(2,1)S(1)}, bf16[4,128,512]{2,1,0:T(8,128)(2,1)S(1)}, u32[]{:S(2)}, u32[]{:S(2)}) collective-permute-start(bf16[4,128,512]{2,1,0:T(8,128)(2,1)S(1)} %bitcast.25), channel_id=1, source_target_pairs={{0,12},{1,13},{2,14},{3,15},{4,8},{5,9},{6,10},{7,11},{8,4},{9,5},... | collective-permute-start | bytes 1572872 | tf_op jit(solution)/shard_map/ppermute | solution.py:32
  25.1 10.3 %collective-permute-start.1 = (bf16[4,128,512]{2,1,0:T(8,128)(2,1)S(1)}, bf16[4,128,512]{2,1,0:T(8,128)(2,1)}, u32[]{:S(2)}, u32[]{:S(2)}) collective-permute-start(bf16[4,128,512]{2,1,0:T(8,128)(2,1)S(1)} %bitcast.26), channel_id=1, source_target_pairs={{0,4},{1,5},{2,6},{3,7},{4,0},{5,1},{6,2},{7,3},{8,12},{9,13},{10,... | collective-permute-start | bytes 1572872 | tf_op jit(solution)/shard_map/ppermute | solution.py:32
  37.7 23.9 %copy-start.16 = (f32[5,2048]{1,0:T(8,128)S(1)}, f32[5,2048]{1,0:T(8,128)}, u32[]{:S(2)}) copy-start(f32[5,2048]{1,0:T(8,128)} %gains.5) | copy-start | bytes 122884
  37.7 18.0 %collective-permute-start.5 = (bf16[3,512,256]{2,1,0:T(8,128)(2,1)}, bf16[3,512,256]{2,1,0:T(8,128)(2,1)S(1)}, u32[]{:S(2)}, u32[]{:S(2)}) collective-permute-start(bf16[3,512,256]{2,1,0:T(8,128)(2,1)} %get-tuple-element.28), channel_id=1, source_target_pairs={{0,48},{1,49},{2,50},{3,51},{4,52},{5,53},{6,54},{7,55},{8,56},{9,... | collective-permute-start | bytes 2359304 | tf_op jit(solution)/shard_map/ppermute | solution.py:32
  42.6 9.5 %collective-permute-start = (bf16[144,2048]{1,0:T(8,128)(2,1)S(1)}, bf16[144,2048]{1,0:T(8,128)(2,1)S(1)}, u32[]{:S(2)}, u32[]{:S(2)}) collective-permute-start(bf16[144,2048]{1,0:T(8,128)(2,1)S(1)} %maximum_maximum_fusion.own), channel_id=1, source_target_pairs={{0,4},{1,5},{2,6},{3,7},{4,0},{5,1},{6,2},{7,3},{8,12},{9,13},{10,... | collective-permute-start | bytes 1769480 | tf_op jit(solution)/shard_map/ppermute | solution.py:32
  43.3 21.0 %collective-permute-start.4 = (bf16[3,512,256]{2,1,0:T(8,128)(2,1)}, bf16[3,512,256]{2,1,0:T(8,128)(2,1)}, u32[]{:S(2)}, u32[]{:S(2)}) collective-permute-start(bf16[3,512,256]{2,1,0:T(8,128)(2,1)} %get-tuple-element.28), channel_id=1, source_target_pairs={{0,16},{1,17},{2,18},{3,19},{4,20},{5,21},{6,22},{7,23},{8,24},{9,... | collective-permute-start | bytes 2359304 | tf_op jit(solution)/shard_map/ppermute | solution.py:32
  45.2 19.8 %collective-permute-start.6 = (bf16[3,512,256]{2,1,0:T(8,128)(2,1)S(1)}, bf16[3,512,256]{2,1,0:T(8,128)(2,1)}, u32[]{:S(2)}, u32[]{:S(2)}) collective-permute-start(bf16[3,512,256]{2,1,0:T(8,128)(2,1)S(1)} %get-tuple-element.29.refs_0_), channel_id=1, source_target_pairs={{0,32},{1,33},{2,34},{3,35},{4,36},{5,37},{6,38},{7,39},{8,40},{9,... | collective-permute-start | bytes 2359304 | tf_op jit(solution)/shard_map/ppermute | solution.py:32
  48.6 22.0 %collective-permute-start.10 = (bf16[1,512,512]{2,1,0:T(8,128)(2,1)S(1)}, bf16[1,512,512]{2,1,0:T(8,128)(2,1)S(1)}, u32[]{:S(2)}, u32[]{:S(2)}) collective-permute-start(bf16[1,512,512]{2,1,0:T(8,128)(2,1)S(1)} %slice.12.refs_0_.refs_8_), channel_id=1, source_target_pairs={{0,32},{1,33},{2,34},{3,35},{4,36},{5,37},{6,38},{7,39},{8,40},{9,... | collective-permute-start | bytes 1572872 | tf_op jit(solution)/shard_map/ppermute | solution.py:32
  52.9 23.3 %collective-permute-start.9 = (bf16[1,512,512]{2,1,0:T(8,128)(2,1)S(1)}, bf16[1,512,512]{2,1,0:T(8,128)(2,1)}, u32[]{:S(2)}, u32[]{:S(2)}) collective-permute-start(bf16[1,512,512]{2,1,0:T(8,128)(2,1)S(1)} %slice.12.refs_0_.refs_8_), channel_id=1, source_target_pairs={{0,48},{1,49},{2,50},{3,51},{4,52},{5,53},{6,54},{7,55},{8,56},{9,... | collective-permute-start | bytes 1572872 | tf_op jit(solution)/shard_map/ppermute | solution.py:32
  55.7 20.6 %collective-permute-start.8 = (bf16[1,512,512]{2,1,0:T(8,128)(2,1)S(1)}, bf16[1,512,512]{2,1,0:T(8,128)(2,1)}, u32[]{:S(2)}, u32[]{:S(2)}) collective-permute-start(bf16[1,512,512]{2,1,0:T(8,128)(2,1)S(1)} %slice.12.refs_0_.refs_8_), channel_id=1, source_target_pairs={{0,16},{1,17},{2,18},{3,19},{4,20},{5,21},{6,22},{7,23},{8,24},{9,... | collective-permute-start | bytes 1572872 | tf_op jit(solution)/shard_map/ppermute | solution.py:32
  65.7 21.3 %copy-start.20 = (bf16[2,64,2048]{2,1,0:T(8,128)(2,1)S(1)}, bf16[2,64,2048]{2,1,0:T(8,128)(2,1)}, u32[]{:S(2)}) copy-start(bf16[2,64,2048]{2,1,0:T(8,128)(2,1)} %copy-done.19) | copy-start | bytes 1572868
  65.7 10.6 %collective-permute-start.7 = (bf16[128,256]{1,0:T(8,128)(2,1)S(1)}, bf16[128,256]{1,0:T(8,128)(2,1)S(1)}, u32[]{:S(2)}, u32[]{:S(2)}) collective-permute-start(bf16[128,256]{1,0:T(8,128)(2,1)S(1)} %get-tuple-element.16), channel_id=1, source_target_pairs={{0,4},{1,5},{2,6},{3,7},{4,0},{5,1},{6,2},{7,3},{8,12},{9,13},{10,... | collective-permute-start | bytes 196616 | tf_op jit(solution)/shard_map/ppermute | solution.py:32
  77.0 10.1 %collective-permute-start.11 = (bf16[64,2048]{1,0:T(8,128)(2,1)S(1)}, bf16[64,2048]{1,0:T(8,128)(2,1)S(1)}, u32[]{:S(2)}, u32[]{:S(2)}) collective-permute-start(bf16[64,2048]{1,0:T(8,128)(2,1)S(1)} %get-tuple-element.18), channel_id=1, source_target_pairs={{0,64},{64,0},{256,320},{320,256},{1,65},{65,1},{257,321},{321,257... | collective-permute-start | bytes 786440 | tf_op jit(solution)/shard_map/ppermute | solution.py:356
  78.3 14.6 %collective-permute-start.18 = (bf16[3,512,256]{2,1,0:T(8,128)(2,1)S(1)}, bf16[3,512,256]{2,1,0:T(8,128)(2,1)S(1)}, u32[]{:S(2)}, u32[]{:S(2)}) collective-permute-start(bf16[3,512,256]{2,1,0:T(8,128)(2,1)S(1)} %get-tuple-element.27.refs_4_), channel_id=1, source_target_pairs={{128,160},{129,161},{130,162},{131,163},{132,164},{133,165},{134,1... | collective-permute-start | bytes 2359304 | tf_op jit(solution)/shard_map/ppermute | solution.py:32
  81.7 19.6 %collective-permute-start.17 = (bf16[3,512,256]{2,1,0:T(8,128)(2,1)S(1)}, bf16[3,512,256]{2,1,0:T(8,128)(2,1)S(1)}, u32[]{:S(2)}, u32[]{:S(2)}) collective-permute-start(bf16[3,512,256]{2,1,0:T(8,128)(2,1)S(1)} %get-tuple-element.27.refs_4_), channel_id=1, source_target_pairs={{128,176},{129,177},{130,178},{131,179},{132,180},{133,181},{134,1... | collective-permute-start | bytes 2359304 | tf_op jit(solution)/shard_map/ppermute | solution.py:32
  84.6 16.7 %collective-permute-start.16 = (bf16[3,512,256]{2,1,0:T(8,128)(2,1)S(1)}, bf16[3,512,256]{2,1,0:T(8,128)(2,1)S(1)}, u32[]{:S(2)}, u32[]{:S(2)}) collective-permute-start(bf16[3,512,256]{2,1,0:T(8,128)(2,1)S(1)} %get-tuple-element.27.refs_4_), channel_id=1, source_target_pairs={{128,144},{129,145},{130,146},{131,147},{132,148},{133,149},{134,1... | collective-permute-start | bytes 2359304 | tf_op jit(solution)/shard_map/ppermute | solution.py:32
  87.8 0.7 collective-permute-start.12
  88.5 16.0 %copy-start.11 = (bf16[64,2048]{1,0:T(8,128)(2,1)}, bf16[64,2048]{1,0:T(8,128)(2,1)S(1)}, u32[]{:S(2)}) copy-start(bf16[64,2048]{1,0:T(8,128)(2,1)S(1)} %collective-permute-done.12.mine.in1m) | copy-start | bytes 786436
  88.5 12.8 %collective-permute-start.13 = (bf16[64,2048]{1,0:T(8,128)(2,1)S(1)}, bf16[64,2048]{1,0:T(8,128)(2,1)S(1)}, u32[]{:S(2)}, u32[]{:S(2)}) collective-permute-start(bf16[64,2048]{1,0:T(8,128)(2,1)S(1)} %collective-permute-done.12.mine.in1m), channel_id=1, source_target_pairs={{128,192},{192,128},{129,193},{193,129},{130,194},{194,130},{131,1... | collective-permute-start | bytes 786440 | tf_op jit(solution)/shard_map/ppermute | solution.py:356
  102.5 2.0 %collective-permute-start.19 = (bf16[64,2048]{1,0:T(8,128)(2,1)S(1)}, bf16[64,2048]{1,0:T(8,128)(2,1)S(1)}, u32[]{:S(2)}, u32[]{:S(2)}) collective-permute-start(bf16[64,2048]{1,0:T(8,128)(2,1)S(1)} %get-tuple-element.20), channel_id=1, source_target_pairs={{128,192},{192,128},{129,193},{193,129},{130,194},{194,130},{131,1... | collective-permute-start | bytes 786440 | tf_op jit(solution)/shard_map/ppermute | solution.py:356
  103.2 34.6 %collective-permute-start.14 = (bf16[64,2048]{1,0:T(8,128)(2,1)S(1)}, bf16[64,2048]{1,0:T(8,128)(2,1)}, u32[]{:S(2)}, u32[]{:S(2)}) collective-permute-start(bf16[64,2048]{1,0:T(8,128)(2,1)S(1)} %get-tuple-element.23), channel_id=1, source_target_pairs={{256,384},{257,385},{258,386},{259,387},{260,388},{261,389},{262,3... | collective-permute-start | bytes 786440 | tf_op jit(solution)/shard_map/ppermute | solution.py:397
  105.6 42.5 %collective-permute-start.21 = (bf16[64,2048]{1,0:T(8,128)(2,1)S(1)}, bf16[64,2048]{1,0:T(8,128)(2,1)}, u32[]{:S(2)}, u32[]{:S(2)}) collective-permute-start(bf16[64,2048]{1,0:T(8,128)(2,1)S(1)} %fusion.2), channel_id=1, source_target_pairs={{128,384},{129,385},{130,386},{131,387},{132,388},{133,389},{134,3... | collective-permute-start | bytes 786440 | tf_op jit(solution)/shard_map/ppermute | solution.py:411
  137.8 12.9 %collective-permute-start.15 = (bf16[64,2048]{1,0:T(8,128)(2,1)}, bf16[64,2048]{1,0:T(8,128)(2,1)}, u32[]{:S(2)}, u32[]{:S(2)}) collective-permute-start(bf16[64,2048]{1,0:T(8,128)(2,1)} %collective-permute-done.14.mine.in3m), channel_id=1, source_target_pairs={{384,448},{448,384},{385,449},{449,385},{386,450},{450,386},{387,4... | collective-permute-start | bytes 786440 | tf_op jit(solution)/shard_map/ppermute | solution.py:356
  148.1 9.3 %collective-permute-start.22 = (bf16[64,2048]{1,0:T(8,128)(2,1)}, bf16[64,2048]{1,0:T(8,128)(2,1)}, u32[]{:S(2)}, u32[]{:S(2)}) collective-permute-start(bf16[64,2048]{1,0:T(8,128)(2,1)} %collective-permute-done.21.mem_mine), channel_id=1, source_target_pairs={{384,448},{448,384},{385,449},{449,385},{386,450},{450,386},{387,4... | collective-permute-start | bytes 786440 | tf_op jit(solution)/shard_map/ppermute | solution.py:356
  164.4 3.8 %collective-permute-start.23 = (bf16[128,2048]{1,0:T(8,128)(2,1)S(1)}, bf16[128,2048]{1,0:T(8,128)(2,1)S(1)}, u32[]{:S(2)}, u32[]{:S(2)}) collective-permute-start(bf16[128,2048]{1,0:T(8,128)(2,1)S(1)} %shard_map.69.own), channel_id=1, source_target_pairs={{384,448},{385,449},{386,450},{387,451},{388,452},{389,453},{390,4... | collective-permute-start | bytes 1572872 | tf_op jit(solution)/shard_map/ppermute | solution.py:436
  165.7 0.7 collective-permute-start.20
  (23 other events, 130.5 us)

commit v9 on v8

--- a/solution.py
+++ b/solution.py
@@ -71,7 +71,7 @@
 
     def take(self, slot):
         self.copies[slot].wait()
-        return self.space[slot]
+        return self.space.at[slot]
 
 
 def put_norm(scal, gains, streams, h3):
@@ -91,16 +91,19 @@
 
 
 def project(scal, h3, pieces, which, space, sems):
-    keys = [(i, m, n) for i in range(SIDE) for m in which for n in range(len(pieces))]
-    fetched = Fetched([pieces[n][i].at[m] for i, m, n in keys], space, sems)
+    keys = [(i, n) for i in range(SIDE) for n in range(len(pieces))]
+    low, high = which[0], which[-1] + 1
+    fetched = Fetched([pieces[n][i].at[low:high] for i, n in keys], space, sems)
 
     def run():
         totals = {}
-        for slot, (i, m, n) in enumerate(keys):
-            if (m, n) == (which[0], 0):
+        for slot, (i, n) in enumerate(keys):
+            if n == 0:
                 h = jnp.concatenate([h3[block_at(scal, TURNS[i], d)] for d in TURNS], axis=1)
-            term = dot(h, fetched.take(slot))
-            totals[m, n] = totals[m, n] + term if i else term
+            tile = fetched.take(slot)
+            for m in which:
+                term = dot(h, tile[m - low])
+                totals[m, n] = totals[m, n] + term if i else term
         sides = range(len(pieces))
         return [jnp.concatenate([totals[m, n] for n in sides], axis=1).astype(BF16) for m in which]
 
@@ -136,7 +139,7 @@
 
 def project_out(scal, mixed, fetched, t3):
     for i, turn in enumerate(TURNS):
-        t = dot_t(mixed, fetched.take(i))
+        t = dot_t(mixed, fetched.take(i)[...])
         for j, d in enumerate(TURNS):
             t3[block_at(scal, turn, d)] = t[:, j * 128:(j + 1) * 128]
 
@@ -238,7 +241,7 @@
 
 VMEM = pl.BlockSpec(memory_space=pltpu.VMEM)
 SMEM = pl.BlockSpec(memory_space=pltpu.SMEM)
-ANY = pl.BlockSpec(memory_space=pl.ANY)
+HBM = pl.BlockSpec(memory_space=pltpu.HBM)
 
 
 def call(kernel, scal, operands, outs, scratch=(), pieces=(), fetches=(), flops=0):
@@ -249,7 +252,7 @@
     return pl.pallas_call(
         kernel,
         out_shape=outs,
-        in_specs=[SMEM] + [VMEM] * len(operands) + [ANY] * len(pieces),
+        in_specs=[SMEM] + [VMEM] * len(operands) + [HBM] * len(pieces),
         out_specs=jax.tree.map(lambda _: VMEM, outs),
         scratch_shapes=shapes,
         compiler_params=pltpu.CompilerParams(vmem_limit_bytes=16 * 1024 * 1024),
@@ -296,7 +299,7 @@
     return [array] + [exchange(array, outer, turn, cubes) for turn in TURNS[1:]]
 
 
-def gather(weights):
+def gather(weights, early, late):
     pair, depth, width = weights.shape[1:]
     halves = weights[0].reshape(pair, depth, 2, width // 2).transpose(2, 0, 1, 3)
     sent = jnp.broadcast_to(halves[:, None], (2, SIDE) + halves.shape[1:])
@@ -304,7 +307,9 @@
     got = lax.all_to_all(sent, ("core", "zl"), 0, 0, tiled=True)
     got = got.reshape(2, SIDE, pair, depth, width // 2).transpose(0, 2, 1, 3, 4)
     got = got.reshape(2 * pair, SIDE * depth, width // 2)
-    block = jnp.concatenate(turns(got, False), axis=1)
+    near = turns(got, False)
+    near[1], early = lax.optimization_barrier((near[1], early))
+    block = jnp.concatenate(near, axis=1)
     zh, core, x = (lax.axis_index(name) for name in ("zh", "core", "x"))
     side = jnp.where(zh % 2 == 0, x % 2, 0)
     across = jnp.where((zh % 2 == 0) & (core == 1), 1 - side, side)
@@ -314,10 +319,9 @@
         return lax.dynamic_slice(block, (0, 0, at * half), (3,) + block.shape[1:2] + (half,))
 
     kept, sent = columns(side), columns(across)
+    sent, late = lax.optimization_barrier((sent, late))
     first = [kept, exchange(sent, True, 1), exchange(sent, True, 3), exchange(kept, True, FAR)]
-    outs = turns(block[3:], True)
-    second = turns(block[:3, :, half:], True, ODD)
-    return first, second, outs
+    return first, block[:3, :, half:], block[3:], early, late
 
 
 def on_device(encoder_embed, decoder_embed, section_weights, norm_gains, input_lengths, target_lengths):
@@ -343,8 +347,6 @@
     ).astype(jnp.int32)
     live = (jnp.arange(rows, dtype=jnp.int32) < row_lengths[core])[:, None]
 
-    parts_a, parts_b, parts_o = gather(section_weights)
-    pieces = [*parts_a, *parts_b, *parts_o]
     source = jnp.where(encoder, encoder_embed, decoder_embed)
     mine, other = source[core], source[1 - core]
 
@@ -356,8 +358,14 @@
         return lax.ppermute(array, SECTION, pairs)
 
     count, width = 2 * rows, mine.shape[1]
+    limits = jnp.broadcast_to(key_lengths.astype(BF16)[:, None], (2, width))
+    limits = jnp.concatenate([limits, jnp.zeros((14, width), BF16)], axis=0)
+    shared = jnp.concatenate([source.reshape(count, width), limits], axis=0)
+    parts_a, rest_b, rest_o, (scal, shared), shared_got = gather(
+        section_weights, (scal, shared), beside(shared)
+    )
     tile = parts_a[0].shape[1:]
-    square = parts_o[0].shape[1:]
+    square = rest_o.shape[1:]
     half = square[1]
     blocks = (16, count, 128)
     work = 2 * count * width * half
@@ -367,21 +375,21 @@
     quarter = jax.ShapeDtypeStruct((count, half // 2), BF16)
     out_fetch = (SIDE,) + square
 
-    limits = jnp.broadcast_to(key_lengths.astype(BF16)[:, None], (2, width))
-    limits = jnp.concatenate([limits, jnp.zeros((14, width), BF16)], axis=0)
-    shared = jnp.concatenate([source.reshape(count, width), limits], axis=0)
     h3, limits = call(
         norm_kernel,
         scal,
-        [norm_gains, shared, beside(shared)],
+        [norm_gains, shared, shared_got],
         (
             jax.ShapeDtypeStruct((16, 2 * count, 128), BF16),
             jax.ShapeDtypeStruct((2, 16, 128), F32),
         ),
     )
+    rest_o, h3 = lax.optimization_barrier((rest_o, h3))
+    parts_o = turns(rest_o, True)
     mixed, mixed_sent = call(
-        first_kernel, scal, [h3, limits], (quarter, quarter), (), parts_a, [(12,) + tile], 3 * work
-    )
+        first_kernel, scal, [h3, limits], (quarter, quarter), (), parts_a, [(4, 3) + tile], 3 * work
+    )
+    rest_b, mixed = lax.optimization_barrier((rest_b, mixed))
     kept, sent = call(
         first_out_kernel,
         scal,
@@ -393,6 +401,7 @@
         work,
     )
     first = added(mine, kept + swapped(sent, (0, 2)).astype(F32), live).astype(BF16)
+    pieces = [*parts_a, *turns(rest_b, True, ODD), *parts_o]
     in1 = lax.ppermute(first, "zh", [(0, 1)])
     in3 = lax.ppermute(first, "zh", [(2, 3)])
     in1_other = swapped(in1, (1,))
@@ -403,7 +412,7 @@
         halves,
         [(blocks, BF16), (blocks, F32)],
         pieces,
-        [(24,) + tile, out_fetch],
+        [(8, 3) + tile, out_fetch],
         4 * work,
     )
     second = added(in1, kept + swapped(sent, (1,)).astype(F32), live).astype(BF16)
@@ -419,7 +428,7 @@
         narrow,
         [(blocks, BF16)],
         pieces,
-        [(8,) + tile],
+        [(8, 1) + tile],
         work,
     )
     mem_other = swapped(mem, (3,))
@@ -430,7 +439,7 @@
         wide,
         [(blocks, BF16), (blocks, F32)],
         pieces,
-        [(16,) + tile, out_fetch],
+        [(8, 2) + tile, out_fetch],
         3 * work,
     )
     got = lax.ppermute(own, SECTION, [(6, 7)])

time: 171 us -> 172 us (level)
  local copies, waits for them, and re-layouts: 14.1 us -> 16.6 us
  Pallas kernels: 14.7 us -> 12.7 us
    unnamed x60 -> x70, local copies, waits for them, and re-layouts: 7.46 us -> 10.9 us
    pallas_call x7, Pallas kernels: 14.7 us -> 12.7 us  [call(): pl.pallas_call(kernel, out_shape=outs, in_specs=[SMEM] + [VMEM] * len(ope...]
  transfers between devices with their start and end apart: 25 -> 25, of which waited for: 13 -> 10; matrix products, arithmetic and copies ran while one was open for 3% -> 4% of each run, Pallas kernels for 3% -> 2%
where the time goes in v9:
time: 172 us; the launch traced here: 171 us
  waiting for transfers between devices  74 us (43%)
  starting transfers between devices  63 us (37%)
  local copies, waits for them, and re-layouts  16.6 us (10%)
  Pallas kernels  12.7 us (7%)
  other arithmetic  3.51 us (2%)
    ppermute x14, starting transfers between devices, moved(): return lax.ppermute(array, AXES, pairs)  38 us
    ppermute x14, waiting for transfers between devices, moved(): return lax.ppermute(array, AXES, pairs)  31.6 us
    ppermute x1, waiting for transfers between devices, on_device(): in3 = lax.ppermute(first, 'zh', [(2, 3)])  30.9 us
    ppermute x5, starting transfers between devices, swapped(): return lax.ppermute(array, SECTION, pairs)  14.2 us
    pallas_call x7, Pallas kernels, call(): pl.pallas_call(kernel, out_shape=outs, in_specs=[SMEM] + [VMEM] * len(ope...  12.7 us
    unnamed x70, local copies, waits for them, and re-layouts  10.9 us
    all_to_all x1, waiting for transfers between devices, gather(): got = lax.all_to_all(sent, ('core', 'zl'), 0, 0, tiled=True)  9.75 us
    all_to_all x1, starting transfers between devices, gather(): got = lax.all_to_all(sent, ('core', 'zl'), 0, 0, tiled=True)  5.63 us
  transfers between devices with their start and end apart: 25, of which 10 were waited for; matrix products, arithmetic and copies ran while one was open for 4% of the time, Pallas kernels for 2%

profile of v9, /device:TPU:481, one launch (start us, length us, event | category | flops | bytes accessed | tf_op | source)
XLA Modules:
  0.0 170.6 jit_solution(321488424642856801)
XLA Ops:
  2.0 5.6 %all-to-all-start = ((bf16[8,2,32,512]{3,2,1,0:T(8,128)(2,1)}), bf16[8,2,32,512]{3,2,1,0:T(8,128)(2,1)S(1)}, u32[]{:S(2)}, u32[]{:S(2)}) async-start(bf16[8,2,32,512]{3,2,1,0:T(8,128)(2,1)} %bitcast.1), calls=%async_computation | async-start | bytes 1048576 | tf_op jit(solution)/shard_map/all_to_all | solution.py:307
  7.8 9.7 %all-to-all-done = bf16[8,2,32,512]{3,2,1,0:T(8,128)(2,1)S(1)} async-done(((bf16[8,2,32,512]{3,2,1,0:T(8,128)(2,1)}), bf16[8,2,32,512]{3,2,1,0:T(8,128)(2,1)S(1)}, u32[]{:S(2)}, u32[]{:S(2)}) %all-to-all-start) | async-done | bytes 524320 | tf_op jit(solution)/shard_map/all_to_all | solution.py:307
  17.6 4.8 %collective-permute-start.2 = (bf16[4,128,512]{2,1,0:T(8,128)(2,1)S(1)}, bf16[4,128,512]{2,1,0:T(8,128)(2,1)S(1)}, u32[]{:S(2)}, u32[]{:S(2)}) collective-permute-start(bf16[4,128,512]{2,1,0:T(8,128)(2,1)S(1)} %bitcast.24), channel_id=1, source_target_pairs={{0,8},{1,9},{2,10},{3,11},{4,12},{5,13},{6,14},{7,15},{8,0},{9,1},... | collective-permute-start | bytes 1572872 | tf_op jit(solution)/shard_map/ppermute | solution.py:32
  22.4 2.7 %collective-permute-start.1 = (bf16[4,128,512]{2,1,0:T(8,128)(2,1)S(1)}, bf16[4,128,512]{2,1,0:T(8,128)(2,1)S(1)}, u32[]{:S(2)}, u32[]{:S(2)}) collective-permute-start(bf16[4,128,512]{2,1,0:T(8,128)(2,1)S(1)} %bitcast.25), channel_id=1, source_target_pairs={{0,12},{1,13},{2,14},{3,15},{4,8},{5,9},{6,10},{7,11},{8,4},{9,5},... | collective-permute-start | bytes 1572872 | tf_op jit(solution)/shard_map/ppermute | solution.py:32
  25.1 1.9 %collective-permute-start = (bf16[4,128,512]{2,1,0:T(8,128)(2,1)S(1)}, bf16[4,128,512]{2,1,0:T(8,128)(2,1)}, u32[]{:S(2)}, u32[]{:S(2)}) collective-permute-start(bf16[4,128,512]{2,1,0:T(8,128)(2,1)S(1)} %bitcast.26), channel_id=1, source_target_pairs={{0,4},{1,5},{2,6},{3,7},{4,0},{5,1},{6,2},{7,3},{8,12},{9,13},{10,... | collective-permute-start | bytes 1572872 | tf_op jit(solution)/shard_map/ppermute | solution.py:32
  28.8 2.7 %stack.27.scal = s32[9]{0:T(128)S(1)} concatenate(s32[1]{0:T(128)} %bitcast.5, s32[1]{0:T(128)} %bitcast.6, s32[1]{0:T(128)} %bitcast.7, s32[1]{0:T(128)} %bitcast.8, s32[1]{0:T(128)} %get-tuple-element.53, s32[1]{0:T(128)} %get-tuple-element.54, s32[1]{0:T(128)} %bitcast.9, s32[1]{0:T(128)} %get-tuple-element.50, s32[1]{0:T(128)} %get-tuple-element.49), dimensions={0} | concatenate | bytes 72 | tf_op jit(solution)/shard_map/stack | solution.py:335
  31.5 3.9 %collective-permute-done = bf16[4,128,512]{2,1,0:T(8,128)(2,1)} collective-permute-done((bf16[4,128,512]{2,1,0:T(8,128)(2,1)S(1)}, bf16[4,128,512]{2,1,0:T(8,128)(2,1)}, u32[]{:S(2)}, u32[]{:S(2)}) %collective-permute-start) | collective-permute-done | bytes 524320 | tf_op jit(solution)/shard_map/ppermute | solution.py:32
  35.5 1.2 pad_maximum_fusion
  37.7 4.4 %collective-permute-start.5 = (bf16[3,512,256]{2,1,0:T(8,128)(2,1)S(1)}, bf16[3,512,256]{2,1,0:T(8,128)(2,1)S(1)}, u32[]{:S(2)}, u32[]{:S(2)}) collective-permute-start(bf16[3,512,256]{2,1,0:T(8,128)(2,1)S(1)} %get-tuple-element.29), channel_id=1, source_target_pairs={{0,48},{1,49},{2,50},{3,51},{4,52},{5,53},{6,54},{7,55},{8,56},{9,... | collective-permute-start | bytes 2359304 | tf_op jit(solution)/shard_map/ppermute | solution.py:32
  42.1 1.9 %collective-permute-start.4 = (bf16[3,512,256]{2,1,0:T(8,128)(2,1)S(1)}, bf16[3,512,256]{2,1,0:T(8,128)(2,1)S(1)}, u32[]{:S(2)}, u32[]{:S(2)}) collective-permute-start(bf16[3,512,256]{2,1,0:T(8,128)(2,1)S(1)} %get-tuple-element.29), channel_id=1, source_target_pairs={{0,16},{1,17},{2,18},{3,19},{4,20},{5,21},{6,22},{7,23},{8,24},{9,... | collective-permute-start | bytes 2359304 | tf_op jit(solution)/shard_map/ppermute | solution.py:32
  44.0 3.3 %collective-permute-start.6 = (bf16[3,512,256]{2,1,0:T(8,128)(2,1)S(1)}, bf16[3,512,256]{2,1,0:T(8,128)(2,1)S(1)}, u32[]{:S(2)}, u32[]{:S(2)}) collective-permute-start(bf16[3,512,256]{2,1,0:T(8,128)(2,1)S(1)} %get-tuple-element.45.refs_0_), channel_id=1, source_target_pairs={{0,32},{1,33},{2,34},{3,35},{4,36},{5,37},{6,38},{7,39},{8,40},{9,... | collective-permute-start | bytes 2359304 | tf_op jit(solution)/shard_map/ppermute | solution.py:32
  49.0 3.5 %collective-permute-start.10 = (bf16[1,512,512]{2,1,0:T(8,128)(2,1)S(1)}, bf16[1,512,512]{2,1,0:T(8,128)(2,1)S(1)}, u32[]{:S(2)}, u32[]{:S(2)}) collective-permute-start(bf16[1,512,512]{2,1,0:T(8,128)(2,1)S(1)} %slice.13.refs_0_.refs_8_), channel_id=1, source_target_pairs={{0,32},{1,33},{2,34},{3,35},{4,36},{5,37},{6,38},{7,39},{8,40},{9,... | collective-permute-start | bytes 1572872 | tf_op jit(solution)/shard_map/ppermute | solution.py:32
  52.5 2.8 %collective-permute-start.9 = (bf16[1,512,512]{2,1,0:T(8,128)(2,1)S(1)}, bf16[1,512,512]{2,1,0:T(8,128)(2,1)S(1)}, u32[]{:S(2)}, u32[]{:S(2)}) collective-permute-start(bf16[1,512,512]{2,1,0:T(8,128)(2,1)S(1)} %slice.13.refs_0_.refs_8_), channel_id=1, source_target_pairs={{0,48},{1,49},{2,50},{3,51},{4,52},{5,53},{6,54},{7,55},{8,56},{9,... | collective-permute-start | bytes 1572872 | tf_op jit(solution)/shard_map/ppermute | solution.py:32
  55.3 2.5 %collective-permute-start.8 = (bf16[1,512,512]{2,1,0:T(8,128)(2,1)S(1)}, bf16[1,512,512]{2,1,0:T(8,128)(2,1)S(1)}, u32[]{:S(2)}, u32[]{:S(2)}) collective-permute-start(bf16[1,512,512]{2,1,0:T(8,128)(2,1)S(1)} %slice.13.refs_0_.refs_8_), channel_id=1, source_target_pairs={{0,16},{1,17},{2,18},{3,19},{4,20},{5,21},{6,22},{7,23},{8,24},{9,... | collective-permute-start | bytes 1572872 | tf_op jit(solution)/shard_map/ppermute | solution.py:32
  57.8 5.7 %collective-permute-done.6.refs_3_ = bf16[3,512,256]{2,1,0:T(8,128)(2,1)S(1)} collective-permute-done((bf16[3,512,256]{2,1,0:T(8,128)(2,1)S(1)}, bf16[3,512,256]{2,1,0:T(8,128)(2,1)S(1)}, u32[]{:S(2)}, u32[]{:S(2)}) %collective-permute-start.6) | collective-permute-done | bytes 786464 | tf_op jit(solution)/shard_map/ppermute | solution.py:32
  64.9 4.2 %collective-permute-done.10.refs_3_.refs_11_ = bf16[1,512,512]{2,1,0:T(8,128)(2,1)S(1)} collective-permute-done((bf16[1,512,512]{2,1,0:T(8,128)(2,1)S(1)}, bf16[1,512,512]{2,1,0:T(8,128)(2,1)S(1)}, u32[]{:S(2)}, u32[]{:S(2)}) %collective-permute-start.10) | collective-permute-done | bytes 524320 | tf_op jit(solution)/shard_map/ppermute | solution.py:32
  69.1 5.6 %collective-permute-done.9.refs_2_.refs_10_ = bf16[1,512,512]{2,1,0:T(8,128)(2,1)S(1)} collective-permute-done((bf16[1,512,512]{2,1,0:T(8,128)(2,1)S(1)}, bf16[1,512,512]{2,1,0:T(8,128)(2,1)S(1)}, u32[]{:S(2)}, u32[]{:S(2)}) %collective-permute-start.9) | collective-permute-done | bytes 524320 | tf_op jit(solution)/shard_map/ppermute | solution.py:32
  76.8 3.4 %collective-permute-start.18 = (bf16[3,512,256]{2,1,0:T(8,128)(2,1)S(1)}, bf16[3,512,256]{2,1,0:T(8,128)(2,1)S(1)}, u32[]{:S(2)}, u32[]{:S(2)}) collective-permute-start(bf16[3,512,256]{2,1,0:T(8,128)(2,1)S(1)} %get-tuple-element.36.refs_4_), channel_id=1, source_target_pairs={{128,160},{129,161},{130,162},{131,163},{132,164},{133,165},{134,1... | collective-permute-start | bytes 2359304 | tf_op jit(solution)/shard_map/ppermute | solution.py:32
  80.2 2.8 %collective-permute-start.17 = (bf16[3,512,256]{2,1,0:T(8,128)(2,1)S(1)}, bf16[3,512,256]{2,1,0:T(8,128)(2,1)S(1)}, u32[]{:S(2)}, u32[]{:S(2)}) collective-permute-start(bf16[3,512,256]{2,1,0:T(8,128)(2,1)S(1)} %get-tuple-element.36.refs_4_), channel_id=1, source_target_pairs={{128,176},{129,177},{130,178},{131,179},{132,180},{133,181},{134,1... | collective-permute-start | bytes 2359304 | tf_op jit(solution)/shard_map/ppermute | solution.py:32
  83.0 2.5 %collective-permute-start.16 = (bf16[3,512,256]{2,1,0:T(8,128)(2,1)S(1)}, bf16[3,512,256]{2,1,0:T(8,128)(2,1)S(1)}, u32[]{:S(2)}, u32[]{:S(2)}) collective-permute-start(bf16[3,512,256]{2,1,0:T(8,128)(2,1)S(1)} %get-tuple-element.36.refs_4_), channel_id=1, source_target_pairs={{128,144},{129,145},{130,146},{131,147},{132,148},{133,149},{134,1... | collective-permute-start | bytes 2359304 | tf_op jit(solution)/shard_map/ppermute | solution.py:32
  87.7 3.7 %collective-permute-done.18.refs_7_ = bf16[3,512,256]{2,1,0:T(8,128)(2,1)S(1)} collective-permute-done((bf16[3,512,256]{2,1,0:T(8,128)(2,1)S(1)}, bf16[3,512,256]{2,1,0:T(8,128)(2,1)S(1)}, u32[]{:S(2)}, u32[]{:S(2)}) %collective-permute-start.18) | collective-permute-done | bytes 786464 | tf_op jit(solution)/shard_map/ppermute | solution.py:32
  91.4 8.4 %collective-permute-done.17.refs_6_ = bf16[3,512,256]{2,1,0:T(8,128)(2,1)S(1)} collective-permute-done((bf16[3,512,256]{2,1,0:T(8,128)(2,1)S(1)}, bf16[3,512,256]{2,1,0:T(8,128)(2,1)S(1)}, u32[]{:S(2)}, u32[]{:S(2)}) %collective-permute-start.17) | collective-permute-done | bytes 786464 | tf_op jit(solution)/shard_map/ppermute | solution.py:32
  101.7 1.3 collective-permute-start.14
  104.1 1.3 collective-permute-start.21
  105.4 30.9 %collective-permute-done.14.mine.in3m = bf16[64,2048]{1,0:T(8,128)(2,1)} collective-permute-done((bf16[64,2048]{1,0:T(8,128)(2,1)S(1)}, bf16[64,2048]{1,0:T(8,128)(2,1)}, u32[]{:S(2)}, u32[]{:S(2)}) %collective-permute-start.14) | collective-permute-done | bytes 262176 | tf_op jit(solution)/shard_map/ppermute | solution.py:406
  136.4 10.0 %collective-permute-start.15 = (bf16[64,2048]{1,0:T(8,128)(2,1)}, bf16[64,2048]{1,0:T(8,128)(2,1)}, u32[]{:S(2)}, u32[]{:S(2)}) collective-permute-start(bf16[64,2048]{1,0:T(8,128)(2,1)} %collective-permute-done.14.mine.in3m), channel_id=1, source_target_pairs={{384,448},{448,384},{385,449},{449,385},{386,450},{450,386},{387,4... | collective-permute-start | bytes 786440 | tf_op jit(solution)/shard_map/ppermute | solution.py:358
  146.3 2.2 %collective-permute-start.22 = (bf16[64,2048]{1,0:T(8,128)(2,1)}, bf16[64,2048]{1,0:T(8,128)(2,1)}, u32[]{:S(2)}, u32[]{:S(2)}) collective-permute-start(bf16[64,2048]{1,0:T(8,128)(2,1)} %collective-permute-done.21.mem_mine), channel_id=1, source_target_pairs={{384,448},{448,384},{385,449},{449,385},{386,450},{450,386},{387,4... | collective-permute-start | bytes 786440 | tf_op jit(solution)/shard_map/ppermute | solution.py:358
  156.4 2.6 %shard_map.68.q = bf16[128,512]{1,0:T(8,128)(2,1)S(1)} custom-call(s32[9]{0:T(128)S(1)} %stack.27.scal, f32[5,2048]{1,0:T(8,128)S(1)} %copy-done.21, bf16[64,2048]{1,0:T(8,128)(2,1)} %collective-permute-done.14.mine.in3m, bf16[64,2048]{1,0:T(8,128)(2,1)} %collective-permute-done.15.other.in3o, bf16[3,512,256]{2,1,0:T(8,128)(2,1)S(1)} %get-tuple-element.45.refs_0_, ...), custom_call_target="tpu_custom_call" | custom-call | flops 268435456 | bytes 8953856 | tf_op jit(solution)/shard_map/pallas_call | solution.py:252
  159.1 5.6 %shard_map.69.own = bf16[128,2048]{1,0:T(8,128)(2,1)S(1)} custom-call(s32[9]{0:T(128)S(1)} %stack.27.scal, bf16[128,512]{1,0:T(8,128)(2,1)S(1)} %shard_map.68.q, bf16[64,2048]{1,0:T(8,128)(2,1)} %collective-permute-done.21.mem_mine, bf16[64,2048]{1,0:T(8,128)(2,1)} %collective-permute-done.22.mem_other, bf16[3,512,256]{2,1,0:T(8,128)(2,1)S(1)} %get-tuple-element.45.refs_0_, ...), custom_call_target="tpu_custom_call" | custom-call | flops 805306368 | bytes 9043968 | tf_op jit(solution)/shard_map/pallas_call | solution.py:252
  164.7 1.3 collective-permute-start.23
  166.8 1.7 collective-permute-done.23.got
  168.5 2.1 %shard_map.70 = bf16[2,64,2048]{2,1,0:T(8,128)(2,1)} custom-call(s32[9]{0:T(128)S(1)} %stack.27.scal, bf16[64,2048]{1,0:T(8,128)(2,1)S(1)} %copy-done.20, bf16[64,2048]{1,0:T(8,128)(2,1)S(1)} %dynamic-slice_bitcast_fusion.other, bf16[64,2048]{1,0:T(8,128)(2,1)S(1)} %copy-done.17, bf16[64,2048]{1,0:T(8,128)(2,1)S(1)} %copy-done.19, ...), custom_call_target="tpu_custom_call" | custom-call | bytes 3145728 | tf_op jit(solution)/shard_map/pallas_call | solution.py:252
  (118 shorter events, 23.6 us)
Async XLA Ops:
  2.0 15.6 %all-to-all-start = ((bf16[8,2,32,512]{3,2,1,0:T(8,128)(2,1)}), bf16[8,2,32,512]{3,2,1,0:T(8,128)(2,1)S(1)}, u32[]{:S(2)}, u32[]{:S(2)}) async-start(bf16[8,2,32,512]{3,2,1,0:T(8,128)(2,1)} %bitcast.1), calls=%async_computation | async-start | bytes 1048576 | tf_op jit(solution)/shard_map/all_to_all | solution.py:307
  7.8 27.7 %copy-start.24 = (bf16[2,64,2048]{2,1,0:T(8,128)(2,1)}, bf16[2,64,2048]{2,1,0:T(8,128)(2,1)S(1)}, u32[]{:S(2)}) copy-start(bf16[2,64,2048]{2,1,0:T(8,128)(2,1)S(1)} %broadcast_select_fusion) | copy-start | bytes 1572868
  17.6 17.9 %collective-permute-start.2 = (bf16[4,128,512]{2,1,0:T(8,128)(2,1)S(1)}, bf16[4,128,512]{2,1,0:T(8,128)(2,1)S(1)}, u32[]{:S(2)}, u32[]{:S(2)}) collective-permute-start(bf16[4,128,512]{2,1,0:T(8,128)(2,1)S(1)} %bitcast.24), channel_id=1, source_target_pairs={{0,8},{1,9},{2,10},{3,11},{4,12},{5,13},{6,14},{7,15},{8,0},{9,1},... | collective-permute-start | bytes 1572872 | tf_op jit(solution)/shard_map/ppermute | solution.py:32
  22.4 13.0 %collective-permute-start.1 = (bf16[4,128,512]{2,1,0:T(8,128)(2,1)S(1)}, bf16[4,128,512]{2,1,0:T(8,128)(2,1)S(1)}, u32[]{:S(2)}, u32[]{:S(2)}) collective-permute-start(bf16[4,128,512]{2,1,0:T(8,128)(2,1)S(1)} %bitcast.25), channel_id=1, source_target_pairs={{0,12},{1,13},{2,14},{3,15},{4,8},{5,9},{6,10},{7,11},{8,4},{9,5},... | collective-permute-start | bytes 1572872 | tf_op jit(solution)/shard_map/ppermute | solution.py:32
  25.1 10.3 %collective-permute-start = (bf16[4,128,512]{2,1,0:T(8,128)(2,1)S(1)}, bf16[4,128,512]{2,1,0:T(8,128)(2,1)}, u32[]{:S(2)}, u32[]{:S(2)}) collective-permute-start(bf16[4,128,512]{2,1,0:T(8,128)(2,1)S(1)} %bitcast.26), channel_id=1, source_target_pairs={{0,4},{1,5},{2,6},{3,7},{4,0},{5,1},{6,2},{7,3},{8,12},{9,13},{10,... | collective-permute-start | bytes 1572872 | tf_op jit(solution)/shard_map/ppermute | solution.py:32
  27.4 9.4 %collective-permute-start.3 = (bf16[144,2048]{1,0:T(8,128)(2,1)S(1)}, bf16[144,2048]{1,0:T(8,128)(2,1)S(1)}, u32[]{:S(2)}, u32[]{:S(2)}) collective-permute-start(bf16[144,2048]{1,0:T(8,128)(2,1)S(1)} %maximum_maximum_fusion.own), channel_id=1, source_target_pairs={{0,4},{1,5},{2,6},{3,7},{4,0},{5,1},{6,2},{7,3},{8,12},{9,13},{10,... | collective-permute-start | bytes 1769480 | tf_op jit(solution)/shard_map/ppermute | solution.py:32
  37.7 17.6 %collective-permute-start.5 = (bf16[3,512,256]{2,1,0:T(8,128)(2,1)S(1)}, bf16[3,512,256]{2,1,0:T(8,128)(2,1)S(1)}, u32[]{:S(2)}, u32[]{:S(2)}) collective-permute-start(bf16[3,512,256]{2,1,0:T(8,128)(2,1)S(1)} %get-tuple-element.29), channel_id=1, source_target_pairs={{0,48},{1,49},{2,50},{3,51},{4,52},{5,53},{6,54},{7,55},{8,56},{9,... | collective-permute-start | bytes 2359304 | tf_op jit(solution)/shard_map/ppermute | solution.py:32
  42.1 15.7 %collective-permute-start.4 = (bf16[3,512,256]{2,1,0:T(8,128)(2,1)S(1)}, bf16[3,512,256]{2,1,0:T(8,128)(2,1)S(1)}, u32[]{:S(2)}, u32[]{:S(2)}) collective-permute-start(bf16[3,512,256]{2,1,0:T(8,128)(2,1)S(1)} %get-tuple-element.29), channel_id=1, source_target_pairs={{0,16},{1,17},{2,18},{3,19},{4,20},{5,21},{6,22},{7,23},{8,24},{9,... | collective-permute-start | bytes 2359304 | tf_op jit(solution)/shard_map/ppermute | solution.py:32
  44.0 19.5 %collective-permute-start.6 = (bf16[3,512,256]{2,1,0:T(8,128)(2,1)S(1)}, bf16[3,512,256]{2,1,0:T(8,128)(2,1)S(1)}, u32[]{:S(2)}, u32[]{:S(2)}) collective-permute-start(bf16[3,512,256]{2,1,0:T(8,128)(2,1)S(1)} %get-tuple-element.45.refs_0_), channel_id=1, source_target_pairs={{0,32},{1,33},{2,34},{3,35},{4,36},{5,37},{6,38},{7,39},{8,40},{9,... | collective-permute-start | bytes 2359304 | tf_op jit(solution)/shard_map/ppermute | solution.py:32
  49.0 20.1 %collective-permute-start.10 = (bf16[1,512,512]{2,1,0:T(8,128)(2,1)S(1)}, bf16[1,512,512]{2,1,0:T(8,128)(2,1)S(1)}, u32[]{:S(2)}, u32[]{:S(2)}) collective-permute-start(bf16[1,512,512]{2,1,0:T(8,128)(2,1)S(1)} %slice.13.refs_0_.refs_8_), channel_id=1, source_target_pairs={{0,32},{1,33},{2,34},{3,35},{4,36},{5,37},{6,38},{7,39},{8,40},{9,... | collective-permute-start | bytes 1572872 | tf_op jit(solution)/shard_map/ppermute | solution.py:32
  52.5 22.2 %collective-permute-start.9 = (bf16[1,512,512]{2,1,0:T(8,128)(2,1)S(1)}, bf16[1,512,512]{2,1,0:T(8,128)(2,1)S(1)}, u32[]{:S(2)}, u32[]{:S(2)}) collective-permute-start(bf16[1,512,512]{2,1,0:T(8,128)(2,1)S(1)} %slice.13.refs_0_.refs_8_), channel_id=1, source_target_pairs={{0,48},{1,49},{2,50},{3,51},{4,52},{5,53},{6,54},{7,55},{8,56},{9,... | collective-permute-start | bytes 1572872 | tf_op jit(solution)/shard_map/ppermute | solution.py:32
  55.3 19.5 %collective-permute-start.8 = (bf16[1,512,512]{2,1,0:T(8,128)(2,1)S(1)}, bf16[1,512,512]{2,1,0:T(8,128)(2,1)S(1)}, u32[]{:S(2)}, u32[]{:S(2)}) collective-permute-start(bf16[1,512,512]{2,1,0:T(8,128)(2,1)S(1)} %slice.13.refs_0_.refs_8_), channel_id=1, source_target_pairs={{0,16},{1,17},{2,18},{3,19},{4,20},{5,21},{6,22},{7,23},{8,24},{9,... | collective-permute-start | bytes 1572872 | tf_op jit(solution)/shard_map/ppermute | solution.py:32
  57.8 42.0 %copy-start = (bf16[3,512,256]{2,1,0:T(8,128)(2,1)}, bf16[3,512,256]{2,1,0:T(8,128)(2,1)S(1)}, u32[]{:S(2)}) copy-start(bf16[3,512,256]{2,1,0:T(8,128)(2,1)S(1)} %collective-permute-done.4.refs_1_) | copy-start | bytes 2359300
  63.5 36.3 %copy-start.3 = (bf16[3,512,256]{2,1,0:T(8,128)(2,1)}, bf16[3,512,256]{2,1,0:T(8,128)(2,1)S(1)}, u32[]{:S(2)}) copy-start(bf16[3,512,256]{2,1,0:T(8,128)(2,1)S(1)} %collective-permute-done.6.refs_3_) | copy-start | bytes 2359300
  64.1 21.4 %copy-start.25 = (bf16[2,64,2048]{2,1,0:T(8,128)(2,1)S(1)}, bf16[2,64,2048]{2,1,0:T(8,128)(2,1)}, u32[]{:S(2)}) copy-start(bf16[2,64,2048]{2,1,0:T(8,128)(2,1)} %copy-done.24) | copy-start | bytes 1572868
  64.1 10.7 %collective-permute-start.7 = (bf16[128,256]{1,0:T(8,128)(2,1)S(1)}, bf16[128,256]{1,0:T(8,128)(2,1)S(1)}, u32[]{:S(2)}, u32[]{:S(2)}) collective-permute-start(bf16[128,256]{1,0:T(8,128)(2,1)S(1)} %get-tuple-element.32), channel_id=1, source_target_pairs={{0,4},{1,5},{2,6},{3,7},{4,0},{5,1},{6,2},{7,3},{8,12},{9,13},{10,... | collective-permute-start | bytes 196616 | tf_op jit(solution)/shard_map/ppermute | solution.py:32
  74.7 25.8 %copy-start.5 = (bf16[1,512,512]{2,1,0:T(8,128)(2,1)}, bf16[1,512,512]{2,1,0:T(8,128)(2,1)S(1)}, u32[]{:S(2)}) copy-start(bf16[1,512,512]{2,1,0:T(8,128)(2,1)S(1)} %collective-permute-done.9.refs_2_.refs_10_) | copy-start | bytes 1572868
  74.8 25.7 %copy-start.7 = (bf16[1,512,512]{2,1,0:T(8,128)(2,1)}, bf16[1,512,512]{2,1,0:T(8,128)(2,1)S(1)}, u32[]{:S(2)}) copy-start(bf16[1,512,512]{2,1,0:T(8,128)(2,1)S(1)} %collective-permute-done.8.refs_1_.refs_9_) | copy-start | bytes 1572868
  75.4 10.1 %collective-permute-start.11 = (bf16[64,2048]{1,0:T(8,128)(2,1)S(1)}, bf16[64,2048]{1,0:T(8,128)(2,1)S(1)}, u32[]{:S(2)}, u32[]{:S(2)}) collective-permute-start(bf16[64,2048]{1,0:T(8,128)(2,1)S(1)} %get-tuple-element.35), channel_id=1, source_target_pairs={{0,64},{64,0},{256,320},{320,256},{1,65},{65,1},{257,321},{321,257... | collective-permute-start | bytes 786440 | tf_op jit(solution)/shard_map/ppermute | solution.py:358
  76.8 14.6 %collective-permute-start.18 = (bf16[3,512,256]{2,1,0:T(8,128)(2,1)S(1)}, bf16[3,512,256]{2,1,0:T(8,128)(2,1)S(1)}, u32[]{:S(2)}, u32[]{:S(2)}) collective-permute-start(bf16[3,512,256]{2,1,0:T(8,128)(2,1)S(1)} %get-tuple-element.36.refs_4_), channel_id=1, source_target_pairs={{128,160},{129,161},{130,162},{131,163},{132,164},{133,165},{134,1... | collective-permute-start | bytes 2359304 | tf_op jit(solution)/shard_map/ppermute | solution.py:32
  80.2 19.6 %collective-permute-start.17 = (bf16[3,512,256]{2,1,0:T(8,128)(2,1)S(1)}, bf16[3,512,256]{2,1,0:T(8,128)(2,1)S(1)}, u32[]{:S(2)}, u32[]{:S(2)}) collective-permute-start(bf16[3,512,256]{2,1,0:T(8,128)(2,1)S(1)} %get-tuple-element.36.refs_4_), channel_id=1, source_target_pairs={{128,176},{129,177},{130,178},{131,179},{132,180},{133,181},{134,1... | collective-permute-start | bytes 2359304 | tf_op jit(solution)/shard_map/ppermute | solution.py:32
  83.0 16.7 %collective-permute-start.16 = (bf16[3,512,256]{2,1,0:T(8,128)(2,1)S(1)}, bf16[3,512,256]{2,1,0:T(8,128)(2,1)S(1)}, u32[]{:S(2)}, u32[]{:S(2)}) collective-permute-start(bf16[3,512,256]{2,1,0:T(8,128)(2,1)S(1)} %get-tuple-element.36.refs_4_), channel_id=1, source_target_pairs={{128,144},{129,145},{130,146},{131,147},{132,148},{133,149},{134,1... | collective-permute-start | bytes 2359304 | tf_op jit(solution)/shard_map/ppermute | solution.py:32
  86.3 0.7 collective-permute-start.12
  87.0 16.1 %copy-start.16 = (bf16[64,2048]{1,0:T(8,128)(2,1)}, bf16[64,2048]{1,0:T(8,128)(2,1)S(1)}, u32[]{:S(2)}) copy-start(bf16[64,2048]{1,0:T(8,128)(2,1)S(1)} %collective-permute-done.12.mine.in1m) | copy-start | bytes 786436
  87.0 12.8 %collective-permute-start.13 = (bf16[64,2048]{1,0:T(8,128)(2,1)S(1)}, bf16[64,2048]{1,0:T(8,128)(2,1)S(1)}, u32[]{:S(2)}, u32[]{:S(2)}) collective-permute-start(bf16[64,2048]{1,0:T(8,128)(2,1)S(1)} %collective-permute-done.12.mine.in1m), channel_id=1, source_target_pairs={{128,192},{192,128},{129,193},{193,129},{130,194},{194,130},{131,1... | collective-permute-start | bytes 786440 | tf_op jit(solution)/shard_map/ppermute | solution.py:358
  101.0 2.0 %collective-permute-start.19 = (bf16[64,2048]{1,0:T(8,128)(2,1)S(1)}, bf16[64,2048]{1,0:T(8,128)(2,1)S(1)}, u32[]{:S(2)}, u32[]{:S(2)}) collective-permute-start(bf16[64,2048]{1,0:T(8,128)(2,1)S(1)} %get-tuple-element.38), channel_id=1, source_target_pairs={{128,192},{192,128},{129,193},{193,129},{130,194},{194,130},{131,1... | collective-permute-start | bytes 786440 | tf_op jit(solution)/shard_map/ppermute | solution.py:358
  101.7 34.6 %collective-permute-start.14 = (bf16[64,2048]{1,0:T(8,128)(2,1)S(1)}, bf16[64,2048]{1,0:T(8,128)(2,1)}, u32[]{:S(2)}, u32[]{:S(2)}) collective-permute-start(bf16[64,2048]{1,0:T(8,128)(2,1)S(1)} %get-tuple-element.41), channel_id=1, source_target_pairs={{256,384},{257,385},{258,386},{259,387},{260,388},{261,389},{262,3... | collective-permute-start | bytes 786440 | tf_op jit(solution)/shard_map/ppermute | solution.py:406
  104.1 42.2 %collective-permute-start.21 = (bf16[64,2048]{1,0:T(8,128)(2,1)S(1)}, bf16[64,2048]{1,0:T(8,128)(2,1)}, u32[]{:S(2)}, u32[]{:S(2)}) collective-permute-start(bf16[64,2048]{1,0:T(8,128)(2,1)S(1)} %fusion.2), channel_id=1, source_target_pairs={{128,384},{129,385},{130,386},{131,387},{132,388},{133,389},{134,3... | collective-permute-start | bytes 786440 | tf_op jit(solution)/shard_map/ppermute | solution.py:420
  136.4 12.2 %collective-permute-start.15 = (bf16[64,2048]{1,0:T(8,128)(2,1)}, bf16[64,2048]{1,0:T(8,128)(2,1)}, u32[]{:S(2)}, u32[]{:S(2)}) collective-permute-start(bf16[64,2048]{1,0:T(8,128)(2,1)} %collective-permute-done.14.mine.in3m), channel_id=1, source_target_pairs={{384,448},{448,384},{385,449},{449,385},{386,450},{450,386},{387,4... | collective-permute-start | bytes 786440 | tf_op jit(solution)/shard_map/ppermute | solution.py:358
  146.3 12.7 %collective-permute-start.22 = (bf16[64,2048]{1,0:T(8,128)(2,1)}, bf16[64,2048]{1,0:T(8,128)(2,1)}, u32[]{:S(2)}, u32[]{:S(2)}) collective-permute-start(bf16[64,2048]{1,0:T(8,128)(2,1)} %collective-permute-done.21.mem_mine), channel_id=1, source_target_pairs={{384,448},{448,384},{385,449},{449,385},{386,450},{450,386},{387,4... | collective-permute-start | bytes 786440 | tf_op jit(solution)/shard_map/ppermute | solution.py:358
  164.7 3.8 %collective-permute-start.23 = (bf16[128,2048]{1,0:T(8,128)(2,1)S(1)}, bf16[128,2048]{1,0:T(8,128)(2,1)S(1)}, u32[]{:S(2)}, u32[]{:S(2)}) collective-permute-start(bf16[128,2048]{1,0:T(8,128)(2,1)S(1)} %shard_map.69.own), channel_id=1, source_target_pairs={{384,448},{385,449},{386,450},{387,451},{388,452},{389,453},{390,4... | collective-permute-start | bytes 1572872 | tf_op jit(solution)/shard_map/ppermute | solution.py:445
  166.0 0.7 collective-permute-start.20
  (28 other events, 135.0 us)

commit v10 on v9

--- a/solution.py
+++ b/solution.py
@@ -38,8 +38,8 @@
     )
 
 
-def beside(array):
-    return moved(array, EVEN, lambda core, y, x: (y, x ^ 1))
+def beside(array, cubes=EVEN):
+    return moved(array, cubes, lambda core, y, x: (y, x ^ 1))
 
 
 def dot(a, b):
@@ -151,30 +151,38 @@
         out_other[:, at] = t3[i, second, :].astype(out_other.dtype)
 
 
-def norm_kernel(scal, gains, own, got, h3, limits):
-    @pl.when(lax.rem(scal[2], 2) == 0)
-    def _():
+def norm_kernel(scal, gains, own, got0, got2, h3):
+    count = own.shape[0]
+
+    def put(part, ref):
         gain = gains[pl.ds(scal[2], 1), :]
-        count = h3.shape[1] // 2
-        for part, ref in enumerate((own, got)):
-            for at in range(0, count, 64):
-                h = rms(ref[at:at + 64, :].astype(F32), gain)
-                to = part * count + at
-                for i in range(16):
-                    h3[i, to:to + 64, :] = h[:, i * 128:(i + 1) * 128]
-            limits[part] = ref[count:, :128].astype(F32)
-
-
-def first_kernel(scal, h3, limits, *refs):
+        for at in range(0, count, 64):
+            h = rms(ref[at:at + 64, :].astype(F32), gain)
+            to = part * count + at
+            for i in range(16):
+                h3[i, to:to + 64, :] = h[:, i * 128:(i + 1) * 128]
+
+    @pl.when(scal[2] == 0)
+    def _():
+        put(0, own)
+        put(1, got0)
+
+    @pl.when(scal[2] == 2)
+    def _():
+        put(0, own)
+        put(1, got2)
+
+
+def first_kernel(scal, h3, own_keys, got_keys, *refs):
     pieces, (own, sent, space, sems) = refs[:SIDE], refs[SIDE:]
 
     @pl.when(lax.rem(scal[2], 2) == 0)
     def _():
         q, k, v = project(scal, h3, [pieces], (0, 1, 2), space, sems)()
         count = own.shape[0]
-        for part, out in enumerate((own, sent)):
+        for part, (keys, out) in enumerate(((own_keys, own), (got_keys, sent))):
             at = slice(part * count, (part + 1) * count)
-            live = mask(scal, limits[part, 0:1, :], limits[part, 1:2, :], count)
+            live = mask(scal, keys[0:1, :], keys[1:2, :], count)
             out[...] = attend(live, q[at], k[at], v[at])
 
 
@@ -241,7 +249,7 @@
 
 VMEM = pl.BlockSpec(memory_space=pltpu.VMEM)
 SMEM = pl.BlockSpec(memory_space=pltpu.SMEM)
-HBM = pl.BlockSpec(memory_space=pltpu.HBM)
+ANY = pl.BlockSpec(memory_space=pl.ANY)
 
 
 def call(kernel, scal, operands, outs, scratch=(), pieces=(), fetches=(), flops=0):
@@ -252,10 +260,10 @@
     return pl.pallas_call(
         kernel,
         out_shape=outs,
-        in_specs=[SMEM] + [VMEM] * len(operands) + [HBM] * len(pieces),
+        in_specs=[SMEM] + [VMEM] * len(operands) + [ANY] * len(pieces),
         out_specs=jax.tree.map(lambda _: VMEM, outs),
         scratch_shapes=shapes,
-        compiler_params=pltpu.CompilerParams(vmem_limit_bytes=16 * 1024 * 1024),
+        compiler_params=pltpu.CompilerParams(vmem_limit_bytes=44 * 1024 * 1024),
         cost_estimate=pl.CostEstimate(flops=flops, bytes_accessed=size, transcendentals=0),
     )(scal, *operands, *pieces)
 
@@ -305,6 +313,7 @@
     sent = jnp.broadcast_to(halves[:, None], (2, SIDE) + halves.shape[1:])
     sent = sent.reshape((2 * SIDE,) + halves.shape[1:])
     got = lax.all_to_all(sent, ("core", "zl"), 0, 0, tiled=True)
+    got, late = lax.optimization_barrier((got, late))
     got = got.reshape(2, SIDE, pair, depth, width // 2).transpose(0, 2, 1, 3, 4)
     got = got.reshape(2 * pair, SIDE * depth, width // 2)
     near = turns(got, False)
@@ -319,7 +328,6 @@
         return lax.dynamic_slice(block, (0, 0, at * half), (3,) + block.shape[1:2] + (half,))
 
     kept, sent = columns(side), columns(across)
-    sent, late = lax.optimization_barrier((sent, late))
     first = [kept, exchange(sent, True, 1), exchange(sent, True, 3), exchange(kept, True, FAR)]
     return first, block[:3, :, half:], block[3:], early, late
 
@@ -358,11 +366,11 @@
         return lax.ppermute(array, SECTION, pairs)
 
     count, width = 2 * rows, mine.shape[1]
-    limits = jnp.broadcast_to(key_lengths.astype(BF16)[:, None], (2, width))
-    limits = jnp.concatenate([limits, jnp.zeros((14, width), BF16)], axis=0)
-    shared = jnp.concatenate([source.reshape(count, width), limits], axis=0)
-    parts_a, rest_b, rest_o, (scal, shared), shared_got = gather(
-        section_weights, (scal, shared), beside(shared)
+    keys = jnp.broadcast_to(key_lengths.astype(F32)[:, None], (2, 128))
+    keys = jnp.concatenate([keys, jnp.zeros((6, 128), F32)], axis=0)
+    streams = (beside(encoder_embed, (0,)), beside(decoder_embed, (2,)))
+    parts_a, rest_b, rest_o, (scal, source, keys_got), (got0, got2) = gather(
+        section_weights, (scal, source, beside(keys)), streams
     )
     tile = parts_a[0].shape[1:]
     square = rest_o.shape[1:]
@@ -375,19 +383,23 @@
     quarter = jax.ShapeDtypeStruct((count, half // 2), BF16)
     out_fetch = (SIDE,) + square
 
-    h3, limits = call(
+    h3 = call(
         norm_kernel,
         scal,
-        [norm_gains, shared, shared_got],
-        (
-            jax.ShapeDtypeStruct((16, 2 * count, 128), BF16),
-            jax.ShapeDtypeStruct((2, 16, 128), F32),
-        ),
+        [norm_gains] + [a.reshape(count, width) for a in (source, got0, got2)],
+        jax.ShapeDtypeStruct((16, 2 * count, 128), BF16),
     )
     rest_o, h3 = lax.optimization_barrier((rest_o, h3))
     parts_o = turns(rest_o, True)
     mixed, mixed_sent = call(
-        first_kernel, scal, [h3, limits], (quarter, quarter), (), parts_a, [(4, 3) + tile], 3 * work
+        first_kernel,
+        scal,
+        [h3, keys, keys_got],
+        (quarter, quarter),
+        (),
+        parts_a,
+        [(4, 3) + tile],
+        3 * work,
     )
     rest_b, mixed = lax.optimization_barrier((rest_b, mixed))
     kept, sent = call(

time: 172 us -> 171 us (level)
  waiting for transfers between devices: 74 us -> 78.7 us
  starting transfers between devices: 63 us -> 58.6 us
  local copies, waits for them, and re-layouts: 16.6 us -> 14.5 us
    ppermute x5, starting transfers between devices: 14.2 us -> 8.3 us  [swapped(): return lax.ppermute(array, SECTION, pairs)]
    ppermute x1, waiting for transfers between devices: 30.9 us -> 36.5 us  [on_device(): in3 = lax.ppermute(first, 'zh', [(2, 3)])]
    unnamed x70 -> x74, local copies, waits for them, and re-layouts: 10.9 us -> 9.04 us
    ppermute x14 -> x16, starting transfers between devices: 38 us -> 39.4 us  [moved(): return lax.ppermute(array, AXES, pairs)]
    ppermute x14 -> x16, waiting for transfers between devices: 31.6 us -> 32 us  [moved(): return lax.ppermute(array, AXES, pairs)]
  transfers between devices with their start and end apart: 25 -> 27, of which waited for: 10 -> 10; matrix products, arithmetic and copies ran while one was open for 4% -> 4% of each run, Pallas kernels for 2% -> 2%
where the time goes in v10:
time: 171 us; the launch traced here: 170 us
  waiting for transfers between devices  78.7 us (46%)
  starting transfers between devices  58.6 us (34%)
  local copies, waits for them, and re-layouts  14.5 us (8%)
  Pallas kernels  12.7 us (7%)
  other arithmetic  4.35 us (3%)
    ppermute x16, starting transfers between devices, moved(): return lax.ppermute(array, AXES, pairs)  39.4 us
    ppermute x1, waiting for transfers between devices, on_device(): in3 = lax.ppermute(first, 'zh', [(2, 3)])  36.5 us
    ppermute x16, waiting for transfers between devices, moved(): return lax.ppermute(array, AXES, pairs)  32 us
    pallas_call x7, Pallas kernels, call(): pl.pallas_call(kernel, out_shape=outs, in_specs=[SMEM] + [VMEM] * len(ope...  12.7 us
    unnamed x74, local copies, waits for them, and re-layouts  9.04 us
    all_to_all x1, waiting for transfers between devices, gather(): got = lax.all_to_all(sent, ('core', 'zl'), 0, 0, tiled=True)  8.49 us
    ppermute x5, starting transfers between devices, swapped(): return lax.ppermute(array, SECTION, pairs)  8.3 us
    all_to_all x1, starting transfers between devices, gather(): got = lax.all_to_all(sent, ('core', 'zl'), 0, 0, tiled=True)  5.62 us
  transfers between devices with their start and end apart: 27, of which 10 were waited for; matrix products, arithmetic and copies ran while one was open for 4% of the time, Pallas kernels for 2%

profile of v10, /device:TPU:481, one launch (start us, length us, event | category | flops | bytes accessed | tf_op | source)
XLA Modules:
  0.0 169.7 jit_solution(9153004455739395330)
XLA Ops:
  2.0 5.6 %all-to-all-start = ((bf16[8,2,32,512]{3,2,1,0:T(8,128)(2,1)}), bf16[8,2,32,512]{3,2,1,0:T(8,128)(2,1)S(1)}, u32[]{:S(2)}, u32[]{:S(2)}) async-start(bf16[8,2,32,512]{3,2,1,0:T(8,128)(2,1)} %bitcast.1), calls=%async_computation | async-start | bytes 1048576 | tf_op jit(solution)/shard_map/all_to_all | solution.py:315
  9.1 8.5 %all-to-all-done = bf16[8,2,32,512]{3,2,1,0:T(8,128)(2,1)S(1)} async-done(((bf16[8,2,32,512]{3,2,1,0:T(8,128)(2,1)}), bf16[8,2,32,512]{3,2,1,0:T(8,128)(2,1)S(1)}, u32[]{:S(2)}, u32[]{:S(2)}) %all-to-all-start) | async-done | bytes 524320 | tf_op jit(solution)/shard_map/all_to_all | solution.py:315
  17.6 4.8 %collective-permute-start.5 = (bf16[4,128,512]{2,1,0:T(8,128)(2,1)S(1)}, bf16[4,128,512]{2,1,0:T(8,128)(2,1)S(1)}, u32[]{:S(2)}, u32[]{:S(2)}) collective-permute-start(bf16[4,128,512]{2,1,0:T(8,128)(2,1)S(1)} %bitcast.28), channel_id=1, source_target_pairs={{0,8},{1,9},{2,10},{3,11},{4,12},{5,13},{6,14},{7,15},{8,0},{9,1},... | collective-permute-start | bytes 1572872 | tf_op jit(solution)/shard_map/ppermute | solution.py:32
  22.4 2.7 %collective-permute-start.4 = (bf16[4,128,512]{2,1,0:T(8,128)(2,1)S(1)}, bf16[4,128,512]{2,1,0:T(8,128)(2,1)}, u32[]{:S(2)}, u32[]{:S(2)}) collective-permute-start(bf16[4,128,512]{2,1,0:T(8,128)(2,1)S(1)} %bitcast.29), channel_id=1, source_target_pairs={{0,12},{1,13},{2,14},{3,15},{4,8},{5,9},{6,10},{7,11},{8,4},{9,5},... | collective-permute-start | bytes 1572872 | tf_op jit(solution)/shard_map/ppermute | solution.py:32
  25.1 1.9 %collective-permute-start.2 = (bf16[4,128,512]{2,1,0:T(8,128)(2,1)S(1)}, bf16[4,128,512]{2,1,0:T(8,128)(2,1)}, u32[]{:S(2)}, u32[]{:S(2)}) collective-permute-start(bf16[4,128,512]{2,1,0:T(8,128)(2,1)S(1)} %bitcast.30), channel_id=1, source_target_pairs={{0,4},{1,5},{2,6},{3,7},{4,0},{5,1},{6,2},{7,3},{8,12},{9,13},{10,... | collective-permute-start | bytes 1572872 | tf_op jit(solution)/shard_map/ppermute | solution.py:32
  29.7 2.5 %stack.27.scal = s32[9]{0:T(128)S(1)} concatenate(s32[1]{0:T(128)} %bitcast.5, s32[1]{0:T(128)} %bitcast.6, s32[1]{0:T(128)} %bitcast.7, s32[1]{0:T(128)} %bitcast.8, s32[1]{0:T(128)} %get-tuple-element.53, s32[1]{0:T(128)} %get-tuple-element.54, s32[1]{0:T(128)} %bitcast.9, s32[1]{0:T(128)} %get-tuple-element.50, s32[1]{0:T(128)} %get-tuple-element.49), dimensions={0} | concatenate | bytes 72 | tf_op jit(solution)/shard_map/stack | solution.py:343
  32.2 3.2 %collective-permute-done.2 = bf16[4,128,512]{2,1,0:T(8,128)(2,1)} collective-permute-done((bf16[4,128,512]{2,1,0:T(8,128)(2,1)S(1)}, bf16[4,128,512]{2,1,0:T(8,128)(2,1)}, u32[]{:S(2)}, u32[]{:S(2)}) %collective-permute-start.2) | collective-permute-done | bytes 524320 | tf_op jit(solution)/shard_map/ppermute | solution.py:32
  35.5 1.3 pad_maximum_fusion
  37.0 4.5 %collective-permute-start.7 = (bf16[3,512,256]{2,1,0:T(8,128)(2,1)S(1)}, bf16[3,512,256]{2,1,0:T(8,128)(2,1)S(1)}, u32[]{:S(2)}, u32[]{:S(2)}) collective-permute-start(bf16[3,512,256]{2,1,0:T(8,128)(2,1)S(1)} %get-tuple-element.45), channel_id=1, source_target_pairs={{0,48},{1,49},{2,50},{3,51},{4,52},{5,53},{6,54},{7,55},{8,56},{9,... | collective-permute-start | bytes 2359304 | tf_op jit(solution)/shard_map/ppermute | solution.py:32
  41.5 1.9 %collective-permute-start.6 = (bf16[3,512,256]{2,1,0:T(8,128)(2,1)S(1)}, bf16[3,512,256]{2,1,0:T(8,128)(2,1)S(1)}, u32[]{:S(2)}, u32[]{:S(2)}) collective-permute-start(bf16[3,512,256]{2,1,0:T(8,128)(2,1)S(1)} %get-tuple-element.45), channel_id=1, source_target_pairs={{0,16},{1,17},{2,18},{3,19},{4,20},{5,21},{6,22},{7,23},{8,24},{9,... | collective-permute-start | bytes 2359304 | tf_op jit(solution)/shard_map/ppermute | solution.py:32
  43.5 3.3 %collective-permute-start.8 = (bf16[3,512,256]{2,1,0:T(8,128)(2,1)S(1)}, bf16[3,512,256]{2,1,0:T(8,128)(2,1)S(1)}, u32[]{:S(2)}, u32[]{:S(2)}) collective-permute-start(bf16[3,512,256]{2,1,0:T(8,128)(2,1)S(1)} %get-tuple-element.46.refs_0_), channel_id=1, source_target_pairs={{0,32},{1,33},{2,34},{3,35},{4,36},{5,37},{6,38},{7,39},{8,40},{9,... | collective-permute-start | bytes 2359304 | tf_op jit(solution)/shard_map/ppermute | solution.py:32
  47.4 3.5 %collective-permute-start.12 = (bf16[1,512,512]{2,1,0:T(8,128)(2,1)S(1)}, bf16[1,512,512]{2,1,0:T(8,128)(2,1)S(1)}, u32[]{:S(2)}, u32[]{:S(2)}) collective-permute-start(bf16[1,512,512]{2,1,0:T(8,128)(2,1)S(1)} %slice.13.refs_0_.refs_8_), channel_id=1, source_target_pairs={{0,32},{1,33},{2,34},{3,35},{4,36},{5,37},{6,38},{7,39},{8,40},{9,... | collective-permute-start | bytes 1572872 | tf_op jit(solution)/shard_map/ppermute | solution.py:32
  50.9 2.8 %collective-permute-start.11 = (bf16[1,512,512]{2,1,0:T(8,128)(2,1)S(1)}, bf16[1,512,512]{2,1,0:T(8,128)(2,1)S(1)}, u32[]{:S(2)}, u32[]{:S(2)}) collective-permute-start(bf16[1,512,512]{2,1,0:T(8,128)(2,1)S(1)} %slice.13.refs_0_.refs_8_), channel_id=1, source_target_pairs={{0,48},{1,49},{2,50},{3,51},{4,52},{5,53},{6,54},{7,55},{8,56},{9,... | collective-permute-start | bytes 1572872 | tf_op jit(solution)/shard_map/ppermute | solution.py:32
  53.7 2.5 %collective-permute-start.10 = (bf16[1,512,512]{2,1,0:T(8,128)(2,1)S(1)}, bf16[1,512,512]{2,1,0:T(8,128)(2,1)S(1)}, u32[]{:S(2)}, u32[]{:S(2)}) collective-permute-start(bf16[1,512,512]{2,1,0:T(8,128)(2,1)S(1)} %slice.13.refs_0_.refs_8_), channel_id=1, source_target_pairs={{0,16},{1,17},{2,18},{3,19},{4,20},{5,21},{6,22},{7,23},{8,24},{9,... | collective-permute-start | bytes 1572872 | tf_op jit(solution)/shard_map/ppermute | solution.py:32
  56.3 6.7 %collective-permute-done.8.refs_3_ = bf16[3,512,256]{2,1,0:T(8,128)(2,1)S(1)} collective-permute-done((bf16[3,512,256]{2,1,0:T(8,128)(2,1)S(1)}, bf16[3,512,256]{2,1,0:T(8,128)(2,1)S(1)}, u32[]{:S(2)}, u32[]{:S(2)}) %collective-permute-start.8) | collective-permute-done | bytes 786464 | tf_op jit(solution)/shard_map/ppermute | solution.py:32
  64.4 4.2 %collective-permute-done.12.refs_3_.refs_11_ = bf16[1,512,512]{2,1,0:T(8,128)(2,1)S(1)} collective-permute-done((bf16[1,512,512]{2,1,0:T(8,128)(2,1)S(1)}, bf16[1,512,512]{2,1,0:T(8,128)(2,1)S(1)}, u32[]{:S(2)}, u32[]{:S(2)}) %collective-permute-start.12) | collective-permute-done | bytes 524320 | tf_op jit(solution)/shard_map/ppermute | solution.py:32
  68.6 5.6 %collective-permute-done.11.refs_2_.refs_10_ = bf16[1,512,512]{2,1,0:T(8,128)(2,1)S(1)} collective-permute-done((bf16[1,512,512]{2,1,0:T(8,128)(2,1)S(1)}, bf16[1,512,512]{2,1,0:T(8,128)(2,1)S(1)}, u32[]{:S(2)}, u32[]{:S(2)}) %collective-permute-start.11) | collective-permute-done | bytes 524320 | tf_op jit(solution)/shard_map/ppermute | solution.py:32
  76.3 3.4 %collective-permute-start.20 = (bf16[3,512,256]{2,1,0:T(8,128)(2,1)S(1)}, bf16[3,512,256]{2,1,0:T(8,128)(2,1)S(1)}, u32[]{:S(2)}, u32[]{:S(2)}) collective-permute-start(bf16[3,512,256]{2,1,0:T(8,128)(2,1)S(1)} %get-tuple-element.36.refs_4_), channel_id=1, source_target_pairs={{128,160},{129,161},{130,162},{131,163},{132,164},{133,165},{134,1... | collective-permute-start | bytes 2359304 | tf_op jit(solution)/shard_map/ppermute | solution.py:32
  79.7 2.8 %collective-permute-start.19 = (bf16[3,512,256]{2,1,0:T(8,128)(2,1)S(1)}, bf16[3,512,256]{2,1,0:T(8,128)(2,1)S(1)}, u32[]{:S(2)}, u32[]{:S(2)}) collective-permute-start(bf16[3,512,256]{2,1,0:T(8,128)(2,1)S(1)} %get-tuple-element.36.refs_4_), channel_id=1, source_target_pairs={{128,176},{129,177},{130,178},{131,179},{132,180},{133,181},{134,1... | collective-permute-start | bytes 2359304 | tf_op jit(solution)/shard_map/ppermute | solution.py:32
  82.5 2.5 %collective-permute-start.18 = (bf16[3,512,256]{2,1,0:T(8,128)(2,1)S(1)}, bf16[3,512,256]{2,1,0:T(8,128)(2,1)S(1)}, u32[]{:S(2)}, u32[]{:S(2)}) collective-permute-start(bf16[3,512,256]{2,1,0:T(8,128)(2,1)S(1)} %get-tuple-element.36.refs_4_), channel_id=1, source_target_pairs={{128,144},{129,145},{130,146},{131,147},{132,148},{133,149},{134,1... | collective-permute-start | bytes 2359304 | tf_op jit(solution)/shard_map/ppermute | solution.py:32
  87.1 3.7 %collective-permute-done.20.refs_7_ = bf16[3,512,256]{2,1,0:T(8,128)(2,1)S(1)} collective-permute-done((bf16[3,512,256]{2,1,0:T(8,128)(2,1)S(1)}, bf16[3,512,256]{2,1,0:T(8,128)(2,1)S(1)}, u32[]{:S(2)}, u32[]{:S(2)}) %collective-permute-start.20) | collective-permute-done | bytes 786464 | tf_op jit(solution)/shard_map/ppermute | solution.py:32
  90.8 8.4 %collective-permute-done.19.refs_6_ = bf16[3,512,256]{2,1,0:T(8,128)(2,1)S(1)} collective-permute-done((bf16[3,512,256]{2,1,0:T(8,128)(2,1)S(1)}, bf16[3,512,256]{2,1,0:T(8,128)(2,1)S(1)}, u32[]{:S(2)}, u32[]{:S(2)}) %collective-permute-start.19) | collective-permute-done | bytes 786464 | tf_op jit(solution)/shard_map/ppermute | solution.py:32
  101.2 1.3 collective-permute-start.16
  103.6 1.3 collective-permute-start.23
  104.9 36.5 %collective-permute-done.16.mine.in3m = bf16[64,2048]{1,0:T(8,128)(2,1)} collective-permute-done((bf16[64,2048]{1,0:T(8,128)(2,1)S(1)}, bf16[64,2048]{1,0:T(8,128)(2,1)}, u32[]{:S(2)}, u32[]{:S(2)}) %collective-permute-start.16) | collective-permute-done | bytes 262176 | tf_op jit(solution)/shard_map/ppermute | solution.py:418
  141.4 4.4 %collective-permute-start.17 = (bf16[64,2048]{1,0:T(8,128)(2,1)}, bf16[64,2048]{1,0:T(8,128)(2,1)}, u32[]{:S(2)}, u32[]{:S(2)}) collective-permute-start(bf16[64,2048]{1,0:T(8,128)(2,1)} %collective-permute-done.16.mine.in3m), channel_id=1, source_target_pairs={{384,448},{448,384},{385,449},{449,385},{386,450},{450,386},{387,4... | collective-permute-start | bytes 786440 | tf_op jit(solution)/shard_map/ppermute | solution.py:366
  145.8 1.9 %collective-permute-start.24 = (bf16[64,2048]{1,0:T(8,128)(2,1)}, bf16[64,2048]{1,0:T(8,128)(2,1)}, u32[]{:S(2)}, u32[]{:S(2)}) collective-permute-start(bf16[64,2048]{1,0:T(8,128)(2,1)} %collective-permute-done.23.mem_mine), channel_id=1, source_target_pairs={{384,448},{448,384},{385,449},{449,385},{386,450},{450,386},{387,4... | collective-permute-start | bytes 786440 | tf_op jit(solution)/shard_map/ppermute | solution.py:366
  155.5 2.6 %shard_map.68.q = bf16[128,512]{1,0:T(8,128)(2,1)S(1)} custom-call(s32[9]{0:T(128)S(1)} %stack.27.scal, f32[5,2048]{1,0:T(8,128)S(1)} %copy-done.24, bf16[64,2048]{1,0:T(8,128)(2,1)} %collective-permute-done.16.mine.in3m, bf16[64,2048]{1,0:T(8,128)(2,1)} %collective-permute-done.17.other.in3o, bf16[3,512,256]{2,1,0:T(8,128)(2,1)S(1)} %get-tuple-element.46.refs_0_, ...), custom_call_target="tpu_custom_call" | custom-call | flops 268435456 | bytes 8953856 | tf_op jit(solution)/shard_map/pallas_call | solution.py:260
  158.3 5.6 %shard_map.69.own = bf16[128,2048]{1,0:T(8,128)(2,1)S(1)} custom-call(s32[9]{0:T(128)S(1)} %stack.27.scal, bf16[128,512]{1,0:T(8,128)(2,1)S(1)} %shard_map.68.q, bf16[64,2048]{1,0:T(8,128)(2,1)} %collective-permute-done.23.mem_mine, bf16[64,2048]{1,0:T(8,128)(2,1)} %collective-permute-done.24.mem_other, bf16[3,512,256]{2,1,0:T(8,128)(2,1)S(1)} %get-tuple-element.46.refs_0_, ...), custom_call_target="tpu_custom_call" | custom-call | flops 805306368 | bytes 9043968 | tf_op jit(solution)/shard_map/pallas_call | solution.py:260
  163.8 1.3 collective-permute-start.25
  165.9 1.7 %collective-permute-done.25.got = bf16[128,2048]{1,0:T(8,128)(2,1)S(1)} collective-permute-done((bf16[128,2048]{1,0:T(8,128)(2,1)S(1)}, bf16[128,2048]{1,0:T(8,128)(2,1)S(1)}, u32[]{:S(2)}, u32[]{:S(2)}) %collective-permute-start.25) | collective-permute-done | bytes 524320 | tf_op jit(solution)/shard_map/ppermute | solution.py:457
  167.7 2.1 %shard_map.70 = bf16[2,64,2048]{2,1,0:T(8,128)(2,1)} custom-call(s32[9]{0:T(128)S(1)} %stack.27.scal, bf16[64,2048]{1,0:T(8,128)(2,1)S(1)} %copy-done.23, bf16[64,2048]{1,0:T(8,128)(2,1)S(1)} %dynamic-slice_bitcast_fusion.other, bf16[64,2048]{1,0:T(8,128)(2,1)S(1)} %copy-done.20, bf16[64,2048]{1,0:T(8,128)(2,1)S(1)} %copy-done.22, ...), custom_call_target="tpu_custom_call" | custom-call | bytes 3145728 | tf_op jit(solution)/shard_map/pallas_call | solution.py:260
  (124 shorter events, 23.8 us)
Async XLA Ops:
  0.0 27.0 %copy-start.35 = (s32[2]{0:T(128)S(1)}, s32[2]{0:T(128)}, u32[]{:S(2)}) copy-start(s32[2]{0:T(128)} %param.11) | copy-start | bytes 28
  0.0 27.1 %copy-start.36 = (s32[2]{0:T(128)S(1)}, s32[2]{0:T(128)}, u32[]{:S(2)}) copy-start(s32[2]{0:T(128)} %param.10) | copy-start | bytes 28
  2.0 15.6 %all-to-all-start = ((bf16[8,2,32,512]{3,2,1,0:T(8,128)(2,1)}), bf16[8,2,32,512]{3,2,1,0:T(8,128)(2,1)S(1)}, u32[]{:S(2)}, u32[]{:S(2)}) async-start(bf16[8,2,32,512]{3,2,1,0:T(8,128)(2,1)} %bitcast.1), calls=%async_computation | async-start | bytes 1048576 | tf_op jit(solution)/shard_map/all_to_all | solution.py:315
  7.6 1.4 collective-permute-start
  8.3 0.7 collective-permute-start.1
  9.0 26.4 %copy-start.25 = (bf16[2,64,2048]{2,1,0:T(8,128)(2,1)}, bf16[2,64,2048]{2,1,0:T(8,128)(2,1)S(1)}, u32[]{:S(2)}) copy-start(bf16[2,64,2048]{2,1,0:T(8,128)(2,1)S(1)} %collective-permute-done) | copy-start | bytes 1572868
  17.6 17.9 %collective-permute-start.5 = (bf16[4,128,512]{2,1,0:T(8,128)(2,1)S(1)}, bf16[4,128,512]{2,1,0:T(8,128)(2,1)S(1)}, u32[]{:S(2)}, u32[]{:S(2)}) collective-permute-start(bf16[4,128,512]{2,1,0:T(8,128)(2,1)S(1)} %bitcast.28), channel_id=1, source_target_pairs={{0,8},{1,9},{2,10},{3,11},{4,12},{5,13},{6,14},{7,15},{8,0},{9,1},... | collective-permute-start | bytes 1572872 | tf_op jit(solution)/shard_map/ppermute | solution.py:32
  22.4 13.0 %collective-permute-start.4 = (bf16[4,128,512]{2,1,0:T(8,128)(2,1)S(1)}, bf16[4,128,512]{2,1,0:T(8,128)(2,1)}, u32[]{:S(2)}, u32[]{:S(2)}) collective-permute-start(bf16[4,128,512]{2,1,0:T(8,128)(2,1)S(1)} %bitcast.29), channel_id=1, source_target_pairs={{0,12},{1,13},{2,14},{3,15},{4,8},{5,9},{6,10},{7,11},{8,4},{9,5},... | collective-permute-start | bytes 1572872 | tf_op jit(solution)/shard_map/ppermute | solution.py:32
  25.1 10.3 %collective-permute-start.2 = (bf16[4,128,512]{2,1,0:T(8,128)(2,1)S(1)}, bf16[4,128,512]{2,1,0:T(8,128)(2,1)}, u32[]{:S(2)}, u32[]{:S(2)}) collective-permute-start(bf16[4,128,512]{2,1,0:T(8,128)(2,1)S(1)} %bitcast.30), channel_id=1, source_target_pairs={{0,4},{1,5},{2,6},{3,7},{4,0},{5,1},{6,2},{7,3},{8,12},{9,13},{10,... | collective-permute-start | bytes 1572872 | tf_op jit(solution)/shard_map/ppermute | solution.py:32
  27.2 5.0 %collective-permute-start.3 = (f32[8,128]{1,0:T(8,128)S(1)}, f32[8,128]{1,0:T(8,128)S(1)}, u32[]{:S(2)}, u32[]{:S(2)}) collective-permute-start(f32[8,128]{1,0:T(8,128)S(1)} %concatenate.9.own_keys), channel_id=1, source_target_pairs={{0,4},{1,5},{2,6},{3,7},{4,0},{5,1},{6,2},{7,3},{8,12},{9,13},{10,... | collective-permute-start | bytes 12296 | tf_op jit(solution)/shard_map/ppermute | solution.py:32
  37.0 16.7 %collective-permute-start.7 = (bf16[3,512,256]{2,1,0:T(8,128)(2,1)S(1)}, bf16[3,512,256]{2,1,0:T(8,128)(2,1)S(1)}, u32[]{:S(2)}, u32[]{:S(2)}) collective-permute-start(bf16[3,512,256]{2,1,0:T(8,128)(2,1)S(1)} %get-tuple-element.45), channel_id=1, source_target_pairs={{0,48},{1,49},{2,50},{3,51},{4,52},{5,53},{6,54},{7,55},{8,56},{9,... | collective-permute-start | bytes 2359304 | tf_op jit(solution)/shard_map/ppermute | solution.py:32
  41.5 14.7 %collective-permute-start.6 = (bf16[3,512,256]{2,1,0:T(8,128)(2,1)S(1)}, bf16[3,512,256]{2,1,0:T(8,128)(2,1)S(1)}, u32[]{:S(2)}, u32[]{:S(2)}) collective-permute-start(bf16[3,512,256]{2,1,0:T(8,128)(2,1)S(1)} %get-tuple-element.45), channel_id=1, source_target_pairs={{0,16},{1,17},{2,18},{3,19},{4,20},{5,21},{6,22},{7,23},{8,24},{9,... | collective-permute-start | bytes 2359304 | tf_op jit(solution)/shard_map/ppermute | solution.py:32
  43.5 19.5 %collective-permute-start.8 = (bf16[3,512,256]{2,1,0:T(8,128)(2,1)S(1)}, bf16[3,512,256]{2,1,0:T(8,128)(2,1)S(1)}, u32[]{:S(2)}, u32[]{:S(2)}) collective-permute-start(bf16[3,512,256]{2,1,0:T(8,128)(2,1)S(1)} %get-tuple-element.46.refs_0_), channel_id=1, source_target_pairs={{0,32},{1,33},{2,34},{3,35},{4,36},{5,37},{6,38},{7,39},{8,40},{9,... | collective-permute-start | bytes 2359304 | tf_op jit(solution)/shard_map/ppermute | solution.py:32
  47.4 21.2 %collective-permute-start.12 = (bf16[1,512,512]{2,1,0:T(8,128)(2,1)S(1)}, bf16[1,512,512]{2,1,0:T(8,128)(2,1)S(1)}, u32[]{:S(2)}, u32[]{:S(2)}) collective-permute-start(bf16[1,512,512]{2,1,0:T(8,128)(2,1)S(1)} %slice.13.refs_0_.refs_8_), channel_id=1, source_target_pairs={{0,32},{1,33},{2,34},{3,35},{4,36},{5,37},{6,38},{7,39},{8,40},{9,... | collective-permute-start | bytes 1572872 | tf_op jit(solution)/shard_map/ppermute | solution.py:32
  50.9 23.2 %collective-permute-start.11 = (bf16[1,512,512]{2,1,0:T(8,128)(2,1)S(1)}, bf16[1,512,512]{2,1,0:T(8,128)(2,1)S(1)}, u32[]{:S(2)}, u32[]{:S(2)}) collective-permute-start(bf16[1,512,512]{2,1,0:T(8,128)(2,1)S(1)} %slice.13.refs_0_.refs_8_), channel_id=1, source_target_pairs={{0,48},{1,49},{2,50},{3,51},{4,52},{5,53},{6,54},{7,55},{8,56},{9,... | collective-permute-start | bytes 1572872 | tf_op jit(solution)/shard_map/ppermute | solution.py:32
  53.7 20.5 %collective-permute-start.10 = (bf16[1,512,512]{2,1,0:T(8,128)(2,1)S(1)}, bf16[1,512,512]{2,1,0:T(8,128)(2,1)S(1)}, u32[]{:S(2)}, u32[]{:S(2)}) collective-permute-start(bf16[1,512,512]{2,1,0:T(8,128)(2,1)S(1)} %slice.13.refs_0_.refs_8_), channel_id=1, source_target_pairs={{0,16},{1,17},{2,18},{3,19},{4,20},{5,21},{6,22},{7,23},{8,24},{9,... | collective-permute-start | bytes 1572872 | tf_op jit(solution)/shard_map/ppermute | solution.py:32
  56.2 43.0 %copy-start = (bf16[3,512,256]{2,1,0:T(8,128)(2,1)}, bf16[3,512,256]{2,1,0:T(8,128)(2,1)S(1)}, u32[]{:S(2)}) copy-start(bf16[3,512,256]{2,1,0:T(8,128)(2,1)S(1)} %collective-permute-done.6.refs_1_) | copy-start | bytes 2359300
  63.0 36.3 %copy-start.3 = (bf16[3,512,256]{2,1,0:T(8,128)(2,1)}, bf16[3,512,256]{2,1,0:T(8,128)(2,1)S(1)}, u32[]{:S(2)}) copy-start(bf16[3,512,256]{2,1,0:T(8,128)(2,1)S(1)} %collective-permute-done.8.refs_3_) | copy-start | bytes 2359300
  63.6 10.7 %collective-permute-start.9 = (bf16[128,256]{1,0:T(8,128)(2,1)S(1)}, bf16[128,256]{1,0:T(8,128)(2,1)S(1)}, u32[]{:S(2)}, u32[]{:S(2)}) collective-permute-start(bf16[128,256]{1,0:T(8,128)(2,1)S(1)} %get-tuple-element.32), channel_id=1, source_target_pairs={{0,4},{1,5},{2,6},{3,7},{4,0},{5,1},{6,2},{7,3},{8,12},{9,13},{10,... | collective-permute-start | bytes 196616 | tf_op jit(solution)/shard_map/ppermute | solution.py:32
  74.9 10.1 %collective-permute-start.13 = (bf16[64,2048]{1,0:T(8,128)(2,1)S(1)}, bf16[64,2048]{1,0:T(8,128)(2,1)S(1)}, u32[]{:S(2)}, u32[]{:S(2)}) collective-permute-start(bf16[64,2048]{1,0:T(8,128)(2,1)S(1)} %get-tuple-element.35), channel_id=1, source_target_pairs={{0,64},{64,0},{256,320},{320,256},{1,65},{65,1},{257,321},{321,257... | collective-permute-start | bytes 786440 | tf_op jit(solution)/shard_map/ppermute | solution.py:366
  76.3 14.6 %collective-permute-start.20 = (bf16[3,512,256]{2,1,0:T(8,128)(2,1)S(1)}, bf16[3,512,256]{2,1,0:T(8,128)(2,1)S(1)}, u32[]{:S(2)}, u32[]{:S(2)}) collective-permute-start(bf16[3,512,256]{2,1,0:T(8,128)(2,1)S(1)} %get-tuple-element.36.refs_4_), channel_id=1, source_target_pairs={{128,160},{129,161},{130,162},{131,163},{132,164},{133,165},{134,1... | collective-permute-start | bytes 2359304 | tf_op jit(solution)/shard_map/ppermute | solution.py:32
  79.7 19.6 %collective-permute-start.19 = (bf16[3,512,256]{2,1,0:T(8,128)(2,1)S(1)}, bf16[3,512,256]{2,1,0:T(8,128)(2,1)S(1)}, u32[]{:S(2)}, u32[]{:S(2)}) collective-permute-start(bf16[3,512,256]{2,1,0:T(8,128)(2,1)S(1)} %get-tuple-element.36.refs_4_), channel_id=1, source_target_pairs={{128,176},{129,177},{130,178},{131,179},{132,180},{133,181},{134,1... | collective-permute-start | bytes 2359304 | tf_op jit(solution)/shard_map/ppermute | solution.py:32
  82.5 16.7 %collective-permute-start.18 = (bf16[3,512,256]{2,1,0:T(8,128)(2,1)S(1)}, bf16[3,512,256]{2,1,0:T(8,128)(2,1)S(1)}, u32[]{:S(2)}, u32[]{:S(2)}) collective-permute-start(bf16[3,512,256]{2,1,0:T(8,128)(2,1)S(1)} %get-tuple-element.36.refs_4_), channel_id=1, source_target_pairs={{128,144},{129,145},{130,146},{131,147},{132,148},{133,149},{134,1... | collective-permute-start | bytes 2359304 | tf_op jit(solution)/shard_map/ppermute | solution.py:32
  85.8 0.7 collective-permute-start.14
  86.4 12.8 %collective-permute-start.15 = (bf16[64,2048]{1,0:T(8,128)(2,1)S(1)}, bf16[64,2048]{1,0:T(8,128)(2,1)S(1)}, u32[]{:S(2)}, u32[]{:S(2)}) collective-permute-start(bf16[64,2048]{1,0:T(8,128)(2,1)S(1)} %collective-permute-done.14.mine.in1m), channel_id=1, source_target_pairs={{128,192},{192,128},{129,193},{193,129},{130,194},{194,130},{131,1... | collective-permute-start | bytes 786440 | tf_op jit(solution)/shard_map/ppermute | solution.py:366
  100.5 2.0 %collective-permute-start.21 = (bf16[64,2048]{1,0:T(8,128)(2,1)S(1)}, bf16[64,2048]{1,0:T(8,128)(2,1)S(1)}, u32[]{:S(2)}, u32[]{:S(2)}) collective-permute-start(bf16[64,2048]{1,0:T(8,128)(2,1)S(1)} %get-tuple-element.38), channel_id=1, source_target_pairs={{128,192},{192,128},{129,193},{193,129},{130,194},{194,130},{131,1... | collective-permute-start | bytes 786440 | tf_op jit(solution)/shard_map/ppermute | solution.py:366
  101.2 40.3 %collective-permute-start.16 = (bf16[64,2048]{1,0:T(8,128)(2,1)S(1)}, bf16[64,2048]{1,0:T(8,128)(2,1)}, u32[]{:S(2)}, u32[]{:S(2)}) collective-permute-start(bf16[64,2048]{1,0:T(8,128)(2,1)S(1)} %get-tuple-element.41), channel_id=1, source_target_pairs={{256,384},{257,385},{258,386},{259,387},{260,388},{261,389},{262,3... | collective-permute-start | bytes 786440 | tf_op jit(solution)/shard_map/ppermute | solution.py:418
  103.6 42.2 %collective-permute-start.23 = (bf16[64,2048]{1,0:T(8,128)(2,1)S(1)}, bf16[64,2048]{1,0:T(8,128)(2,1)}, u32[]{:S(2)}, u32[]{:S(2)}) collective-permute-start(bf16[64,2048]{1,0:T(8,128)(2,1)S(1)} %fusion.2), channel_id=1, source_target_pairs={{128,384},{129,385},{130,386},{131,387},{132,388},{133,389},{134,3... | collective-permute-start | bytes 786440 | tf_op jit(solution)/shard_map/ppermute | solution.py:432
  141.4 6.3 %collective-permute-start.17 = (bf16[64,2048]{1,0:T(8,128)(2,1)}, bf16[64,2048]{1,0:T(8,128)(2,1)}, u32[]{:S(2)}, u32[]{:S(2)}) collective-permute-start(bf16[64,2048]{1,0:T(8,128)(2,1)} %collective-permute-done.16.mine.in3m), channel_id=1, source_target_pairs={{384,448},{448,384},{385,449},{449,385},{386,450},{450,386},{387,4... | collective-permute-start | bytes 786440 | tf_op jit(solution)/shard_map/ppermute | solution.py:366
  145.8 12.4 %collective-permute-start.24 = (bf16[64,2048]{1,0:T(8,128)(2,1)}, bf16[64,2048]{1,0:T(8,128)(2,1)}, u32[]{:S(2)}, u32[]{:S(2)}) collective-permute-start(bf16[64,2048]{1,0:T(8,128)(2,1)} %collective-permute-done.23.mem_mine), channel_id=1, source_target_pairs={{384,448},{448,384},{385,449},{449,385},{386,450},{450,386},{387,4... | collective-permute-start | bytes 786440 | tf_op jit(solution)/shard_map/ppermute | solution.py:366
  163.8 3.8 %collective-permute-start.25 = (bf16[128,2048]{1,0:T(8,128)(2,1)S(1)}, bf16[128,2048]{1,0:T(8,128)(2,1)S(1)}, u32[]{:S(2)}, u32[]{:S(2)}) collective-permute-start(bf16[128,2048]{1,0:T(8,128)(2,1)S(1)} %shard_map.69.own), channel_id=1, source_target_pairs={{384,448},{385,449},{386,450},{387,451},{388,452},{389,453},{390,4... | collective-permute-start | bytes 1572872 | tf_op jit(solution)/shard_map/ppermute | solution.py:457
  165.2 0.7 collective-permute-start.22
  (32 other events, 270.8 us)

commit v11 on v10

--- a/solution.py
+++ b/solution.py
@@ -12,6 +12,7 @@
 SIDE = 4
 TURNS = (0, 1, 3, 2)
 FAR = 2
+NORM_COST = 5 * 10**9
 EVEN = (0, 2)
 ODD = (1, 3)
 AXES = ("zh", "core", "y", "x", "zl")
@@ -207,29 +208,28 @@
     return [refs[:SIDE], refs[SIDE:2 * SIDE]], refs[2 * SIDE:3 * SIDE], refs[3 * SIDE:]
 
 
-def second_kernel(scal, gains, mine, other, *refs):
+def received_kernel(scal, gains, mine, other, h3):
+    @pl.when(lax.rem(scal[2], 2) == 1)
+    def _():
+        put_norm(scal, gains, (mine, other), h3)
+
+
+def second_kernel(scal, h3, *refs):
     pieces, outs, rest = split(refs)
-    out_mine, out_other, h3, t3, space, sems, out_space, out_sems = rest
+    out_mine, out_other, query, t3, space, sems, out_space, out_sems = rest
 
     @pl.when(scal[2] == 1)
     def _():
         run = project(scal, h3, pieces, (0, 1, 2), space, sems)
         fetched = Fetched([ref.at[0] for ref in outs], out_space, out_sems)
-        put_norm(scal, gains, (mine, other), h3)
-        rows = mine.shape[0]
+        rows = out_mine.shape[0]
         mixed = attend(local_mask(scal, 2 * rows), *run())
         project_out(scal, mixed, fetched, t3)
         put_out(t3, slice(0, rows), slice(rows, 2 * rows), out_mine, out_other)
 
-
-def query_kernel(scal, gains, mine, other, *refs):
-    pieces, _, (q, h3, space, sems) = split(refs)
-
     @pl.when(scal[2] == 3)
     def _():
-        run = project(scal, h3, pieces, (0,), space, sems)
-        put_norm(scal, gains, (mine, other), h3)
-        q[...] = run()[0]
+        query[...] = project(scal, h3, pieces, (0,), space.at[:, :1], sems)()[0]
 
 
 def third_kernel(scal, q, mem_mine, mem_other, *refs):
@@ -263,12 +263,12 @@
         in_specs=[SMEM] + [VMEM] * len(operands) + [ANY] * len(pieces),
         out_specs=jax.tree.map(lambda _: VMEM, outs),
         scratch_shapes=shapes,
-        compiler_params=pltpu.CompilerParams(vmem_limit_bytes=44 * 1024 * 1024),
+        compiler_params=pltpu.CompilerParams(vmem_limit_bytes=16 * 1024 * 1024),
         cost_estimate=pl.CostEstimate(flops=flops, bytes_accessed=size, transcendentals=0),
     )(scal, *operands, *pieces)
 
 
-def finish_kernel(scal, mine, other, in1m, in1o, in3m, in3o, early_m, early_o, own, got, out):
+def finish_kernel(scal, mine, other, hop_m, hop_o, early_m, early_o, own, got, out):
     rows = mine.shape[0]
     cube, core = scal[2], scal[6]
     even = (cube == 0) | (cube == 2)
@@ -281,13 +281,9 @@
     def _():
         put(mine, other)
 
-    @pl.when((core == 0) & (cube == 1))
-    def _():
-        put(in1m, in1o)
-
-    @pl.when((core == 0) & (cube == 3))
-    def _():
-        put(in3m, in3o)
+    @pl.when((core == 0) & jnp.logical_not(even))
+    def _():
+        put(hop_m, hop_o)
 
     @pl.when((core == 1) & (cube != 3))
     def _():
@@ -297,7 +293,7 @@
     def _():
         at = lax.broadcasted_iota(jnp.int32, mine.shape, 0)
         low, high = slice(0, rows), slice(rows, 2 * rows)
-        for slot, base, a, b, live in ((1, in3m, low, high, scal[7]), (0, in3o, high, low, scal[8])):
+        for slot, base, a, b, live in ((1, hop_m, low, high, scal[7]), (0, hop_o, high, low, scal[8])):
             term = own[a, :].astype(F32) + got[b, :].astype(F32)
             term = jnp.where(at < live, term, 0.0)
             out[slot] = (base[...].astype(F32) + term).astype(BF16)
@@ -414,35 +410,30 @@
     )
     first = added(mine, kept + swapped(sent, (0, 2)).astype(F32), live).astype(BF16)
     pieces = [*parts_a, *turns(rest_b, True, ODD), *parts_o]
-    in1 = lax.ppermute(first, "zh", [(0, 1)])
-    in3 = lax.ppermute(first, "zh", [(2, 3)])
-    in1_other = swapped(in1, (1,))
-    kept, sent = call(
+    hop = lax.ppermute(first, "zh", [(0, 1), (2, 3)])
+    hop_other = swapped(hop, ODD)
+    h3 = call(
+        received_kernel,
+        scal,
+        [norm_gains, hop, hop_other],
+        jax.ShapeDtypeStruct(blocks, BF16),
+        flops=NORM_COST,
+    )
+    kept, sent, query = call(
         second_kernel,
         scal,
-        [norm_gains, in1, in1_other],
-        halves,
-        [(blocks, BF16), (blocks, F32)],
+        [h3],
+        (*halves, narrow),
+        [(blocks, F32)],
         pieces,
         [(8, 3) + tile, out_fetch],
         4 * work,
     )
-    second = added(in1, kept + swapped(sent, (1,)).astype(F32), live).astype(BF16)
+    second = added(hop, kept + swapped(sent, (1,)).astype(F32), live).astype(BF16)
     memory = rms(second.astype(F32), norm_gains[4:5])
     mem = lax.ppermute(memory, "zh", [(1, 3)])
     early = jnp.where(zh == 1, second, first)
     early_other = lax.ppermute(early, SECTION, [(0, 1), (2, 3), (4, 5)])
-    in3_other = swapped(in3, (3,))
-    query = call(
-        query_kernel,
-        scal,
-        [norm_gains, in3, in3_other],
-        narrow,
-        [(blocks, BF16)],
-        pieces,
-        [(8, 1) + tile],
-        work,
-    )
     mem_other = swapped(mem, (3,))
     own = call(
         third_kernel,
@@ -455,7 +446,7 @@
         3 * work,
     )
     got = lax.ppermute(own, SECTION, [(6, 7)])
-    parts = [mine, other, in1, in1_other, in3, in3_other, early, early_other, own, got]
+    parts = [mine, other, hop, hop_other, early, early_other, own, got]
     out = call(finish_kernel, scal, parts, jax.ShapeDtypeStruct((2, rows, width), BF16))
     return out[None]
 

time: 171 us -> 174 us (1.018)
  waiting for transfers between devices: 78.7 us -> 85.3 us
  starting transfers between devices: 58.6 us -> 56.6 us
    ppermute x1, waiting for transfers between devices: 0.01 us -> 16.9 us  [on_device(): mem = lax.ppermute(memory, 'zh', [(1, 3)])]
    ppermute x2 -> x1, waiting for transfers between devices: 36.5 us -> 30 us  [on_device(): hop = lax.ppermute(first, 'zh', [(0, 1), (2, 3)])]
    ppermute x16, waiting for transfers between devices: 32 us -> 25.5 us  [moved(): return lax.ppermute(array, AXES, pairs)]
    ppermute x5 -> x4, waiting for transfers between devices: 0.01 us -> 2.62 us  [swapped(): return lax.ppermute(array, SECTION, pairs)]
    ppermute x5 -> x4, starting transfers between devices: 8.3 us -> 6.8 us  [swapped(): return lax.ppermute(array, SECTION, pairs)]
    unnamed x74 -> x70, local copies, waits for them, and re-layouts: 9.04 us -> 8.57 us
  transfers between devices with their start and end apart: 27 -> 25, of which waited for: 10 -> 11; matrix products, arithmetic and copies ran while one was open for 4% -> 3% of each run, Pallas kernels for 2% -> 1%
where the time goes in v11:
time: 174 us; the launch traced here: 173 us
  waiting for transfers between devices  85.3 us (49%)
  starting transfers between devices  56.6 us (33%)
  local copies, waits for them, and re-layouts  14.3 us (8%)
  Pallas kernels  11.5 us (7%)
  other arithmetic  4.36 us (3%)
    ppermute x16, starting transfers between devices, moved(): return lax.ppermute(array, AXES, pairs)  39.7 us
    ppermute x1, waiting for transfers between devices, on_device(): hop = lax.ppermute(first, 'zh', [(0, 1), (2, 3)])  30 us
    ppermute x16, waiting for transfers between devices, moved(): return lax.ppermute(array, AXES, pairs)  25.5 us
    ppermute x1, waiting for transfers between devices, on_device(): mem = lax.ppermute(memory, 'zh', [(1, 3)])  16.9 us
    pallas_call x7, Pallas kernels, call(): pl.pallas_call(kernel, out_shape=outs, in_specs=[SMEM] + [VMEM] * len(ope...  11.5 us
    unnamed x70, local copies, waits for them, and re-layouts  8.57 us
    all_to_all x1, waiting for transfers between devices, gather(): got = lax.all_to_all(sent, ('core', 'zl'), 0, 0, tiled=True)  8.49 us
    ppermute x4, starting transfers between devices, swapped(): return lax.ppermute(array, SECTION, pairs)  6.8 us
  transfers between devices with their start and end apart: 25, of which 11 were waited for; matrix products, arithmetic and copies ran while one was open for 3% of the time, Pallas kernels for 1%

profile of v11, /device:TPU:481, one launch (start us, length us, event | category | flops | bytes accessed | tf_op | source)
XLA Modules:
  0.0 172.9 jit_solution(1506285151882212875)
XLA Ops:
  2.0 5.6 %all-to-all-start = ((bf16[8,2,32,512]{3,2,1,0:T(8,128)(2,1)}), bf16[8,2,32,512]{3,2,1,0:T(8,128)(2,1)S(1)}, u32[]{:S(2)}, u32[]{:S(2)}) async-start(bf16[8,2,32,512]{3,2,1,0:T(8,128)(2,1)} %bitcast.1), calls=%async_computation | async-start | bytes 1048576 | tf_op jit(solution)/shard_map/all_to_all | solution.py:311
  9.1 8.5 %all-to-all-done = bf16[8,2,32,512]{3,2,1,0:T(8,128)(2,1)S(1)} async-done(((bf16[8,2,32,512]{3,2,1,0:T(8,128)(2,1)}), bf16[8,2,32,512]{3,2,1,0:T(8,128)(2,1)S(1)}, u32[]{:S(2)}, u32[]{:S(2)}) %all-to-all-start) | async-done | bytes 524320 | tf_op jit(solution)/shard_map/all_to_all | solution.py:311
  17.6 3.2 %collective-permute-start.2 = (bf16[4,128,512]{2,1,0:T(8,128)(2,1)S(1)}, bf16[4,128,512]{2,1,0:T(8,128)(2,1)S(1)}, u32[]{:S(2)}, u32[]{:S(2)}) collective-permute-start(bf16[4,128,512]{2,1,0:T(8,128)(2,1)S(1)} %bitcast.28), channel_id=1, source_target_pairs={{0,4},{1,5},{2,6},{3,7},{4,0},{5,1},{6,2},{7,3},{8,12},{9,13},{10,... | collective-permute-start | bytes 1572872 | tf_op jit(solution)/shard_map/ppermute | solution.py:33
  20.8 4.5 %collective-permute-start.5 = (bf16[4,128,512]{2,1,0:T(8,128)(2,1)S(1)}, bf16[4,128,512]{2,1,0:T(8,128)(2,1)}, u32[]{:S(2)}, u32[]{:S(2)}) collective-permute-start(bf16[4,128,512]{2,1,0:T(8,128)(2,1)S(1)} %bitcast.29), channel_id=1, source_target_pairs={{0,8},{1,9},{2,10},{3,11},{4,12},{5,13},{6,14},{7,15},{8,0},{9,1},... | collective-permute-start | bytes 1572872 | tf_op jit(solution)/shard_map/ppermute | solution.py:33
  25.3 1.9 %collective-permute-start.4 = (bf16[4,128,512]{2,1,0:T(8,128)(2,1)S(1)}, bf16[4,128,512]{2,1,0:T(8,128)(2,1)}, u32[]{:S(2)}, u32[]{:S(2)}) collective-permute-start(bf16[4,128,512]{2,1,0:T(8,128)(2,1)S(1)} %bitcast.30), channel_id=1, source_target_pairs={{0,12},{1,13},{2,14},{3,15},{4,8},{5,9},{6,10},{7,11},{8,4},{9,5},... | collective-permute-start | bytes 1572872 | tf_op jit(solution)/shard_map/ppermute | solution.py:33
  30.0 2.6 %stack.27.scal = s32[9]{0:T(128)S(1)} concatenate(s32[1]{0:T(128)} %bitcast.5, s32[1]{0:T(128)} %bitcast.6, s32[1]{0:T(128)} %bitcast.7, s32[1]{0:T(128)} %bitcast.8, s32[1]{0:T(128)} %get-tuple-element.55, s32[1]{0:T(128)} %get-tuple-element.56, s32[1]{0:T(128)} %bitcast.9, s32[1]{0:T(128)} %get-tuple-element.52, s32[1]{0:T(128)} %get-tuple-element.51), dimensions={0} | concatenate | bytes 72 | tf_op jit(solution)/shard_map/stack | solution.py:339
  32.6 3.4 %collective-permute-done.5 = bf16[4,128,512]{2,1,0:T(8,128)(2,1)} collective-permute-done((bf16[4,128,512]{2,1,0:T(8,128)(2,1)S(1)}, bf16[4,128,512]{2,1,0:T(8,128)(2,1)}, u32[]{:S(2)}, u32[]{:S(2)}) %collective-permute-start.5) | collective-permute-done | bytes 524320 | tf_op jit(solution)/shard_map/ppermute | solution.py:33
  36.0 5.6 %collective-permute-done.4 = bf16[4,128,512]{2,1,0:T(8,128)(2,1)} collective-permute-done((bf16[4,128,512]{2,1,0:T(8,128)(2,1)S(1)}, bf16[4,128,512]{2,1,0:T(8,128)(2,1)}, u32[]{:S(2)}, u32[]{:S(2)}) %collective-permute-start.4) | collective-permute-done | bytes 524320 | tf_op jit(solution)/shard_map/ppermute | solution.py:33
  41.6 1.3 pad_maximum_fusion
  43.2 3.0 %collective-permute-start.6 = (bf16[3,512,256]{2,1,0:T(8,128)(2,1)S(1)}, bf16[3,512,256]{2,1,0:T(8,128)(2,1)S(1)}, u32[]{:S(2)}, u32[]{:S(2)}) collective-permute-start(bf16[3,512,256]{2,1,0:T(8,128)(2,1)S(1)} %get-tuple-element.47), channel_id=1, source_target_pairs={{0,16},{1,17},{2,18},{3,19},{4,20},{5,21},{6,22},{7,23},{8,24},{9,... | collective-permute-start | bytes 2359304 | tf_op jit(solution)/shard_map/ppermute | solution.py:33
  46.1 3.7 %collective-permute-start.7 = (bf16[3,512,256]{2,1,0:T(8,128)(2,1)S(1)}, bf16[3,512,256]{2,1,0:T(8,128)(2,1)S(1)}, u32[]{:S(2)}, u32[]{:S(2)}) collective-permute-start(bf16[3,512,256]{2,1,0:T(8,128)(2,1)S(1)} %get-tuple-element.47), channel_id=1, source_target_pairs={{0,48},{1,49},{2,50},{3,51},{4,52},{5,53},{6,54},{7,55},{8,56},{9,... | collective-permute-start | bytes 2359304 | tf_op jit(solution)/shard_map/ppermute | solution.py:33
  49.8 2.6 %collective-permute-start.8 = (bf16[3,512,256]{2,1,0:T(8,128)(2,1)S(1)}, bf16[3,512,256]{2,1,0:T(8,128)(2,1)S(1)}, u32[]{:S(2)}, u32[]{:S(2)}) collective-permute-start(bf16[3,512,256]{2,1,0:T(8,128)(2,1)S(1)} %get-tuple-element.48.refs_0_), channel_id=1, source_target_pairs={{0,32},{1,33},{2,34},{3,35},{4,36},{5,37},{6,38},{7,39},{8,40},{9,... | collective-permute-start | bytes 2359304 | tf_op jit(solution)/shard_map/ppermute | solution.py:33
  53.1 2.7 %collective-permute-start.10 = (bf16[1,512,512]{2,1,0:T(8,128)(2,1)S(1)}, bf16[1,512,512]{2,1,0:T(8,128)(2,1)S(1)}, u32[]{:S(2)}, u32[]{:S(2)}) collective-permute-start(bf16[1,512,512]{2,1,0:T(8,128)(2,1)S(1)} %slice.13.refs_0_.refs_8_), channel_id=1, source_target_pairs={{0,16},{1,17},{2,18},{3,19},{4,20},{5,21},{6,22},{7,23},{8,24},{9,... | collective-permute-start | bytes 1572872 | tf_op jit(solution)/shard_map/ppermute | solution.py:33
  55.8 3.7 %collective-permute-start.11 = (bf16[1,512,512]{2,1,0:T(8,128)(2,1)S(1)}, bf16[1,512,512]{2,1,0:T(8,128)(2,1)S(1)}, u32[]{:S(2)}, u32[]{:S(2)}) collective-permute-start(bf16[1,512,512]{2,1,0:T(8,128)(2,1)S(1)} %slice.13.refs_0_.refs_8_), channel_id=1, source_target_pairs={{0,48},{1,49},{2,50},{3,51},{4,52},{5,53},{6,54},{7,55},{8,56},{9,... | collective-permute-start | bytes 1572872 | tf_op jit(solution)/shard_map/ppermute | solution.py:33
  59.5 2.6 %collective-permute-start.12 = (bf16[1,512,512]{2,1,0:T(8,128)(2,1)S(1)}, bf16[1,512,512]{2,1,0:T(8,128)(2,1)S(1)}, u32[]{:S(2)}, u32[]{:S(2)}) collective-permute-start(bf16[1,512,512]{2,1,0:T(8,128)(2,1)S(1)} %slice.13.refs_0_.refs_8_), channel_id=1, source_target_pairs={{0,32},{1,33},{2,34},{3,35},{4,36},{5,37},{6,38},{7,39},{8,40},{9,... | collective-permute-start | bytes 1572872 | tf_op jit(solution)/shard_map/ppermute | solution.py:33
  62.1 6.7 %collective-permute-done.7.refs_2_ = bf16[3,512,256]{2,1,0:T(8,128)(2,1)S(1)} collective-permute-done((bf16[3,512,256]{2,1,0:T(8,128)(2,1)S(1)}, bf16[3,512,256]{2,1,0:T(8,128)(2,1)S(1)}, u32[]{:S(2)}, u32[]{:S(2)}) %collective-permute-start.7) | collective-permute-done | bytes 786464 | tf_op jit(solution)/shard_map/ppermute | solution.py:33
  70.4 9.6 %collective-permute-done.11.refs_2_.refs_10_ = bf16[1,512,512]{2,1,0:T(8,128)(2,1)S(1)} collective-permute-done((bf16[1,512,512]{2,1,0:T(8,128)(2,1)S(1)}, bf16[1,512,512]{2,1,0:T(8,128)(2,1)S(1)}, u32[]{:S(2)}, u32[]{:S(2)}) %collective-permute-start.11) | collective-permute-done | bytes 524320 | tf_op jit(solution)/shard_map/ppermute | solution.py:33
  82.8 1.3 collective-permute-start.14
  84.1 1.9 %collective-permute-start.16 = (bf16[3,512,256]{2,1,0:T(8,128)(2,1)S(1)}, bf16[3,512,256]{2,1,0:T(8,128)(2,1)S(1)}, u32[]{:S(2)}, u32[]{:S(2)}) collective-permute-start(bf16[3,512,256]{2,1,0:T(8,128)(2,1)S(1)} %get-tuple-element.37.refs_4_), channel_id=1, source_target_pairs={{128,144},{129,145},{130,146},{131,147},{132,148},{133,149},{134,1... | collective-permute-start | bytes 2359304 | tf_op jit(solution)/shard_map/ppermute | solution.py:33
  86.0 3.7 %collective-permute-start.17 = (bf16[3,512,256]{2,1,0:T(8,128)(2,1)S(1)}, bf16[3,512,256]{2,1,0:T(8,128)(2,1)S(1)}, u32[]{:S(2)}, u32[]{:S(2)}) collective-permute-start(bf16[3,512,256]{2,1,0:T(8,128)(2,1)S(1)} %get-tuple-element.37.refs_4_), channel_id=1, source_target_pairs={{128,176},{129,177},{130,178},{131,179},{132,180},{133,181},{134,1... | collective-permute-start | bytes 2359304 | tf_op jit(solution)/shard_map/ppermute | solution.py:33
  89.8 3.3 %collective-permute-start.18 = (bf16[3,512,256]{2,1,0:T(8,128)(2,1)S(1)}, bf16[3,512,256]{2,1,0:T(8,128)(2,1)S(1)}, u32[]{:S(2)}, u32[]{:S(2)}) collective-permute-start(bf16[3,512,256]{2,1,0:T(8,128)(2,1)S(1)} %get-tuple-element.37.refs_4_), channel_id=1, source_target_pairs={{128,160},{129,161},{130,162},{131,163},{132,164},{133,165},{134,1... | collective-permute-start | bytes 2359304 | tf_op jit(solution)/shard_map/ppermute | solution.py:33
  93.1 30.0 %collective-permute-done.14.mine.hop_m = bf16[64,2048]{1,0:T(8,128)(2,1)S(1)} collective-permute-done((bf16[64,2048]{1,0:T(8,128)(2,1)S(1)}, bf16[64,2048]{1,0:T(8,128)(2,1)S(1)}, u32[]{:S(2)}, u32[]{:S(2)}) %collective-permute-start.14) | collective-permute-done | bytes 262176 | tf_op jit(solution)/shard_map/ppermute | solution.py:413
  123.1 2.3 %collective-permute-start.15 = (bf16[64,2048]{1,0:T(8,128)(2,1)S(1)}, bf16[64,2048]{1,0:T(8,128)(2,1)S(1)}, u32[]{:S(2)}, u32[]{:S(2)}) collective-permute-start(bf16[64,2048]{1,0:T(8,128)(2,1)S(1)} %collective-permute-done.14.mine.hop_m), channel_id=1, source_target_pairs={{128,192},{192,128},{384,448},{448,384},{129,193},{193,129},{385,4... | collective-permute-start | bytes 786440 | tf_op jit(solution)/shard_map/ppermute | solution.py:362
  127.5 1.9 %shard_map.68 = (f32[64,2048]{1,0:T(8,128)S(1)}, bf16[64,2048]{1,0:T(8,128)(2,1)S(1)}, bf16[128,512]{1,0:T(8,128)(2,1)S(1)}) custom-call(s32[9]{0:T(128)S(1)} %stack.27.scal, bf16[16,128,128]{2,1,0:T(8,128)(2,1)S(1)} %shard_map.67.h3, bf16[3,512,256]{2,1,0:T(8,128)(2,1)S(1)} %get-tuple-element.48.refs_0_, ...), custom_call_target="tpu_custom_call" | custom-call | flops 1073741824 | bytes 8912896 | tf_op jit(solution)/shard_map/pallas_call | solution.py:260
  131.3 1.3 collective-permute-start.21
  132.6 16.9 %collective-permute-done.21.mem_mine = bf16[64,2048]{1,0:T(8,128)(2,1)} collective-permute-done((bf16[64,2048]{1,0:T(8,128)(2,1)S(1)}, bf16[64,2048]{1,0:T(8,128)(2,1)}, u32[]{:S(2)}, u32[]{:S(2)}) %collective-permute-start.21) | collective-permute-done | bytes 262176 | tf_op jit(solution)/shard_map/ppermute | solution.py:434
  149.5 3.1 %collective-permute-start.22 = (bf16[64,2048]{1,0:T(8,128)(2,1)}, bf16[64,2048]{1,0:T(8,128)(2,1)}, u32[]{:S(2)}, u32[]{:S(2)}) collective-permute-start(bf16[64,2048]{1,0:T(8,128)(2,1)} %collective-permute-done.21.mem_mine), channel_id=1, source_target_pairs={{384,448},{448,384},{385,449},{449,385},{386,450},{450,386},{387,4... | collective-permute-start | bytes 786440 | tf_op jit(solution)/shard_map/ppermute | solution.py:362
  152.6 1.5 collective-permute-done.22.mem_other
  161.9 5.6 %shard_map.69.own = bf16[128,2048]{1,0:T(8,128)(2,1)S(1)} custom-call(s32[9]{0:T(128)S(1)} %stack.27.scal, bf16[128,512]{1,0:T(8,128)(2,1)S(1)} %get-tuple-element.40.q, bf16[64,2048]{1,0:T(8,128)(2,1)} %collective-permute-done.21.mem_mine, bf16[64,2048]{1,0:T(8,128)(2,1)} %collective-permute-done.22.mem_other, ...), custom_call_target="tpu_custom_call" | custom-call | flops 805306368 | bytes 9043968 | tf_op jit(solution)/shard_map/pallas_call | solution.py:260
  167.5 1.3 collective-permute-start.23
  169.6 1.7 collective-permute-done.23.got
  171.3 1.6 shard_map.70
  (116 shorter events, 23.4 us)
Async XLA Ops:
  2.0 15.6 %all-to-all-start = ((bf16[8,2,32,512]{3,2,1,0:T(8,128)(2,1)}), bf16[8,2,32,512]{3,2,1,0:T(8,128)(2,1)S(1)}, u32[]{:S(2)}, u32[]{:S(2)}) async-start(bf16[8,2,32,512]{3,2,1,0:T(8,128)(2,1)} %bitcast.1), calls=%async_computation | async-start | bytes 1048576 | tf_op jit(solution)/shard_map/all_to_all | solution.py:311
  7.6 1.4 collective-permute-start
  8.3 0.7 collective-permute-start.1
  9.0 32.6 %copy-start.20 = (bf16[2,64,2048]{2,1,0:T(8,128)(2,1)}, bf16[2,64,2048]{2,1,0:T(8,128)(2,1)S(1)}, u32[]{:S(2)}) copy-start(bf16[2,64,2048]{2,1,0:T(8,128)(2,1)S(1)} %collective-permute-done) | copy-start | bytes 1572868
  9.0 32.6 %copy-start.22 = (bf16[2,64,2048]{2,1,0:T(8,128)(2,1)}, bf16[2,64,2048]{2,1,0:T(8,128)(2,1)S(1)}, u32[]{:S(2)}) copy-start(bf16[2,64,2048]{2,1,0:T(8,128)(2,1)S(1)} %collective-permute-done.1) | copy-start | bytes 1572868
  17.6 15.0 %collective-permute-start.2 = (bf16[4,128,512]{2,1,0:T(8,128)(2,1)S(1)}, bf16[4,128,512]{2,1,0:T(8,128)(2,1)S(1)}, u32[]{:S(2)}, u32[]{:S(2)}) collective-permute-start(bf16[4,128,512]{2,1,0:T(8,128)(2,1)S(1)} %bitcast.28), channel_id=1, source_target_pairs={{0,4},{1,5},{2,6},{3,7},{4,0},{5,1},{6,2},{7,3},{8,12},{9,13},{10,... | collective-permute-start | bytes 1572872 | tf_op jit(solution)/shard_map/ppermute | solution.py:33
  20.8 15.2 %collective-permute-start.5 = (bf16[4,128,512]{2,1,0:T(8,128)(2,1)S(1)}, bf16[4,128,512]{2,1,0:T(8,128)(2,1)}, u32[]{:S(2)}, u32[]{:S(2)}) collective-permute-start(bf16[4,128,512]{2,1,0:T(8,128)(2,1)S(1)} %bitcast.29), channel_id=1, source_target_pairs={{0,8},{1,9},{2,10},{3,11},{4,12},{5,13},{6,14},{7,15},{8,0},{9,1},... | collective-permute-start | bytes 1572872 | tf_op jit(solution)/shard_map/ppermute | solution.py:33
  25.3 16.3 %collective-permute-start.4 = (bf16[4,128,512]{2,1,0:T(8,128)(2,1)S(1)}, bf16[4,128,512]{2,1,0:T(8,128)(2,1)}, u32[]{:S(2)}, u32[]{:S(2)}) collective-permute-start(bf16[4,128,512]{2,1,0:T(8,128)(2,1)S(1)} %bitcast.30), channel_id=1, source_target_pairs={{0,12},{1,13},{2,14},{3,15},{4,8},{5,9},{6,10},{7,11},{8,4},{9,5},... | collective-permute-start | bytes 1572872 | tf_op jit(solution)/shard_map/ppermute | solution.py:33
  27.4 5.2 %collective-permute-start.3 = (f32[8,128]{1,0:T(8,128)S(1)}, f32[8,128]{1,0:T(8,128)S(1)}, u32[]{:S(2)}, u32[]{:S(2)}) collective-permute-start(f32[8,128]{1,0:T(8,128)S(1)} %concatenate.9.own_keys), channel_id=1, source_target_pairs={{0,4},{1,5},{2,6},{3,7},{4,0},{5,1},{6,2},{7,3},{8,12},{9,13},{10,... | collective-permute-start | bytes 12296 | tf_op jit(solution)/shard_map/ppermute | solution.py:33
  43.2 16.4 %collective-permute-start.6 = (bf16[3,512,256]{2,1,0:T(8,128)(2,1)S(1)}, bf16[3,512,256]{2,1,0:T(8,128)(2,1)S(1)}, u32[]{:S(2)}, u32[]{:S(2)}) collective-permute-start(bf16[3,512,256]{2,1,0:T(8,128)(2,1)S(1)} %get-tuple-element.47), channel_id=1, source_target_pairs={{0,16},{1,17},{2,18},{3,19},{4,20},{5,21},{6,22},{7,23},{8,24},{9,... | collective-permute-start | bytes 2359304 | tf_op jit(solution)/shard_map/ppermute | solution.py:33
  46.1 22.7 %collective-permute-start.7 = (bf16[3,512,256]{2,1,0:T(8,128)(2,1)S(1)}, bf16[3,512,256]{2,1,0:T(8,128)(2,1)S(1)}, u32[]{:S(2)}, u32[]{:S(2)}) collective-permute-start(bf16[3,512,256]{2,1,0:T(8,128)(2,1)S(1)} %get-tuple-element.47), channel_id=1, source_target_pairs={{0,48},{1,49},{2,50},{3,51},{4,52},{5,53},{6,54},{7,55},{8,56},{9,... | collective-permute-start | bytes 2359304 | tf_op jit(solution)/shard_map/ppermute | solution.py:33
  49.8 18.9 %collective-permute-start.8 = (bf16[3,512,256]{2,1,0:T(8,128)(2,1)S(1)}, bf16[3,512,256]{2,1,0:T(8,128)(2,1)S(1)}, u32[]{:S(2)}, u32[]{:S(2)}) collective-permute-start(bf16[3,512,256]{2,1,0:T(8,128)(2,1)S(1)} %get-tuple-element.48.refs_0_), channel_id=1, source_target_pairs={{0,32},{1,33},{2,34},{3,35},{4,36},{5,37},{6,38},{7,39},{8,40},{9,... | collective-permute-start | bytes 2359304 | tf_op jit(solution)/shard_map/ppermute | solution.py:33
  53.1 17.3 %collective-permute-start.10 = (bf16[1,512,512]{2,1,0:T(8,128)(2,1)S(1)}, bf16[1,512,512]{2,1,0:T(8,128)(2,1)S(1)}, u32[]{:S(2)}, u32[]{:S(2)}) collective-permute-start(bf16[1,512,512]{2,1,0:T(8,128)(2,1)S(1)} %slice.13.refs_0_.refs_8_), channel_id=1, source_target_pairs={{0,16},{1,17},{2,18},{3,19},{4,20},{5,21},{6,22},{7,23},{8,24},{9,... | collective-permute-start | bytes 1572872 | tf_op jit(solution)/shard_map/ppermute | solution.py:33
  55.8 24.2 %collective-permute-start.11 = (bf16[1,512,512]{2,1,0:T(8,128)(2,1)S(1)}, bf16[1,512,512]{2,1,0:T(8,128)(2,1)S(1)}, u32[]{:S(2)}, u32[]{:S(2)}) collective-permute-start(bf16[1,512,512]{2,1,0:T(8,128)(2,1)S(1)} %slice.13.refs_0_.refs_8_), channel_id=1, source_target_pairs={{0,48},{1,49},{2,50},{3,51},{4,52},{5,53},{6,54},{7,55},{8,56},{9,... | collective-permute-start | bytes 1572872 | tf_op jit(solution)/shard_map/ppermute | solution.py:33
  59.5 20.5 %collective-permute-start.12 = (bf16[1,512,512]{2,1,0:T(8,128)(2,1)S(1)}, bf16[1,512,512]{2,1,0:T(8,128)(2,1)S(1)}, u32[]{:S(2)}, u32[]{:S(2)}) collective-permute-start(bf16[1,512,512]{2,1,0:T(8,128)(2,1)S(1)} %slice.13.refs_0_.refs_8_), channel_id=1, source_target_pairs={{0,32},{1,33},{2,34},{3,35},{4,36},{5,37},{6,38},{7,39},{8,40},{9,... | collective-permute-start | bytes 1572872 | tf_op jit(solution)/shard_map/ppermute | solution.py:33
  68.8 58.7 %copy-start = (bf16[3,512,256]{2,1,0:T(8,128)(2,1)}, bf16[3,512,256]{2,1,0:T(8,128)(2,1)S(1)}, u32[]{:S(2)}) copy-start(bf16[3,512,256]{2,1,0:T(8,128)(2,1)S(1)} %collective-permute-done.7.refs_2_) | copy-start | bytes 2359300
  68.8 58.7 %copy-start.2 = (bf16[3,512,256]{2,1,0:T(8,128)(2,1)}, bf16[3,512,256]{2,1,0:T(8,128)(2,1)S(1)}, u32[]{:S(2)}) copy-start(bf16[3,512,256]{2,1,0:T(8,128)(2,1)S(1)} %collective-permute-done.8.refs_3_) | copy-start | bytes 2359300
  69.4 10.6 %collective-permute-start.9 = (bf16[128,256]{1,0:T(8,128)(2,1)S(1)}, bf16[128,256]{1,0:T(8,128)(2,1)S(1)}, u32[]{:S(2)}, u32[]{:S(2)}) collective-permute-start(bf16[128,256]{1,0:T(8,128)(2,1)S(1)} %get-tuple-element.33), channel_id=1, source_target_pairs={{0,4},{1,5},{2,6},{3,7},{4,0},{5,1},{6,2},{7,3},{8,12},{9,13},{10,... | collective-permute-start | bytes 196616 | tf_op jit(solution)/shard_map/ppermute | solution.py:33
  80.0 47.5 %copy-start.4 = (bf16[1,512,512]{2,1,0:T(8,128)(2,1)}, bf16[1,512,512]{2,1,0:T(8,128)(2,1)S(1)}, u32[]{:S(2)}) copy-start(bf16[1,512,512]{2,1,0:T(8,128)(2,1)S(1)} %collective-permute-done.11.refs_2_.refs_10_) | copy-start | bytes 1572868
  80.0 47.5 %copy-start.6 = (bf16[1,512,512]{2,1,0:T(8,128)(2,1)}, bf16[1,512,512]{2,1,0:T(8,128)(2,1)S(1)}, u32[]{:S(2)}) copy-start(bf16[1,512,512]{2,1,0:T(8,128)(2,1)S(1)} %collective-permute-done.12.refs_3_.refs_11_) | copy-start | bytes 1572868
  80.6 1.4 collective-permute-start.13
  82.8 44.6 %copy-start.29 = (bf16[64,2048]{1,0:T(8,128)(2,1)}, bf16[64,2048]{1,0:T(8,128)(2,1)S(1)}, u32[]{:S(2)}) copy-start(bf16[64,2048]{1,0:T(8,128)(2,1)S(1)} %get-tuple-element.43) | copy-start | bytes 786436
  82.8 40.3 %collective-permute-start.14 = (bf16[64,2048]{1,0:T(8,128)(2,1)S(1)}, bf16[64,2048]{1,0:T(8,128)(2,1)S(1)}, u32[]{:S(2)}, u32[]{:S(2)}) collective-permute-start(bf16[64,2048]{1,0:T(8,128)(2,1)S(1)} %get-tuple-element.43), channel_id=1, source_target_pairs={{0,128},{256,384},{1,129},{257,385},{2,130},{258,386},{3,131},{259... | collective-permute-start | bytes 786440 | tf_op jit(solution)/shard_map/ppermute | solution.py:413
  84.1 43.3 %collective-permute-start.16 = (bf16[3,512,256]{2,1,0:T(8,128)(2,1)S(1)}, bf16[3,512,256]{2,1,0:T(8,128)(2,1)S(1)}, u32[]{:S(2)}, u32[]{:S(2)}) collective-permute-start(bf16[3,512,256]{2,1,0:T(8,128)(2,1)S(1)} %get-tuple-element.37.refs_4_), channel_id=1, source_target_pairs={{128,144},{129,145},{130,146},{131,147},{132,148},{133,149},{134,1... | collective-permute-start | bytes 2359304 | tf_op jit(solution)/shard_map/ppermute | solution.py:33
  86.0 41.4 %collective-permute-start.17 = (bf16[3,512,256]{2,1,0:T(8,128)(2,1)S(1)}, bf16[3,512,256]{2,1,0:T(8,128)(2,1)S(1)}, u32[]{:S(2)}, u32[]{:S(2)}) collective-permute-start(bf16[3,512,256]{2,1,0:T(8,128)(2,1)S(1)} %get-tuple-element.37.refs_4_), channel_id=1, source_target_pairs={{128,176},{129,177},{130,178},{131,179},{132,180},{133,181},{134,1... | collective-permute-start | bytes 2359304 | tf_op jit(solution)/shard_map/ppermute | solution.py:33
  89.8 37.7 %collective-permute-start.18 = (bf16[3,512,256]{2,1,0:T(8,128)(2,1)S(1)}, bf16[3,512,256]{2,1,0:T(8,128)(2,1)S(1)}, u32[]{:S(2)}, u32[]{:S(2)}) collective-permute-start(bf16[3,512,256]{2,1,0:T(8,128)(2,1)S(1)} %get-tuple-element.37.refs_4_), channel_id=1, source_target_pairs={{128,160},{129,161},{130,162},{131,163},{132,164},{133,165},{134,1... | collective-permute-start | bytes 2359304 | tf_op jit(solution)/shard_map/ppermute | solution.py:33
  123.1 3.5 %collective-permute-start.15 = (bf16[64,2048]{1,0:T(8,128)(2,1)S(1)}, bf16[64,2048]{1,0:T(8,128)(2,1)S(1)}, u32[]{:S(2)}, u32[]{:S(2)}) collective-permute-start(bf16[64,2048]{1,0:T(8,128)(2,1)S(1)} %collective-permute-done.14.mine.hop_m), channel_id=1, source_target_pairs={{128,192},{192,128},{384,448},{448,384},{129,193},{193,129},{385,4... | collective-permute-start | bytes 786440 | tf_op jit(solution)/shard_map/ppermute | solution.py:362
  129.4 0.7 collective-permute-start.19
  131.3 18.2 %collective-permute-start.21 = (bf16[64,2048]{1,0:T(8,128)(2,1)S(1)}, bf16[64,2048]{1,0:T(8,128)(2,1)}, u32[]{:S(2)}, u32[]{:S(2)}) collective-permute-start(bf16[64,2048]{1,0:T(8,128)(2,1)S(1)} %fusion.2), channel_id=1, source_target_pairs={{128,384},{129,385},{130,386},{131,387},{132,388},{133,389},{134,3... | collective-permute-start | bytes 786440 | tf_op jit(solution)/shard_map/ppermute | solution.py:434
  149.5 4.6 %collective-permute-start.22 = (bf16[64,2048]{1,0:T(8,128)(2,1)}, bf16[64,2048]{1,0:T(8,128)(2,1)}, u32[]{:S(2)}, u32[]{:S(2)}) collective-permute-start(bf16[64,2048]{1,0:T(8,128)(2,1)} %collective-permute-done.21.mem_mine), channel_id=1, source_target_pairs={{384,448},{448,384},{385,449},{449,385},{386,450},{450,386},{387,4... | collective-permute-start | bytes 786440 | tf_op jit(solution)/shard_map/ppermute | solution.py:362
  167.5 3.8 %collective-permute-start.23 = (bf16[128,2048]{1,0:T(8,128)(2,1)S(1)}, bf16[128,2048]{1,0:T(8,128)(2,1)S(1)}, u32[]{:S(2)}, u32[]{:S(2)}) collective-permute-start(bf16[128,2048]{1,0:T(8,128)(2,1)S(1)} %shard_map.69.own), channel_id=1, source_target_pairs={{384,448},{385,449},{386,450},{387,451},{388,452},{389,453},{390,4... | collective-permute-start | bytes 1572872 | tf_op jit(solution)/shard_map/ppermute | solution.py:448
  168.8 0.7 collective-permute-start.20
  (28 other events, 206.8 us)

commit v12 on v7

--- a/solution.py
+++ b/solution.py
@@ -167,7 +167,7 @@
 
 
 def second_kernel(scal, gains, mine, other, *refs):
-    pieces, (out_mine, out_other, h3, t3, space, sems) = refs[:9], refs[9:]
+    pieces, (out_mine, out_other, query, h3, t3, space, sems) = refs[:9], refs[9:]
 
     @pl.when(scal[2] == 1)
     def _():
@@ -176,15 +176,11 @@
         done = project(scal, h3, fetched, TURNS, (0, 1, 2))
         project_out(scal, attend(scal, *done), fetched, t3, out_mine, out_other)
 
-
-def query_kernel(scal, gains, mine, other, *refs):
-    pieces, (q, h3, space, sems) = refs[:9], refs[9:]
-
     @pl.when(scal[2] == 3)
     def _():
         fetched = Fetched(pieces, QUERY, space, sems)
         put_norm(scal, gains, (mine, other), h3)
-        q[...] = project(scal, h3, fetched, TURNS, (0,))[0].astype(BF16)
+        query[...] = project(scal, h3, fetched, TURNS, (0,))[0].astype(BF16)
 
 
 def third_kernel(scal, q, mem_mine, mem_other, *refs):
@@ -222,7 +218,7 @@
     )(scal, *operands, *pieces)
 
 
-def finish_kernel(scal, mine, other, in1m, in1o, in3m, in3o, early_m, early_o, own, got, out):
+def finish_kernel(scal, mine, other, hop_m, hop_o, early_m, early_o, own, got, out):
     rows = mine.shape[0]
     cube, core = scal[2], scal[6]
     even = (cube == 0) | (cube == 2)
@@ -235,13 +231,9 @@
     def _():
         put(mine, other)
 
-    @pl.when((core == 0) & (cube == 1))
-    def _():
-        put(in1m, in1o)
-
-    @pl.when((core == 0) & (cube == 3))
-    def _():
-        put(in3m, in3o)
+    @pl.when((core == 0) & jnp.logical_not(even))
+    def _():
+        put(hop_m, hop_o)
 
     @pl.when((core == 1) & (cube != 3))
     def _():
@@ -251,7 +243,7 @@
     def _():
         at = lax.broadcasted_iota(jnp.int32, mine.shape, 0)
         low, high = slice(0, rows), slice(rows, 2 * rows)
-        for slot, base, a, b, live in ((1, in3m, low, high, scal[7]), (0, in3o, high, low, scal[8])):
+        for slot, base, a, b, live in ((1, hop_m, low, high, scal[7]), (0, hop_o, high, low, scal[8])):
             term = own[a, :].astype(F32) + got[b, :].astype(F32)
             term = jnp.where(at < live, term, 0.0)
             out[slot] = (base[...].astype(F32) + term).astype(BF16)
@@ -343,35 +335,23 @@
         2 * work,
     )
     first = added(mine, kept + swapped(sent, (0, 2)).astype(F32), live).astype(BF16)
-    in1 = lax.ppermute(first, "zh", [(0, 1)])
-    in3 = lax.ppermute(first, "zh", [(2, 3)])
-    in1_other = swapped(in1, (1,))
-    kept, sent = call(
+    hop = lax.ppermute(first, "zh", [(0, 1), (2, 3)])
+    hop_other = swapped(hop, (1, 3))
+    kept, sent, query = call(
         second_kernel,
         scal,
-        [norm_gains, in1, in1_other],
-        halves,
+        [norm_gains, hop, hop_other],
+        (*halves, narrow),
         [(blocks, BF16), (blocks, F32)],
         pieces,
         len(SECOND),
         4 * work,
     )
-    second = added(in1, kept + swapped(sent, (1,)).astype(F32), live).astype(BF16)
+    second = added(hop, kept + swapped(sent, (1,)).astype(F32), live).astype(BF16)
     memory = rms(second.astype(F32), norm_gains[4:5])
     mem = lax.ppermute(memory, "zh", [(1, 3)])
     early = jnp.where(zh == 1, second, first)
     early_other = lax.ppermute(early, SECTION, [(0, 1), (2, 3), (4, 5)])
-    in3_other = swapped(in3, (3,))
-    query = call(
-        query_kernel,
-        scal,
-        [norm_gains, in3, in3_other],
-        narrow,
-        [(blocks, BF16)],
-        pieces,
-        len(QUERY),
-        work,
-    )
     mem_other = swapped(mem, (3,))
     own = call(
         third_kernel,
@@ -384,7 +364,7 @@
         3 * work,
     )
     got = lax.ppermute(own, SECTION, [(6, 7)])
-    parts = [mine, other, in1, in1_other, in3, in3_other, early, early_other, own, got]
+    parts = [mine, other, hop, hop_other, early, early_other, own, got]
     out = call(finish_kernel, scal, parts, jax.ShapeDtypeStruct((2, rows, width), BF16))
     return out[None]
 

time: 163 us -> 167 us (1.025)
  waiting for transfers between devices: 70.8 us -> 82.1 us
  starting transfers between devices: 49.1 us -> 42.6 us
    ppermute x1, waiting for transfers between devices: 10.5 us -> 16.9 us  [on_device(): mem = lax.ppermute(memory, 'zh', [(1, 3)])]
    ppermute x5 -> x4, starting transfers between devices: 13 us -> 7.23 us  [swapped(): return lax.ppermute(array, SECTION, pairs)]
    ppermute x5 -> x4, waiting for transfers between devices: 0.01 us -> 2.61 us  [swapped(): return lax.ppermute(array, SECTION, pairs)]
    ppermute x2 -> x1, waiting for transfers between devices: 33.2 us -> 35.5 us  [on_device(): hop = lax.ppermute(first, 'zh', [(0, 1), (2, 3)])]
    pallas_call x6 -> x5, Pallas kernels: 12.6 us -> 11 us  [call(): pl.pallas_call(kernel, out_shape=outs, in_specs=[SMEM] + [VMEM] * len(ope...]
  transfers between devices with their start and end apart: 20 -> 18, of which waited for: 9 -> 11; matrix products, arithmetic and copies ran while one was open for 6% -> 6% of each run, Pallas kernels for 2% -> 0%
where the time goes in v12:
time: 167 us; the launch traced here: 166 us
  waiting for transfers between devices  82.1 us (49%)
  starting transfers between devices  42.6 us (26%)
  blocking collectives  16.6 us (10%)
  Pallas kernels  11 us (7%)
  local copies, waits for them, and re-layouts  10 us (6%)
  other arithmetic  3.25 us (2%)
    ppermute x1, waiting for transfers between devices, on_device(): hop = lax.ppermute(first, 'zh', [(0, 1), (2, 3)])  35.5 us
    ppermute x10, starting transfers between devices, exchange(): return lax.ppermute(array, AXES, pairs)  30.8 us
    ppermute x10, waiting for transfers between devices, exchange(): return lax.ppermute(array, AXES, pairs)  25.3 us
    ppermute x1, waiting for transfers between devices, on_device(): mem = lax.ppermute(memory, 'zh', [(1, 3)])  16.9 us
    all_to_all x1, blocking collectives, gather(): got = lax.all_to_all(sent, ('core', 'zl'), 0, 0, tiled=True)  16.6 us
    pallas_call x5, Pallas kernels, call(): pl.pallas_call(kernel, out_shape=outs, in_specs=[SMEM] + [VMEM] * len(ope...  11 us
    ppermute x4, starting transfers between devices, swapped(): return lax.ppermute(array, SECTION, pairs)  7.23 us
  transfers between devices with their start and end apart: 18, of which 11 were waited for; matrix products, arithmetic and copies ran while one was open for 6% of the time, Pallas kernels for 0%

profile of v12, /device:TPU:481, one launch (start us, length us, event | category | flops | bytes accessed | tf_op | source)
XLA Modules:
  0.0 166.1 jit_solution(9156406112306083257)
XLA Ops:
  1.1 16.6 %all_to_all.5 = bf16[8,2,32,512]{3,2,1,0:T(8,128)(2,1)S(1)} all-to-all(bf16[8,2,32,512]{3,2,1,0:T(8,128)(2,1)S(1)} %bitcast.24), channel_id=1, replica_groups=mesh['zh'=4,'core'=2,'y'=4,'x'=4,'zl'=4] {'core','zl'}, dimensions={0} | all-to-all | bytes 1048576 | tf_op jit(solution)/shard_map/all_to_all | solution.py:261
  17.7 4.8 %collective-permute-start.2 = (bf16[4,128,512]{2,1,0:T(8,128)(2,1)S(1)}, bf16[4,128,512]{2,1,0:T(8,128)(2,1)S(1)}, u32[]{:S(2)}, u32[]{:S(2)}) collective-permute-start(bf16[4,128,512]{2,1,0:T(8,128)(2,1)S(1)} %bitcast.27), channel_id=1, source_target_pairs={{0,8},{1,9},{2,10},{3,11},{4,12},{5,13},{6,14},{7,15},{8,0},{9,1},... | collective-permute-start | bytes 1572872 | tf_op jit(solution)/shard_map/ppermute | solution.py:32
  22.5 2.7 %collective-permute-start.1 = (bf16[4,128,512]{2,1,0:T(8,128)(2,1)S(1)}, bf16[4,128,512]{2,1,0:T(8,128)(2,1)S(1)}, u32[]{:S(2)}, u32[]{:S(2)}) collective-permute-start(bf16[4,128,512]{2,1,0:T(8,128)(2,1)S(1)} %bitcast.28), channel_id=1, source_target_pairs={{0,12},{1,13},{2,14},{3,15},{4,8},{5,9},{6,10},{7,11},{8,4},{9,5},... | collective-permute-start | bytes 1572872 | tf_op jit(solution)/shard_map/ppermute | solution.py:32
  25.2 1.9 %collective-permute-start = (bf16[4,128,512]{2,1,0:T(8,128)(2,1)S(1)}, bf16[4,128,512]{2,1,0:T(8,128)(2,1)S(1)}, u32[]{:S(2)}, u32[]{:S(2)}) collective-permute-start(bf16[4,128,512]{2,1,0:T(8,128)(2,1)S(1)} %bitcast.29), channel_id=1, source_target_pairs={{0,4},{1,5},{2,6},{3,7},{4,0},{5,1},{6,2},{7,3},{8,12},{9,13},{10,... | collective-permute-start | bytes 1572872 | tf_op jit(solution)/shard_map/ppermute | solution.py:32
  27.2 2.2 %collective-permute-done.2 = bf16[4,128,512]{2,1,0:T(8,128)(2,1)S(1)} collective-permute-done((bf16[4,128,512]{2,1,0:T(8,128)(2,1)S(1)}, bf16[4,128,512]{2,1,0:T(8,128)(2,1)S(1)}, u32[]{:S(2)}, u32[]{:S(2)}) %collective-permute-start.2) | collective-permute-done | bytes 524320 | tf_op jit(solution)/shard_map/ppermute | solution.py:32
  29.4 5.6 %collective-permute-done.1 = bf16[4,128,512]{2,1,0:T(8,128)(2,1)S(1)} collective-permute-done((bf16[4,128,512]{2,1,0:T(8,128)(2,1)S(1)}, bf16[4,128,512]{2,1,0:T(8,128)(2,1)S(1)}, u32[]{:S(2)}, u32[]{:S(2)}) %collective-permute-start.1) | collective-permute-done | bytes 524320 | tf_op jit(solution)/shard_map/ppermute | solution.py:32
  35.5 4.4 %collective-permute-start.5 = (bf16[2,512,512]{2,1,0:T(8,128)(2,1)S(1)}, bf16[2,512,512]{2,1,0:T(8,128)(2,1)S(1)}, u32[]{:S(2)}, u32[]{:S(2)}) collective-permute-start(bf16[2,512,512]{2,1,0:T(8,128)(2,1)S(1)} %pad_maximum_fusion.refs_0_), channel_id=1, source_target_pairs={{0,48},{1,49},{2,50},{3,51},{4,52},{5,53},{6,54},{7,55},{8,56},{9,... | collective-permute-start | bytes 3145736 | tf_op jit(solution)/shard_map/ppermute | solution.py:32
  39.9 1.9 %collective-permute-start.3 = (bf16[2,512,512]{2,1,0:T(8,128)(2,1)S(1)}, bf16[2,512,512]{2,1,0:T(8,128)(2,1)}, u32[]{:S(2)}, u32[]{:S(2)}) collective-permute-start(bf16[2,512,512]{2,1,0:T(8,128)(2,1)S(1)} %pad_maximum_fusion.refs_0_), channel_id=1, source_target_pairs={{0,16},{1,17},{2,18},{3,19},{4,20},{5,21},{6,22},{7,23},{8,24},{9,... | collective-permute-start | bytes 3145736 | tf_op jit(solution)/shard_map/ppermute | solution.py:32
  42.0 2.7 %collective-permute-start.6 = (bf16[2,512,512]{2,1,0:T(8,128)(2,1)S(1)}, bf16[2,512,512]{2,1,0:T(8,128)(2,1)}, u32[]{:S(2)}, u32[]{:S(2)}) collective-permute-start(bf16[2,512,512]{2,1,0:T(8,128)(2,1)S(1)} %pad_maximum_fusion.1.refs_1_), channel_id=1, source_target_pairs={{0,48},{1,49},{2,50},{3,51},{4,52},{5,53},{6,54},{7,55},{8,56},{9,... | collective-permute-start | bytes 3145736 | tf_op jit(solution)/shard_map/ppermute | solution.py:32
  44.7 2.6 %collective-permute-start.4 = (bf16[2,512,512]{2,1,0:T(8,128)(2,1)S(1)}, bf16[2,512,512]{2,1,0:T(8,128)(2,1)}, u32[]{:S(2)}, u32[]{:S(2)}) collective-permute-start(bf16[2,512,512]{2,1,0:T(8,128)(2,1)S(1)} %pad_maximum_fusion.1.refs_1_), channel_id=1, source_target_pairs={{0,16},{1,17},{2,18},{3,19},{4,20},{5,21},{6,22},{7,23},{8,24},{9,... | collective-permute-start | bytes 3145736 | tf_op jit(solution)/shard_map/ppermute | solution.py:32
  47.3 4.3 %collective-permute-start.9 = (bf16[2,512,512]{2,1,0:T(8,128)(2,1)S(1)}, bf16[2,512,512]{2,1,0:T(8,128)(2,1)}, u32[]{:S(2)}, u32[]{:S(2)}) collective-permute-start(bf16[2,512,512]{2,1,0:T(8,128)(2,1)S(1)} %pad_maximum_fusion.1.refs_1_), channel_id=1, source_target_pairs={{0,32},{1,33},{2,34},{3,35},{4,36},{5,37},{6,38},{7,39},{8,40},{9,... | collective-permute-start | bytes 3145736 | tf_op jit(solution)/shard_map/ppermute | solution.py:32
  51.6 1.9 %broadcast_select_fusion = bf16[2,64,2048]{2,1,0:T(8,128)(2,1)} fusion(bf16[2,64,2048]{2,1,0:T(8,128)(2,1)} %param.6, bf16[2,64,2048]{2,1,0:T(8,128)(2,1)} %param.7, pred[]{:T(512)S(6)} %lt.26), kind=kLoop, calls=%fused_computation.9 | loop fusion | flops 262144 | bytes 1572865 | tf_op jit(solution)/shard_map/jit(_where)/select_n | solution.py:298
  54.3 2.3 %collective-permute-start.7 = (bf16[1,512,512]{2,1,0:T(8,128)(2,1)}, bf16[1,512,512]{2,1,0:T(8,128)(2,1)}, u32[]{:S(2)}, u32[]{:S(2)}) collective-permute-start(bf16[1,512,512]{2,1,0:T(8,128)(2,1)} %slice.60), channel_id=1, source_target_pairs={{0,16},{1,17},{2,18},{3,19},{4,20},{5,21},{6,22},{7,23},{8,24},{9,... | collective-permute-start | bytes 1572872 | tf_op jit(solution)/shard_map/ppermute | solution.py:32
  56.6 1.9 %slice.61 = bf16[1,512,512]{2,1,0:T(8,128)(2,1)} slice(bf16[2,512,512]{2,1,0:T(8,128)(2,1)} %collective-permute-done.3.refs_2_), slice={[1:2], [0:512], [0:512]} | slice | bytes 1048576 | tf_op jit(solution)/shard_map/slice | solution.py:269
  58.5 3.2 %collective-permute-start.8 = (bf16[1,512,512]{2,1,0:T(8,128)(2,1)}, bf16[1,512,512]{2,1,0:T(8,128)(2,1)}, u32[]{:S(2)}, u32[]{:S(2)}) collective-permute-start(bf16[1,512,512]{2,1,0:T(8,128)(2,1)} %slice.61), channel_id=1, source_target_pairs={{0,48},{1,49},{2,50},{3,51},{4,52},{5,53},{6,54},{7,55},{8,56},{9,... | collective-permute-start | bytes 1572872 | tf_op jit(solution)/shard_map/ppermute | solution.py:32
  62.5 2.6 %stack.27.scal = s32[9]{0:T(128)S(1)} concatenate(s32[1]{0:T(128)} %bitcast, s32[1]{0:T(128)} %bitcast.1, s32[1]{0:T(128)} %bitcast.2, s32[1]{0:T(128)} %bitcast.3, s32[1]{0:T(128)} %get-tuple-element.41, s32[1]{0:T(128)} %get-tuple-element.42, s32[1]{0:T(128)} %bitcast.4, s32[1]{0:T(128)} %get-tuple-element.38, s32[1]{0:T(128)} %get-tuple-element.37), dimensions={0} | concatenate | bytes 72 | tf_op jit(solution)/shard_map/stack | solution.py:281
  65.1 1.1 dynamic-slice_bitcast_fusion
  67.8 10.5 %collective-permute-done.9.refs_8_ = bf16[2,512,512]{2,1,0:T(8,128)(2,1)} collective-permute-done((bf16[2,512,512]{2,1,0:T(8,128)(2,1)S(1)}, bf16[2,512,512]{2,1,0:T(8,128)(2,1)}, u32[]{:S(2)}, u32[]{:S(2)}) %collective-permute-start.9) | collective-permute-done | bytes 1048608 | tf_op jit(solution)/shard_map/ppermute | solution.py:32
  78.3 5.7 %collective-permute-done.7.refs_6_ = bf16[1,512,512]{2,1,0:T(8,128)(2,1)} collective-permute-done((bf16[1,512,512]{2,1,0:T(8,128)(2,1)}, bf16[1,512,512]{2,1,0:T(8,128)(2,1)}, u32[]{:S(2)}, u32[]{:S(2)}) %collective-permute-start.7) | collective-permute-done | bytes 524320 | tf_op jit(solution)/shard_map/ppermute | solution.py:32
  86.1 1.3 collective-permute-start.11
  87.4 35.5 %collective-permute-done.11.mine.hop_m = bf16[64,2048]{1,0:T(8,128)(2,1)S(1)} collective-permute-done((bf16[64,2048]{1,0:T(8,128)(2,1)S(1)}, bf16[64,2048]{1,0:T(8,128)(2,1)S(1)}, u32[]{:S(2)}, u32[]{:S(2)}) %collective-permute-start.11) | collective-permute-done | bytes 262176 | tf_op jit(solution)/shard_map/ppermute | solution.py:338
  122.9 2.8 %collective-permute-start.12 = (bf16[64,2048]{1,0:T(8,128)(2,1)S(1)}, bf16[64,2048]{1,0:T(8,128)(2,1)S(1)}, u32[]{:S(2)}, u32[]{:S(2)}) collective-permute-start(bf16[64,2048]{1,0:T(8,128)(2,1)S(1)} %collective-permute-done.11.mine.hop_m), channel_id=1, source_target_pairs={{128,192},{192,128},{384,448},{448,384},{129,193},{193,129},{385,4... | collective-permute-start | bytes 786440 | tf_op jit(solution)/shard_map/ppermute | solution.py:306
  125.7 1.1 collective-permute-done.12.other.hop_o
  126.9 2.3 %shard_map.66 = (f32[64,2048]{1,0:T(8,128)S(1)}, bf16[64,2048]{1,0:T(8,128)(2,1)S(1)}, bf16[128,512]{1,0:T(8,128)(2,1)S(1)}) custom-call(s32[9]{0:T(128)S(1)} %stack.27.scal, f32[5,2048]{1,0:T(8,128)S(1)} %copy-done.6, bf16[64,2048]{1,0:T(8,128)(2,1)S(1)} %collective-permute-done.11.mine.hop_m, bf16[64,2048]{1,0:T(8,128)(2,1)S(1)} %collective-permute-done.12.other.hop_o, ...), custom_call_target="tpu_custom_call" | custom-call | flops 1073741824 | bytes 8953856 | tf_op jit(solution)/shard_map/pallas_call | solution.py:210
  131.1 1.3 collective-permute-start.15
  132.4 16.9 %collective-permute-done.15.mem_mine = bf16[64,2048]{1,0:T(8,128)(2,1)} collective-permute-done((bf16[64,2048]{1,0:T(8,128)(2,1)S(1)}, bf16[64,2048]{1,0:T(8,128)(2,1)}, u32[]{:S(2)}, u32[]{:S(2)}) %collective-permute-start.15) | collective-permute-done | bytes 262176 | tf_op jit(solution)/shard_map/ppermute | solution.py:352
  149.3 3.1 %collective-permute-start.16 = (bf16[64,2048]{1,0:T(8,128)(2,1)}, bf16[64,2048]{1,0:T(8,128)(2,1)}, u32[]{:S(2)}, u32[]{:S(2)}) collective-permute-start(bf16[64,2048]{1,0:T(8,128)(2,1)} %collective-permute-done.15.mem_mine), channel_id=1, source_target_pairs={{384,448},{448,384},{385,449},{449,385},{386,450},{450,386},{387,4... | collective-permute-start | bytes 786440 | tf_op jit(solution)/shard_map/ppermute | solution.py:306
  152.4 1.5 collective-permute-done.16.mem_other
  154.8 5.8 %shard_map.67.own = bf16[128,2048]{1,0:T(8,128)(2,1)S(1)} custom-call(s32[9]{0:T(128)S(1)} %stack.27.scal, bf16[128,512]{1,0:T(8,128)(2,1)S(1)} %copy-done.8, bf16[64,2048]{1,0:T(8,128)(2,1)} %collective-permute-done.15.mem_mine, bf16[64,2048]{1,0:T(8,128)(2,1)} %collective-permute-done.16.mem_other, bf16[2,512,512]{2,1,0:T(8,128)(2,1)S(1)} %pad_maximum_fusion.refs_0_, ...), custom_call_target="tpu_custom_call" | custom-call | flops 805306368 | bytes 9043968 | tf_op jit(solution)/shard_map/pallas_call | solution.py:210
  160.7 1.3 collective-permute-start.17
  162.7 1.8 %collective-permute-done.17.got = bf16[128,2048]{1,0:T(8,128)(2,1)S(1)} collective-permute-done((bf16[128,2048]{1,0:T(8,128)(2,1)S(1)}, bf16[128,2048]{1,0:T(8,128)(2,1)S(1)}, u32[]{:S(2)}, u32[]{:S(2)}) %collective-permute-start.17) | collective-permute-done | bytes 524320 | tf_op jit(solution)/shard_map/ppermute | solution.py:366
  164.5 1.6 shard_map.68
  (66 shorter events, 10.3 us)
Async XLA Ops:
  17.7 11.7 %collective-permute-start.2 = (bf16[4,128,512]{2,1,0:T(8,128)(2,1)S(1)}, bf16[4,128,512]{2,1,0:T(8,128)(2,1)S(1)}, u32[]{:S(2)}, u32[]{:S(2)}) collective-permute-start(bf16[4,128,512]{2,1,0:T(8,128)(2,1)S(1)} %bitcast.27), channel_id=1, source_target_pairs={{0,8},{1,9},{2,10},{3,11},{4,12},{5,13},{6,14},{7,15},{8,0},{9,1},... | collective-permute-start | bytes 1572872 | tf_op jit(solution)/shard_map/ppermute | solution.py:32
  22.5 12.5 %collective-permute-start.1 = (bf16[4,128,512]{2,1,0:T(8,128)(2,1)S(1)}, bf16[4,128,512]{2,1,0:T(8,128)(2,1)S(1)}, u32[]{:S(2)}, u32[]{:S(2)}) collective-permute-start(bf16[4,128,512]{2,1,0:T(8,128)(2,1)S(1)} %bitcast.28), channel_id=1, source_target_pairs={{0,12},{1,13},{2,14},{3,15},{4,8},{5,9},{6,10},{7,11},{8,4},{9,5},... | collective-permute-start | bytes 1572872 | tf_op jit(solution)/shard_map/ppermute | solution.py:32
  25.2 10.2 %collective-permute-start = (bf16[4,128,512]{2,1,0:T(8,128)(2,1)S(1)}, bf16[4,128,512]{2,1,0:T(8,128)(2,1)S(1)}, u32[]{:S(2)}, u32[]{:S(2)}) collective-permute-start(bf16[4,128,512]{2,1,0:T(8,128)(2,1)S(1)} %bitcast.29), channel_id=1, source_target_pairs={{0,4},{1,5},{2,6},{3,7},{4,0},{5,1},{6,2},{7,3},{8,12},{9,13},{10,... | collective-permute-start | bytes 1572872 | tf_op jit(solution)/shard_map/ppermute | solution.py:32
  35.5 18.0 %collective-permute-start.5 = (bf16[2,512,512]{2,1,0:T(8,128)(2,1)S(1)}, bf16[2,512,512]{2,1,0:T(8,128)(2,1)S(1)}, u32[]{:S(2)}, u32[]{:S(2)}) collective-permute-start(bf16[2,512,512]{2,1,0:T(8,128)(2,1)S(1)} %pad_maximum_fusion.refs_0_), channel_id=1, source_target_pairs={{0,48},{1,49},{2,50},{3,51},{4,52},{5,53},{6,54},{7,55},{8,56},{9,... | collective-permute-start | bytes 3145736 | tf_op jit(solution)/shard_map/ppermute | solution.py:32
  39.9 16.7 %collective-permute-start.3 = (bf16[2,512,512]{2,1,0:T(8,128)(2,1)S(1)}, bf16[2,512,512]{2,1,0:T(8,128)(2,1)}, u32[]{:S(2)}, u32[]{:S(2)}) collective-permute-start(bf16[2,512,512]{2,1,0:T(8,128)(2,1)S(1)} %pad_maximum_fusion.refs_0_), channel_id=1, source_target_pairs={{0,16},{1,17},{2,18},{3,19},{4,20},{5,21},{6,22},{7,23},{8,24},{9,... | collective-permute-start | bytes 3145736 | tf_op jit(solution)/shard_map/ppermute | solution.py:32
  42.0 24.2 %collective-permute-start.6 = (bf16[2,512,512]{2,1,0:T(8,128)(2,1)S(1)}, bf16[2,512,512]{2,1,0:T(8,128)(2,1)}, u32[]{:S(2)}, u32[]{:S(2)}) collective-permute-start(bf16[2,512,512]{2,1,0:T(8,128)(2,1)S(1)} %pad_maximum_fusion.1.refs_1_), channel_id=1, source_target_pairs={{0,48},{1,49},{2,50},{3,51},{4,52},{5,53},{6,54},{7,55},{8,56},{9,... | collective-permute-start | bytes 3145736 | tf_op jit(solution)/shard_map/ppermute | solution.py:32
  44.7 22.4 %collective-permute-start.4 = (bf16[2,512,512]{2,1,0:T(8,128)(2,1)S(1)}, bf16[2,512,512]{2,1,0:T(8,128)(2,1)}, u32[]{:S(2)}, u32[]{:S(2)}) collective-permute-start(bf16[2,512,512]{2,1,0:T(8,128)(2,1)S(1)} %pad_maximum_fusion.1.refs_1_), channel_id=1, source_target_pairs={{0,16},{1,17},{2,18},{3,19},{4,20},{5,21},{6,22},{7,23},{8,24},{9,... | collective-permute-start | bytes 3145736 | tf_op jit(solution)/shard_map/ppermute | solution.py:32
  47.3 31.0 %collective-permute-start.9 = (bf16[2,512,512]{2,1,0:T(8,128)(2,1)S(1)}, bf16[2,512,512]{2,1,0:T(8,128)(2,1)}, u32[]{:S(2)}, u32[]{:S(2)}) collective-permute-start(bf16[2,512,512]{2,1,0:T(8,128)(2,1)S(1)} %pad_maximum_fusion.1.refs_1_), channel_id=1, source_target_pairs={{0,32},{1,33},{2,34},{3,35},{4,36},{5,37},{6,38},{7,39},{8,40},{9,... | collective-permute-start | bytes 3145736 | tf_op jit(solution)/shard_map/ppermute | solution.py:32
  53.5 8.3 %copy-start.13 = (s32[2]{0:T(128)S(1)}, s32[2]{0:T(128)}, u32[]{:S(2)}) copy-start(s32[2]{0:T(128)} %param.10) | copy-start | bytes 28
  53.5 8.3 %copy-start.14 = (s32[2]{0:T(128)S(1)}, s32[2]{0:T(128)}, u32[]{:S(2)}) copy-start(s32[2]{0:T(128)} %param.11) | copy-start | bytes 28
  54.3 12.8 %copy-start.6 = (f32[5,2048]{1,0:T(8,128)S(1)}, f32[5,2048]{1,0:T(8,128)}, u32[]{:S(2)}) copy-start(f32[5,2048]{1,0:T(8,128)} %gains.3) | copy-start | bytes 122884
  54.3 29.7 %collective-permute-start.7 = (bf16[1,512,512]{2,1,0:T(8,128)(2,1)}, bf16[1,512,512]{2,1,0:T(8,128)(2,1)}, u32[]{:S(2)}, u32[]{:S(2)}) collective-permute-start(bf16[1,512,512]{2,1,0:T(8,128)(2,1)} %slice.60), channel_id=1, source_target_pairs={{0,16},{1,17},{2,18},{3,19},{4,20},{5,21},{6,22},{7,23},{8,24},{9,... | collective-permute-start | bytes 1572872 | tf_op jit(solution)/shard_map/ppermute | solution.py:32
  58.5 25.5 %collective-permute-start.8 = (bf16[1,512,512]{2,1,0:T(8,128)(2,1)}, bf16[1,512,512]{2,1,0:T(8,128)(2,1)}, u32[]{:S(2)}, u32[]{:S(2)}) collective-permute-start(bf16[1,512,512]{2,1,0:T(8,128)(2,1)} %slice.61), channel_id=1, source_target_pairs={{0,48},{1,49},{2,50},{3,51},{4,52},{5,53},{6,54},{7,55},{8,56},{9,... | collective-permute-start | bytes 1572872 | tf_op jit(solution)/shard_map/ppermute | solution.py:32
  66.2 1.6 copy-start
  84.6 1.3 collective-permute-start.10
  86.1 39.6 %copy-start.11 = (bf16[64,2048]{1,0:T(8,128)(2,1)}, bf16[64,2048]{1,0:T(8,128)(2,1)S(1)}, u32[]{:S(2)}) copy-start(bf16[64,2048]{1,0:T(8,128)(2,1)S(1)} %add_convert_fusion.1) | copy-start | bytes 786436
  86.1 36.8 %collective-permute-start.11 = (bf16[64,2048]{1,0:T(8,128)(2,1)S(1)}, bf16[64,2048]{1,0:T(8,128)(2,1)S(1)}, u32[]{:S(2)}, u32[]{:S(2)}) collective-permute-start(bf16[64,2048]{1,0:T(8,128)(2,1)S(1)} %add_convert_fusion.1), channel_id=1, source_target_pairs={{0,128},{256,384},{1,129},{257,385},{2,130},{258,386},{3,131},{259... | collective-permute-start | bytes 786440 | tf_op jit(solution)/shard_map/ppermute | solution.py:338
  122.9 7.0 %copy-start.2 = (bf16[64,2048]{1,0:T(8,128)(2,1)}, bf16[64,2048]{1,0:T(8,128)(2,1)S(1)}, u32[]{:S(2)}) copy-start(bf16[64,2048]{1,0:T(8,128)(2,1)S(1)} %collective-permute-done.11.mine.hop_m) | copy-start | bytes 786436
  122.9 3.9 %collective-permute-start.12 = (bf16[64,2048]{1,0:T(8,128)(2,1)S(1)}, bf16[64,2048]{1,0:T(8,128)(2,1)S(1)}, u32[]{:S(2)}, u32[]{:S(2)}) collective-permute-start(bf16[64,2048]{1,0:T(8,128)(2,1)S(1)} %collective-permute-done.11.mine.hop_m), channel_id=1, source_target_pairs={{128,192},{192,128},{384,448},{448,384},{129,193},{193,129},{385,4... | collective-permute-start | bytes 786440 | tf_op jit(solution)/shard_map/ppermute | solution.py:306
  126.9 2.3 %copy-start.4 = (bf16[64,2048]{1,0:T(8,128)(2,1)}, bf16[64,2048]{1,0:T(8,128)(2,1)S(1)}, u32[]{:S(2)}) copy-start(bf16[64,2048]{1,0:T(8,128)(2,1)S(1)} %collective-permute-done.12.other.hop_o) | copy-start | bytes 786436
  129.2 1.0 copy-start.7
  129.2 0.7 collective-permute-start.13
  131.1 18.2 %collective-permute-start.15 = (bf16[64,2048]{1,0:T(8,128)(2,1)S(1)}, bf16[64,2048]{1,0:T(8,128)(2,1)}, u32[]{:S(2)}, u32[]{:S(2)}) collective-permute-start(bf16[64,2048]{1,0:T(8,128)(2,1)S(1)} %fusion.2), channel_id=1, source_target_pairs={{128,384},{129,385},{130,386},{131,387},{132,388},{133,389},{134,3... | collective-permute-start | bytes 786440 | tf_op jit(solution)/shard_map/ppermute | solution.py:352
  149.3 4.6 %collective-permute-start.16 = (bf16[64,2048]{1,0:T(8,128)(2,1)}, bf16[64,2048]{1,0:T(8,128)(2,1)}, u32[]{:S(2)}, u32[]{:S(2)}) collective-permute-start(bf16[64,2048]{1,0:T(8,128)(2,1)} %collective-permute-done.15.mem_mine), channel_id=1, source_target_pairs={{384,448},{448,384},{385,449},{449,385},{386,450},{450,386},{387,4... | collective-permute-start | bytes 786440 | tf_op jit(solution)/shard_map/ppermute | solution.py:306
  153.9 0.9 copy-start.8
  154.8 7.2 %copy-start.10 = (bf16[64,2048]{1,0:T(8,128)(2,1)S(1)}, bf16[64,2048]{1,0:T(8,128)(2,1)}, u32[]{:S(2)}) copy-start(bf16[64,2048]{1,0:T(8,128)(2,1)} %copy-done.9) | copy-start | bytes 786436
  154.8 7.2 %copy-start.12 = (bf16[64,2048]{1,0:T(8,128)(2,1)S(1)}, bf16[64,2048]{1,0:T(8,128)(2,1)}, u32[]{:S(2)}) copy-start(bf16[64,2048]{1,0:T(8,128)(2,1)} %copy-done.11) | copy-start | bytes 786436
  154.8 9.7 %copy-start.1 = (bf16[64,2048]{1,0:T(8,128)(2,1)S(1)}, bf16[64,2048]{1,0:T(8,128)(2,1)}, u32[]{:S(2)}) copy-start(bf16[64,2048]{1,0:T(8,128)(2,1)} %copy-done) | copy-start | bytes 786436
  154.8 9.7 %copy-start.3 = (bf16[64,2048]{1,0:T(8,128)(2,1)S(1)}, bf16[64,2048]{1,0:T(8,128)(2,1)}, u32[]{:S(2)}) copy-start(bf16[64,2048]{1,0:T(8,128)(2,1)} %copy-done.2) | copy-start | bytes 786436
  154.8 9.7 %copy-start.5 = (bf16[64,2048]{1,0:T(8,128)(2,1)S(1)}, bf16[64,2048]{1,0:T(8,128)(2,1)}, u32[]{:S(2)}) copy-start(bf16[64,2048]{1,0:T(8,128)(2,1)} %copy-done.4) | copy-start | bytes 786436
  160.7 3.8 %collective-permute-start.17 = (bf16[128,2048]{1,0:T(8,128)(2,1)S(1)}, bf16[128,2048]{1,0:T(8,128)(2,1)S(1)}, u32[]{:S(2)}, u32[]{:S(2)}) collective-permute-start(bf16[128,2048]{1,0:T(8,128)(2,1)S(1)} %shard_map.67.own), channel_id=1, source_target_pairs={{384,448},{385,449},{386,450},{387,451},{388,452},{389,453},{390,4... | collective-permute-start | bytes 1572872 | tf_op jit(solution)/shard_map/ppermute | solution.py:366
  162.0 0.7 collective-permute-start.14
  (1 other events, 0.7 us)

commit v13 on v7

--- a/solution.py
+++ b/solution.py
@@ -52,10 +52,7 @@
 
 
 def weight(pieces, turn, which):
-    chunk, at = divmod(which, 2)
-    if turn == FAR:
-        return pieces[8].at[at] if chunk else pieces[6 + which].at[0]
-    return pieces[2 * TURNS.index(turn) + chunk].at[at]
+    return pieces[4 * TURNS.index(turn) + which].at[0]
 
 
 class Fetched:
@@ -139,14 +136,15 @@
 
 
 EARLY = wanted(TURNS[:3], (0, 1, 2), False)
-FIRST = wanted(TURNS[3:], (0, 1, 2))
+FIRST = wanted(TURNS[3:], (0, 1, 2), False)
+OUT = wanted((), ())
 SECOND = wanted(TURNS, (0, 1, 2))
 QUERY = wanted(TURNS, (0,), False)
 THIRD = wanted(TURNS, (1, 2))
 
 
 def early_kernel(scal, gains, mine, other, *refs):
-    pieces, (h3, q, k, v, space, sems) = refs[:6], refs[6:]
+    pieces, (h3, q, k, v, space, sems) = refs[:12], refs[12:]
 
     @pl.when(lax.rem(scal[2], 2) == 0)
     def _():
@@ -156,18 +154,27 @@
 
 
 def first_kernel(scal, h3, q, k, v, *refs):
-    pieces, (out_mine, out_other, t3, space, sems) = refs[:9], refs[9:]
+    pieces, (mixed, space, sems) = (None,) * 12 + refs[:3], refs[3:]
 
     @pl.when(lax.rem(scal[2], 2) == 0)
     def _():
         fetched = Fetched(pieces, FIRST, space, sems)
         done = (q[...], k[...], v[...])
-        done = project(scal, h3, fetched, TURNS[3:], (0, 1, 2), done)
-        project_out(scal, attend(scal, *done), fetched, t3, out_mine, out_other)
+        mixed[...] = attend(scal, *project(scal, h3, fetched, TURNS[3:], (0, 1, 2), done))
+
+
+def first_out_kernel(scal, mixed, *refs):
+    pieces, (out_mine, out_other, t3, space, sems) = refs[:4], refs[4:]
+
+    @pl.when(lax.rem(scal[2], 2) == 0)
+    def _():
+        spread = [ref for piece in pieces for ref in (None, None, None, piece)]
+        fetched = Fetched(spread, OUT, space, sems)
+        project_out(scal, mixed[...], fetched, t3, out_mine, out_other)
 
 
 def second_kernel(scal, gains, mine, other, *refs):
-    pieces, (out_mine, out_other, h3, t3, space, sems) = refs[:9], refs[9:]
+    pieces, (out_mine, out_other, h3, t3, space, sems) = refs[:16], refs[16:]
 
     @pl.when(scal[2] == 1)
     def _():
@@ -178,7 +185,7 @@
 
 
 def query_kernel(scal, gains, mine, other, *refs):
-    pieces, (q, h3, space, sems) = refs[:9], refs[9:]
+    pieces, (q, h3, space, sems) = refs[:16], refs[16:]
 
     @pl.when(scal[2] == 3)
     def _():
@@ -188,7 +195,7 @@
 
 
 def third_kernel(scal, q, mem_mine, mem_other, *refs):
-    pieces, (out, m3, t3, space, sems) = refs[:9], refs[9:]
+    pieces, (out, m3, t3, space, sems) = refs[:16], refs[16:]
 
     @pl.when(scal[2] == 3)
     def _():
@@ -270,12 +277,11 @@
     got = got.reshape(2, SIDE, pair, depth, width // 2).transpose(0, 2, 1, 3, 4)
     got = got.reshape(2 * pair, SIDE * depth, width // 2)
     near = turns(got, False)
-    chunks = [jnp.concatenate([a[i:i + pair] for a in near], axis=1) for i in (0, pair)]
-    by1 = [exchange(a, True, 1) for a in chunks]
-    by3 = [exchange(a, True, 3) for a in chunks]
-    across = exchange(chunks[1], True, FAR)
-    far = [exchange(by3[0][:1], True, 1), exchange(by1[0][1:], True, 3), across]
-    return [*chunks, *by1, *by3], far
+    parts = [jnp.concatenate([a[i:i + 1] for a in near], axis=1) for i in range(2 * pair)]
+    by1 = [exchange(a, True, 1) for a in parts]
+    by3 = [exchange(a, True, 3) for a in parts]
+    far = [exchange((by1, by3)[i % 2][i], True, (3, 1)[i % 2]) for i in range(2 * pair)]
+    return [*parts, *by1, *by3], far
 
 
 def on_device(encoder_embed, decoder_embed, section_weights, norm_gains, input_lengths, target_lengths):
@@ -332,15 +338,11 @@
         len(EARLY),
         3 * work,
     )
+    mixed = call(
+        first_kernel, scal, [*started], narrow, (), far[:3], len(FIRST), work
+    )
     kept, sent = call(
-        first_kernel,
-        scal,
-        [*started],
-        halves,
-        [(blocks, F32)],
-        pieces,
-        len(FIRST),
-        2 * work,
+        first_out_kernel, scal, [mixed], halves, [(blocks, F32)], pieces[3::4], len(OUT), work
     )
     first = added(mine, kept + swapped(sent, (0, 2)).astype(F32), live).astype(BF16)
     in1 = lax.ppermute(first, "zh", [(0, 1)])

time: 163 us -> 165 us (1.012)
  starting transfers between devices: 49.1 us -> 56.3 us
  waiting for transfers between devices: 70.8 us -> 64.4 us
    ppermute x10 -> x15, waiting for transfers between devices: 25.3 us -> 11.2 us  [exchange(): return lax.ppermute(array, AXES, pairs)]
    ppermute x10 -> x15, starting transfers between devices: 30.8 us -> 43.5 us  [exchange(): return lax.ppermute(array, AXES, pairs)]
    ppermute x1, waiting for transfers between devices: 10.5 us -> 16.7 us  [on_device(): mem = lax.ppermute(memory, 'zh', [(1, 3)])]
    ppermute x5, starting transfers between devices: 13 us -> 7.43 us  [swapped(): return lax.ppermute(array, SECTION, pairs)]
    unnamed x26 -> x40, local copies, waits for them, and re-layouts: 0.76 us -> 3.62 us
    slice x8 -> x4, local copies, waits for them, and re-layouts: 2.9 us -> 0.14 us  [gather(): a[i:i + 1]]
    pallas_call x6 -> x7, Pallas kernels: 12.6 us -> 12.9 us  [call(): pl.pallas_call(kernel, out_shape=outs, in_specs=[SMEM] + [VMEM] * len(ope...]
  transfers between devices with their start and end apart: 20 -> 25, of which waited for: 9 -> 8; matrix products, arithmetic and copies ran while one was open for 6% -> 5% of each run, Pallas kernels for 2% -> 2%
where the time goes in v13:
time: 165 us; the launch traced here: 164 us
  waiting for transfers between devices  64.4 us (39%)
  starting transfers between devices  56.3 us (34%)
  blocking collectives  16.6 us (10%)
  Pallas kernels  12.9 us (8%)
  local copies, waits for them, and re-layouts  9.25 us (6%)
  other arithmetic  3.34 us (2%)
    ppermute x15, starting transfers between devices, exchange(): return lax.ppermute(array, AXES, pairs)  43.5 us
    ppermute x1, waiting for transfers between devices, on_device(): in3 = lax.ppermute(first, 'zh', [(2, 3)])  34.7 us
    ppermute x1, waiting for transfers between devices, on_device(): mem = lax.ppermute(memory, 'zh', [(1, 3)])  16.7 us
    all_to_all x1, blocking collectives, gather(): got = lax.all_to_all(sent, ('core', 'zl'), 0, 0, tiled=True)  16.6 us
    pallas_call x7, Pallas kernels, call(): pl.pallas_call(kernel, out_shape=outs, in_specs=[SMEM] + [VMEM] * len(ope...  12.9 us
    ppermute x15, waiting for transfers between devices, exchange(): return lax.ppermute(array, AXES, pairs)  11.2 us
    ppermute x5, starting transfers between devices, swapped(): return lax.ppermute(array, SECTION, pairs)  7.43 us
    unnamed x40, local copies, waits for them, and re-layouts  3.62 us
  transfers between devices with their start and end apart: 25, of which 8 were waited for; matrix products, arithmetic and copies ran while one was open for 5% of the time, Pallas kernels for 2%

profile of v13, /device:TPU:481, one launch (start us, length us, event | category | flops | bytes accessed | tf_op | source)
XLA Modules:
  0.0 163.5 jit_solution(14038532314119301631)
XLA Ops:
  1.1 16.6 %all_to_all.5 = bf16[8,2,32,512]{3,2,1,0:T(8,128)(2,1)S(1)} all-to-all(bf16[8,2,32,512]{3,2,1,0:T(8,128)(2,1)S(1)} %bitcast.20), channel_id=1, replica_groups=mesh['zh'=4,'core'=2,'y'=4,'x'=4,'zl'=4] {'core','zl'}, dimensions={0} | all-to-all | bytes 1048576 | tf_op jit(solution)/shard_map/all_to_all | solution.py:276
  17.7 4.8 %collective-permute-start.2 = (bf16[4,128,512]{2,1,0:T(8,128)(2,1)S(1)}, bf16[4,128,512]{2,1,0:T(8,128)(2,1)S(1)}, u32[]{:S(2)}, u32[]{:S(2)}) collective-permute-start(bf16[4,128,512]{2,1,0:T(8,128)(2,1)S(1)} %bitcast.21), channel_id=1, source_target_pairs={{0,8},{1,9},{2,10},{3,11},{4,12},{5,13},{6,14},{7,15},{8,0},{9,1},... | collective-permute-start | bytes 1572872 | tf_op jit(solution)/shard_map/ppermute | solution.py:32
  22.5 2.7 %collective-permute-start.1 = (bf16[4,128,512]{2,1,0:T(8,128)(2,1)S(1)}, bf16[4,128,512]{2,1,0:T(8,128)(2,1)S(1)}, u32[]{:S(2)}, u32[]{:S(2)}) collective-permute-start(bf16[4,128,512]{2,1,0:T(8,128)(2,1)S(1)} %bitcast.22), channel_id=1, source_target_pairs={{0,12},{1,13},{2,14},{3,15},{4,8},{5,9},{6,10},{7,11},{8,4},{9,5},... | collective-permute-start | bytes 1572872 | tf_op jit(solution)/shard_map/ppermute | solution.py:32
  25.2 1.9 %collective-permute-start = (bf16[4,128,512]{2,1,0:T(8,128)(2,1)S(1)}, bf16[4,128,512]{2,1,0:T(8,128)(2,1)S(1)}, u32[]{:S(2)}, u32[]{:S(2)}) collective-permute-start(bf16[4,128,512]{2,1,0:T(8,128)(2,1)S(1)} %bitcast.23), channel_id=1, source_target_pairs={{0,4},{1,5},{2,6},{3,7},{4,0},{5,1},{6,2},{7,3},{8,12},{9,13},{10,... | collective-permute-start | bytes 1572872 | tf_op jit(solution)/shard_map/ppermute | solution.py:32
  27.2 2.2 %collective-permute-done.2 = bf16[4,128,512]{2,1,0:T(8,128)(2,1)S(1)} collective-permute-done((bf16[4,128,512]{2,1,0:T(8,128)(2,1)S(1)}, bf16[4,128,512]{2,1,0:T(8,128)(2,1)S(1)}, u32[]{:S(2)}, u32[]{:S(2)}) %collective-permute-start.2) | collective-permute-done | bytes 524320 | tf_op jit(solution)/shard_map/ppermute | solution.py:32
  29.4 5.6 %collective-permute-done.1 = bf16[4,128,512]{2,1,0:T(8,128)(2,1)S(1)} collective-permute-done((bf16[4,128,512]{2,1,0:T(8,128)(2,1)S(1)}, bf16[4,128,512]{2,1,0:T(8,128)(2,1)S(1)}, u32[]{:S(2)}, u32[]{:S(2)}) %collective-permute-start.1) | collective-permute-done | bytes 524320 | tf_op jit(solution)/shard_map/ppermute | solution.py:32
  35.5 4.4 %collective-permute-start.7 = (bf16[1,512,512]{2,1,0:T(8,128)(2,1)S(1)}, bf16[1,512,512]{2,1,0:T(8,128)(2,1)S(1)}, u32[]{:S(2)}, u32[]{:S(2)}) collective-permute-start(bf16[1,512,512]{2,1,0:T(8,128)(2,1)S(1)} %pad_maximum_fusion.refs_0_), channel_id=1, source_target_pairs={{0,48},{1,49},{2,50},{3,51},{4,52},{5,53},{6,54},{7,55},{8,56},{9,... | collective-permute-start | bytes 1572872 | tf_op jit(solution)/shard_map/ppermute | solution.py:32
  39.9 1.9 %collective-permute-start.3 = (bf16[1,512,512]{2,1,0:T(8,128)(2,1)S(1)}, bf16[1,512,512]{2,1,0:T(8,128)(2,1)S(1)}, u32[]{:S(2)}, u32[]{:S(2)}) collective-permute-start(bf16[1,512,512]{2,1,0:T(8,128)(2,1)S(1)} %pad_maximum_fusion.refs_0_), channel_id=1, source_target_pairs={{0,16},{1,17},{2,18},{3,19},{4,20},{5,21},{6,22},{7,23},{8,24},{9,... | collective-permute-start | bytes 1572872 | tf_op jit(solution)/shard_map/ppermute | solution.py:32
  41.9 2.7 %collective-permute-start.8 = (bf16[1,512,512]{2,1,0:T(8,128)(2,1)S(1)}, bf16[1,512,512]{2,1,0:T(8,128)(2,1)}, u32[]{:S(2)}, u32[]{:S(2)}) collective-permute-start(bf16[1,512,512]{2,1,0:T(8,128)(2,1)S(1)} %pad_maximum_fusion.1.refs_1_), channel_id=1, source_target_pairs={{0,48},{1,49},{2,50},{3,51},{4,52},{5,53},{6,54},{7,55},{8,56},{9,... | collective-permute-start | bytes 1572872 | tf_op jit(solution)/shard_map/ppermute | solution.py:32
  44.6 2.6 %collective-permute-start.4 = (bf16[1,512,512]{2,1,0:T(8,128)(2,1)S(1)}, bf16[1,512,512]{2,1,0:T(8,128)(2,1)}, u32[]{:S(2)}, u32[]{:S(2)}) collective-permute-start(bf16[1,512,512]{2,1,0:T(8,128)(2,1)S(1)} %pad_maximum_fusion.1.refs_1_), channel_id=1, source_target_pairs={{0,16},{1,17},{2,18},{3,19},{4,20},{5,21},{6,22},{7,23},{8,24},{9,... | collective-permute-start | bytes 1572872 | tf_op jit(solution)/shard_map/ppermute | solution.py:32
  47.2 4.0 %collective-permute-start.9 = (bf16[1,512,512]{2,1,0:T(8,128)(2,1)S(1)}, bf16[1,512,512]{2,1,0:T(8,128)(2,1)}, u32[]{:S(2)}, u32[]{:S(2)}) collective-permute-start(bf16[1,512,512]{2,1,0:T(8,128)(2,1)S(1)} %pad_maximum_fusion.2.refs_2_), channel_id=1, source_target_pairs={{0,48},{1,49},{2,50},{3,51},{4,52},{5,53},{6,54},{7,55},{8,56},{9,... | collective-permute-start | bytes 1572872 | tf_op jit(solution)/shard_map/ppermute | solution.py:32
  52.0 1.9 %collective-permute-start.5 = (bf16[1,512,512]{2,1,0:T(8,128)(2,1)S(1)}, bf16[1,512,512]{2,1,0:T(8,128)(2,1)}, u32[]{:S(2)}, u32[]{:S(2)}) collective-permute-start(bf16[1,512,512]{2,1,0:T(8,128)(2,1)S(1)} %pad_maximum_fusion.2.refs_2_), channel_id=1, source_target_pairs={{0,16},{1,17},{2,18},{3,19},{4,20},{5,21},{6,22},{7,23},{8,24},{9,... | collective-permute-start | bytes 1572872 | tf_op jit(solution)/shard_map/ppermute | solution.py:32
  54.0 2.7 %collective-permute-start.10 = (bf16[1,512,512]{2,1,0:T(8,128)(2,1)S(1)}, bf16[1,512,512]{2,1,0:T(8,128)(2,1)S(1)}, u32[]{:S(2)}, u32[]{:S(2)}) collective-permute-start(bf16[1,512,512]{2,1,0:T(8,128)(2,1)S(1)} %pad_maximum_fusion.3.refs_3_.refs_0_), channel_id=1, source_target_pairs={{0,48},{1,49},{2,50},{3,51},{4,52},{5,53},{6,54},{7,55},{8,56},{9,... | collective-permute-start | bytes 1572872 | tf_op jit(solution)/shard_map/ppermute | solution.py:32
  56.7 2.6 %collective-permute-start.6 = (bf16[1,512,512]{2,1,0:T(8,128)(2,1)S(1)}, bf16[1,512,512]{2,1,0:T(8,128)(2,1)S(1)}, u32[]{:S(2)}, u32[]{:S(2)}) collective-permute-start(bf16[1,512,512]{2,1,0:T(8,128)(2,1)S(1)} %pad_maximum_fusion.3.refs_3_.refs_0_), channel_id=1, source_target_pairs={{0,16},{1,17},{2,18},{3,19},{4,20},{5,21},{6,22},{7,23},{8,24},{9,... | collective-permute-start | bytes 1572872 | tf_op jit(solution)/shard_map/ppermute | solution.py:32
  59.3 1.9 %broadcast_select_fusion = bf16[2,64,2048]{2,1,0:T(8,128)(2,1)} fusion(bf16[2,64,2048]{2,1,0:T(8,128)(2,1)} %param.6, bf16[2,64,2048]{2,1,0:T(8,128)(2,1)} %param.7, pred[]{:T(512)S(6)} %lt.26), kind=kLoop, calls=%fused_computation.11 | loop fusion | flops 262144 | bytes 1572865 | tf_op jit(solution)/shard_map/jit(_where)/select_n | solution.py:312
  61.3 4.1 %collective-permute-start.11 = (bf16[1,512,512]{2,1,0:T(8,128)(2,1)}, bf16[1,512,512]{2,1,0:T(8,128)(2,1)}, u32[]{:S(2)}, u32[]{:S(2)}) collective-permute-start(bf16[1,512,512]{2,1,0:T(8,128)(2,1)} %copy-done.4), channel_id=1, source_target_pairs={{0,48},{1,49},{2,50},{3,51},{4,52},{5,53},{6,54},{7,55},{8,56},{9,... | collective-permute-start | bytes 1572872 | tf_op jit(solution)/shard_map/ppermute | solution.py:32
  65.4 1.9 %collective-permute-start.12 = (bf16[1,512,512]{2,1,0:T(8,128)(2,1)}, bf16[1,512,512]{2,1,0:T(8,128)(2,1)}, u32[]{:S(2)}, u32[]{:S(2)}) collective-permute-start(bf16[1,512,512]{2,1,0:T(8,128)(2,1)} %collective-permute-done.8.refs_9_), channel_id=1, source_target_pairs={{0,16},{1,17},{2,18},{3,19},{4,20},{5,21},{6,22},{7,23},{8,24},{9,... | collective-permute-start | bytes 1572872 | tf_op jit(solution)/shard_map/ppermute | solution.py:32
  67.3 2.7 %collective-permute-start.13 = (bf16[1,512,512]{2,1,0:T(8,128)(2,1)}, bf16[1,512,512]{2,1,0:T(8,128)(2,1)}, u32[]{:S(2)}, u32[]{:S(2)}) collective-permute-start(bf16[1,512,512]{2,1,0:T(8,128)(2,1)} %collective-permute-done.5.refs_6_), channel_id=1, source_target_pairs={{0,48},{1,49},{2,50},{3,51},{4,52},{5,53},{6,54},{7,55},{8,56},{9,... | collective-permute-start | bytes 1572872 | tf_op jit(solution)/shard_map/ppermute | solution.py:32
  70.0 2.6 %collective-permute-start.14 = (bf16[1,512,512]{2,1,0:T(8,128)(2,1)S(1)}, bf16[1,512,512]{2,1,0:T(8,128)(2,1)}, u32[]{:S(2)}, u32[]{:S(2)}) collective-permute-start(bf16[1,512,512]{2,1,0:T(8,128)(2,1)S(1)} %collective-permute-done.10.refs_11_.refs_2_), channel_id=1, source_target_pairs={{0,16},{1,17},{2,18},{3,19},{4,20},{5,21},{6,22},{7,23},{8,24},{9,... | collective-permute-start | bytes 1572872 | tf_op jit(solution)/shard_map/ppermute | solution.py:32
  73.3 2.6 %stack.27.scal = s32[9]{0:T(128)S(1)} concatenate(s32[1]{0:T(128)} %bitcast, s32[1]{0:T(128)} %bitcast.1, s32[1]{0:T(128)} %bitcast.2, s32[1]{0:T(128)} %bitcast.3, s32[1]{0:T(128)} %get-tuple-element.47, s32[1]{0:T(128)} %get-tuple-element.48, s32[1]{0:T(128)} %bitcast.4, s32[1]{0:T(128)} %get-tuple-element.44, s32[1]{0:T(128)} %get-tuple-element.43), dimensions={0} | concatenate | bytes 72 | tf_op jit(solution)/shard_map/stack | solution.py:295
  79.7 1.9 %collective-permute-done.14.refs_3_.refs_15_ = bf16[1,512,512]{2,1,0:T(8,128)(2,1)} collective-permute-done((bf16[1,512,512]{2,1,0:T(8,128)(2,1)S(1)}, bf16[1,512,512]{2,1,0:T(8,128)(2,1)}, u32[]{:S(2)}, u32[]{:S(2)}) %collective-permute-start.14) | collective-permute-done | bytes 524320 | tf_op jit(solution)/shard_map/ppermute | solution.py:32
  86.5 1.3 collective-permute-start.18
  88.8 1.3 collective-permute-start.22
  90.1 34.7 %collective-permute-done.18.mine.in3m = bf16[64,2048]{1,0:T(8,128)(2,1)} collective-permute-done((bf16[64,2048]{1,0:T(8,128)(2,1)S(1)}, bf16[64,2048]{1,0:T(8,128)(2,1)}, u32[]{:S(2)}, u32[]{:S(2)}) %collective-permute-start.18) | collective-permute-done | bytes 262176 | tf_op jit(solution)/shard_map/ppermute | solution.py:349
  124.8 2.8 %collective-permute-start.19 = (bf16[64,2048]{1,0:T(8,128)(2,1)}, bf16[64,2048]{1,0:T(8,128)(2,1)}, u32[]{:S(2)}, u32[]{:S(2)}) collective-permute-start(bf16[64,2048]{1,0:T(8,128)(2,1)} %collective-permute-done.18.mine.in3m), channel_id=1, source_target_pairs={{384,448},{448,384},{385,449},{449,385},{386,450},{450,386},{387,4... | collective-permute-start | bytes 786440 | tf_op jit(solution)/shard_map/ppermute | solution.py:320
  127.6 16.7 %collective-permute-done.22.mem_mine = bf16[64,2048]{1,0:T(8,128)(2,1)} collective-permute-done((bf16[64,2048]{1,0:T(8,128)(2,1)S(1)}, bf16[64,2048]{1,0:T(8,128)(2,1)}, u32[]{:S(2)}, u32[]{:S(2)}) %collective-permute-start.22) | collective-permute-done | bytes 262176 | tf_op jit(solution)/shard_map/ppermute | solution.py:363
  144.3 2.6 %collective-permute-start.23 = (bf16[64,2048]{1,0:T(8,128)(2,1)}, bf16[64,2048]{1,0:T(8,128)(2,1)}, u32[]{:S(2)}, u32[]{:S(2)}) collective-permute-start(bf16[64,2048]{1,0:T(8,128)(2,1)} %collective-permute-done.22.mem_mine), channel_id=1, source_target_pairs={{384,448},{448,384},{385,449},{449,385},{386,450},{450,386},{387,4... | collective-permute-start | bytes 786440 | tf_op jit(solution)/shard_map/ppermute | solution.py:320
  149.0 2.5 %shard_map.68.q = bf16[128,512]{1,0:T(8,128)(2,1)S(1)} custom-call(s32[9]{0:T(128)S(1)} %stack.27.scal, f32[5,2048]{1,0:T(8,128)S(1)} %copy-done.13, bf16[64,2048]{1,0:T(8,128)(2,1)} %collective-permute-done.18.mine.in3m, bf16[64,2048]{1,0:T(8,128)(2,1)} %collective-permute-done.19.other.in3o, bf16[1,512,512]{2,1,0:T(8,128)(2,1)S(1)} %pad_maximum_fusion.refs_0_, ...), custom_call_target="tpu_custom_call" | custom-call | flops 268435456 | bytes 8953856 | tf_op jit(solution)/shard_map/pallas_call | solution.py:221
  151.6 5.8 %shard_map.69.own = bf16[128,2048]{1,0:T(8,128)(2,1)S(1)} custom-call(s32[9]{0:T(128)S(1)} %stack.27.scal, bf16[128,512]{1,0:T(8,128)(2,1)S(1)} %shard_map.68.q, bf16[64,2048]{1,0:T(8,128)(2,1)} %collective-permute-done.22.mem_mine, bf16[64,2048]{1,0:T(8,128)(2,1)} %collective-permute-done.23.mem_other, bf16[1,512,512]{2,1,0:T(8,128)(2,1)S(1)} %pad_maximum_fusion.refs_0_, ...), custom_call_target="tpu_custom_call" | custom-call | flops 805306368 | bytes 9043968 | tf_op jit(solution)/shard_map/pallas_call | solution.py:221
  157.5 1.4 collective-permute-start.24
  159.7 1.8 %collective-permute-done.24.got = bf16[128,2048]{1,0:T(8,128)(2,1)S(1)} collective-permute-done((bf16[128,2048]{1,0:T(8,128)(2,1)S(1)}, bf16[128,2048]{1,0:T(8,128)(2,1)S(1)}, u32[]{:S(2)}, u32[]{:S(2)}) %collective-permute-start.24) | collective-permute-done | bytes 524320 | tf_op jit(solution)/shard_map/ppermute | solution.py:388
  161.4 2.1 %shard_map.70 = bf16[2,64,2048]{2,1,0:T(8,128)(2,1)} custom-call(s32[9]{0:T(128)S(1)} %stack.27.scal, bf16[64,2048]{1,0:T(8,128)(2,1)S(1)} %get-tuple-element.40.mine, bf16[64,2048]{1,0:T(8,128)(2,1)S(1)} %copy-done.8, bf16[64,2048]{1,0:T(8,128)(2,1)S(1)} %copy-done.10, bf16[64,2048]{1,0:T(8,128)(2,1)S(1)} %copy-done.12, ...), custom_call_target="tpu_custom_call" | custom-call | bytes 3145728 | tf_op jit(solution)/shard_map/pallas_call | solution.py:221
  (90 shorter events, 15.5 us)
Async XLA Ops:
  17.7 11.7 %collective-permute-start.2 = (bf16[4,128,512]{2,1,0:T(8,128)(2,1)S(1)}, bf16[4,128,512]{2,1,0:T(8,128)(2,1)S(1)}, u32[]{:S(2)}, u32[]{:S(2)}) collective-permute-start(bf16[4,128,512]{2,1,0:T(8,128)(2,1)S(1)} %bitcast.21), channel_id=1, source_target_pairs={{0,8},{1,9},{2,10},{3,11},{4,12},{5,13},{6,14},{7,15},{8,0},{9,1},... | collective-permute-start | bytes 1572872 | tf_op jit(solution)/shard_map/ppermute | solution.py:32
  22.5 12.5 %collective-permute-start.1 = (bf16[4,128,512]{2,1,0:T(8,128)(2,1)S(1)}, bf16[4,128,512]{2,1,0:T(8,128)(2,1)S(1)}, u32[]{:S(2)}, u32[]{:S(2)}) collective-permute-start(bf16[4,128,512]{2,1,0:T(8,128)(2,1)S(1)} %bitcast.22), channel_id=1, source_target_pairs={{0,12},{1,13},{2,14},{3,15},{4,8},{5,9},{6,10},{7,11},{8,4},{9,5},... | collective-permute-start | bytes 1572872 | tf_op jit(solution)/shard_map/ppermute | solution.py:32
  25.2 10.2 %collective-permute-start = (bf16[4,128,512]{2,1,0:T(8,128)(2,1)S(1)}, bf16[4,128,512]{2,1,0:T(8,128)(2,1)S(1)}, u32[]{:S(2)}, u32[]{:S(2)}) collective-permute-start(bf16[4,128,512]{2,1,0:T(8,128)(2,1)S(1)} %bitcast.23), channel_id=1, source_target_pairs={{0,4},{1,5},{2,6},{3,7},{4,0},{5,1},{6,2},{7,3},{8,12},{9,13},{10,... | collective-permute-start | bytes 1572872 | tf_op jit(solution)/shard_map/ppermute | solution.py:32
  35.5 15.7 %collective-permute-start.7 = (bf16[1,512,512]{2,1,0:T(8,128)(2,1)S(1)}, bf16[1,512,512]{2,1,0:T(8,128)(2,1)S(1)}, u32[]{:S(2)}, u32[]{:S(2)}) collective-permute-start(bf16[1,512,512]{2,1,0:T(8,128)(2,1)S(1)} %pad_maximum_fusion.refs_0_), channel_id=1, source_target_pairs={{0,48},{1,49},{2,50},{3,51},{4,52},{5,53},{6,54},{7,55},{8,56},{9,... | collective-permute-start | bytes 1572872 | tf_op jit(solution)/shard_map/ppermute | solution.py:32
  39.9 14.1 %collective-permute-start.3 = (bf16[1,512,512]{2,1,0:T(8,128)(2,1)S(1)}, bf16[1,512,512]{2,1,0:T(8,128)(2,1)S(1)}, u32[]{:S(2)}, u32[]{:S(2)}) collective-permute-start(bf16[1,512,512]{2,1,0:T(8,128)(2,1)S(1)} %pad_maximum_fusion.refs_0_), channel_id=1, source_target_pairs={{0,16},{1,17},{2,18},{3,19},{4,20},{5,21},{6,22},{7,23},{8,24},{9,... | collective-permute-start | bytes 1572872 | tf_op jit(solution)/shard_map/ppermute | solution.py:32
  41.9 14.8 %collective-permute-start.8 = (bf16[1,512,512]{2,1,0:T(8,128)(2,1)S(1)}, bf16[1,512,512]{2,1,0:T(8,128)(2,1)}, u32[]{:S(2)}, u32[]{:S(2)}) collective-permute-start(bf16[1,512,512]{2,1,0:T(8,128)(2,1)S(1)} %pad_maximum_fusion.1.refs_1_), channel_id=1, source_target_pairs={{0,48},{1,49},{2,50},{3,51},{4,52},{5,53},{6,54},{7,55},{8,56},{9,... | collective-permute-start | bytes 1572872 | tf_op jit(solution)/shard_map/ppermute | solution.py:32
  44.6 16.7 %collective-permute-start.4 = (bf16[1,512,512]{2,1,0:T(8,128)(2,1)S(1)}, bf16[1,512,512]{2,1,0:T(8,128)(2,1)}, u32[]{:S(2)}, u32[]{:S(2)}) collective-permute-start(bf16[1,512,512]{2,1,0:T(8,128)(2,1)S(1)} %pad_maximum_fusion.1.refs_1_), channel_id=1, source_target_pairs={{0,16},{1,17},{2,18},{3,19},{4,20},{5,21},{6,22},{7,23},{8,24},{9,... | collective-permute-start | bytes 1572872 | tf_op jit(solution)/shard_map/ppermute | solution.py:32
  47.2 18.2 %collective-permute-start.9 = (bf16[1,512,512]{2,1,0:T(8,128)(2,1)S(1)}, bf16[1,512,512]{2,1,0:T(8,128)(2,1)}, u32[]{:S(2)}, u32[]{:S(2)}) collective-permute-start(bf16[1,512,512]{2,1,0:T(8,128)(2,1)S(1)} %pad_maximum_fusion.2.refs_2_), channel_id=1, source_target_pairs={{0,48},{1,49},{2,50},{3,51},{4,52},{5,53},{6,54},{7,55},{8,56},{9,... | collective-permute-start | bytes 1572872 | tf_op jit(solution)/shard_map/ppermute | solution.py:32
  52.0 15.3 %collective-permute-start.5 = (bf16[1,512,512]{2,1,0:T(8,128)(2,1)S(1)}, bf16[1,512,512]{2,1,0:T(8,128)(2,1)}, u32[]{:S(2)}, u32[]{:S(2)}) collective-permute-start(bf16[1,512,512]{2,1,0:T(8,128)(2,1)S(1)} %pad_maximum_fusion.2.refs_2_), channel_id=1, source_target_pairs={{0,16},{1,17},{2,18},{3,19},{4,20},{5,21},{6,22},{7,23},{8,24},{9,... | collective-permute-start | bytes 1572872 | tf_op jit(solution)/shard_map/ppermute | solution.py:32
  54.0 16.1 %collective-permute-start.10 = (bf16[1,512,512]{2,1,0:T(8,128)(2,1)S(1)}, bf16[1,512,512]{2,1,0:T(8,128)(2,1)S(1)}, u32[]{:S(2)}, u32[]{:S(2)}) collective-permute-start(bf16[1,512,512]{2,1,0:T(8,128)(2,1)S(1)} %pad_maximum_fusion.3.refs_3_.refs_0_), channel_id=1, source_target_pairs={{0,48},{1,49},{2,50},{3,51},{4,52},{5,53},{6,54},{7,55},{8,56},{9,... | collective-permute-start | bytes 1572872 | tf_op jit(solution)/shard_map/ppermute | solution.py:32
  56.7 20.4 %collective-permute-start.6 = (bf16[1,512,512]{2,1,0:T(8,128)(2,1)S(1)}, bf16[1,512,512]{2,1,0:T(8,128)(2,1)S(1)}, u32[]{:S(2)}, u32[]{:S(2)}) collective-permute-start(bf16[1,512,512]{2,1,0:T(8,128)(2,1)S(1)} %pad_maximum_fusion.3.refs_3_.refs_0_), channel_id=1, source_target_pairs={{0,16},{1,17},{2,18},{3,19},{4,20},{5,21},{6,22},{7,23},{8,24},{9,... | collective-permute-start | bytes 1572872 | tf_op jit(solution)/shard_map/ppermute | solution.py:32
  59.3 17.8 %copy-start.13 = (f32[5,2048]{1,0:T(8,128)S(1)}, f32[5,2048]{1,0:T(8,128)}, u32[]{:S(2)}) copy-start(f32[5,2048]{1,0:T(8,128)} %gains.5) | copy-start | bytes 122884
  61.3 11.4 %copy-start.18 = (s32[2]{0:T(128)S(1)}, s32[2]{0:T(128)}, u32[]{:S(2)}) copy-start(s32[2]{0:T(128)} %param.10) | copy-start | bytes 28
  61.3 11.4 %copy-start.19 = (s32[2]{0:T(128)S(1)}, s32[2]{0:T(128)}, u32[]{:S(2)}) copy-start(s32[2]{0:T(128)} %param.11) | copy-start | bytes 28
  61.3 16.6 %collective-permute-start.11 = (bf16[1,512,512]{2,1,0:T(8,128)(2,1)}, bf16[1,512,512]{2,1,0:T(8,128)(2,1)}, u32[]{:S(2)}, u32[]{:S(2)}) collective-permute-start(bf16[1,512,512]{2,1,0:T(8,128)(2,1)} %copy-done.4), channel_id=1, source_target_pairs={{0,48},{1,49},{2,50},{3,51},{4,52},{5,53},{6,54},{7,55},{8,56},{9,... | collective-permute-start | bytes 1572872 | tf_op jit(solution)/shard_map/ppermute | solution.py:32
  65.4 12.5 %collective-permute-start.12 = (bf16[1,512,512]{2,1,0:T(8,128)(2,1)}, bf16[1,512,512]{2,1,0:T(8,128)(2,1)}, u32[]{:S(2)}, u32[]{:S(2)}) collective-permute-start(bf16[1,512,512]{2,1,0:T(8,128)(2,1)} %collective-permute-done.8.refs_9_), channel_id=1, source_target_pairs={{0,16},{1,17},{2,18},{3,19},{4,20},{5,21},{6,22},{7,23},{8,24},{9,... | collective-permute-start | bytes 1572872 | tf_op jit(solution)/shard_map/ppermute | solution.py:32
  67.3 11.7 %collective-permute-start.13 = (bf16[1,512,512]{2,1,0:T(8,128)(2,1)}, bf16[1,512,512]{2,1,0:T(8,128)(2,1)}, u32[]{:S(2)}, u32[]{:S(2)}) collective-permute-start(bf16[1,512,512]{2,1,0:T(8,128)(2,1)} %collective-permute-done.5.refs_6_), channel_id=1, source_target_pairs={{0,48},{1,49},{2,50},{3,51},{4,52},{5,53},{6,54},{7,55},{8,56},{9,... | collective-permute-start | bytes 1572872 | tf_op jit(solution)/shard_map/ppermute | solution.py:32
  70.0 11.5 %collective-permute-start.14 = (bf16[1,512,512]{2,1,0:T(8,128)(2,1)S(1)}, bf16[1,512,512]{2,1,0:T(8,128)(2,1)}, u32[]{:S(2)}, u32[]{:S(2)}) collective-permute-start(bf16[1,512,512]{2,1,0:T(8,128)(2,1)S(1)} %collective-permute-done.10.refs_11_.refs_2_), channel_id=1, source_target_pairs={{0,16},{1,17},{2,18},{3,19},{4,20},{5,21},{6,22},{7,23},{8,24},{9,... | collective-permute-start | bytes 1572872 | tf_op jit(solution)/shard_map/ppermute | solution.py:32
  82.1 1.4 collective-permute-start.15
  83.7 0.7 collective-permute-start.16
  84.4 0.7 collective-permute-start.17
  85.8 2.0 %collective-permute-start.20 = (bf16[64,2048]{1,0:T(8,128)(2,1)S(1)}, bf16[64,2048]{1,0:T(8,128)(2,1)S(1)}, u32[]{:S(2)}, u32[]{:S(2)}) collective-permute-start(bf16[64,2048]{1,0:T(8,128)(2,1)S(1)} %get-tuple-element.20), channel_id=1, source_target_pairs={{128,192},{192,128},{129,193},{193,129},{130,194},{194,130},{131,1... | collective-permute-start | bytes 786440 | tf_op jit(solution)/shard_map/ppermute | solution.py:320
  86.5 38.3 %collective-permute-start.18 = (bf16[64,2048]{1,0:T(8,128)(2,1)S(1)}, bf16[64,2048]{1,0:T(8,128)(2,1)}, u32[]{:S(2)}, u32[]{:S(2)}) collective-permute-start(bf16[64,2048]{1,0:T(8,128)(2,1)S(1)} %add_convert_fusion.1), channel_id=1, source_target_pairs={{256,384},{257,385},{258,386},{259,387},{260,388},{261,389},{262,3... | collective-permute-start | bytes 786440 | tf_op jit(solution)/shard_map/ppermute | solution.py:349
  88.8 55.5 %collective-permute-start.22 = (bf16[64,2048]{1,0:T(8,128)(2,1)S(1)}, bf16[64,2048]{1,0:T(8,128)(2,1)}, u32[]{:S(2)}, u32[]{:S(2)}) collective-permute-start(bf16[64,2048]{1,0:T(8,128)(2,1)S(1)} %fusion.2), channel_id=1, source_target_pairs={{128,384},{129,385},{130,386},{131,387},{132,388},{133,389},{134,3... | collective-permute-start | bytes 786440 | tf_op jit(solution)/shard_map/ppermute | solution.py:363
  124.8 22.1 %collective-permute-start.19 = (bf16[64,2048]{1,0:T(8,128)(2,1)}, bf16[64,2048]{1,0:T(8,128)(2,1)}, u32[]{:S(2)}, u32[]{:S(2)}) collective-permute-start(bf16[64,2048]{1,0:T(8,128)(2,1)} %collective-permute-done.18.mine.in3m), channel_id=1, source_target_pairs={{384,448},{448,384},{385,449},{449,385},{386,450},{450,386},{387,4... | collective-permute-start | bytes 786440 | tf_op jit(solution)/shard_map/ppermute | solution.py:320
  144.3 7.3 %collective-permute-start.23 = (bf16[64,2048]{1,0:T(8,128)(2,1)}, bf16[64,2048]{1,0:T(8,128)(2,1)}, u32[]{:S(2)}, u32[]{:S(2)}) collective-permute-start(bf16[64,2048]{1,0:T(8,128)(2,1)} %collective-permute-done.22.mem_mine), channel_id=1, source_target_pairs={{384,448},{448,384},{385,449},{449,385},{386,450},{450,386},{387,4... | collective-permute-start | bytes 786440 | tf_op jit(solution)/shard_map/ppermute | solution.py:320
  151.6 7.3 %copy-start.15 = (bf16[64,2048]{1,0:T(8,128)(2,1)S(1)}, bf16[64,2048]{1,0:T(8,128)(2,1)}, u32[]{:S(2)}) copy-start(bf16[64,2048]{1,0:T(8,128)(2,1)} %copy-done.14) | copy-start | bytes 786436
  151.6 7.3 %copy-start.17 = (bf16[64,2048]{1,0:T(8,128)(2,1)S(1)}, bf16[64,2048]{1,0:T(8,128)(2,1)}, u32[]{:S(2)}) copy-start(bf16[64,2048]{1,0:T(8,128)(2,1)} %copy-done.16) | copy-start | bytes 786436
  157.4 4.0 %copy-start.8 = (bf16[64,2048]{1,0:T(8,128)(2,1)S(1)}, bf16[64,2048]{1,0:T(8,128)(2,1)}, u32[]{:S(2)}) copy-start(bf16[64,2048]{1,0:T(8,128)(2,1)} %copy-done.7) | copy-start | bytes 786436
  157.5 4.0 %copy-start.10 = (bf16[64,2048]{1,0:T(8,128)(2,1)S(1)}, bf16[64,2048]{1,0:T(8,128)(2,1)}, u32[]{:S(2)}) copy-start(bf16[64,2048]{1,0:T(8,128)(2,1)} %copy-done.9) | copy-start | bytes 786436
  157.5 3.9 %collective-permute-start.24 = (bf16[128,2048]{1,0:T(8,128)(2,1)S(1)}, bf16[128,2048]{1,0:T(8,128)(2,1)S(1)}, u32[]{:S(2)}, u32[]{:S(2)}) collective-permute-start(bf16[128,2048]{1,0:T(8,128)(2,1)S(1)} %shard_map.69.own), channel_id=1, source_target_pairs={{384,448},{385,449},{386,450},{387,451},{388,452},{389,453},{390,4... | collective-permute-start | bytes 1572872 | tf_op jit(solution)/shard_map/ppermute | solution.py:388
  159.0 0.7 collective-permute-start.21
  (13 other events, 23.3 us)

commit v14 on v13

--- a/solution.py
+++ b/solution.py
@@ -268,7 +268,7 @@
     return [array] + [exchange(array, outer, turn) for turn in TURNS[1:]]
 
 
-def gather(weights):
+def gather(weights, early):
     pair, depth, width = weights.shape[1:]
     halves = weights[0].reshape(pair, depth, 2, width // 2).transpose(2, 0, 1, 3)
     sent = jnp.broadcast_to(halves[:, None], (2, SIDE) + halves.shape[1:])
@@ -277,11 +277,12 @@
     got = got.reshape(2, SIDE, pair, depth, width // 2).transpose(0, 2, 1, 3, 4)
     got = got.reshape(2 * pair, SIDE * depth, width // 2)
     near = turns(got, False)
+    near[1], early = lax.optimization_barrier((near[1], early))
     parts = [jnp.concatenate([a[i:i + 1] for a in near], axis=1) for i in range(2 * pair)]
     by1 = [exchange(a, True, 1) for a in parts]
     by3 = [exchange(a, True, 3) for a in parts]
     far = [exchange((by1, by3)[i % 2][i], True, (3, 1)[i % 2]) for i in range(2 * pair)]
-    return [*parts, *by1, *by3], far
+    return [*parts, *by1, *by3], far, early
 
 
 def on_device(encoder_embed, decoder_embed, section_weights, norm_gains, input_lengths, target_lengths):
@@ -307,10 +308,10 @@
     ).astype(jnp.int32)
     live = (jnp.arange(rows, dtype=jnp.int32) < row_lengths[core])[:, None]
 
-    near, far = gather(section_weights)
+    source = jnp.where(encoder, encoder_embed, decoder_embed)
+    early = (scal, source[core], source[1 - core])
+    near, far, (scal, mine, other) = gather(section_weights, early)
     pieces = near + far
-    source = jnp.where(encoder, encoder_embed, decoder_embed)
-    mine, other = source[core], source[1 - core]
 
     def added(stream, term, alive):
         return stream.astype(F32) + jnp.where(alive, term, 0.0)

time: 165 us -> 172 us (1.042)
  blocking collectives: 16.6 us -> 0 us
  waiting for transfers between devices: 64.4 us -> 77.1 us
  local copies, waits for them, and re-layouts: 9.25 us -> 17.1 us
  starting transfers between devices: 56.3 us -> 62.1 us
  other arithmetic: 3.34 us -> 1.46 us
    all_to_all x1 -> x0, blocking collectives: 16.6 us -> none  [gather(): got = lax.all_to_all(sent, ('core', 'zl'), 0, 0, tiled=True)]
    all_to_all x0 -> x1, waiting for transfers between devices: none -> 9.88 us  [gather(): got = lax.all_to_all(sent, ('core', 'zl'), 0, 0, tiled=True)]
    unnamed x40 -> x78, local copies, waits for them, and re-layouts: 3.62 us -> 11.1 us
    ppermute x15, waiting for transfers between devices: 11.2 us -> 17.2 us  [exchange(): return lax.ppermute(array, AXES, pairs)]
    all_to_all x0 -> x1, starting transfers between devices: none -> 5.76 us  [gather(): got = lax.all_to_all(sent, ('core', 'zl'), 0, 0, tiled=True)]
    ppermute x1, waiting for transfers between devices: 34.7 us -> 32.6 us  [on_device(): in3 = lax.ppermute(first, 'zh', [(2, 3)])]
    select_n x1, other arithmetic: 1.93 us -> 0.06 us  [on_device(): source = jnp.where(encoder, encoder_embed, decoder_embed)]
  transfers between devices with their start and end apart: 25 -> 26, of which waited for: 8 -> 9; matrix products, arithmetic and copies ran while one was open for 5% -> 3% of each run, Pallas kernels for 2% -> 2%
where the time goes in v14:
time: 172 us; the launch traced here: 171 us
  waiting for transfers between devices  77.1 us (45%)
  starting transfers between devices  62.1 us (36%)
  local copies, waits for them, and re-layouts  17.1 us (10%)
  Pallas kernels  12.3 us (7%)
    ppermute x15, starting transfers between devices, exchange(): return lax.ppermute(array, AXES, pairs)  43.5 us
    ppermute x1, waiting for transfers between devices, on_device(): in3 = lax.ppermute(first, 'zh', [(2, 3)])  32.6 us
    ppermute x15, waiting for transfers between devices, exchange(): return lax.ppermute(array, AXES, pairs)  17.2 us
    ppermute x1, waiting for transfers between devices, on_device(): mem = lax.ppermute(memory, 'zh', [(1, 3)])  15.6 us
    pallas_call x7, Pallas kernels, call(): pl.pallas_call(kernel, out_shape=outs, in_specs=[SMEM] + [VMEM] * len(ope...  12.3 us
    unnamed x78, local copies, waits for them, and re-layouts  11.1 us
    all_to_all x1, waiting for transfers between devices, gather(): got = lax.all_to_all(sent, ('core', 'zl'), 0, 0, tiled=True)  9.88 us
    ppermute x5, starting transfers between devices, swapped(): return lax.ppermute(array, SECTION, pairs)  7.42 us
  transfers between devices with their start and end apart: 26, of which 9 were waited for; matrix products, arithmetic and copies ran while one was open for 3% of the time, Pallas kernels for 2%

profile of v14, /device:TPU:481, one launch (start us, length us, event | category | flops | bytes accessed | tf_op | source)
XLA Modules:
  0.0 170.9 jit_solution(15864898465155801384)
XLA Ops:
  1.9 5.8 %all-to-all-start = ((bf16[8,2,32,512]{3,2,1,0:T(8,128)(2,1)}), bf16[8,2,32,512]{3,2,1,0:T(8,128)(2,1)S(1)}, u32[]{:S(2)}, u32[]{:S(2)}) async-start(bf16[8,2,32,512]{3,2,1,0:T(8,128)(2,1)} %bitcast.1), calls=%async_computation | async-start | bytes 1048576 | tf_op jit(solution)/shard_map/all_to_all | solution.py:276
  7.7 9.9 %all-to-all-done = bf16[8,2,32,512]{3,2,1,0:T(8,128)(2,1)S(1)} async-done(((bf16[8,2,32,512]{3,2,1,0:T(8,128)(2,1)}), bf16[8,2,32,512]{3,2,1,0:T(8,128)(2,1)S(1)}, u32[]{:S(2)}, u32[]{:S(2)}) %all-to-all-start) | async-done | bytes 524320 | tf_op jit(solution)/shard_map/all_to_all | solution.py:276
  17.6 3.2 %collective-permute-start = (bf16[4,128,512]{2,1,0:T(8,128)(2,1)S(1)}, bf16[4,128,512]{2,1,0:T(8,128)(2,1)S(1)}, u32[]{:S(2)}, u32[]{:S(2)}) collective-permute-start(bf16[4,128,512]{2,1,0:T(8,128)(2,1)S(1)} %bitcast.20), channel_id=1, source_target_pairs={{0,4},{1,5},{2,6},{3,7},{4,0},{5,1},{6,2},{7,3},{8,12},{9,13},{10,... | collective-permute-start | bytes 1572872 | tf_op jit(solution)/shard_map/ppermute | solution.py:32
  21.6 4.6 %collective-permute-start.2 = (bf16[4,128,512]{2,1,0:T(8,128)(2,1)S(1)}, bf16[4,128,512]{2,1,0:T(8,128)(2,1)S(1)}, u32[]{:S(2)}, u32[]{:S(2)}) collective-permute-start(bf16[4,128,512]{2,1,0:T(8,128)(2,1)S(1)} %bitcast.21), channel_id=1, source_target_pairs={{0,8},{1,9},{2,10},{3,11},{4,12},{5,13},{6,14},{7,15},{8,0},{9,1},... | collective-permute-start | bytes 1572872 | tf_op jit(solution)/shard_map/ppermute | solution.py:32
  27.0 2.6 %stack.27.scal = s32[9]{0:T(128)S(1)} concatenate(s32[1]{0:T(128)} %bitcast.5, s32[1]{0:T(128)} %bitcast.6, s32[1]{0:T(128)} %bitcast.7, s32[1]{0:T(128)} %bitcast.8, s32[1]{0:T(128)} %get-tuple-element.55, s32[1]{0:T(128)} %get-tuple-element.56, s32[1]{0:T(128)} %bitcast.9, s32[1]{0:T(128)} %get-tuple-element.52, s32[1]{0:T(128)} %get-tuple-element.51), dimensions={0} | concatenate | bytes 72 | tf_op jit(solution)/shard_map/stack | solution.py:296
  29.6 1.9 %collective-permute-start.1 = (bf16[4,128,512]{2,1,0:T(8,128)(2,1)S(1)}, bf16[4,128,512]{2,1,0:T(8,128)(2,1)S(1)}, u32[]{:S(2)}, u32[]{:S(2)}) collective-permute-start(bf16[4,128,512]{2,1,0:T(8,128)(2,1)S(1)} %bitcast.22), channel_id=1, source_target_pairs={{0,12},{1,13},{2,14},{3,15},{4,8},{5,9},{6,10},{7,11},{8,4},{9,5},... | collective-permute-start | bytes 1572872 | tf_op jit(solution)/shard_map/ppermute | solution.py:32
  31.6 4.3 %collective-permute-done.2 = bf16[4,128,512]{2,1,0:T(8,128)(2,1)S(1)} collective-permute-done((bf16[4,128,512]{2,1,0:T(8,128)(2,1)S(1)}, bf16[4,128,512]{2,1,0:T(8,128)(2,1)S(1)}, u32[]{:S(2)}, u32[]{:S(2)}) %collective-permute-start.2) | collective-permute-done | bytes 524320 | tf_op jit(solution)/shard_map/ppermute | solution.py:32
  36.0 5.6 %collective-permute-done.1 = bf16[4,128,512]{2,1,0:T(8,128)(2,1)S(1)} collective-permute-done((bf16[4,128,512]{2,1,0:T(8,128)(2,1)S(1)}, bf16[4,128,512]{2,1,0:T(8,128)(2,1)S(1)}, u32[]{:S(2)}, u32[]{:S(2)}) %collective-permute-start.1) | collective-permute-done | bytes 524320 | tf_op jit(solution)/shard_map/ppermute | solution.py:32
  41.6 4.1 %collective-permute-start.7 = (bf16[1,512,512]{2,1,0:T(8,128)(2,1)S(1)}, bf16[1,512,512]{2,1,0:T(8,128)(2,1)S(1)}, u32[]{:S(2)}, u32[]{:S(2)}) collective-permute-start(bf16[1,512,512]{2,1,0:T(8,128)(2,1)S(1)} %pad_maximum_fusion.refs_0_), channel_id=1, source_target_pairs={{0,48},{1,49},{2,50},{3,51},{4,52},{5,53},{6,54},{7,55},{8,56},{9,... | collective-permute-start | bytes 1572872 | tf_op jit(solution)/shard_map/ppermute | solution.py:32
  45.7 1.9 %collective-permute-start.3 = (bf16[1,512,512]{2,1,0:T(8,128)(2,1)S(1)}, bf16[1,512,512]{2,1,0:T(8,128)(2,1)S(1)}, u32[]{:S(2)}, u32[]{:S(2)}) collective-permute-start(bf16[1,512,512]{2,1,0:T(8,128)(2,1)S(1)} %pad_maximum_fusion.refs_0_), channel_id=1, source_target_pairs={{0,16},{1,17},{2,18},{3,19},{4,20},{5,21},{6,22},{7,23},{8,24},{9,... | collective-permute-start | bytes 1572872 | tf_op jit(solution)/shard_map/ppermute | solution.py:32
  47.7 2.7 %collective-permute-start.8 = (bf16[1,512,512]{2,1,0:T(8,128)(2,1)S(1)}, bf16[1,512,512]{2,1,0:T(8,128)(2,1)S(1)}, u32[]{:S(2)}, u32[]{:S(2)}) collective-permute-start(bf16[1,512,512]{2,1,0:T(8,128)(2,1)S(1)} %pad_maximum_fusion.1.refs_1_), channel_id=1, source_target_pairs={{0,48},{1,49},{2,50},{3,51},{4,52},{5,53},{6,54},{7,55},{8,56},{9,... | collective-permute-start | bytes 1572872 | tf_op jit(solution)/shard_map/ppermute | solution.py:32
  50.4 2.6 %collective-permute-start.4 = (bf16[1,512,512]{2,1,0:T(8,128)(2,1)S(1)}, bf16[1,512,512]{2,1,0:T(8,128)(2,1)S(1)}, u32[]{:S(2)}, u32[]{:S(2)}) collective-permute-start(bf16[1,512,512]{2,1,0:T(8,128)(2,1)S(1)} %pad_maximum_fusion.1.refs_1_), channel_id=1, source_target_pairs={{0,16},{1,17},{2,18},{3,19},{4,20},{5,21},{6,22},{7,23},{8,24},{9,... | collective-permute-start | bytes 1572872 | tf_op jit(solution)/shard_map/ppermute | solution.py:32
  53.0 4.0 %collective-permute-start.9 = (bf16[1,512,512]{2,1,0:T(8,128)(2,1)S(1)}, bf16[1,512,512]{2,1,0:T(8,128)(2,1)S(1)}, u32[]{:S(2)}, u32[]{:S(2)}) collective-permute-start(bf16[1,512,512]{2,1,0:T(8,128)(2,1)S(1)} %pad_maximum_fusion.2.refs_2_), channel_id=1, source_target_pairs={{0,48},{1,49},{2,50},{3,51},{4,52},{5,53},{6,54},{7,55},{8,56},{9,... | collective-permute-start | bytes 1572872 | tf_op jit(solution)/shard_map/ppermute | solution.py:32
  57.0 1.9 %collective-permute-start.5 = (bf16[1,512,512]{2,1,0:T(8,128)(2,1)S(1)}, bf16[1,512,512]{2,1,0:T(8,128)(2,1)S(1)}, u32[]{:S(2)}, u32[]{:S(2)}) collective-permute-start(bf16[1,512,512]{2,1,0:T(8,128)(2,1)S(1)} %pad_maximum_fusion.2.refs_2_), channel_id=1, source_target_pairs={{0,16},{1,17},{2,18},{3,19},{4,20},{5,21},{6,22},{7,23},{8,24},{9,... | collective-permute-start | bytes 1572872 | tf_op jit(solution)/shard_map/ppermute | solution.py:32
  59.0 2.8 %collective-permute-start.10 = (bf16[1,512,512]{2,1,0:T(8,128)(2,1)S(1)}, bf16[1,512,512]{2,1,0:T(8,128)(2,1)S(1)}, u32[]{:S(2)}, u32[]{:S(2)}) collective-permute-start(bf16[1,512,512]{2,1,0:T(8,128)(2,1)S(1)} %pad_maximum_fusion.3.refs_3_.refs_0_), channel_id=1, source_target_pairs={{0,48},{1,49},{2,50},{3,51},{4,52},{5,53},{6,54},{7,55},{8,56},{9,... | collective-permute-start | bytes 1572872 | tf_op jit(solution)/shard_map/ppermute | solution.py:32
  61.9 2.6 %collective-permute-start.6 = (bf16[1,512,512]{2,1,0:T(8,128)(2,1)S(1)}, bf16[1,512,512]{2,1,0:T(8,128)(2,1)S(1)}, u32[]{:S(2)}, u32[]{:S(2)}) collective-permute-start(bf16[1,512,512]{2,1,0:T(8,128)(2,1)S(1)} %pad_maximum_fusion.3.refs_3_.refs_0_), channel_id=1, source_target_pairs={{0,16},{1,17},{2,18},{3,19},{4,20},{5,21},{6,22},{7,23},{8,24},{9,... | collective-permute-start | bytes 1572872 | tf_op jit(solution)/shard_map/ppermute | solution.py:32
  64.5 4.0 %collective-permute-start.11 = (bf16[1,512,512]{2,1,0:T(8,128)(2,1)S(1)}, bf16[1,512,512]{2,1,0:T(8,128)(2,1)S(1)}, u32[]{:S(2)}, u32[]{:S(2)}) collective-permute-start(bf16[1,512,512]{2,1,0:T(8,128)(2,1)S(1)} %collective-permute-done.3.refs_4_), channel_id=1, source_target_pairs={{0,48},{1,49},{2,50},{3,51},{4,52},{5,53},{6,54},{7,55},{8,56},{9,... | collective-permute-start | bytes 1572872 | tf_op jit(solution)/shard_map/ppermute | solution.py:32
  68.5 1.9 %collective-permute-start.12 = (bf16[1,512,512]{2,1,0:T(8,128)(2,1)S(1)}, bf16[1,512,512]{2,1,0:T(8,128)(2,1)S(1)}, u32[]{:S(2)}, u32[]{:S(2)}) collective-permute-start(bf16[1,512,512]{2,1,0:T(8,128)(2,1)S(1)} %collective-permute-done.8.refs_9_), channel_id=1, source_target_pairs={{0,16},{1,17},{2,18},{3,19},{4,20},{5,21},{6,22},{7,23},{8,24},{9,... | collective-permute-start | bytes 1572872 | tf_op jit(solution)/shard_map/ppermute | solution.py:32
  70.5 2.7 %collective-permute-start.13 = (bf16[1,512,512]{2,1,0:T(8,128)(2,1)S(1)}, bf16[1,512,512]{2,1,0:T(8,128)(2,1)S(1)}, u32[]{:S(2)}, u32[]{:S(2)}) collective-permute-start(bf16[1,512,512]{2,1,0:T(8,128)(2,1)S(1)} %collective-permute-done.5.refs_6_), channel_id=1, source_target_pairs={{0,48},{1,49},{2,50},{3,51},{4,52},{5,53},{6,54},{7,55},{8,56},{9,... | collective-permute-start | bytes 1572872 | tf_op jit(solution)/shard_map/ppermute | solution.py:32
  73.2 2.6 %collective-permute-start.14 = (bf16[1,512,512]{2,1,0:T(8,128)(2,1)S(1)}, bf16[1,512,512]{2,1,0:T(8,128)(2,1)S(1)}, u32[]{:S(2)}, u32[]{:S(2)}) collective-permute-start(bf16[1,512,512]{2,1,0:T(8,128)(2,1)S(1)} %collective-permute-done.10.refs_11_.refs_2_), channel_id=1, source_target_pairs={{0,16},{1,17},{2,18},{3,19},{4,20},{5,21},{6,22},{7,23},{8,24},{9,... | collective-permute-start | bytes 1572872 | tf_op jit(solution)/shard_map/ppermute | solution.py:32
  76.5 2.3 %collective-permute-done.12.refs_1_.refs_13_ = bf16[1,512,512]{2,1,0:T(8,128)(2,1)S(1)} collective-permute-done((bf16[1,512,512]{2,1,0:T(8,128)(2,1)S(1)}, bf16[1,512,512]{2,1,0:T(8,128)(2,1)S(1)}, u32[]{:S(2)}, u32[]{:S(2)}) %collective-permute-start.12) | collective-permute-done | bytes 524320 | tf_op jit(solution)/shard_map/ppermute | solution.py:32
  78.7 3.2 %collective-permute-done.13.refs_2_.refs_14_ = bf16[1,512,512]{2,1,0:T(8,128)(2,1)S(1)} collective-permute-done((bf16[1,512,512]{2,1,0:T(8,128)(2,1)S(1)}, bf16[1,512,512]{2,1,0:T(8,128)(2,1)S(1)}, u32[]{:S(2)}, u32[]{:S(2)}) %collective-permute-start.13) | collective-permute-done | bytes 524320 | tf_op jit(solution)/shard_map/ppermute | solution.py:32
  82.5 1.9 %collective-permute-done.14.refs_3_.refs_15_ = bf16[1,512,512]{2,1,0:T(8,128)(2,1)S(1)} collective-permute-done((bf16[1,512,512]{2,1,0:T(8,128)(2,1)S(1)}, bf16[1,512,512]{2,1,0:T(8,128)(2,1)S(1)}, u32[]{:S(2)}, u32[]{:S(2)}) %collective-permute-start.14) | collective-permute-done | bytes 524320 | tf_op jit(solution)/shard_map/ppermute | solution.py:32
  93.0 32.6 %collective-permute-done.18.mine.in3m = bf16[64,2048]{1,0:T(8,128)(2,1)} collective-permute-done((bf16[64,2048]{1,0:T(8,128)(2,1)S(1)}, bf16[64,2048]{1,0:T(8,128)(2,1)}, u32[]{:S(2)}, u32[]{:S(2)}) %collective-permute-start.18) | collective-permute-done | bytes 262176 | tf_op jit(solution)/shard_map/ppermute | solution.py:350
  125.6 2.8 %collective-permute-start.19 = (bf16[64,2048]{1,0:T(8,128)(2,1)}, bf16[64,2048]{1,0:T(8,128)(2,1)}, u32[]{:S(2)}, u32[]{:S(2)}) collective-permute-start(bf16[64,2048]{1,0:T(8,128)(2,1)} %collective-permute-done.18.mine.in3m), channel_id=1, source_target_pairs={{384,448},{448,384},{385,449},{449,385},{386,450},{450,386},{387,4... | collective-permute-start | bytes 786440 | tf_op jit(solution)/shard_map/ppermute | solution.py:321
  128.4 15.6 %collective-permute-done.22.mem_mine = bf16[64,2048]{1,0:T(8,128)(2,1)} collective-permute-done((bf16[64,2048]{1,0:T(8,128)(2,1)S(1)}, bf16[64,2048]{1,0:T(8,128)(2,1)}, u32[]{:S(2)}, u32[]{:S(2)}) %collective-permute-start.22) | collective-permute-done | bytes 262176 | tf_op jit(solution)/shard_map/ppermute | solution.py:364
  144.0 2.6 %collective-permute-start.23 = (bf16[64,2048]{1,0:T(8,128)(2,1)}, bf16[64,2048]{1,0:T(8,128)(2,1)}, u32[]{:S(2)}, u32[]{:S(2)}) collective-permute-start(bf16[64,2048]{1,0:T(8,128)(2,1)} %collective-permute-done.22.mem_mine), channel_id=1, source_target_pairs={{384,448},{448,384},{385,449},{449,385},{386,450},{450,386},{387,4... | collective-permute-start | bytes 786440 | tf_op jit(solution)/shard_map/ppermute | solution.py:321
  157.1 2.2 %shard_map.68.q = bf16[128,512]{1,0:T(8,128)(2,1)S(1)} custom-call(s32[9]{0:T(128)S(1)} %stack.27.scal, f32[5,2048]{1,0:T(8,128)S(1)} %copy-done.30, bf16[64,2048]{1,0:T(8,128)(2,1)} %collective-permute-done.18.mine.in3m, bf16[64,2048]{1,0:T(8,128)(2,1)} %collective-permute-done.19.other.in3o, bf16[1,512,512]{2,1,0:T(8,128)(2,1)S(1)} %pad_maximum_fusion.refs_0_, ...), custom_call_target="tpu_custom_call" | custom-call | flops 268435456 | bytes 8953856 | tf_op jit(solution)/shard_map/pallas_call | solution.py:221
  159.3 5.5 %shard_map.69.own = bf16[128,2048]{1,0:T(8,128)(2,1)S(1)} custom-call(s32[9]{0:T(128)S(1)} %stack.27.scal, bf16[128,512]{1,0:T(8,128)(2,1)S(1)} %shard_map.68.q, bf16[64,2048]{1,0:T(8,128)(2,1)} %collective-permute-done.22.mem_mine, bf16[64,2048]{1,0:T(8,128)(2,1)} %collective-permute-done.23.mem_other, bf16[1,512,512]{2,1,0:T(8,128)(2,1)S(1)} %pad_maximum_fusion.refs_0_, ...), custom_call_target="tpu_custom_call" | custom-call | flops 805306368 | bytes 9043968 | tf_op jit(solution)/shard_map/pallas_call | solution.py:221
  164.9 1.4 collective-permute-start.24
  167.1 1.8 %collective-permute-done.24.got = bf16[128,2048]{1,0:T(8,128)(2,1)S(1)} collective-permute-done((bf16[128,2048]{1,0:T(8,128)(2,1)S(1)}, bf16[128,2048]{1,0:T(8,128)(2,1)S(1)}, u32[]{:S(2)}, u32[]{:S(2)}) %collective-permute-start.24) | collective-permute-done | bytes 524320 | tf_op jit(solution)/shard_map/ppermute | solution.py:389
  168.8 2.1 %shard_map.70 = bf16[2,64,2048]{2,1,0:T(8,128)(2,1)} custom-call(s32[9]{0:T(128)S(1)} %stack.27.scal, bf16[64,2048]{1,0:T(8,128)(2,1)S(1)} %get-tuple-element.18.mine, bf16[64,2048]{1,0:T(8,128)(2,1)S(1)} %copy-done.25, bf16[64,2048]{1,0:T(8,128)(2,1)S(1)} %copy-done.27, bf16[64,2048]{1,0:T(8,128)(2,1)S(1)} %copy-done.29, ...), custom_call_target="tpu_custom_call" | custom-call | bytes 3145728 | tf_op jit(solution)/shard_map/pallas_call | solution.py:221
  (129 shorter events, 24.5 us)
Async XLA Ops:
  1.9 15.7 %all-to-all-start = ((bf16[8,2,32,512]{3,2,1,0:T(8,128)(2,1)}), bf16[8,2,32,512]{3,2,1,0:T(8,128)(2,1)S(1)}, u32[]{:S(2)}, u32[]{:S(2)}) async-start(bf16[8,2,32,512]{3,2,1,0:T(8,128)(2,1)} %bitcast.1), calls=%async_computation | async-start | bytes 1048576 | tf_op jit(solution)/shard_map/all_to_all | solution.py:276
  17.6 13.9 %collective-permute-start = (bf16[4,128,512]{2,1,0:T(8,128)(2,1)S(1)}, bf16[4,128,512]{2,1,0:T(8,128)(2,1)S(1)}, u32[]{:S(2)}, u32[]{:S(2)}) collective-permute-start(bf16[4,128,512]{2,1,0:T(8,128)(2,1)S(1)} %bitcast.20), channel_id=1, source_target_pairs={{0,4},{1,5},{2,6},{3,7},{4,0},{5,1},{6,2},{7,3},{8,12},{9,13},{10,... | collective-permute-start | bytes 1572872 | tf_op jit(solution)/shard_map/ppermute | solution.py:32
  21.6 14.3 %collective-permute-start.2 = (bf16[4,128,512]{2,1,0:T(8,128)(2,1)S(1)}, bf16[4,128,512]{2,1,0:T(8,128)(2,1)S(1)}, u32[]{:S(2)}, u32[]{:S(2)}) collective-permute-start(bf16[4,128,512]{2,1,0:T(8,128)(2,1)S(1)} %bitcast.21), channel_id=1, source_target_pairs={{0,8},{1,9},{2,10},{3,11},{4,12},{5,13},{6,14},{7,15},{8,0},{9,1},... | collective-permute-start | bytes 1572872 | tf_op jit(solution)/shard_map/ppermute | solution.py:32
  29.6 12.0 %collective-permute-start.1 = (bf16[4,128,512]{2,1,0:T(8,128)(2,1)S(1)}, bf16[4,128,512]{2,1,0:T(8,128)(2,1)S(1)}, u32[]{:S(2)}, u32[]{:S(2)}) collective-permute-start(bf16[4,128,512]{2,1,0:T(8,128)(2,1)S(1)} %bitcast.22), channel_id=1, source_target_pairs={{0,12},{1,13},{2,14},{3,15},{4,8},{5,9},{6,10},{7,11},{8,4},{9,5},... | collective-permute-start | bytes 1572872 | tf_op jit(solution)/shard_map/ppermute | solution.py:32
  41.6 15.4 %collective-permute-start.7 = (bf16[1,512,512]{2,1,0:T(8,128)(2,1)S(1)}, bf16[1,512,512]{2,1,0:T(8,128)(2,1)S(1)}, u32[]{:S(2)}, u32[]{:S(2)}) collective-permute-start(bf16[1,512,512]{2,1,0:T(8,128)(2,1)S(1)} %pad_maximum_fusion.refs_0_), channel_id=1, source_target_pairs={{0,48},{1,49},{2,50},{3,51},{4,52},{5,53},{6,54},{7,55},{8,56},{9,... | collective-permute-start | bytes 1572872 | tf_op jit(solution)/shard_map/ppermute | solution.py:32
  45.7 13.3 %collective-permute-start.3 = (bf16[1,512,512]{2,1,0:T(8,128)(2,1)S(1)}, bf16[1,512,512]{2,1,0:T(8,128)(2,1)S(1)}, u32[]{:S(2)}, u32[]{:S(2)}) collective-permute-start(bf16[1,512,512]{2,1,0:T(8,128)(2,1)S(1)} %pad_maximum_fusion.refs_0_), channel_id=1, source_target_pairs={{0,16},{1,17},{2,18},{3,19},{4,20},{5,21},{6,22},{7,23},{8,24},{9,... | collective-permute-start | bytes 1572872 | tf_op jit(solution)/shard_map/ppermute | solution.py:32
  47.7 14.2 %collective-permute-start.8 = (bf16[1,512,512]{2,1,0:T(8,128)(2,1)S(1)}, bf16[1,512,512]{2,1,0:T(8,128)(2,1)S(1)}, u32[]{:S(2)}, u32[]{:S(2)}) collective-permute-start(bf16[1,512,512]{2,1,0:T(8,128)(2,1)S(1)} %pad_maximum_fusion.1.refs_1_), channel_id=1, source_target_pairs={{0,48},{1,49},{2,50},{3,51},{4,52},{5,53},{6,54},{7,55},{8,56},{9,... | collective-permute-start | bytes 1572872 | tf_op jit(solution)/shard_map/ppermute | solution.py:32
  50.4 14.1 %collective-permute-start.4 = (bf16[1,512,512]{2,1,0:T(8,128)(2,1)S(1)}, bf16[1,512,512]{2,1,0:T(8,128)(2,1)S(1)}, u32[]{:S(2)}, u32[]{:S(2)}) collective-permute-start(bf16[1,512,512]{2,1,0:T(8,128)(2,1)S(1)} %pad_maximum_fusion.1.refs_1_), channel_id=1, source_target_pairs={{0,16},{1,17},{2,18},{3,19},{4,20},{5,21},{6,22},{7,23},{8,24},{9,... | collective-permute-start | bytes 1572872 | tf_op jit(solution)/shard_map/ppermute | solution.py:32
  53.0 15.5 %collective-permute-start.9 = (bf16[1,512,512]{2,1,0:T(8,128)(2,1)S(1)}, bf16[1,512,512]{2,1,0:T(8,128)(2,1)S(1)}, u32[]{:S(2)}, u32[]{:S(2)}) collective-permute-start(bf16[1,512,512]{2,1,0:T(8,128)(2,1)S(1)} %pad_maximum_fusion.2.refs_2_), channel_id=1, source_target_pairs={{0,48},{1,49},{2,50},{3,51},{4,52},{5,53},{6,54},{7,55},{8,56},{9,... | collective-permute-start | bytes 1572872 | tf_op jit(solution)/shard_map/ppermute | solution.py:32
  57.0 30.9 %copy-start.9 = (bf16[1,512,512]{2,1,0:T(8,128)(2,1)}, bf16[1,512,512]{2,1,0:T(8,128)(2,1)S(1)}, u32[]{:S(2)}) copy-start(bf16[1,512,512]{2,1,0:T(8,128)(2,1)S(1)} %collective-permute-done.7.refs_8_) | copy-start | bytes 1572868
  57.0 13.4 %collective-permute-start.5 = (bf16[1,512,512]{2,1,0:T(8,128)(2,1)S(1)}, bf16[1,512,512]{2,1,0:T(8,128)(2,1)S(1)}, u32[]{:S(2)}, u32[]{:S(2)}) collective-permute-start(bf16[1,512,512]{2,1,0:T(8,128)(2,1)S(1)} %pad_maximum_fusion.2.refs_2_), channel_id=1, source_target_pairs={{0,16},{1,17},{2,18},{3,19},{4,20},{5,21},{6,22},{7,23},{8,24},{9,... | collective-permute-start | bytes 1572872 | tf_op jit(solution)/shard_map/ppermute | solution.py:32
  59.0 28.9 %copy-start.12 = (bf16[1,512,512]{2,1,0:T(8,128)(2,1)}, bf16[1,512,512]{2,1,0:T(8,128)(2,1)S(1)}, u32[]{:S(2)}) copy-start(bf16[1,512,512]{2,1,0:T(8,128)(2,1)S(1)} %collective-permute-done.3.refs_4_) | copy-start | bytes 1572868
  59.0 14.1 %collective-permute-start.10 = (bf16[1,512,512]{2,1,0:T(8,128)(2,1)S(1)}, bf16[1,512,512]{2,1,0:T(8,128)(2,1)S(1)}, u32[]{:S(2)}, u32[]{:S(2)}) collective-permute-start(bf16[1,512,512]{2,1,0:T(8,128)(2,1)S(1)} %pad_maximum_fusion.3.refs_3_.refs_0_), channel_id=1, source_target_pairs={{0,48},{1,49},{2,50},{3,51},{4,52},{5,53},{6,54},{7,55},{8,56},{9,... | collective-permute-start | bytes 1572872 | tf_op jit(solution)/shard_map/ppermute | solution.py:32
  61.9 26.0 %copy-start.15 = (bf16[1,512,512]{2,1,0:T(8,128)(2,1)}, bf16[1,512,512]{2,1,0:T(8,128)(2,1)S(1)}, u32[]{:S(2)}) copy-start(bf16[1,512,512]{2,1,0:T(8,128)(2,1)S(1)} %collective-permute-done.8.refs_9_) | copy-start | bytes 1572868
  61.9 13.9 %collective-permute-start.6 = (bf16[1,512,512]{2,1,0:T(8,128)(2,1)S(1)}, bf16[1,512,512]{2,1,0:T(8,128)(2,1)S(1)}, u32[]{:S(2)}, u32[]{:S(2)}) collective-permute-start(bf16[1,512,512]{2,1,0:T(8,128)(2,1)S(1)} %pad_maximum_fusion.3.refs_3_.refs_0_), channel_id=1, source_target_pairs={{0,16},{1,17},{2,18},{3,19},{4,20},{5,21},{6,22},{7,23},{8,24},{9,... | collective-permute-start | bytes 1572872 | tf_op jit(solution)/shard_map/ppermute | solution.py:32
  64.5 23.4 %copy-start.18 = (bf16[1,512,512]{2,1,0:T(8,128)(2,1)}, bf16[1,512,512]{2,1,0:T(8,128)(2,1)S(1)}, u32[]{:S(2)}) copy-start(bf16[1,512,512]{2,1,0:T(8,128)(2,1)S(1)} %collective-permute-done.4.refs_5_) | copy-start | bytes 1572868
  64.5 11.9 %collective-permute-start.11 = (bf16[1,512,512]{2,1,0:T(8,128)(2,1)S(1)}, bf16[1,512,512]{2,1,0:T(8,128)(2,1)S(1)}, u32[]{:S(2)}, u32[]{:S(2)}) collective-permute-start(bf16[1,512,512]{2,1,0:T(8,128)(2,1)S(1)} %collective-permute-done.3.refs_4_), channel_id=1, source_target_pairs={{0,48},{1,49},{2,50},{3,51},{4,52},{5,53},{6,54},{7,55},{8,56},{9,... | collective-permute-start | bytes 1572872 | tf_op jit(solution)/shard_map/ppermute | solution.py:32
  68.5 19.4 %copy-start.20 = (bf16[1,512,512]{2,1,0:T(8,128)(2,1)}, bf16[1,512,512]{2,1,0:T(8,128)(2,1)S(1)}, u32[]{:S(2)}) copy-start(bf16[1,512,512]{2,1,0:T(8,128)(2,1)S(1)} %collective-permute-done.9.refs_10_) | copy-start | bytes 1572868
  68.5 10.2 %collective-permute-start.12 = (bf16[1,512,512]{2,1,0:T(8,128)(2,1)S(1)}, bf16[1,512,512]{2,1,0:T(8,128)(2,1)S(1)}, u32[]{:S(2)}, u32[]{:S(2)}) collective-permute-start(bf16[1,512,512]{2,1,0:T(8,128)(2,1)S(1)} %collective-permute-done.8.refs_9_), channel_id=1, source_target_pairs={{0,16},{1,17},{2,18},{3,19},{4,20},{5,21},{6,22},{7,23},{8,24},{9,... | collective-permute-start | bytes 1572872 | tf_op jit(solution)/shard_map/ppermute | solution.py:32
  70.4 17.5 %copy-start.22 = (bf16[1,512,512]{2,1,0:T(8,128)(2,1)}, bf16[1,512,512]{2,1,0:T(8,128)(2,1)S(1)}, u32[]{:S(2)}) copy-start(bf16[1,512,512]{2,1,0:T(8,128)(2,1)S(1)} %collective-permute-done.5.refs_6_) | copy-start | bytes 1572868
  70.5 11.4 %collective-permute-start.13 = (bf16[1,512,512]{2,1,0:T(8,128)(2,1)S(1)}, bf16[1,512,512]{2,1,0:T(8,128)(2,1)S(1)}, u32[]{:S(2)}, u32[]{:S(2)}) collective-permute-start(bf16[1,512,512]{2,1,0:T(8,128)(2,1)S(1)} %collective-permute-done.5.refs_6_), channel_id=1, source_target_pairs={{0,48},{1,49},{2,50},{3,51},{4,52},{5,53},{6,54},{7,55},{8,56},{9,... | collective-permute-start | bytes 1572872 | tf_op jit(solution)/shard_map/ppermute | solution.py:32
  73.2 11.2 %collective-permute-start.14 = (bf16[1,512,512]{2,1,0:T(8,128)(2,1)S(1)}, bf16[1,512,512]{2,1,0:T(8,128)(2,1)S(1)}, u32[]{:S(2)}, u32[]{:S(2)}) collective-permute-start(bf16[1,512,512]{2,1,0:T(8,128)(2,1)S(1)} %collective-permute-done.10.refs_11_.refs_2_), channel_id=1, source_target_pairs={{0,16},{1,17},{2,18},{3,19},{4,20},{5,21},{6,22},{7,23},{8,24},{9,... | collective-permute-start | bytes 1572872 | tf_op jit(solution)/shard_map/ppermute | solution.py:32
  84.9 1.4 collective-permute-start.15
  86.5 0.7 collective-permute-start.16
  87.2 0.7 collective-permute-start.17
  88.7 2.0 %collective-permute-start.20 = (bf16[64,2048]{1,0:T(8,128)(2,1)S(1)}, bf16[64,2048]{1,0:T(8,128)(2,1)S(1)}, u32[]{:S(2)}, u32[]{:S(2)}) collective-permute-start(bf16[64,2048]{1,0:T(8,128)(2,1)S(1)} %get-tuple-element.28), channel_id=1, source_target_pairs={{128,192},{192,128},{129,193},{193,129},{130,194},{194,130},{131,1... | collective-permute-start | bytes 786440 | tf_op jit(solution)/shard_map/ppermute | solution.py:321
  89.4 36.2 %collective-permute-start.18 = (bf16[64,2048]{1,0:T(8,128)(2,1)S(1)}, bf16[64,2048]{1,0:T(8,128)(2,1)}, u32[]{:S(2)}, u32[]{:S(2)}) collective-permute-start(bf16[64,2048]{1,0:T(8,128)(2,1)S(1)} %add_convert_fusion.1), channel_id=1, source_target_pairs={{256,384},{257,385},{258,386},{259,387},{260,388},{261,389},{262,3... | collective-permute-start | bytes 786440 | tf_op jit(solution)/shard_map/ppermute | solution.py:350
  91.7 52.3 %collective-permute-start.22 = (bf16[64,2048]{1,0:T(8,128)(2,1)S(1)}, bf16[64,2048]{1,0:T(8,128)(2,1)}, u32[]{:S(2)}, u32[]{:S(2)}) collective-permute-start(bf16[64,2048]{1,0:T(8,128)(2,1)S(1)} %fusion.2), channel_id=1, source_target_pairs={{128,384},{129,385},{130,386},{131,387},{132,388},{133,389},{134,3... | collective-permute-start | bytes 786440 | tf_op jit(solution)/shard_map/ppermute | solution.py:364
  125.6 21.0 %collective-permute-start.19 = (bf16[64,2048]{1,0:T(8,128)(2,1)}, bf16[64,2048]{1,0:T(8,128)(2,1)}, u32[]{:S(2)}, u32[]{:S(2)}) collective-permute-start(bf16[64,2048]{1,0:T(8,128)(2,1)} %collective-permute-done.18.mine.in3m), channel_id=1, source_target_pairs={{384,448},{448,384},{385,449},{449,385},{386,450},{450,386},{387,4... | collective-permute-start | bytes 786440 | tf_op jit(solution)/shard_map/ppermute | solution.py:321
  144.0 15.3 %collective-permute-start.23 = (bf16[64,2048]{1,0:T(8,128)(2,1)}, bf16[64,2048]{1,0:T(8,128)(2,1)}, u32[]{:S(2)}, u32[]{:S(2)}) collective-permute-start(bf16[64,2048]{1,0:T(8,128)(2,1)} %collective-permute-done.22.mem_mine), channel_id=1, source_target_pairs={{384,448},{448,384},{385,449},{449,385},{386,450},{450,386},{387,4... | collective-permute-start | bytes 786440 | tf_op jit(solution)/shard_map/ppermute | solution.py:321
  164.9 3.9 %collective-permute-start.24 = (bf16[128,2048]{1,0:T(8,128)(2,1)S(1)}, bf16[128,2048]{1,0:T(8,128)(2,1)S(1)}, u32[]{:S(2)}, u32[]{:S(2)}) collective-permute-start(bf16[128,2048]{1,0:T(8,128)(2,1)S(1)} %shard_map.69.own), channel_id=1, source_target_pairs={{384,448},{385,449},{386,450},{387,451},{388,452},{389,453},{390,4... | collective-permute-start | bytes 1572872 | tf_op jit(solution)/shard_map/ppermute | solution.py:389
  166.4 0.7 collective-permute-start.21
  (33 other events, 138.3 us)

commit v15 on v5

--- a/solution.py
+++ b/solution.py
@@ -12,6 +12,8 @@
 SIDE = 4
 TURNS = (0, 1, 3, 2)
 FAR = 2
+FIRST_HELD = (1, 3, 5, 6, 7, 8, 9)
+QUERY_HELD = (0, 2, 4, 6)
 AXES = ("zh", "core", "y", "x", "zl")
 DP = ("y", "x", "zl")
 SECTION = ("zh", "core")
@@ -127,8 +129,16 @@
         q[...], k[...], v[...] = project(scal, h3, pieces, TURNS[:3], (0, 1, 2))
 
 
+def spread(refs, held):
+    pieces = [None] * 10
+    for at, ref in zip(held, refs):
+        pieces[at] = ref
+    return pieces
+
+
 def first_kernel(scal, h3, q, k, v, *refs):
-    pieces, (out_mine, out_other, t3) = refs[:10], refs[10:]
+    count = len(FIRST_HELD)
+    pieces, (out_mine, out_other, t3) = spread(refs, FIRST_HELD), refs[count:]
 
     @pl.when(lax.rem(scal[2], 2) == 0)
     def _():
@@ -148,7 +158,8 @@
 
 
 def query_kernel(scal, gains, mine, other, *refs):
-    pieces, (q, h3) = refs[:10], refs[10:]
+    count = len(QUERY_HELD)
+    pieces, (q, h3) = spread(refs, QUERY_HELD), refs[count:]
 
     @pl.when(scal[2] == 3)
     def _():
@@ -295,7 +306,7 @@
         3 * work,
     )
     kept, sent = call(
-        first_kernel, scal, [*started, *pieces], halves, [(blocks, F32)], 2 * work
+        first_kernel, scal, [*started, *(pieces[i] for i in FIRST_HELD)], halves, [(blocks, F32)], 2 * work
     )
     first = added(mine, kept + swapped(sent, (0, 2)).astype(F32), live).astype(BF16)
     in1 = lax.ppermute(first, "zh", [(0, 1)])
@@ -316,7 +327,12 @@
     early_other = lax.ppermute(early, SECTION, [(0, 1), (2, 3), (4, 5)])
     in3_other = swapped(in3, (3,))
     query = call(
-        query_kernel, scal, [norm_gains, in3, in3_other, *pieces], narrow, [(blocks, BF16)], work
+        query_kernel,
+        scal,
+        [norm_gains, in3, in3_other, *(pieces[i] for i in QUERY_HELD)],
+        narrow,
+        [(blocks, BF16)],
+        work,
     )
     mem_other = swapped(mem, (3,))
     own = call(

time: 162 us -> 160 us (0.988)
  no operation moved by 1% of the time
where the time goes in v15:
time: 160 us; the launch traced here: 159 us
  waiting for transfers between devices  63.7 us (40%)
  starting transfers between devices  46.1 us (29%)
  blocking collectives  16.6 us (10%)
  Pallas kernels  16.3 us (10%)
  local copies, waits for them, and re-layouts  12.8 us (8%)
  other arithmetic  3.29 us (2%)
    ppermute x1, waiting for transfers between devices, on_device(): in3 = lax.ppermute(first, 'zh', [(2, 3)])  37.5 us
    ppermute x11, starting transfers between devices, exchange(): return lax.ppermute(array, AXES, pairs)  33.4 us
    all_to_all x1, blocking collectives, gather(): got = lax.all_to_all(sent, ('core', 'zl'), 0, 0, tiled=True)  16.6 us
    pallas_call x6, Pallas kernels, call(): pl.pallas_call(kernel, out_shape=outs, in_specs=[SMEM] + [VMEM] * len(ope...  16.3 us
    ppermute x11, waiting for transfers between devices, exchange(): return lax.ppermute(array, AXES, pairs)  15.1 us
    ppermute x1, waiting for transfers between devices, on_device(): mem = lax.ppermute(memory, 'zh', [(1, 3)])  9.28 us
    ppermute x5, starting transfers between devices, swapped(): return lax.ppermute(array, SECTION, pairs)  7.43 us
    slice x4, local copies, waits for them, and re-layouts, gather(): far += [exchange(b[:1], True, 1), exchange(a[1:], True, 3)]  6.47 us
  transfers between devices with their start and end apart: 21, of which 10 were waited for; matrix products, arithmetic and copies ran while one was open for 9% of the time, Pallas kernels for 3%

profile of v15, /device:TPU:481, one launch (start us, length us, event | category | flops | bytes accessed | tf_op | source)
XLA Modules:
  0.0 159.4 jit_solution(17797165171159666969)
XLA Ops:
  1.1 16.6 %all_to_all.5 = bf16[8,2,32,512]{3,2,1,0:T(8,128)(2,1)S(1)} all-to-all(bf16[8,2,32,512]{3,2,1,0:T(8,128)(2,1)S(1)} %bitcast.24), channel_id=1, replica_groups=mesh['zh'=4,'core'=2,'y'=4,'x'=4,'zl'=4] {'core','zl'}, dimensions={0} | all-to-all | bytes 1048576 | tf_op jit(solution)/shard_map/all_to_all | solution.py:243
  17.7 4.8 %collective-permute-start.2 = (bf16[4,128,512]{2,1,0:T(8,128)(2,1)S(1)}, bf16[4,128,512]{2,1,0:T(8,128)(2,1)S(1)}, u32[]{:S(2)}, u32[]{:S(2)}) collective-permute-start(bf16[4,128,512]{2,1,0:T(8,128)(2,1)S(1)} %bitcast.27), channel_id=1, source_target_pairs={{0,8},{1,9},{2,10},{3,11},{4,12},{5,13},{6,14},{7,15},{8,0},{9,1},... | collective-permute-start | bytes 1572872 | tf_op jit(solution)/shard_map/ppermute | solution.py:34
  22.5 2.7 %collective-permute-start.1 = (bf16[4,128,512]{2,1,0:T(8,128)(2,1)S(1)}, bf16[4,128,512]{2,1,0:T(8,128)(2,1)S(1)}, u32[]{:S(2)}, u32[]{:S(2)}) collective-permute-start(bf16[4,128,512]{2,1,0:T(8,128)(2,1)S(1)} %bitcast.28), channel_id=1, source_target_pairs={{0,12},{1,13},{2,14},{3,15},{4,8},{5,9},{6,10},{7,11},{8,4},{9,5},... | collective-permute-start | bytes 1572872 | tf_op jit(solution)/shard_map/ppermute | solution.py:34
  25.2 1.9 %collective-permute-start = (bf16[4,128,512]{2,1,0:T(8,128)(2,1)S(1)}, bf16[4,128,512]{2,1,0:T(8,128)(2,1)S(1)}, u32[]{:S(2)}, u32[]{:S(2)}) collective-permute-start(bf16[4,128,512]{2,1,0:T(8,128)(2,1)S(1)} %bitcast.29), channel_id=1, source_target_pairs={{0,4},{1,5},{2,6},{3,7},{4,0},{5,1},{6,2},{7,3},{8,12},{9,13},{10,... | collective-permute-start | bytes 1572872 | tf_op jit(solution)/shard_map/ppermute | solution.py:34
  27.2 2.2 %collective-permute-done.2 = bf16[4,128,512]{2,1,0:T(8,128)(2,1)S(1)} collective-permute-done((bf16[4,128,512]{2,1,0:T(8,128)(2,1)S(1)}, bf16[4,128,512]{2,1,0:T(8,128)(2,1)S(1)}, u32[]{:S(2)}, u32[]{:S(2)}) %collective-permute-start.2) | collective-permute-done | bytes 524320 | tf_op jit(solution)/shard_map/ppermute | solution.py:34
  29.4 5.6 %collective-permute-done.1 = bf16[4,128,512]{2,1,0:T(8,128)(2,1)S(1)} collective-permute-done((bf16[4,128,512]{2,1,0:T(8,128)(2,1)S(1)}, bf16[4,128,512]{2,1,0:T(8,128)(2,1)S(1)}, u32[]{:S(2)}, u32[]{:S(2)}) %collective-permute-start.1) | collective-permute-done | bytes 524320 | tf_op jit(solution)/shard_map/ppermute | solution.py:34
  35.5 4.4 %collective-permute-start.5 = (bf16[2,512,512]{2,1,0:T(8,128)(2,1)S(1)}, bf16[2,512,512]{2,1,0:T(8,128)(2,1)S(1)}, u32[]{:S(2)}, u32[]{:S(2)}) collective-permute-start(bf16[2,512,512]{2,1,0:T(8,128)(2,1)S(1)} %pad_maximum_fusion.refs_0_), channel_id=1, source_target_pairs={{0,48},{1,49},{2,50},{3,51},{4,52},{5,53},{6,54},{7,55},{8,56},{9,... | collective-permute-start | bytes 3145736 | tf_op jit(solution)/shard_map/ppermute | solution.py:34
  39.9 1.9 %collective-permute-start.3 = (bf16[2,512,512]{2,1,0:T(8,128)(2,1)S(1)}, bf16[2,512,512]{2,1,0:T(8,128)(2,1)}, u32[]{:S(2)}, u32[]{:S(2)}) collective-permute-start(bf16[2,512,512]{2,1,0:T(8,128)(2,1)S(1)} %pad_maximum_fusion.refs_0_), channel_id=1, source_target_pairs={{0,16},{1,17},{2,18},{3,19},{4,20},{5,21},{6,22},{7,23},{8,24},{9,... | collective-permute-start | bytes 3145736 | tf_op jit(solution)/shard_map/ppermute | solution.py:34
  41.9 2.7 %collective-permute-start.6 = (bf16[2,512,512]{2,1,0:T(8,128)(2,1)S(1)}, bf16[2,512,512]{2,1,0:T(8,128)(2,1)}, u32[]{:S(2)}, u32[]{:S(2)}) collective-permute-start(bf16[2,512,512]{2,1,0:T(8,128)(2,1)S(1)} %pad_maximum_fusion.1.refs_1_.refs_0_), channel_id=1, source_target_pairs={{0,48},{1,49},{2,50},{3,51},{4,52},{5,53},{6,54},{7,55},{8,56},{9,... | collective-permute-start | bytes 3145736 | tf_op jit(solution)/shard_map/ppermute | solution.py:34
  44.6 2.6 %collective-permute-start.4 = (bf16[2,512,512]{2,1,0:T(8,128)(2,1)S(1)}, bf16[2,512,512]{2,1,0:T(8,128)(2,1)}, u32[]{:S(2)}, u32[]{:S(2)}) collective-permute-start(bf16[2,512,512]{2,1,0:T(8,128)(2,1)S(1)} %pad_maximum_fusion.1.refs_1_.refs_0_), channel_id=1, source_target_pairs={{0,16},{1,17},{2,18},{3,19},{4,20},{5,21},{6,22},{7,23},{8,24},{9,... | collective-permute-start | bytes 3145736 | tf_op jit(solution)/shard_map/ppermute | solution.py:34
  47.3 1.9 %broadcast_select_fusion = bf16[2,64,2048]{2,1,0:T(8,128)(2,1)} fusion(bf16[2,64,2048]{2,1,0:T(8,128)(2,1)} %param.6, bf16[2,64,2048]{2,1,0:T(8,128)(2,1)} %param.7, pred[]{:T(512)S(6)} %lt.26), kind=kLoop, calls=%fused_computation.9 | loop fusion | flops 262144 | bytes 1572865 | tf_op jit(solution)/shard_map/jit(_where)/select_n | solution.py:281
  49.2 3.4 %collective-permute-done.5.refs_4_.refs_2_ = bf16[2,512,512]{2,1,0:T(8,128)(2,1)S(1)} collective-permute-done((bf16[2,512,512]{2,1,0:T(8,128)(2,1)S(1)}, bf16[2,512,512]{2,1,0:T(8,128)(2,1)S(1)}, u32[]{:S(2)}, u32[]{:S(2)}) %collective-permute-start.5) | collective-permute-done | bytes 1048608 | tf_op jit(solution)/shard_map/ppermute | solution.py:34
  53.4 2.0 %collective-permute-start.7 = (bf16[1,512,512]{2,1,0:T(8,128)(2,1)}, bf16[1,512,512]{2,1,0:T(8,128)(2,1)}, u32[]{:S(2)}, u32[]{:S(2)}) collective-permute-start(bf16[1,512,512]{2,1,0:T(8,128)(2,1)} %slice.68), channel_id=1, source_target_pairs={{0,16},{1,17},{2,18},{3,19},{4,20},{5,21},{6,22},{7,23},{8,24},{9,... | collective-permute-start | bytes 1572872 | tf_op jit(solution)/shard_map/ppermute | solution.py:34
  55.9 1.9 %slice.69 = bf16[1,512,512]{2,1,0:T(8,128)(2,1)} slice(bf16[2,512,512]{2,1,0:T(8,128)(2,1)} %collective-permute-done.3.refs_2_.refs_1_), slice={[1:2], [0:512], [0:512]} | slice | bytes 1048576 | tf_op jit(solution)/shard_map/slice | solution.py:252
  57.8 4.0 %collective-permute-start.8 = (bf16[1,512,512]{2,1,0:T(8,128)(2,1)}, bf16[1,512,512]{2,1,0:T(8,128)(2,1)}, u32[]{:S(2)}, u32[]{:S(2)}) collective-permute-start(bf16[1,512,512]{2,1,0:T(8,128)(2,1)} %slice.69), channel_id=1, source_target_pairs={{0,48},{1,49},{2,50},{3,51},{4,52},{5,53},{6,54},{7,55},{8,56},{9,... | collective-permute-start | bytes 1572872 | tf_op jit(solution)/shard_map/ppermute | solution.py:34
  61.8 2.2 %collective-permute-done.6.refs_5_.refs_2_ = bf16[2,512,512]{2,1,0:T(8,128)(2,1)} collective-permute-done((bf16[2,512,512]{2,1,0:T(8,128)(2,1)S(1)}, bf16[2,512,512]{2,1,0:T(8,128)(2,1)}, u32[]{:S(2)}, u32[]{:S(2)}) %collective-permute-start.6) | collective-permute-done | bytes 1048608 | tf_op jit(solution)/shard_map/ppermute | solution.py:34
  63.9 1.9 %slice.70 = bf16[1,512,512]{2,1,0:T(8,128)(2,1)} slice(bf16[2,512,512]{2,1,0:T(8,128)(2,1)} %collective-permute-done.6.refs_5_.refs_2_), slice={[0:1], [0:512], [0:512]} | slice | bytes 1048576 | tf_op jit(solution)/shard_map/slice | solution.py:252
  65.8 2.0 %collective-permute-start.9 = (bf16[1,512,512]{2,1,0:T(8,128)(2,1)}, bf16[1,512,512]{2,1,0:T(8,128)(2,1)}, u32[]{:S(2)}, u32[]{:S(2)}) collective-permute-start(bf16[1,512,512]{2,1,0:T(8,128)(2,1)} %slice.70), channel_id=1, source_target_pairs={{0,16},{1,17},{2,18},{3,19},{4,20},{5,21},{6,22},{7,23},{8,24},{9,... | collective-permute-start | bytes 1572872 | tf_op jit(solution)/shard_map/ppermute | solution.py:34
  67.9 1.9 %slice.71 = bf16[1,512,512]{2,1,0:T(8,128)(2,1)} slice(bf16[2,512,512]{2,1,0:T(8,128)(2,1)} %collective-permute-done.4.refs_3_.refs_1_), slice={[1:2], [0:512], [0:512]} | slice | bytes 1048576 | tf_op jit(solution)/shard_map/slice | solution.py:252
  69.7 4.4 %collective-permute-start.10 = (bf16[1,512,512]{2,1,0:T(8,128)(2,1)}, bf16[1,512,512]{2,1,0:T(8,128)(2,1)}, u32[]{:S(2)}, u32[]{:S(2)}) collective-permute-start(bf16[1,512,512]{2,1,0:T(8,128)(2,1)} %slice.71), channel_id=1, source_target_pairs={{0,48},{1,49},{2,50},{3,51},{4,52},{5,53},{6,54},{7,55},{8,56},{9,... | collective-permute-start | bytes 1572872 | tf_op jit(solution)/shard_map/ppermute | solution.py:34
  74.8 2.6 %stack.27.scal = s32[9]{0:T(128)S(1)} concatenate(s32[1]{0:T(128)} %bitcast, s32[1]{0:T(128)} %bitcast.1, s32[1]{0:T(128)} %bitcast.2, s32[1]{0:T(128)} %bitcast.3, s32[1]{0:T(128)} %get-tuple-element.39, s32[1]{0:T(128)} %get-tuple-element.40, s32[1]{0:T(128)} %bitcast.4, s32[1]{0:T(128)} %get-tuple-element.36, s32[1]{0:T(128)} %get-tuple-element.35), dimensions={0} | concatenate | bytes 72 | tf_op jit(solution)/shard_map/stack | solution.py:264
  78.5 2.0 %shard_map.64 = (bf16[16,128,128]{2,1,0:T(8,128)(2,1)S(1)}, f32[128,512]{1,0:T(8,128)S(1)}, f32[128,512]{1,0:T(8,128)S(1)}, f32[128,512]{1,0:T(8,128)S(1)}) custom-call(s32[9]{0:T(128)S(1)} %stack.27.scal, f32[5,2048]{1,0:T(8,128)S(1)} %copy-done.6, bf16[64,2048]{1,0:T(8,128)(2,1)S(1)} %get-tuple-element.32.mine, ...), custom_call_target="tpu_custom_call" | custom-call | flops 805306368 | bytes 6856704 | tf_op jit(solution)/shard_map/pallas_call | solution.py:188
  81.5 2.2 %shard_map.65 = (f32[64,2048]{1,0:T(8,128)S(1)}, bf16[64,2048]{1,0:T(8,128)(2,1)S(1)}) custom-call(s32[9]{0:T(128)S(1)} %stack.27.scal, bf16[16,128,128]{2,1,0:T(8,128)(2,1)S(1)} %get-tuple-element.13.h3, f32[128,512]{1,0:T(8,128)S(1)} %get-tuple-element.14.q, f32[128,512]{1,0:T(8,128)S(1)} %get-tuple-element.15.k, f32[128,512]{1,0:T(8,128)S(1)} %get-tuple-element.16.v, ...), custom_call_target="tpu_custom_call" | custom-call | flops 536870912 | bytes 6553600 | tf_op jit(solution)/shard_map/pallas_call | solution.py:188
  86.6 2.6 %shard_map.66 = (f32[64,2048]{1,0:T(8,128)S(1)}, bf16[64,2048]{1,0:T(8,128)(2,1)S(1)}) custom-call(s32[9]{0:T(128)S(1)} %stack.27.scal, f32[5,2048]{1,0:T(8,128)S(1)} %copy-done.6, bf16[64,2048]{1,0:T(8,128)(2,1)S(1)} %collective-permute-done.12.mine.in1m, bf16[64,2048]{1,0:T(8,128)(2,1)S(1)} %collective-permute-done.13.other.in1o, ...), custom_call_target="tpu_custom_call" | custom-call | flops 1073741824 | bytes 8953856 | tf_op jit(solution)/shard_map/pallas_call | solution.py:188
  93.6 37.5 %collective-permute-done.14.mine.in3m = bf16[64,2048]{1,0:T(8,128)(2,1)} collective-permute-done((bf16[64,2048]{1,0:T(8,128)(2,1)S(1)}, bf16[64,2048]{1,0:T(8,128)(2,1)}, u32[]{:S(2)}, u32[]{:S(2)}) %collective-permute-start.14) | collective-permute-done | bytes 262176 | tf_op jit(solution)/shard_map/ppermute | solution.py:313
  131.1 2.8 %collective-permute-start.15 = (bf16[64,2048]{1,0:T(8,128)(2,1)}, bf16[64,2048]{1,0:T(8,128)(2,1)}, u32[]{:S(2)}, u32[]{:S(2)}) collective-permute-start(bf16[64,2048]{1,0:T(8,128)(2,1)} %collective-permute-done.14.mine.in3m), channel_id=1, source_target_pairs={{384,448},{448,384},{385,449},{449,385},{386,450},{450,386},{387,4... | collective-permute-start | bytes 786440 | tf_op jit(solution)/shard_map/ppermute | solution.py:289
  133.9 9.3 %collective-permute-done.18.mem_mine = bf16[64,2048]{1,0:T(8,128)(2,1)} collective-permute-done((bf16[64,2048]{1,0:T(8,128)(2,1)S(1)}, bf16[64,2048]{1,0:T(8,128)(2,1)}, u32[]{:S(2)}, u32[]{:S(2)}) %collective-permute-start.18) | collective-permute-done | bytes 262176 | tf_op jit(solution)/shard_map/ppermute | solution.py:325
  143.2 2.6 %collective-permute-start.19 = (bf16[64,2048]{1,0:T(8,128)(2,1)}, bf16[64,2048]{1,0:T(8,128)(2,1)}, u32[]{:S(2)}, u32[]{:S(2)}) collective-permute-start(bf16[64,2048]{1,0:T(8,128)(2,1)} %collective-permute-done.18.mem_mine), channel_id=1, source_target_pairs={{384,448},{448,384},{385,449},{449,385},{386,450},{450,386},{387,4... | collective-permute-start | bytes 786440 | tf_op jit(solution)/shard_map/ppermute | solution.py:289
  145.8 2.2 %shard_map.67.q = bf16[128,512]{1,0:T(8,128)(2,1)S(1)} custom-call(s32[9]{0:T(128)S(1)} %stack.27.scal, f32[5,2048]{1,0:T(8,128)S(1)} %copy-done.6, bf16[64,2048]{1,0:T(8,128)(2,1)} %collective-permute-done.14.mine.in3m, bf16[64,2048]{1,0:T(8,128)(2,1)} %collective-permute-done.15.other.in3o, bf16[2,512,512]{2,1,0:T(8,128)(2,1)S(1)} %pad_maximum_fusion.refs_0_, ...), custom_call_target="tpu_custom_call" | custom-call | flops 268435456 | bytes 4235264 | tf_op jit(solution)/shard_map/pallas_call | solution.py:188
  148.1 5.3 %shard_map.68.own = bf16[128,2048]{1,0:T(8,128)(2,1)S(1)} custom-call(s32[9]{0:T(128)S(1)} %stack.27.scal, bf16[128,512]{1,0:T(8,128)(2,1)S(1)} %shard_map.67.q, bf16[64,2048]{1,0:T(8,128)(2,1)} %collective-permute-done.18.mem_mine, bf16[64,2048]{1,0:T(8,128)(2,1)} %collective-permute-done.19.mem_other, bf16[2,512,512]{2,1,0:T(8,128)(2,1)S(1)} %pad_maximum_fusion.refs_0_, ...), custom_call_target="tpu_custom_call" | custom-call | flops 805306368 | bytes 9043968 | tf_op jit(solution)/shard_map/pallas_call | solution.py:188
  155.5 1.8 %collective-permute-done.20.got = bf16[128,2048]{1,0:T(8,128)(2,1)S(1)} collective-permute-done((bf16[128,2048]{1,0:T(8,128)(2,1)S(1)}, bf16[128,2048]{1,0:T(8,128)(2,1)S(1)}, u32[]{:S(2)}, u32[]{:S(2)}) %collective-permute-start.20) | collective-permute-done | bytes 524320 | tf_op jit(solution)/shard_map/ppermute | solution.py:346
  157.3 2.1 %shard_map.69 = bf16[2,64,2048]{2,1,0:T(8,128)(2,1)} custom-call(s32[9]{0:T(128)S(1)} %stack.27.scal, bf16[64,2048]{1,0:T(8,128)(2,1)S(1)} %get-tuple-element.32.mine, bf16[64,2048]{1,0:T(8,128)(2,1)S(1)} %copy-done.1, bf16[64,2048]{1,0:T(8,128)(2,1)S(1)} %copy-done.3, bf16[64,2048]{1,0:T(8,128)(2,1)S(1)} %copy-done.5, ...), custom_call_target="tpu_custom_call" | custom-call | bytes 3145728 | tf_op jit(solution)/shard_map/pallas_call | solution.py:188
  (71 shorter events, 15.1 us)
Async XLA Ops:
  17.7 11.7 %collective-permute-start.2 = (bf16[4,128,512]{2,1,0:T(8,128)(2,1)S(1)}, bf16[4,128,512]{2,1,0:T(8,128)(2,1)S(1)}, u32[]{:S(2)}, u32[]{:S(2)}) collective-permute-start(bf16[4,128,512]{2,1,0:T(8,128)(2,1)S(1)} %bitcast.27), channel_id=1, source_target_pairs={{0,8},{1,9},{2,10},{3,11},{4,12},{5,13},{6,14},{7,15},{8,0},{9,1},... | collective-permute-start | bytes 1572872 | tf_op jit(solution)/shard_map/ppermute | solution.py:34
  22.5 12.5 %collective-permute-start.1 = (bf16[4,128,512]{2,1,0:T(8,128)(2,1)S(1)}, bf16[4,128,512]{2,1,0:T(8,128)(2,1)S(1)}, u32[]{:S(2)}, u32[]{:S(2)}) collective-permute-start(bf16[4,128,512]{2,1,0:T(8,128)(2,1)S(1)} %bitcast.28), channel_id=1, source_target_pairs={{0,12},{1,13},{2,14},{3,15},{4,8},{5,9},{6,10},{7,11},{8,4},{9,5},... | collective-permute-start | bytes 1572872 | tf_op jit(solution)/shard_map/ppermute | solution.py:34
  25.2 10.2 %collective-permute-start = (bf16[4,128,512]{2,1,0:T(8,128)(2,1)S(1)}, bf16[4,128,512]{2,1,0:T(8,128)(2,1)S(1)}, u32[]{:S(2)}, u32[]{:S(2)}) collective-permute-start(bf16[4,128,512]{2,1,0:T(8,128)(2,1)S(1)} %bitcast.29), channel_id=1, source_target_pairs={{0,4},{1,5},{2,6},{3,7},{4,0},{5,1},{6,2},{7,3},{8,12},{9,13},{10,... | collective-permute-start | bytes 1572872 | tf_op jit(solution)/shard_map/ppermute | solution.py:34
  35.5 17.0 %collective-permute-start.5 = (bf16[2,512,512]{2,1,0:T(8,128)(2,1)S(1)}, bf16[2,512,512]{2,1,0:T(8,128)(2,1)S(1)}, u32[]{:S(2)}, u32[]{:S(2)}) collective-permute-start(bf16[2,512,512]{2,1,0:T(8,128)(2,1)S(1)} %pad_maximum_fusion.refs_0_), channel_id=1, source_target_pairs={{0,48},{1,49},{2,50},{3,51},{4,52},{5,53},{6,54},{7,55},{8,56},{9,... | collective-permute-start | bytes 3145736 | tf_op jit(solution)/shard_map/ppermute | solution.py:34
  39.9 15.9 %collective-permute-start.3 = (bf16[2,512,512]{2,1,0:T(8,128)(2,1)S(1)}, bf16[2,512,512]{2,1,0:T(8,128)(2,1)}, u32[]{:S(2)}, u32[]{:S(2)}) collective-permute-start(bf16[2,512,512]{2,1,0:T(8,128)(2,1)S(1)} %pad_maximum_fusion.refs_0_), channel_id=1, source_target_pairs={{0,16},{1,17},{2,18},{3,19},{4,20},{5,21},{6,22},{7,23},{8,24},{9,... | collective-permute-start | bytes 3145736 | tf_op jit(solution)/shard_map/ppermute | solution.py:34
  41.9 22.0 %collective-permute-start.6 = (bf16[2,512,512]{2,1,0:T(8,128)(2,1)S(1)}, bf16[2,512,512]{2,1,0:T(8,128)(2,1)}, u32[]{:S(2)}, u32[]{:S(2)}) collective-permute-start(bf16[2,512,512]{2,1,0:T(8,128)(2,1)S(1)} %pad_maximum_fusion.1.refs_1_.refs_0_), channel_id=1, source_target_pairs={{0,48},{1,49},{2,50},{3,51},{4,52},{5,53},{6,54},{7,55},{8,56},{9,... | collective-permute-start | bytes 3145736 | tf_op jit(solution)/shard_map/ppermute | solution.py:34
  44.6 23.2 %collective-permute-start.4 = (bf16[2,512,512]{2,1,0:T(8,128)(2,1)S(1)}, bf16[2,512,512]{2,1,0:T(8,128)(2,1)}, u32[]{:S(2)}, u32[]{:S(2)}) collective-permute-start(bf16[2,512,512]{2,1,0:T(8,128)(2,1)S(1)} %pad_maximum_fusion.1.refs_1_.refs_0_), channel_id=1, source_target_pairs={{0,16},{1,17},{2,18},{3,19},{4,20},{5,21},{6,22},{7,23},{8,24},{9,... | collective-permute-start | bytes 3145736 | tf_op jit(solution)/shard_map/ppermute | solution.py:34
  53.4 27.0 %collective-permute-start.7 = (bf16[1,512,512]{2,1,0:T(8,128)(2,1)}, bf16[1,512,512]{2,1,0:T(8,128)(2,1)}, u32[]{:S(2)}, u32[]{:S(2)}) collective-permute-start(bf16[1,512,512]{2,1,0:T(8,128)(2,1)} %slice.68), channel_id=1, source_target_pairs={{0,16},{1,17},{2,18},{3,19},{4,20},{5,21},{6,22},{7,23},{8,24},{9,... | collective-permute-start | bytes 1572872 | tf_op jit(solution)/shard_map/ppermute | solution.py:34
  57.8 16.4 %copy-start.11 = (s32[2]{0:T(128)S(1)}, s32[2]{0:T(128)}, u32[]{:S(2)}) copy-start(s32[2]{0:T(128)} %param.10) | copy-start | bytes 28
  57.8 16.4 %copy-start.12 = (s32[2]{0:T(128)S(1)}, s32[2]{0:T(128)}, u32[]{:S(2)}) copy-start(s32[2]{0:T(128)} %param.11) | copy-start | bytes 28
  57.8 22.7 %collective-permute-start.8 = (bf16[1,512,512]{2,1,0:T(8,128)(2,1)}, bf16[1,512,512]{2,1,0:T(8,128)(2,1)}, u32[]{:S(2)}, u32[]{:S(2)}) collective-permute-start(bf16[1,512,512]{2,1,0:T(8,128)(2,1)} %slice.69), channel_id=1, source_target_pairs={{0,48},{1,49},{2,50},{3,51},{4,52},{5,53},{6,54},{7,55},{8,56},{9,... | collective-permute-start | bytes 1572872 | tf_op jit(solution)/shard_map/ppermute | solution.py:34
  65.8 12.7 %copy-start.6 = (f32[5,2048]{1,0:T(8,128)S(1)}, f32[5,2048]{1,0:T(8,128)}, u32[]{:S(2)}) copy-start(f32[5,2048]{1,0:T(8,128)} %gains.5) | copy-start | bytes 122884
  65.8 14.7 %collective-permute-start.9 = (bf16[1,512,512]{2,1,0:T(8,128)(2,1)}, bf16[1,512,512]{2,1,0:T(8,128)(2,1)}, u32[]{:S(2)}, u32[]{:S(2)}) collective-permute-start(bf16[1,512,512]{2,1,0:T(8,128)(2,1)} %slice.70), channel_id=1, source_target_pairs={{0,16},{1,17},{2,18},{3,19},{4,20},{5,21},{6,22},{7,23},{8,24},{9,... | collective-permute-start | bytes 1572872 | tf_op jit(solution)/shard_map/ppermute | solution.py:34
  69.7 11.7 %collective-permute-start.10 = (bf16[1,512,512]{2,1,0:T(8,128)(2,1)}, bf16[1,512,512]{2,1,0:T(8,128)(2,1)}, u32[]{:S(2)}, u32[]{:S(2)}) collective-permute-start(bf16[1,512,512]{2,1,0:T(8,128)(2,1)} %slice.71), channel_id=1, source_target_pairs={{0,48},{1,49},{2,50},{3,51},{4,52},{5,53},{6,54},{7,55},{8,56},{9,... | collective-permute-start | bytes 1572872 | tf_op jit(solution)/shard_map/ppermute | solution.py:34
  83.6 1.4 collective-permute-start.11
  85.2 4.7 %copy-start.9 = (bf16[64,2048]{1,0:T(8,128)(2,1)}, bf16[64,2048]{1,0:T(8,128)(2,1)S(1)}, u32[]{:S(2)}) copy-start(bf16[64,2048]{1,0:T(8,128)(2,1)S(1)} %add_convert_fusion.1) | copy-start | bytes 786436
  85.2 0.7 collective-permute-start.12
  85.9 5.3 %copy-start.2 = (bf16[64,2048]{1,0:T(8,128)(2,1)}, bf16[64,2048]{1,0:T(8,128)(2,1)S(1)}, u32[]{:S(2)}) copy-start(bf16[64,2048]{1,0:T(8,128)(2,1)S(1)} %collective-permute-done.12.mine.in1m) | copy-start | bytes 786436
  85.9 0.7 collective-permute-start.13
  86.6 2.6 %copy-start.4 = (bf16[64,2048]{1,0:T(8,128)(2,1)}, bf16[64,2048]{1,0:T(8,128)(2,1)S(1)}, u32[]{:S(2)}) copy-start(bf16[64,2048]{1,0:T(8,128)(2,1)S(1)} %collective-permute-done.13.other.in1o) | copy-start | bytes 786436
  89.2 2.0 %collective-permute-start.16 = (bf16[64,2048]{1,0:T(8,128)(2,1)S(1)}, bf16[64,2048]{1,0:T(8,128)(2,1)S(1)}, u32[]{:S(2)}, u32[]{:S(2)}) collective-permute-start(bf16[64,2048]{1,0:T(8,128)(2,1)S(1)} %get-tuple-element.20), channel_id=1, source_target_pairs={{128,192},{192,128},{129,193},{193,129},{130,194},{194,130},{131,1... | collective-permute-start | bytes 786440 | tf_op jit(solution)/shard_map/ppermute | solution.py:289
  89.9 41.2 %collective-permute-start.14 = (bf16[64,2048]{1,0:T(8,128)(2,1)S(1)}, bf16[64,2048]{1,0:T(8,128)(2,1)}, u32[]{:S(2)}, u32[]{:S(2)}) collective-permute-start(bf16[64,2048]{1,0:T(8,128)(2,1)S(1)} %add_convert_fusion.1), channel_id=1, source_target_pairs={{256,384},{257,385},{258,386},{259,387},{260,388},{261,389},{262,3... | collective-permute-start | bytes 786440 | tf_op jit(solution)/shard_map/ppermute | solution.py:313
  92.3 50.9 %collective-permute-start.18 = (bf16[64,2048]{1,0:T(8,128)(2,1)S(1)}, bf16[64,2048]{1,0:T(8,128)(2,1)}, u32[]{:S(2)}, u32[]{:S(2)}) collective-permute-start(bf16[64,2048]{1,0:T(8,128)(2,1)S(1)} %fusion.2), channel_id=1, source_target_pairs={{128,384},{129,385},{130,386},{131,387},{132,388},{133,389},{134,3... | collective-permute-start | bytes 786440 | tf_op jit(solution)/shard_map/ppermute | solution.py:325
  131.1 14.7 %collective-permute-start.15 = (bf16[64,2048]{1,0:T(8,128)(2,1)}, bf16[64,2048]{1,0:T(8,128)(2,1)}, u32[]{:S(2)}, u32[]{:S(2)}) collective-permute-start(bf16[64,2048]{1,0:T(8,128)(2,1)} %collective-permute-done.14.mine.in3m), channel_id=1, source_target_pairs={{384,448},{448,384},{385,449},{449,385},{386,450},{450,386},{387,4... | collective-permute-start | bytes 786440 | tf_op jit(solution)/shard_map/ppermute | solution.py:289
  143.2 4.9 %collective-permute-start.19 = (bf16[64,2048]{1,0:T(8,128)(2,1)}, bf16[64,2048]{1,0:T(8,128)(2,1)}, u32[]{:S(2)}, u32[]{:S(2)}) collective-permute-start(bf16[64,2048]{1,0:T(8,128)(2,1)} %collective-permute-done.18.mem_mine), channel_id=1, source_target_pairs={{384,448},{448,384},{385,449},{449,385},{386,450},{450,386},{387,4... | collective-permute-start | bytes 786440 | tf_op jit(solution)/shard_map/ppermute | solution.py:289
  148.0 6.7 %copy-start.8 = (bf16[64,2048]{1,0:T(8,128)(2,1)S(1)}, bf16[64,2048]{1,0:T(8,128)(2,1)}, u32[]{:S(2)}) copy-start(bf16[64,2048]{1,0:T(8,128)(2,1)} %copy-done.7) | copy-start | bytes 786436
  148.0 6.7 %copy-start.10 = (bf16[64,2048]{1,0:T(8,128)(2,1)S(1)}, bf16[64,2048]{1,0:T(8,128)(2,1)}, u32[]{:S(2)}) copy-start(bf16[64,2048]{1,0:T(8,128)(2,1)} %copy-done.9) | copy-start | bytes 786436
  148.1 9.2 %copy-start.1 = (bf16[64,2048]{1,0:T(8,128)(2,1)S(1)}, bf16[64,2048]{1,0:T(8,128)(2,1)}, u32[]{:S(2)}) copy-start(bf16[64,2048]{1,0:T(8,128)(2,1)} %copy-done) | copy-start | bytes 786436
  148.1 9.2 %copy-start.3 = (bf16[64,2048]{1,0:T(8,128)(2,1)S(1)}, bf16[64,2048]{1,0:T(8,128)(2,1)}, u32[]{:S(2)}) copy-start(bf16[64,2048]{1,0:T(8,128)(2,1)} %copy-done.2) | copy-start | bytes 786436
  148.1 9.2 %copy-start.5 = (bf16[64,2048]{1,0:T(8,128)(2,1)S(1)}, bf16[64,2048]{1,0:T(8,128)(2,1)}, u32[]{:S(2)}) copy-start(bf16[64,2048]{1,0:T(8,128)(2,1)} %copy-done.4) | copy-start | bytes 786436
  153.5 3.8 %collective-permute-start.20 = (bf16[128,2048]{1,0:T(8,128)(2,1)S(1)}, bf16[128,2048]{1,0:T(8,128)(2,1)S(1)}, u32[]{:S(2)}, u32[]{:S(2)}) collective-permute-start(bf16[128,2048]{1,0:T(8,128)(2,1)S(1)} %shard_map.68.own), channel_id=1, source_target_pairs={{384,448},{385,449},{386,450},{387,451},{388,452},{389,453},{390,4... | collective-permute-start | bytes 1572872 | tf_op jit(solution)/shard_map/ppermute | solution.py:346
  154.8 0.7 collective-permute-start.17
  (2 other events, 2.7 us)

commit v16 on v15

--- a/solution.py
+++ b/solution.py
@@ -14,6 +14,7 @@
 FAR = 2
 FIRST_HELD = (1, 3, 5, 6, 7, 8, 9)
 QUERY_HELD = (0, 2, 4, 6)
+THIRD_HELD = (0, 1, 2, 3, 4, 5, 7, 8, 9)
 AXES = ("zh", "core", "y", "x", "zl")
 DP = ("y", "x", "zl")
 SECTION = ("zh", "core")
@@ -168,7 +169,8 @@
 
 
 def third_kernel(scal, q, mem_mine, mem_other, *refs):
-    pieces, (out, m3, t3) = refs[:10], refs[10:]
+    count = len(THIRD_HELD)
+    pieces, (out, m3, t3) = spread(refs, THIRD_HELD), refs[count:]
 
     @pl.when(scal[2] == 3)
     def _():
@@ -181,29 +183,34 @@
 
 VMEM = pl.BlockSpec(memory_space=pltpu.VMEM)
 SMEM = pl.BlockSpec(memory_space=pltpu.SMEM)
-
-
-def call(kernel, scal, operands, outs, scratch=(), flops=0):
+ANY = pl.BlockSpec(memory_space=pl.ANY)
+
+
+def call(kernel, scal, operands, outs, scratch=(), flops=0, passed=(), sems=0):
     size = sum(a.size * a.dtype.itemsize for a in operands)
     return pl.pallas_call(
         kernel,
         out_shape=outs,
-        in_specs=[SMEM] + [VMEM] * len(operands),
+        in_specs=[SMEM] + [VMEM] * len(operands) + [ANY] * len(passed),
         out_specs=jax.tree.map(lambda _: VMEM, outs),
-        scratch_shapes=[pltpu.VMEM(shape, kind) for shape, kind in scratch],
+        scratch_shapes=[pltpu.VMEM(shape, kind) for shape, kind in scratch]
+        + [pltpu.SemaphoreType.DMA((sems,))] * (sems > 0),
         compiler_params=pltpu.CompilerParams(vmem_limit_bytes=12 * 1024 * 1024),
         cost_estimate=pl.CostEstimate(flops=flops, bytes_accessed=size, transcendentals=0),
-    )(scal, *operands)
-
-
-def finish_kernel(scal, mine, other, in1m, in1o, in3m, in3o, early_m, early_o, own, got, out):
+    )(scal, *operands, *passed)
+
+
+def finish_kernel(scal, in3m, in3o, own, got, mine, other, in1m, in1o, early_m, early_o, out, sems):
     rows = mine.shape[0]
     cube, core = scal[2], scal[6]
     even = (cube == 0) | (cube == 2)
 
     def put(doc0, doc1):
-        out[0] = doc0[...]
-        out[1] = doc1[...]
+        copies = [pltpu.make_async_copy(d, out.at[i], sems.at[i]) for i, d in enumerate((doc0, doc1))]
+        for copy in copies:
+            copy.start()
+        for copy in copies:
+            copy.wait()
 
     @pl.when((core == 0) & even)
     def _():
@@ -215,7 +222,8 @@
 
     @pl.when((core == 0) & (cube == 3))
     def _():
-        put(in3m, in3o)
+        out[0] = in3m[...]
+        out[1] = in3o[...]
 
     @pl.when((core == 1) & (cube != 3))
     def _():
@@ -338,14 +346,16 @@
     own = call(
         third_kernel,
         scal,
-        [query, mem, mem_other, *pieces],
+        [query, mem, mem_other, *(pieces[i] for i in THIRD_HELD)],
         wide,
         [(blocks, BF16), (blocks, F32)],
         3 * work,
     )
     got = lax.ppermute(own, SECTION, [(6, 7)])
-    parts = [mine, other, in1, in1_other, in3, in3_other, early, early_other, own, got]
-    out = call(finish_kernel, scal, parts, jax.ShapeDtypeStruct((2, rows, width), BF16))
+    parts = [in3, in3_other, own, got]
+    passed = [mine, other, in1, in1_other, early, early_other]
+    whole = jax.ShapeDtypeStruct((2, rows, width), BF16)
+    out = call(finish_kernel, scal, parts, whole, passed=passed, sems=2)
     return out[None]
 
 

time: 160 us -> 165 us (1.031)
  waiting for transfers between devices: 63.7 us -> 66.5 us
    ppermute x11, waiting for transfers between devices: 15.1 us -> 19.7 us  [exchange(): return lax.ppermute(array, AXES, pairs)]
  transfers between devices with their start and end apart: 21 -> 21, of which waited for: 10 -> 8; matrix products, arithmetic and copies ran while one was open for 9% -> 9% of each run, Pallas kernels for 3% -> 2%
where the time goes in v16:
time: 165 us; the launch traced here: 164 us
  waiting for transfers between devices  66.5 us (40%)
  starting transfers between devices  46.6 us (28%)
  blocking collectives  16.6 us (10%)
  Pallas kernels  16.1 us (10%)
  local copies, waits for them, and re-layouts  12.9 us (8%)
  other arithmetic  4.58 us (3%)
    ppermute x1, waiting for transfers between devices, on_device(): in3 = lax.ppermute(first, 'zh', [(2, 3)])  37 us
    ppermute x11, starting transfers between devices, exchange(): return lax.ppermute(array, AXES, pairs)  33.1 us
    ppermute x11, waiting for transfers between devices, exchange(): return lax.ppermute(array, AXES, pairs)  19.7 us
    all_to_all x1, blocking collectives, gather(): got = lax.all_to_all(sent, ('core', 'zl'), 0, 0, tiled=True)  16.6 us
    pallas_call x6, Pallas kernels, call(): pl.pallas_call(kernel, out_shape=outs, in_specs=[SMEM] + [VMEM] * len(ope...  16.1 us
    ppermute x5, starting transfers between devices, swapped(): return lax.ppermute(array, SECTION, pairs)  8.28 us
    ppermute x1, waiting for transfers between devices, on_device(): mem = lax.ppermute(memory, 'zh', [(1, 3)])  7.98 us
    slice x4, local copies, waits for them, and re-layouts, gather(): far += [exchange(b[:1], True, 1), exchange(a[1:], True, 3)]  6.44 us
  transfers between devices with their start and end apart: 21, of which 8 were waited for; matrix products, arithmetic and copies ran while one was open for 9% of the time, Pallas kernels for 2%

profile of v16, /device:TPU:481, one launch (start us, length us, event | category | flops | bytes accessed | tf_op | source)
XLA Modules:
  0.0 163.8 jit_solution(4986649761579411423)
XLA Ops:
  1.1 16.6 %all_to_all.5 = bf16[8,2,32,512]{3,2,1,0:T(8,128)(2,1)S(1)} all-to-all(bf16[8,2,32,512]{3,2,1,0:T(8,128)(2,1)S(1)} %bitcast.24), channel_id=1, replica_groups=mesh['zh'=4,'core'=2,'y'=4,'x'=4,'zl'=4] {'core','zl'}, dimensions={0} | all-to-all | bytes 1048576 | tf_op jit(solution)/shard_map/all_to_all | solution.py:251
  17.7 3.2 %collective-permute-start = (bf16[4,128,512]{2,1,0:T(8,128)(2,1)S(1)}, bf16[4,128,512]{2,1,0:T(8,128)(2,1)S(1)}, u32[]{:S(2)}, u32[]{:S(2)}) collective-permute-start(bf16[4,128,512]{2,1,0:T(8,128)(2,1)S(1)} %bitcast.27), channel_id=1, source_target_pairs={{0,4},{1,5},{2,6},{3,7},{4,0},{5,1},{6,2},{7,3},{8,12},{9,13},{10,... | collective-permute-start | bytes 1572872 | tf_op jit(solution)/shard_map/ppermute | solution.py:35
  20.9 3.8 %collective-permute-start.1 = (bf16[4,128,512]{2,1,0:T(8,128)(2,1)S(1)}, bf16[4,128,512]{2,1,0:T(8,128)(2,1)S(1)}, u32[]{:S(2)}, u32[]{:S(2)}) collective-permute-start(bf16[4,128,512]{2,1,0:T(8,128)(2,1)S(1)} %bitcast.28), channel_id=1, source_target_pairs={{0,12},{1,13},{2,14},{3,15},{4,8},{5,9},{6,10},{7,11},{8,4},{9,5},... | collective-permute-start | bytes 1572872 | tf_op jit(solution)/shard_map/ppermute | solution.py:35
  24.7 2.6 %collective-permute-start.2 = (bf16[4,128,512]{2,1,0:T(8,128)(2,1)S(1)}, bf16[4,128,512]{2,1,0:T(8,128)(2,1)S(1)}, u32[]{:S(2)}, u32[]{:S(2)}) collective-permute-start(bf16[4,128,512]{2,1,0:T(8,128)(2,1)S(1)} %bitcast.29), channel_id=1, source_target_pairs={{0,8},{1,9},{2,10},{3,11},{4,12},{5,13},{6,14},{7,15},{8,0},{9,1},... | collective-permute-start | bytes 1572872 | tf_op jit(solution)/shard_map/ppermute | solution.py:35
  27.9 10.0 %collective-permute-done.1 = bf16[4,128,512]{2,1,0:T(8,128)(2,1)S(1)} collective-permute-done((bf16[4,128,512]{2,1,0:T(8,128)(2,1)S(1)}, bf16[4,128,512]{2,1,0:T(8,128)(2,1)S(1)}, u32[]{:S(2)}, u32[]{:S(2)}) %collective-permute-start.1) | collective-permute-done | bytes 524320 | tf_op jit(solution)/shard_map/ppermute | solution.py:35
  38.1 2.8 %collective-permute-start.4 = (bf16[2,512,512]{2,1,0:T(8,128)(2,1)S(1)}, bf16[2,512,512]{2,1,0:T(8,128)(2,1)}, u32[]{:S(2)}, u32[]{:S(2)}) collective-permute-start(bf16[2,512,512]{2,1,0:T(8,128)(2,1)S(1)} %pad_maximum_fusion.1.refs_1_.refs_0_), channel_id=1, source_target_pairs={{0,16},{1,17},{2,18},{3,19},{4,20},{5,21},{6,22},{7,23},{8,24},{9,... | collective-permute-start | bytes 3145736 | tf_op jit(solution)/shard_map/ppermute | solution.py:35
  40.9 3.7 %collective-permute-start.6 = (bf16[2,512,512]{2,1,0:T(8,128)(2,1)S(1)}, bf16[2,512,512]{2,1,0:T(8,128)(2,1)}, u32[]{:S(2)}, u32[]{:S(2)}) collective-permute-start(bf16[2,512,512]{2,1,0:T(8,128)(2,1)S(1)} %pad_maximum_fusion.1.refs_1_.refs_0_), channel_id=1, source_target_pairs={{0,48},{1,49},{2,50},{3,51},{4,52},{5,53},{6,54},{7,55},{8,56},{9,... | collective-permute-start | bytes 3145736 | tf_op jit(solution)/shard_map/ppermute | solution.py:35
  44.8 2.8 %collective-permute-start.5 = (bf16[2,512,512]{2,1,0:T(8,128)(2,1)S(1)}, bf16[2,512,512]{2,1,0:T(8,128)(2,1)S(1)}, u32[]{:S(2)}, u32[]{:S(2)}) collective-permute-start(bf16[2,512,512]{2,1,0:T(8,128)(2,1)S(1)} %pad_maximum_fusion.refs_0_), channel_id=1, source_target_pairs={{0,48},{1,49},{2,50},{3,51},{4,52},{5,53},{6,54},{7,55},{8,56},{9,... | collective-permute-start | bytes 3145736 | tf_op jit(solution)/shard_map/ppermute | solution.py:35
  47.5 1.9 %collective-permute-start.3 = (bf16[2,512,512]{2,1,0:T(8,128)(2,1)S(1)}, bf16[2,512,512]{2,1,0:T(8,128)(2,1)}, u32[]{:S(2)}, u32[]{:S(2)}) collective-permute-start(bf16[2,512,512]{2,1,0:T(8,128)(2,1)S(1)} %pad_maximum_fusion.refs_0_), channel_id=1, source_target_pairs={{0,16},{1,17},{2,18},{3,19},{4,20},{5,21},{6,22},{7,23},{8,24},{9,... | collective-permute-start | bytes 3145736 | tf_op jit(solution)/shard_map/ppermute | solution.py:35
  49.5 1.9 %broadcast_select_fusion = bf16[2,64,2048]{2,1,0:T(8,128)(2,1)} fusion(bf16[2,64,2048]{2,1,0:T(8,128)(2,1)} %param.6, bf16[2,64,2048]{2,1,0:T(8,128)(2,1)} %param.7, pred[]{:T(512)S(6)} %lt.26), kind=kLoop, calls=%fused_computation.9 | loop fusion | flops 262144 | bytes 1572865 | tf_op jit(solution)/shard_map/jit(_where)/select_n | solution.py:289
  51.4 2.7 %collective-permute-done.4.refs_3_.refs_1_ = bf16[2,512,512]{2,1,0:T(8,128)(2,1)} collective-permute-done((bf16[2,512,512]{2,1,0:T(8,128)(2,1)S(1)}, bf16[2,512,512]{2,1,0:T(8,128)(2,1)}, u32[]{:S(2)}, u32[]{:S(2)}) %collective-permute-start.4) | collective-permute-done | bytes 1048608 | tf_op jit(solution)/shard_map/ppermute | solution.py:35
  54.1 1.9 %slice.71 = bf16[1,512,512]{2,1,0:T(8,128)(2,1)} slice(bf16[2,512,512]{2,1,0:T(8,128)(2,1)} %collective-permute-done.4.refs_3_.refs_1_), slice={[1:2], [0:512], [0:512]} | slice | bytes 1048576 | tf_op jit(solution)/shard_map/slice | solution.py:260
  55.9 4.4 %collective-permute-start.10 = (bf16[1,512,512]{2,1,0:T(8,128)(2,1)}, bf16[1,512,512]{2,1,0:T(8,128)(2,1)}, u32[]{:S(2)}, u32[]{:S(2)}) collective-permute-start(bf16[1,512,512]{2,1,0:T(8,128)(2,1)} %slice.71), channel_id=1, source_target_pairs={{0,48},{1,49},{2,50},{3,51},{4,52},{5,53},{6,54},{7,55},{8,56},{9,... | collective-permute-start | bytes 1572872 | tf_op jit(solution)/shard_map/ppermute | solution.py:35
  60.3 1.9 %slice.70 = bf16[1,512,512]{2,1,0:T(8,128)(2,1)} slice(bf16[2,512,512]{2,1,0:T(8,128)(2,1)} %collective-permute-done.6.refs_5_.refs_2_), slice={[0:1], [0:512], [0:512]} | slice | bytes 1048576 | tf_op jit(solution)/shard_map/slice | solution.py:260
  62.2 2.0 %collective-permute-start.9 = (bf16[1,512,512]{2,1,0:T(8,128)(2,1)}, bf16[1,512,512]{2,1,0:T(8,128)(2,1)}, u32[]{:S(2)}, u32[]{:S(2)}) collective-permute-start(bf16[1,512,512]{2,1,0:T(8,128)(2,1)} %slice.70), channel_id=1, source_target_pairs={{0,16},{1,17},{2,18},{3,19},{4,20},{5,21},{6,22},{7,23},{8,24},{9,... | collective-permute-start | bytes 1572872 | tf_op jit(solution)/shard_map/ppermute | solution.py:35
  64.2 5.0 %collective-permute-done.5.refs_4_.refs_2_ = bf16[2,512,512]{2,1,0:T(8,128)(2,1)S(1)} collective-permute-done((bf16[2,512,512]{2,1,0:T(8,128)(2,1)S(1)}, bf16[2,512,512]{2,1,0:T(8,128)(2,1)S(1)}, u32[]{:S(2)}, u32[]{:S(2)}) %collective-permute-start.5) | collective-permute-done | bytes 1048608 | tf_op jit(solution)/shard_map/ppermute | solution.py:35
  70.1 2.0 %collective-permute-start.7 = (bf16[1,512,512]{2,1,0:T(8,128)(2,1)}, bf16[1,512,512]{2,1,0:T(8,128)(2,1)}, u32[]{:S(2)}, u32[]{:S(2)}) collective-permute-start(bf16[1,512,512]{2,1,0:T(8,128)(2,1)} %slice.68), channel_id=1, source_target_pairs={{0,16},{1,17},{2,18},{3,19},{4,20},{5,21},{6,22},{7,23},{8,24},{9,... | collective-permute-start | bytes 1572872 | tf_op jit(solution)/shard_map/ppermute | solution.py:35
  72.1 1.9 %slice.69 = bf16[1,512,512]{2,1,0:T(8,128)(2,1)} slice(bf16[2,512,512]{2,1,0:T(8,128)(2,1)} %collective-permute-done.3.refs_2_.refs_1_), slice={[1:2], [0:512], [0:512]} | slice | bytes 1048576 | tf_op jit(solution)/shard_map/slice | solution.py:260
  74.0 3.7 %collective-permute-start.8 = (bf16[1,512,512]{2,1,0:T(8,128)(2,1)}, bf16[1,512,512]{2,1,0:T(8,128)(2,1)}, u32[]{:S(2)}, u32[]{:S(2)}) collective-permute-start(bf16[1,512,512]{2,1,0:T(8,128)(2,1)} %slice.69), channel_id=1, source_target_pairs={{0,48},{1,49},{2,50},{3,51},{4,52},{5,53},{6,54},{7,55},{8,56},{9,... | collective-permute-start | bytes 1572872 | tf_op jit(solution)/shard_map/ppermute | solution.py:35
  78.4 2.6 %stack.27.scal = s32[9]{0:T(128)S(1)} concatenate(s32[1]{0:T(128)} %bitcast, s32[1]{0:T(128)} %bitcast.1, s32[1]{0:T(128)} %bitcast.2, s32[1]{0:T(128)} %bitcast.3, s32[1]{0:T(128)} %get-tuple-element.39, s32[1]{0:T(128)} %get-tuple-element.40, s32[1]{0:T(128)} %bitcast.4, s32[1]{0:T(128)} %get-tuple-element.36, s32[1]{0:T(128)} %get-tuple-element.35), dimensions={0} | concatenate | bytes 72 | tf_op jit(solution)/shard_map/stack | solution.py:272
  82.1 2.0 %shard_map.64 = (bf16[16,128,128]{2,1,0:T(8,128)(2,1)S(1)}, f32[128,512]{1,0:T(8,128)S(1)}, f32[128,512]{1,0:T(8,128)S(1)}, f32[128,512]{1,0:T(8,128)S(1)}) custom-call(s32[9]{0:T(128)S(1)} %stack.27.scal, f32[5,2048]{1,0:T(8,128)S(1)} %copy-done.6, bf16[64,2048]{1,0:T(8,128)(2,1)S(1)} %get-tuple-element.32.mine, ...), custom_call_target="tpu_custom_call" | custom-call | flops 805306368 | bytes 6856704 | tf_op jit(solution)/shard_map/pallas_call | solution.py:191
  84.1 1.6 collective-permute-done.8.refs_4_.refs_7_.refs_6_
  85.7 2.2 %shard_map.65 = (f32[64,2048]{1,0:T(8,128)S(1)}, bf16[64,2048]{1,0:T(8,128)(2,1)S(1)}) custom-call(s32[9]{0:T(128)S(1)} %stack.27.scal, bf16[16,128,128]{2,1,0:T(8,128)(2,1)S(1)} %get-tuple-element.13.h3, f32[128,512]{1,0:T(8,128)S(1)} %get-tuple-element.14.q, f32[128,512]{1,0:T(8,128)S(1)} %get-tuple-element.15.k, f32[128,512]{1,0:T(8,128)S(1)} %get-tuple-element.16.v, ...), custom_call_target="tpu_custom_call" | custom-call | flops 536870912 | bytes 6553600 | tf_op jit(solution)/shard_map/pallas_call | solution.py:191
  90.8 3.3 %shard_map.67 = (f32[64,2048]{1,0:T(8,128)S(1)}, bf16[64,2048]{1,0:T(8,128)(2,1)}) custom-call(s32[9]{0:T(128)S(1)} %stack.27.scal, f32[5,2048]{1,0:T(8,128)S(1)} %copy-done.6, bf16[64,2048]{1,0:T(8,128)(2,1)S(1)} %collective-permute-done.14.mine.in1m, bf16[64,2048]{1,0:T(8,128)(2,1)S(1)} %collective-permute-done.15.other.in1o, ...), custom_call_target="tpu_custom_call" | custom-call | flops 1073741824 | bytes 8953856 | tf_op jit(solution)/shard_map/pallas_call | solution.py:191
  100.7 37.0 %collective-permute-done.12.mine.in3m = bf16[64,2048]{1,0:T(8,128)(2,1)S(1)} collective-permute-done((bf16[64,2048]{1,0:T(8,128)(2,1)}, bf16[64,2048]{1,0:T(8,128)(2,1)S(1)}, u32[]{:S(2)}, u32[]{:S(2)}) %collective-permute-start.12) | collective-permute-done | bytes 262176 | tf_op jit(solution)/shard_map/ppermute | solution.py:321
  137.7 2.8 %collective-permute-start.13 = (bf16[64,2048]{1,0:T(8,128)(2,1)S(1)}, bf16[64,2048]{1,0:T(8,128)(2,1)S(1)}, u32[]{:S(2)}, u32[]{:S(2)}) collective-permute-start(bf16[64,2048]{1,0:T(8,128)(2,1)S(1)} %collective-permute-done.12.mine.in3m), channel_id=1, source_target_pairs={{384,448},{448,384},{385,449},{449,385},{386,450},{450,386},{387,4... | collective-permute-start | bytes 786440 | tf_op jit(solution)/shard_map/ppermute | solution.py:297
  140.5 8.0 %collective-permute-done.17.mem_mine = bf16[64,2048]{1,0:T(8,128)(2,1)S(1)} collective-permute-done((bf16[64,2048]{1,0:T(8,128)(2,1)S(1)}, bf16[64,2048]{1,0:T(8,128)(2,1)S(1)}, u32[]{:S(2)}, u32[]{:S(2)}) %collective-permute-start.17) | collective-permute-done | bytes 262176 | tf_op jit(solution)/shard_map/ppermute | solution.py:333
  148.4 2.8 %collective-permute-start.18 = (bf16[64,2048]{1,0:T(8,128)(2,1)S(1)}, bf16[64,2048]{1,0:T(8,128)(2,1)S(1)}, u32[]{:S(2)}, u32[]{:S(2)}) collective-permute-start(bf16[64,2048]{1,0:T(8,128)(2,1)S(1)} %collective-permute-done.17.mem_mine), channel_id=1, source_target_pairs={{384,448},{448,384},{385,449},{449,385},{386,450},{450,386},{387,4... | collective-permute-start | bytes 786440 | tf_op jit(solution)/shard_map/ppermute | solution.py:297
  151.2 2.0 %shard_map.66.q = bf16[128,512]{1,0:T(8,128)(2,1)S(1)} custom-call(s32[9]{0:T(128)S(1)} %stack.27.scal, f32[5,2048]{1,0:T(8,128)S(1)} %copy-done.6, bf16[64,2048]{1,0:T(8,128)(2,1)S(1)} %collective-permute-done.12.mine.in3m, bf16[64,2048]{1,0:T(8,128)(2,1)S(1)} %collective-permute-done.13.other.in3o, bf16[2,512,512]{2,1,0:T(8,128)(2,1)S(1)} %pad_maximum_fusion.refs_0_, ...), custom_call_target="tpu_custom_call" | custom-call | flops 268435456 | bytes 4235264 | tf_op jit(solution)/shard_map/pallas_call | solution.py:191
  153.3 5.0 %shard_map.68.own = bf16[128,2048]{1,0:T(8,128)(2,1)S(1)} custom-call(s32[9]{0:T(128)S(1)} %stack.27.scal, bf16[128,512]{1,0:T(8,128)(2,1)S(1)} %shard_map.66.q, bf16[64,2048]{1,0:T(8,128)(2,1)S(1)} %collective-permute-done.17.mem_mine, bf16[64,2048]{1,0:T(8,128)(2,1)S(1)} %collective-permute-done.18.mem_other, ...), custom_call_target="tpu_custom_call" | custom-call | flops 805306368 | bytes 8519680 | tf_op jit(solution)/shard_map/pallas_call | solution.py:191
  160.3 1.8 %collective-permute-done.19.got = bf16[128,2048]{1,0:T(8,128)(2,1)S(1)} collective-permute-done((bf16[128,2048]{1,0:T(8,128)(2,1)S(1)}, bf16[128,2048]{1,0:T(8,128)(2,1)S(1)}, u32[]{:S(2)}, u32[]{:S(2)}) %collective-permute-start.19) | collective-permute-done | bytes 524320 | tf_op jit(solution)/shard_map/ppermute | solution.py:354
  162.2 1.6 shard_map.69
  (67 shorter events, 15.8 us)
Async XLA Ops:
  17.7 10.2 %collective-permute-start = (bf16[4,128,512]{2,1,0:T(8,128)(2,1)S(1)}, bf16[4,128,512]{2,1,0:T(8,128)(2,1)S(1)}, u32[]{:S(2)}, u32[]{:S(2)}) collective-permute-start(bf16[4,128,512]{2,1,0:T(8,128)(2,1)S(1)} %bitcast.27), channel_id=1, source_target_pairs={{0,4},{1,5},{2,6},{3,7},{4,0},{5,1},{6,2},{7,3},{8,12},{9,13},{10,... | collective-permute-start | bytes 1572872 | tf_op jit(solution)/shard_map/ppermute | solution.py:35
  20.9 17.0 %collective-permute-start.1 = (bf16[4,128,512]{2,1,0:T(8,128)(2,1)S(1)}, bf16[4,128,512]{2,1,0:T(8,128)(2,1)S(1)}, u32[]{:S(2)}, u32[]{:S(2)}) collective-permute-start(bf16[4,128,512]{2,1,0:T(8,128)(2,1)S(1)} %bitcast.28), channel_id=1, source_target_pairs={{0,12},{1,13},{2,14},{3,15},{4,8},{5,9},{6,10},{7,11},{8,4},{9,5},... | collective-permute-start | bytes 1572872 | tf_op jit(solution)/shard_map/ppermute | solution.py:35
  24.7 13.3 %collective-permute-start.2 = (bf16[4,128,512]{2,1,0:T(8,128)(2,1)S(1)}, bf16[4,128,512]{2,1,0:T(8,128)(2,1)S(1)}, u32[]{:S(2)}, u32[]{:S(2)}) collective-permute-start(bf16[4,128,512]{2,1,0:T(8,128)(2,1)S(1)} %bitcast.29), channel_id=1, source_target_pairs={{0,8},{1,9},{2,10},{3,11},{4,12},{5,13},{6,14},{7,15},{8,0},{9,1},... | collective-permute-start | bytes 1572872 | tf_op jit(solution)/shard_map/ppermute | solution.py:35
  38.1 15.9 %collective-permute-start.4 = (bf16[2,512,512]{2,1,0:T(8,128)(2,1)S(1)}, bf16[2,512,512]{2,1,0:T(8,128)(2,1)}, u32[]{:S(2)}, u32[]{:S(2)}) collective-permute-start(bf16[2,512,512]{2,1,0:T(8,128)(2,1)S(1)} %pad_maximum_fusion.1.refs_1_.refs_0_), channel_id=1, source_target_pairs={{0,16},{1,17},{2,18},{3,19},{4,20},{5,21},{6,22},{7,23},{8,24},{9,... | collective-permute-start | bytes 3145736 | tf_op jit(solution)/shard_map/ppermute | solution.py:35
  40.9 19.4 %collective-permute-start.6 = (bf16[2,512,512]{2,1,0:T(8,128)(2,1)S(1)}, bf16[2,512,512]{2,1,0:T(8,128)(2,1)}, u32[]{:S(2)}, u32[]{:S(2)}) collective-permute-start(bf16[2,512,512]{2,1,0:T(8,128)(2,1)S(1)} %pad_maximum_fusion.1.refs_1_.refs_0_), channel_id=1, source_target_pairs={{0,48},{1,49},{2,50},{3,51},{4,52},{5,53},{6,54},{7,55},{8,56},{9,... | collective-permute-start | bytes 3145736 | tf_op jit(solution)/shard_map/ppermute | solution.py:35
  44.8 24.5 %collective-permute-start.5 = (bf16[2,512,512]{2,1,0:T(8,128)(2,1)S(1)}, bf16[2,512,512]{2,1,0:T(8,128)(2,1)S(1)}, u32[]{:S(2)}, u32[]{:S(2)}) collective-permute-start(bf16[2,512,512]{2,1,0:T(8,128)(2,1)S(1)} %pad_maximum_fusion.refs_0_), channel_id=1, source_target_pairs={{0,48},{1,49},{2,50},{3,51},{4,52},{5,53},{6,54},{7,55},{8,56},{9,... | collective-permute-start | bytes 3145736 | tf_op jit(solution)/shard_map/ppermute | solution.py:35
  47.5 24.6 %collective-permute-start.3 = (bf16[2,512,512]{2,1,0:T(8,128)(2,1)S(1)}, bf16[2,512,512]{2,1,0:T(8,128)(2,1)}, u32[]{:S(2)}, u32[]{:S(2)}) collective-permute-start(bf16[2,512,512]{2,1,0:T(8,128)(2,1)S(1)} %pad_maximum_fusion.refs_0_), channel_id=1, source_target_pairs={{0,16},{1,17},{2,18},{3,19},{4,20},{5,21},{6,22},{7,23},{8,24},{9,... | collective-permute-start | bytes 3145736 | tf_op jit(solution)/shard_map/ppermute | solution.py:35
  55.9 28.2 %collective-permute-start.10 = (bf16[1,512,512]{2,1,0:T(8,128)(2,1)}, bf16[1,512,512]{2,1,0:T(8,128)(2,1)}, u32[]{:S(2)}, u32[]{:S(2)}) collective-permute-start(bf16[1,512,512]{2,1,0:T(8,128)(2,1)} %slice.71), channel_id=1, source_target_pairs={{0,48},{1,49},{2,50},{3,51},{4,52},{5,53},{6,54},{7,55},{8,56},{9,... | collective-permute-start | bytes 1572872 | tf_op jit(solution)/shard_map/ppermute | solution.py:35
  62.2 15.5 %copy-start.9 = (s32[2]{0:T(128)S(1)}, s32[2]{0:T(128)}, u32[]{:S(2)}) copy-start(s32[2]{0:T(128)} %param.10) | copy-start | bytes 28
  62.2 15.5 %copy-start.10 = (s32[2]{0:T(128)S(1)}, s32[2]{0:T(128)}, u32[]{:S(2)}) copy-start(s32[2]{0:T(128)} %param.11) | copy-start | bytes 28
  62.2 21.9 %collective-permute-start.9 = (bf16[1,512,512]{2,1,0:T(8,128)(2,1)}, bf16[1,512,512]{2,1,0:T(8,128)(2,1)}, u32[]{:S(2)}, u32[]{:S(2)}) collective-permute-start(bf16[1,512,512]{2,1,0:T(8,128)(2,1)} %slice.70), channel_id=1, source_target_pairs={{0,16},{1,17},{2,18},{3,19},{4,20},{5,21},{6,22},{7,23},{8,24},{9,... | collective-permute-start | bytes 1572872 | tf_op jit(solution)/shard_map/ppermute | solution.py:35
  70.1 12.1 %copy-start.6 = (f32[5,2048]{1,0:T(8,128)S(1)}, f32[5,2048]{1,0:T(8,128)}, u32[]{:S(2)}) copy-start(f32[5,2048]{1,0:T(8,128)} %gains.5) | copy-start | bytes 122884
  70.1 14.1 %collective-permute-start.7 = (bf16[1,512,512]{2,1,0:T(8,128)(2,1)}, bf16[1,512,512]{2,1,0:T(8,128)(2,1)}, u32[]{:S(2)}, u32[]{:S(2)}) collective-permute-start(bf16[1,512,512]{2,1,0:T(8,128)(2,1)} %slice.68), channel_id=1, source_target_pairs={{0,16},{1,17},{2,18},{3,19},{4,20},{5,21},{6,22},{7,23},{8,24},{9,... | collective-permute-start | bytes 1572872 | tf_op jit(solution)/shard_map/ppermute | solution.py:35
  74.0 11.7 %collective-permute-start.8 = (bf16[1,512,512]{2,1,0:T(8,128)(2,1)}, bf16[1,512,512]{2,1,0:T(8,128)(2,1)}, u32[]{:S(2)}, u32[]{:S(2)}) collective-permute-start(bf16[1,512,512]{2,1,0:T(8,128)(2,1)} %slice.69), channel_id=1, source_target_pairs={{0,48},{1,49},{2,50},{3,51},{4,52},{5,53},{6,54},{7,55},{8,56},{9,... | collective-permute-start | bytes 1572872 | tf_op jit(solution)/shard_map/ppermute | solution.py:35
  82.1 2.0 %copy-start = (bf16[64,2048]{1,0:T(8,128)(2,1)}, bf16[64,2048]{1,0:T(8,128)(2,1)S(1)}, u32[]{:S(2)}) copy-start(bf16[64,2048]{1,0:T(8,128)(2,1)S(1)} %get-tuple-element.31.other) | copy-start | bytes 786436
  87.9 1.3 collective-permute-start.11
  89.4 1.4 copy-start.8
  89.4 0.7 collective-permute-start.14
  90.1 4.0 %copy-start.2 = (bf16[64,2048]{1,0:T(8,128)(2,1)}, bf16[64,2048]{1,0:T(8,128)(2,1)S(1)}, u32[]{:S(2)}) copy-start(bf16[64,2048]{1,0:T(8,128)(2,1)S(1)} %collective-permute-done.14.mine.in1m) | copy-start | bytes 786436
  90.1 0.7 collective-permute-start.15
  90.8 3.3 %copy-start.4 = (bf16[64,2048]{1,0:T(8,128)(2,1)}, bf16[64,2048]{1,0:T(8,128)(2,1)S(1)}, u32[]{:S(2)}) copy-start(bf16[64,2048]{1,0:T(8,128)(2,1)S(1)} %collective-permute-done.15.other.in1o) | copy-start | bytes 786436
  94.1 0.8 copy-start.7
  94.9 2.7 %collective-permute-start.16 = (bf16[64,2048]{1,0:T(8,128)(2,1)}, bf16[64,2048]{1,0:T(8,128)(2,1)}, u32[]{:S(2)}, u32[]{:S(2)}) collective-permute-start(bf16[64,2048]{1,0:T(8,128)(2,1)} %get-tuple-element.20), channel_id=1, source_target_pairs={{128,192},{192,128},{129,193},{193,129},{130,194},{194,130},{131,1... | collective-permute-start | bytes 786440 | tf_op jit(solution)/shard_map/ppermute | solution.py:297
  96.3 41.4 %collective-permute-start.12 = (bf16[64,2048]{1,0:T(8,128)(2,1)}, bf16[64,2048]{1,0:T(8,128)(2,1)S(1)}, u32[]{:S(2)}, u32[]{:S(2)}) collective-permute-start(bf16[64,2048]{1,0:T(8,128)(2,1)} %copy-done.8), channel_id=1, source_target_pairs={{256,384},{257,385},{258,386},{259,387},{260,388},{261,389},{262,3... | collective-permute-start | bytes 786440 | tf_op jit(solution)/shard_map/ppermute | solution.py:321
  99.4 49.1 %collective-permute-start.17 = (bf16[64,2048]{1,0:T(8,128)(2,1)S(1)}, bf16[64,2048]{1,0:T(8,128)(2,1)S(1)}, u32[]{:S(2)}, u32[]{:S(2)}) collective-permute-start(bf16[64,2048]{1,0:T(8,128)(2,1)S(1)} %fusion.2), channel_id=1, source_target_pairs={{128,384},{129,385},{130,386},{131,387},{132,388},{133,389},{134,3... | collective-permute-start | bytes 786440 | tf_op jit(solution)/shard_map/ppermute | solution.py:333
  137.7 13.6 %collective-permute-start.13 = (bf16[64,2048]{1,0:T(8,128)(2,1)S(1)}, bf16[64,2048]{1,0:T(8,128)(2,1)S(1)}, u32[]{:S(2)}, u32[]{:S(2)}) collective-permute-start(bf16[64,2048]{1,0:T(8,128)(2,1)S(1)} %collective-permute-done.12.mine.in3m), channel_id=1, source_target_pairs={{384,448},{448,384},{385,449},{449,385},{386,450},{450,386},{387,4... | collective-permute-start | bytes 786440 | tf_op jit(solution)/shard_map/ppermute | solution.py:297
  148.4 4.9 %collective-permute-start.18 = (bf16[64,2048]{1,0:T(8,128)(2,1)S(1)}, bf16[64,2048]{1,0:T(8,128)(2,1)S(1)}, u32[]{:S(2)}, u32[]{:S(2)}) collective-permute-start(bf16[64,2048]{1,0:T(8,128)(2,1)S(1)} %collective-permute-done.17.mem_mine), channel_id=1, source_target_pairs={{384,448},{448,384},{385,449},{449,385},{386,450},{450,386},{387,4... | collective-permute-start | bytes 786440 | tf_op jit(solution)/shard_map/ppermute | solution.py:297
  153.3 8.9 %copy-start.1 = (bf16[64,2048]{1,0:T(8,128)(2,1)S(1)}, bf16[64,2048]{1,0:T(8,128)(2,1)}, u32[]{:S(2)}) copy-start(bf16[64,2048]{1,0:T(8,128)(2,1)} %copy-done) | copy-start | bytes 786436
  153.3 8.9 %copy-start.3 = (bf16[64,2048]{1,0:T(8,128)(2,1)S(1)}, bf16[64,2048]{1,0:T(8,128)(2,1)}, u32[]{:S(2)}) copy-start(bf16[64,2048]{1,0:T(8,128)(2,1)} %copy-done.2) | copy-start | bytes 786436
  153.3 8.9 %copy-start.5 = (bf16[64,2048]{1,0:T(8,128)(2,1)S(1)}, bf16[64,2048]{1,0:T(8,128)(2,1)}, u32[]{:S(2)}) copy-start(bf16[64,2048]{1,0:T(8,128)(2,1)} %copy-done.4) | copy-start | bytes 786436
  158.3 3.8 %collective-permute-start.19 = (bf16[128,2048]{1,0:T(8,128)(2,1)S(1)}, bf16[128,2048]{1,0:T(8,128)(2,1)S(1)}, u32[]{:S(2)}, u32[]{:S(2)}) collective-permute-start(bf16[128,2048]{1,0:T(8,128)(2,1)S(1)} %shard_map.68.own), channel_id=1, source_target_pairs={{384,448},{385,449},{386,450},{387,451},{388,452},{389,453},{390,4... | collective-permute-start | bytes 1572872 | tf_op jit(solution)/shard_map/ppermute | solution.py:354
  159.6 0.7 collective-permute-start.20
